TPU v7x, 32 devices: a whole 2x2x4 slice. The times are simulated.
32 devices in a mesh: dp: 16 (over z, x, core), tensor: 2 (over y).
Axes of the slice: x: 2, y: 2, z: 4, core: 2. Of those that a mesh axis runs over, the one named last changes fastest.
Arguments:
- lang_input: bfloat16 [32, 320, 768], P('dp', 'tensor'), may hold values from -6 to 6
- visn_input: bfloat16 [32, 576, 768], P('dp', 'tensor'), may hold values from -6 to 6
- word_seg: int32 [32, 320], P('dp'), may hold values from 0 to 3, as said below
- region_seg: int32 [32, 576], P('dp'), may hold values from 0 to 3, as said below
- in_proj: bfloat16 [3, 3, 768, 768], P(None, None, None, 'tensor'), may hold values from -0.21875 to 0.21875
- out_proj: bfloat16 [3, 768, 768], P(None, 'tensor'), may hold values from -2 to 2
- up_proj: bfloat16 [2, 768, 3072], P(None, None, 'tensor'), may hold values from -0.21875 to 0.21875
- down_proj: bfloat16 [2, 3072, 768], P(None, 'tensor'), may hold values from -0.109375 to 0.109375
- ln_gain: float32 [5, 768], replicated, may hold values from 0.25 to 1.75
- ln_bias: float32 [5, 768], replicated, may hold values from -1.5 to 1.5
- lang_cotan: bfloat16 [32, 320, 768], P('dp', 'tensor'), may hold values from -6 to 6
- visn_cotan: bfloat16 [32, 576, 768], P('dp', 'tensor'), may hold values from -6 to 6
Outputs:
- lang_out: bfloat16 [32, 320, 768], P('dp', 'tensor')
- visn_out: bfloat16 [32, 576, 768], P('dp', 'tensor')
- lang_grad: float32 [32, 320, 768], P('dp', 'tensor')
- visn_grad: float32 [32, 576, 768], P('dp', 'tensor')
- inproj_grad: float32 [3, 3, 768, 768], P(None, None, 'dp', 'tensor')
- outproj_grad: float32 [3, 768, 768], P(None, 'tensor', 'dp')
- upproj_grad: float32 [2, 768, 3072], P(None, 'dp', 'tensor')
- downproj_grad: float32 [2, 3072, 768], P(None, 'tensor', 'dp')
- gain_grad: float32 [5, 768], P(None, ('dp', 'tensor'))
- bias_grad: float32 [5, 768], P(None, ('dp', 'tensor'))
Inputs may be any that keep to these rules, and one draw needn't show every extreme that they name: `word_seg`: in each row the numbers never fall along the positions, each of 0 to 3 names at least one word, and number 1 holds at positions 159 and 160. `region_seg`: in each row the numbers never fall along the positions, each of 0 to 3 names at least one region, and number 1 holds at positions 287 and 288.
All inputs are finite; a program needn't handle non-finite values.
Results may differ from a plain program's by a relative error of at most 0.028.
Values may be sent and summed in bfloat16 or wider, within the bound.
No kernel may reach another device: no remote copies, remote signals or barrier semaphores. Data moves between devices by JAX's collectives and lax.ppermute only.
A program may use at most 256 MiB of HBM per device.

v0:
```python
import math

import jax
import jax.numpy as jnp
from jax import lax
from jax.sharding import PartitionSpec as P

HD = 64


norm_eps = 1e-06


def layer_norm(tensor_in, gain_vec, bias_vec):
    row_mean = jnp.mean(tensor_in, axis=-1, keepdims=True)
    centered = tensor_in - row_mean
    spread = jnp.mean(centered * centered, axis=-1, keepdims=True)
    return centered * lax.rsqrt(spread + norm_eps) * gain_vec + bias_vec


def norm_back(tensor_in, gain_vec, bias_vec, grad_out):
    normed, pullback = jax.vjp(layer_norm, tensor_in, gain_vec, bias_vec)
    return pullback(grad_out)


def gelu_exact(tensor_in):
    return jax.nn.gelu(tensor_in, approximate=False)


def product(first_op, second_op):
    return jnp.einsum("brk,kn->brn", first_op, second_op, preferred_element_type=jnp.float32)


def product_back(first_op, second_op):
    return jnp.einsum("brn,kn->brk", first_op, second_op, preferred_element_type=jnp.float32)


def weight_grad(first_op, second_op):
    return jnp.einsum("brk,brn->kn", first_op, second_op, preferred_element_type=jnp.float32)


def split_heads(tensor_in):
    return tensor_in.reshape(tensor_in.shape[0], tensor_in.shape[1], -1, HD)


def merge_heads(tensor_in):
    return tensor_in.reshape(tensor_in.shape[0], tensor_in.shape[1], -1)


def attend_scores(queries, key_proj, allowed):
    score_raw = jnp.einsum(
        "bqhe,bkhe->bhqk",
        split_heads(queries),
        split_heads(key_proj),
        preferred_element_type=jnp.float32,
    )
    return jnp.where(allowed[:, None], 1.0 / math.sqrt(HD) * score_raw, -1000000000.0)


def attend_forward(query_in, key_in, w_query, w_key, w_value, allowed):
    queries = product(query_in, w_query).astype(jnp.bfloat16)
    key_proj = product(key_in, w_key).astype(jnp.bfloat16)
    value_proj = product(key_in, w_value).astype(jnp.bfloat16)
    masked = attend_scores(queries, key_proj, allowed)
    top_score = jnp.max(masked, axis=-1, keepdims=True)
    exp_scores = jnp.exp(masked - top_score)
    totals = jnp.sum(exp_scores, axis=-1, keepdims=True)
    attn_probs = (exp_scores / totals).astype(jnp.bfloat16)
    context = jnp.einsum(
        "bhqk,bkhe->bqhe", attn_probs, split_heads(value_proj), preferred_element_type=jnp.float32
    )
    return (
        queries,
        key_proj,
        value_proj,
        top_score + jnp.log(totals),
        merge_heads(context).astype(jnp.bfloat16),
    )


def attend_backward(query_in, key_in, w_query, w_key, w_value, allowed, saved_fwd, context_grad):
    queries = saved_fwd[0]
    key_proj = saved_fwd[1]
    value_proj = saved_fwd[2]
    masked = attend_scores(queries, key_proj, allowed)
    attn_probs = jnp.exp(masked - saved_fwd[3])
    grad_heads = split_heads(context_grad)
    probs_grad = jnp.einsum(
        "bqhe,bkhe->bhqk", grad_heads, split_heads(value_proj), preferred_element_type=jnp.float32
    )
    value_grad = merge_heads(
        jnp.einsum(
            "bhqk,bqhe->bkhe",
            attn_probs.astype(jnp.bfloat16),
            grad_heads,
            preferred_element_type=jnp.float32,
        )
    ).astype(jnp.bfloat16)
    row_inner = jnp.sum(attn_probs * probs_grad, axis=-1, keepdims=True)
    score_grad = (attn_probs * (probs_grad - row_inner) * (1.0 / math.sqrt(HD))).astype(
        jnp.bfloat16
    )
    query_grad = merge_heads(
        jnp.einsum(
            "bhqk,bkhe->bqhe", score_grad, split_heads(key_proj), preferred_element_type=jnp.float32
        )
    ).astype(jnp.bfloat16)
    key_grad = merge_heads(
        jnp.einsum(
            "bhqk,bqhe->bkhe", score_grad, split_heads(queries), preferred_element_type=jnp.float32
        )
    ).astype(jnp.bfloat16)
    return (
        weight_grad(query_in, query_grad),
        weight_grad(key_in, key_grad),
        weight_grad(key_in, value_grad),
        product_back(query_grad, w_query),
        product_back(key_grad, w_key) + product_back(value_grad, w_value),
    )


def ffn_back(normed_full, up_raw, hidden, grad_full, up_weight, down_weight):
    down_grad = weight_grad(hidden, grad_full)
    hidden_grad = product_back(grad_full, down_weight)
    gelu_out, gelu_pull = jax.vjp(gelu_exact, up_raw)
    up_low = gelu_pull(hidden_grad)[0].astype(jnp.bfloat16)
    return (weight_grad(normed_full, up_low), down_grad, product_back(up_low, up_weight))


def reduce_ffn(up_grads, down_grads):
    return (
        lax.psum_scatter(up_grads, "dp", scatter_dimension=1, tiled=True),
        lax.psum_scatter(down_grads, "dp", scatter_dimension=2, tiled=True),
    )


def spread_columns(stat_rows, data_count, tensor_count):
    return (
        stat_rows.reshape(stat_rows.shape[0], data_count, tensor_count, -1)
        .transpose(0, 2, 1, 3)
        .reshape(stat_rows.shape[0], -1)
    )


def on_device(
    lang_input,
    visn_input,
    word_seg,
    region_seg,
    in_proj,
    out_proj,
    up_proj,
    down_proj,
    ln_gain,
    ln_bias,
    lang_cotan,
    visn_cotan,
):
    lang_full, visn_full = (
        lax.all_gather(lang_input, "tensor", axis=1, tiled=True),
        lax.all_gather(visn_input, "tensor", axis=1, tiled=True),
    )
    cross_mask = word_seg[:, :, None] == region_seg[:, None, :]
    cross_back = jnp.swapaxes(cross_mask, 1, 2)
    word_mask = word_seg[:, :, None] == word_seg[:, None, :]
    region_mask = region_seg[:, :, None] == region_seg[:, None, :]

    def cross_forward():
        lang_saved = attend_forward(
            lang_full, visn_full, in_proj[0, 0], in_proj[0, 1], in_proj[0, 2], cross_mask
        )
        visn_saved = attend_forward(
            visn_full, lang_full, in_proj[0, 0], in_proj[0, 1], in_proj[0, 2], cross_back
        )
        return (lang_saved, visn_saved)

    lang_cross, visn_cross = cross_forward()
    lang_catt, visn_catt = (
        lax.psum_scatter(
            product(lang_cross[4], out_proj[0]), "tensor", scatter_dimension=1, tiled=True
        ),
        lax.psum_scatter(
            product(visn_cross[4], out_proj[0]), "tensor", scatter_dimension=1, tiled=True
        ),
    )
    lang_sum1 = lang_input.astype(jnp.float32) + lang_catt
    visn_sum1 = visn_input.astype(jnp.float32) + visn_catt
    lang_one = layer_norm(lang_sum1, ln_gain[0], ln_bias[0])
    visn_one = layer_norm(visn_sum1, ln_gain[0], ln_bias[0])
    lang_one_full, visn_one_full = (
        lax.all_gather(lang_one.astype(jnp.bfloat16), "tensor", axis=1, tiled=True),
        lax.all_gather(visn_one.astype(jnp.bfloat16), "tensor", axis=1, tiled=True),
    )
    lang_self = attend_forward(
        lang_one_full, lang_one_full, in_proj[1, 0], in_proj[1, 1], in_proj[1, 2], word_mask
    )
    visn_self = attend_forward(
        visn_one_full, visn_one_full, in_proj[2, 0], in_proj[2, 1], in_proj[2, 2], region_mask
    )
    lang_satt, visn_satt = (
        lax.psum_scatter(
            product(lang_self[4], out_proj[1]).astype(jnp.bfloat16),
            "tensor",
            scatter_dimension=1,
            tiled=True,
        ).astype(jnp.float32),
        lax.psum_scatter(
            product(visn_self[4], out_proj[2]).astype(jnp.bfloat16),
            "tensor",
            scatter_dimension=1,
            tiled=True,
        ).astype(jnp.float32),
    )
    lang_sum2 = lang_one + lang_satt
    visn_sum2 = visn_one + visn_satt
    lang_two = layer_norm(lang_sum2, ln_gain[1], ln_bias[1])
    visn_two = layer_norm(visn_sum2, ln_gain[2], ln_bias[2])
    lang_two_full, visn_two_full = (
        lax.all_gather(lang_two.astype(jnp.bfloat16), "tensor", axis=1, tiled=True),
        lax.all_gather(visn_two.astype(jnp.bfloat16), "tensor", axis=1, tiled=True),
    )
    lang_up = product(lang_two_full, up_proj[0])
    visn_up = product(visn_two_full, up_proj[1])
    lang_hidden = gelu_exact(lang_up).astype(jnp.bfloat16)
    visn_hidden = gelu_exact(visn_up).astype(jnp.bfloat16)
    lang_ffn, visn_ffn = (
        lax.psum_scatter(
            product(lang_hidden, down_proj[0]).astype(jnp.bfloat16),
            "tensor",
            scatter_dimension=1,
            tiled=True,
        ).astype(jnp.float32),
        lax.psum_scatter(
            product(visn_hidden, down_proj[1]).astype(jnp.bfloat16),
            "tensor",
            scatter_dimension=1,
            tiled=True,
        ).astype(jnp.float32),
    )
    lang_sum3 = lang_two + lang_ffn
    visn_sum3 = visn_two + visn_ffn
    lang_three = layer_norm(lang_sum3, ln_gain[3], ln_bias[3])
    visn_three = layer_norm(visn_sum3, ln_gain[4], ln_bias[4])
    lang_into3, gain_three, bias_three = norm_back(
        lang_sum3, ln_gain[3], ln_bias[3], lang_cotan.astype(jnp.float32)
    )
    visn_into3, gain_four, bias_four = norm_back(
        visn_sum3, ln_gain[4], ln_bias[4], visn_cotan.astype(jnp.float32)
    )
    lang_fgrad, visn_fgrad = (
        lax.all_gather(lang_into3.astype(jnp.bfloat16), "tensor", axis=1, tiled=True),
        lax.all_gather(visn_into3.astype(jnp.bfloat16), "tensor", axis=1, tiled=True),
    )
    lang_upg, lang_downg, lang_ffn_in = ffn_back(
        lang_two_full, lang_up, lang_hidden, lang_fgrad, up_proj[0], down_proj[0]
    )
    visn_upg, visn_downg, visn_ffn_in = ffn_back(
        visn_two_full, visn_up, visn_hidden, visn_fgrad, up_proj[1], down_proj[1]
    )
    up_grads = jnp.stack([lang_upg, visn_upg])
    down_grads = jnp.stack([lang_downg, visn_downg])
    lang_fback, visn_fback = (
        lax.psum_scatter(
            lang_ffn_in.astype(jnp.bfloat16), "tensor", scatter_dimension=1, tiled=True
        ).astype(jnp.float32),
        lax.psum_scatter(
            visn_ffn_in.astype(jnp.bfloat16), "tensor", scatter_dimension=1, tiled=True
        ).astype(jnp.float32),
    )
    lang_into2, gain_one, bias_one = norm_back(
        lang_sum2, ln_gain[1], ln_bias[1], lang_into3 + lang_fback
    )
    visn_into2, gain_two, bias_two = norm_back(
        visn_sum2, ln_gain[2], ln_bias[2], visn_into3 + visn_fback
    )
    lang_sgrad, visn_sgrad = (
        lax.all_gather(lang_into2.astype(jnp.bfloat16), "tensor", axis=1, tiled=True),
        lax.all_gather(visn_into2.astype(jnp.bfloat16), "tensor", axis=1, tiled=True),
    )
    lang_sctx = product_back(lang_sgrad, out_proj[1]).astype(jnp.bfloat16)
    visn_sctx = product_back(visn_sgrad, out_proj[2]).astype(jnp.bfloat16)
    lang_sback = attend_backward(
        lang_one_full,
        lang_one_full,
        in_proj[1, 0],
        in_proj[1, 1],
        in_proj[1, 2],
        word_mask,
        lang_self,
        lang_sctx,
    )
    visn_sback = attend_backward(
        visn_one_full,
        visn_one_full,
        in_proj[2, 0],
        in_proj[2, 1],
        in_proj[2, 2],
        region_mask,
        visn_self,
        visn_sctx,
    )
    lang_sret, visn_sret = (
        lax.psum_scatter(
            (lang_sback[3] + lang_sback[4]).astype(jnp.bfloat16),
            "tensor",
            scatter_dimension=1,
            tiled=True,
        ).astype(jnp.float32),
        lax.psum_scatter(
            (visn_sback[3] + visn_sback[4]).astype(jnp.bfloat16),
            "tensor",
            scatter_dimension=1,
            tiled=True,
        ).astype(jnp.float32),
    )
    lang_into1, gain_zl, bias_zl = norm_back(
        lang_sum1, ln_gain[0], ln_bias[0], lang_into2 + lang_sret
    )
    visn_into1, gain_zv, bias_zv = norm_back(
        visn_sum1, ln_gain[0], ln_bias[0], visn_into2 + visn_sret
    )
    lang_cgrad, visn_cgrad = (
        lax.all_gather(lang_into1.astype(jnp.bfloat16), "tensor", axis=1, tiled=True),
        lax.all_gather(visn_into1.astype(jnp.bfloat16), "tensor", axis=1, tiled=True),
    )
    lang_again, visn_again = cross_forward()
    lang_cctx = product_back(lang_cgrad, out_proj[0]).astype(jnp.bfloat16)
    visn_cctx = product_back(visn_cgrad, out_proj[0]).astype(jnp.bfloat16)
    lang_cback = attend_backward(
        lang_full,
        visn_full,
        in_proj[0, 0],
        in_proj[0, 1],
        in_proj[0, 2],
        cross_mask,
        lang_again,
        lang_cctx,
    )
    visn_cback = attend_backward(
        visn_full,
        lang_full,
        in_proj[0, 0],
        in_proj[0, 1],
        in_proj[0, 2],
        cross_back,
        visn_again,
        visn_cctx,
    )
    data_count = lax.axis_size("dp")
    tensor_count = lax.axis_size("tensor")
    gain_stack = jnp.stack([gain_zl + gain_zv, gain_one, gain_two, gain_three, gain_four])
    bias_stack = jnp.stack([bias_zl + bias_zv, bias_one, bias_two, bias_three, bias_four])
    lang_cret, visn_cret, gain_half, bias_half = (
        lax.psum_scatter(
            (lang_cback[3] + visn_cback[4]).astype(jnp.bfloat16),
            "tensor",
            scatter_dimension=1,
            tiled=True,
        ).astype(jnp.float32),
        lax.psum_scatter(
            (visn_cback[3] + lang_cback[4]).astype(jnp.bfloat16),
            "tensor",
            scatter_dimension=1,
            tiled=True,
        ).astype(jnp.float32),
        lax.psum_scatter(
            spread_columns(gain_stack, data_count, tensor_count).astype(jnp.bfloat16),
            "tensor",
            scatter_dimension=1,
            tiled=True,
        ).astype(jnp.float32),
        lax.psum_scatter(
            spread_columns(bias_stack, data_count, tensor_count).astype(jnp.bfloat16),
            "tensor",
            scatter_dimension=1,
            tiled=True,
        ).astype(jnp.float32),
    )
    cross_inproj = jnp.stack(
        [
            lang_cback[0] + visn_cback[0],
            lang_cback[1] + visn_cback[1],
            lang_cback[2] + visn_cback[2],
        ]
    )
    lang_inproj = jnp.stack([lang_sback[0], lang_sback[1], lang_sback[2]])
    visn_inproj = jnp.stack([visn_sback[0], visn_sback[1], visn_sback[2]])
    inproj_local = jnp.stack([cross_inproj, lang_inproj, visn_inproj])
    outproj_local = jnp.stack(
        [
            weight_grad(lang_again[4], lang_cgrad) + weight_grad(visn_again[4], visn_cgrad),
            weight_grad(lang_self[4], lang_sgrad),
            weight_grad(visn_self[4], visn_sgrad),
        ]
    )
    inproj_summed, outproj_summed, gain_summed, bias_summed = (
        lax.psum_scatter(inproj_local, "dp", scatter_dimension=2, tiled=True),
        lax.psum_scatter(outproj_local, "dp", scatter_dimension=2, tiled=True),
        lax.psum_scatter(gain_half, "dp", scatter_dimension=1, tiled=True),
        lax.psum_scatter(bias_half, "dp", scatter_dimension=1, tiled=True),
    )
    up_summed, down_summed = reduce_ffn(up_grads, down_grads)
    return (
        lang_three.astype(jnp.bfloat16),
        visn_three.astype(jnp.bfloat16),
        lang_into1 + lang_cret,
        visn_into1 + visn_cret,
        inproj_summed,
        outproj_summed,
        up_summed,
        down_summed,
        gain_summed,
        bias_summed,
    )


def solution(mesh):
    placed = (
        P("dp", "tensor", None),
        P("dp", "tensor", None),
        P("dp", None),
        P("dp", None),
        P(None, None, None, "tensor"),
        P(None, "tensor", None),
        P(None, None, "tensor"),
        P(None, "tensor", None),
        P(),
        P(),
        P("dp", "tensor", None),
        P("dp", "tensor", None),
    )
    return jax.shard_map(
        on_device,
        mesh=mesh,
        in_specs=placed,
        out_specs=(
            P("dp", "tensor", None),
            P("dp", "tensor", None),
            P("dp", "tensor", None),
            P("dp", "tensor", None),
            P(None, None, "dp", "tensor"),
            P(None, "tensor", "dp"),
            P(None, "dp", "tensor"),
            P(None, "tensor", "dp"),
            P(None, ("dp", "tensor")),
            P(None, ("dp", "tensor")),
        ),
        check_vma=False,
    )
```

profile of v0, /device:TPU:0, one launch (start us, length us, event | category | flops | bytes accessed | tf_op | source)
XLA Modules:
  0.0 1572.0 jit_solution(11654233313361249562)
XLA Ops:
  8.0 17.4 %all_gather.37 = bf16[2,320,768]{2,1,0:T(8,128)(2,1)S(1)} all-gather(bf16[2,160,768]{2,1,0:T(8,128)(2,1)} %param.12), channel_id=1, replica_groups=mesh['dp'=16,'tensor'=2] {'tensor'}, dimensions={1}, use_global_device_ids=true | all-gather | bytes 1474560 | tf_op jit(solution)/shard_map/all_gather | solution.py:160
  30.4 11.8 all-gather.7.cloned.1.call-done
  45.6 3.9 convolution_convert_fusion.9
  67.3 3.7 convolution_convert_fusion.7
  82.6 4.0 fusion.264
  88.0 8.5 reduce-scatter.22.cloned.1.call-done
  98.5 20.7 %all_gather.38 = bf16[2,320,768]{2,1,0:T(8,128)(2,1)S(1)} all-gather(bf16[2,160,768]{2,1,0:T(8,128)(2,1)S(1)} %fusion.224), channel_id=1, replica_groups=mesh['dp'=16,'tensor'=2] {'tensor'}, dimensions={1}, use_global_device_ids=true | all-gather | bytes 1474560 | tf_op jit(solution)/shard_map/all_gather | solution.py:191
  131.8 4.5 fusion.122
  136.3 16.0 %reduce-scatter.28.cloned.1.call-done = f32[2,288,768]{2,1,0:T(8,128)} async-done(((f32[2,576,768]{2,1,0:T(8,128)}), f32[2,288,768]{2,1,0:T(8,128)}) %reduce-scatter.28.cloned.1.call-update) | async-done | bytes 1769488 | tf_op jit(solution)/shard_map/reduce_scatter | solution.py:182
  156.0 4.1 fusion.53
  167.2 18.3 %all-gather.9.cloned.1.call-done = bf16[2,576,768]{2,1,0:T(8,128)(2,1)} async-done(((bf16[2,288,768]{2,1,0:T(8,128)(2,1)}), bf16[2,576,768]{2,1,0:T(8,128)(2,1)}) %all-gather.9.cloned.1.call-update) | async-done | bytes 1769488 | tf_op jit(solution)/shard_map/all_gather | solution.py:192
  185.5 3.6 convolution_convert_fusion.5
  191.4 3.6 convolution_convert_fusion.4
  197.2 3.6 convolution_convert_fusion.6
  203.2 10.6 fusion.6
  213.8 10.4 fusion.5
  224.2 11.7 fusion.169
  245.8 24.7 %all_gather.39 = bf16[2,320,768]{2,1,0:T(8,128)(2,1)S(1)} all-gather(bf16[2,160,768]{2,1,0:T(8,128)(2,1)S(1)} %fusion.225), channel_id=1, replica_groups=mesh['dp'=16,'tensor'=2] {'tensor'}, dimensions={1}, use_global_device_ids=true | all-gather | bytes 1474560 | tf_op jit(solution)/shard_map/all_gather | solution.py:219
  271.5 7.3 fusion.223
  282.7 10.9 multiply_convert_fusion.5
  295.0 4.3 fusion.176
  299.8 12.4 all-gather.11.cloned.1.call-done
  312.2 7.0 fusion.155
  319.2 17.0 %multiply_convert_fusion.3 = (bf16[2,576,1536]{2,1,0:T(8,128)(2,1)S(1)}, f32[2,576,1536]{2,1,0:T(8,128)}) fusion(f32[2,576,1536]{2,1,0:T(8,128)S(1)} %get-tuple-element.124, u8[576,1536]{1,0:T(8,128)(4,1)S(1)} %get-tuple-element.51, u8[576,1536]{1,0:T(8,128)(4,1)S(1)} %get-tuple-element.50), kind=kLoop, calls=%fused_computation.54 | loop fusion | flops 123863040 | bytes 19464192 | tf_op jit(solution)/shard_map/convert_element_type | solution.py:225
  338.1 5.8 fusion.159
  348.6 24.6 %all_gather.42 = bf16[2,320,768]{2,1,0:T(8,128)(2,1)S(1)} all-gather(bf16[2,160,768]{2,1,0:T(8,128)(2,1)S(1)} %add_convert_fusion.13), channel_id=1, replica_groups=mesh['dp'=16,'tensor'=2] {'tensor'}, dimensions={1}, use_global_device_ids=true | all-gather | bytes 1474560 | tf_op jit(solution)/shard_map/all_gather | solution.py:251
  373.2 4.7 add_convert_fusion.1
  392.9 6.0 convolution_bitcast_fusion
  399.6 4.7 reduce-scatter.34.cloned.1.call-done
  406.9 29.1 %all-gather.13.cloned.1.call-done = bf16[2,576,768]{2,1,0:T(8,128)(2,1)} async-done(((bf16[2,288,768]{2,1,0:T(8,128)(2,1)}), bf16[2,576,768]{2,1,0:T(8,128)(2,1)}) %all-gather.13.cloned.1.call-update) | async-done | bytes 1769488 | tf_op jit(solution)/shard_map/all_gather | solution.py:252
  436.0 10.8 add_convert_fusion
  448.6 5.8 fusion.156
  457.3 24.0 %all_gather.43 = bf16[2,320,768]{2,1,0:T(8,128)(2,1)S(1)} all-gather(bf16[2,160,768]{2,1,0:T(8,128)(2,1)S(1)} %add_convert_fusion.12), channel_id=1, replica_groups=mesh['dp'=16,'tensor'=2] {'tensor'}, dimensions={1}, use_global_device_ids=true | all-gather | bytes 1474560 | tf_op jit(solution)/shard_map/all_gather | solution.py:277
  491.8 10.8 fusion.206
  502.6 11.7 fusion.203
  518.3 4.2 fusion.200
  549.8 27.7 %all-gather.15.cloned.1.call-done = bf16[2,576,768]{2,1,0:T(8,128)(2,1)} async-done(((bf16[2,288,768]{2,1,0:T(8,128)(2,1)}), bf16[2,576,768]{2,1,0:T(8,128)(2,1)}) %all-gather.15.cloned.1.call-update) | async-done | bytes 1769488 | tf_op jit(solution)/shard_map/all_gather | solution.py:278
  577.4 3.6 convolution_convert_fusion.3
  583.4 9.9 fusion.382
  593.4 10.5 fusion.170
  603.9 27.1 %fusion.185 = bf16[2,6,64,576]{3,2,1,0:T(8,128)(2,1)} fusion(bf16[2,576,6,64]{1,3,2,0:T(8,128)(2,1)} %bitcast.429, f32[2,6,576,576]{2,3,1,0:T(8,128)} %fusion.382, f32[2,6,576,576]{2,3,1,0:T(8,128)} %get-tuple-element.123, f32[2,6,576]{2,1,0:T(8,128)S(1)} %copy-done.139, pred[2,576,576]{1,2,0:T(8,128)(4,1)S(1)} %copy-done.27), kind=kOutput, calls=%fused_computation.215 | convolution fusion | flops 553852224 | bytes 34311168 | tf_op jit(solution)/shard_map/bhqk,bqhe->bkhe/dot_general | solution.py:109
  631.0 27.0 %fusion.182 = bf16[2,6,64,576]{3,2,1,0:T(8,128)(2,1)} fusion(bf16[2,576,6,64]{1,3,2,0:T(8,128)(2,1)} %bitcast.431, f32[2,6,576,576]{2,3,1,0:T(8,128)} %fusion.382, f32[2,6,576,576]{2,3,1,0:T(8,128)} %get-tuple-element.123, f32[2,6,576]{2,1,0:T(8,128)S(1)} %copy-done.139, pred[2,576,576]{1,2,0:T(8,128)(4,1)S(1)} %copy-done.27), kind=kOutput, calls=%fused_computation.214 | convolution fusion | flops 553852224 | bytes 34311168 | tf_op jit(solution)/shard_map/bhqk,bkhe->bqhe/dot_general | solution.py:104
  666.5 20.7 %all_gather.44 = bf16[2,320,768]{2,1,0:T(8,128)(2,1)S(1)} all-gather(bf16[2,160,768]{2,1,0:T(8,128)(2,1)S(1)} %add_convert_fusion.11), channel_id=1, replica_groups=mesh['dp'=16,'tensor'=2] {'tensor'}, dimensions={1}, use_global_device_ids=true | all-gather | bytes 1474560 | tf_op jit(solution)/shard_map/all_gather | solution.py:323
  692.8 5.2 fusion.381
  698.0 35.7 %fusion.215 = bf16[2,6,64,320]{3,2,1,0:T(8,128)(2,1)} fusion(bf16[2,576,6,64]{1,3,2,0:T(8,128)(2,1)S(1)} %bitcast.415, f32[2,6,320,576]{3,2,1,0:T(8,128)} %fusion.381, f32[2,6,320,576]{3,2,1,0:T(8,128)} %copy-done.3, f32[2,6,320]{2,1,0:T(8,128)} %log_add_fusion.2, pred[2,320,576]{2,1,0:T(8,128)(4,1)} %copy-done.46), kind=kOutput, calls=%fused_computation.257 | convolution fusion | flops 307695936 | bytes 19454976 | tf_op jit(solution)/shard_map/bhqk,bkhe->bqhe/dot_general | solution.py:104
  736.4 34.9 %fusion.166 = bf16[2,6,64,576]{3,2,1,0:T(8,128)(2,1)S(1)} fusion(bf16[2,320,6,64]{1,3,2,0:T(8,128)(2,1)S(1)} %bitcast.437, f32[2,6,320,576]{3,2,1,0:T(8,128)} %fusion.381, f32[2,6,320,576]{3,2,1,0:T(8,128)} %copy-done.3, f32[2,6,320]{2,1,0:T(8,128)} %log_add_fusion.2, pred[2,320,576]{2,1,0:T(8,128)(4,1)} %copy-done.46), kind=kOutput, calls=%fused_computation.207 | convolution fusion | flops 307892544 | bytes 19454976 | tf_op jit(solution)/shard_map/bhqk,bqhe->bkhe/dot_general | solution.py:109
  774.8 3.9 fusion.244
  778.8 7.6 fusion.179
  794.7 8.0 convolution_bitcast_fusion.2
  805.4 18.7 %all-gather.17.cloned.1.call-done = bf16[2,576,768]{2,1,0:T(8,128)(2,1)} async-done(((bf16[2,288,768]{2,1,0:T(8,128)(2,1)}), bf16[2,576,768]{2,1,0:T(8,128)(2,1)}) %all-gather.17.cloned.1.call-update) | async-done | bytes 1769488 | tf_op jit(solution)/shard_map/all_gather | solution.py:324
  827.7 5.2 fusion.383
  832.9 6.4 fusion.209
  839.3 18.7 %fusion.212 = bf16[2,6,64,320]{3,2,1,0:T(8,128)(2,1)S(1)} fusion(bf16[2,576,6,64]{1,3,2,0:T(8,128)(2,1)S(1)} %bitcast.413, f32[2,6,576,320]{2,3,1,0:T(8,128)} %fusion.383, f32[2,6,576,320]{2,3,1,0:T(8,128)} %copy-done.2, f32[2,6,576]{2,1,0:T(8,128)S(1)} %copy-done.137, pred[2,576,320]{1,2,0:T(8,128)(4,1)S(1)} %copy-done.45), kind=kOutput, calls=%fused_computation.256 | convolution fusion | flops 307698752 | bytes 19467264 | tf_op jit(solution)/shard_map/bhqk,bqhe->bkhe/dot_general | solution.py:109
  862.9 8.0 pad_maximum_fusion.2
  870.9 15.4 copy.299
  888.8 18.9 %fusion.163 = bf16[2,6,64,576]{3,2,1,0:T(8,128)(2,1)S(1)} fusion(bf16[2,320,6,64]{1,3,2,0:T(8,128)(2,1)S(1)} %bitcast.433, f32[2,6,576,320]{2,3,1,0:T(8,128)} %fusion.383, f32[2,6,576,320]{2,3,1,0:T(8,128)} %copy-done.2, f32[2,6,576]{2,1,0:T(8,128)S(1)} %copy-done.138, pred[2,576,320]{1,2,0:T(8,128)(4,1)S(1)} %copy-done.45), kind=kOutput, calls=%fused_computation.206 | convolution fusion | flops 307895360 | bytes 19467264 | tf_op jit(solution)/shard_map/bhqk,bkhe->bqhe/dot_general | solution.py:104
  924.6 4.1 copy.298
  939.5 5.0 pad_maximum_fusion
  944.5 16.4 %copy.293 = f32[3,3,768,384]{3,1,0,2:T(4,128)} copy(f32[3,3,768,384]{2,3,1,0:T(8,128)} %pad_maximum_fusion) | data formatting | bytes 21233664 | tf_op jit(solution)/shard_map/stack | solution.py:388
  962.2 3.7 convolution_bitcast_fusion.1
  969.2 4.5 pad_maximum_fusion.1
  978.2 65.0 %all-reduce.5 = (f32[5,384]{1,0:T(8,128)S(1)}, f32[5,384]{1,0:T(8,128)S(1)}) all-reduce(bf16[5,384]{1,0:T(8,128)(2,1)S(1)} %copy.358, bf16[5,384]{1,0:T(8,128)(2,1)S(1)} %copy.362), channel_id=19, replica_groups=mesh['dp'=16,'tensor'=2] {'dp'}, use_global_device_ids=true, to_apply=%region_59.60.clone | all-reduce | flops 3840 | bytes 23040
  1049.4 398.9 %all-reduce.9.cloned.1.call-done = (f32[3,3,768,384]{3,1,0,2:T(4,128)}, f32[3,384,768]{1,0,2:T(4,128)}, f32[2,1536,768]{1,0,2:T(2,128)}) async-done(((f32[3,3,768,384]{3,1,0,2:T(4,128)}, f32[3,384,768]{1,0,2:T(4,128)}, f32[2,1536,768]{1,0,2:T(2,128)}), (f32[3,3,768,384]{3,1,0,2:T(4,128)}, f32[3,384,768]{1,0,2:T(4,128)}, f32[2,1536,768]{1,0,2:T(2,128)})) %all-reduce.9.cloned.1.call-update) | async-done | bytes 23592976
  1454.3 110.7 %reduce-scatter.46.cloned.1.call-done = f32[2,48,1536]{2,1,0:T(8,128)} async-done(((f32[2,768,1536]{2,1,0:T(8,128)}), f32[2,48,1536]{2,1,0:T(8,128)}) %reduce-scatter.46.cloned.1.call-update) | async-done | bytes 589840 | tf_op jit(solution)/shard_map/reduce_scatter | solution.py:132
  (622 shorter events, 249.6 us)
Async XLA Ops:
  7.2 35.1 %all-gather.7.cloned.1.call-start = ((), (), s32[]{:S(2)}) async-start(), calls=%async_computation.15 | async-start | bytes 2654208 | tf_op jit(solution)/shard_map/all_gather | solution.py:161
  7.9 88.7 %reduce-scatter.22.cloned.1.call-start = ((), (), s32[]{:S(2)}) async-start(), calls=%async_computation.16 | async-start | bytes 2949120 | tf_op jit(solution)/shard_map/reduce_scatter | solution.py:179
  25.4 16.9 %copy-start.80 = (bf16[2,320,768]{2,1,0:T(8,128)(2,1)}, bf16[2,320,768]{2,1,0:T(8,128)(2,1)S(1)}, u32[]{:S(2)}) copy-start(bf16[2,320,768]{2,1,0:T(8,128)(2,1)S(1)} %all_gather.37) | copy-start | bytes 2949124
  27.8 44.8 %copy-start.51 = (bf16[2,320,384]{1,2,0:T(8,128)(2,1)}, bf16[2,320,384]{1,2,0:T(8,128)(2,1)S(1)}, u32[]{:S(2)}) copy-start(bf16[2,320,384]{1,2,0:T(8,128)(2,1)S(1)} %copy.246) | copy-start | bytes 1474564
  30.1 21.0 %copy-start.55 = (bf16[2,320,384]{1,2,0:T(8,128)(2,1)}, bf16[2,320,384]{1,2,0:T(8,128)(2,1)S(1)}, u32[]{:S(2)}) copy-start(bf16[2,320,384]{1,2,0:T(8,128)(2,1)S(1)} %copy.236) | copy-start | bytes 1474564
  30.4 25.7 %copy-start.46 = (pred[2,320,576]{2,1,0:T(8,128)(4,1)}, pred[2,320,576]{2,1,0:T(8,128)(4,1)S(1)}, u32[]{:S(2)}) copy-start(pred[2,320,576]{2,1,0:T(8,128)(4,1)S(1)} %broadcast_compare_fusion.2) | copy-start | bytes 1105924
  64.6 87.7 %reduce-scatter.28.cloned.1.call-start = ((), (), s32[]{:S(2)}) async-start(), calls=%async_computation.19 | async-start | bytes 5308416 | tf_op jit(solution)/shard_map/reduce_scatter | solution.py:182
  82.6 14.0 copy-start.69
  86.6 98.9 %all-gather.9.cloned.1.call-start = ((), (), s32[]{:S(2)}) async-start(), calls=%async_computation.20 | async-start | bytes 2654208 | tf_op jit(solution)/shard_map/all_gather | solution.py:192
  87.3 34.6 %copy-start.111 = (f32[768]{0:T(1024)}, f32[768]{0:T(1024)S(1)}, u32[]{:S(2)}) copy-start(f32[768]{0:T(1024)S(1)} %get-tuple-element.78) | copy-start | bytes 9220
  87.5 44.3 %copy-start.64 = (pred[2,320,320]{1,2,0:T(8,128)(4,1)}, pred[2,320,320]{1,2,0:T(8,128)(4,1)S(1)}, u32[]{:S(2)}) copy-start(pred[2,320,320]{1,2,0:T(8,128)(4,1)S(1)} %broadcast_compare_fusion.3) | copy-start | bytes 614404
  88.0 136.2 %copy-start.26 = (pred[2,576,576]{1,2,0:T(8,128)(4,1)}, pred[2,576,576]{1,2,0:T(8,128)(4,1)S(1)}, u32[]{:S(2)}) copy-start(pred[2,576,576]{1,2,0:T(8,128)(4,1)S(1)} %broadcast_compare_fusion) | copy-start | bytes 1990660
  98.0 145.2 %copy-start.4 = (f32[2,160,768]{2,1,0:T(8,128)}, f32[2,160,768]{2,1,0:T(8,128)S(1)}, u32[]{:S(2)}) copy-start(f32[2,160,768]{2,1,0:T(8,128)S(1)} %get-tuple-element.112) | copy-start | bytes 2949124
  98.0 27.4 %copy-start.123 = (f32[2,160]{1,0:T(2,128)}, f32[2,160]{1,0:T(2,128)S(1)}, u32[]{:S(2)}) copy-start(f32[2,160]{1,0:T(2,128)S(1)} %broadcast_multiply_fusion.5) | copy-start | bytes 3844
  98.3 27.1 %copy-start.161 = (f32[2,160]{1,0:T(2,128)}, f32[2,160]{1,0:T(2,128)S(1)}, u32[]{:S(2)}) copy-start(f32[2,160]{1,0:T(2,128)S(1)} %multiply_reduce_fusion.17) | copy-start | bytes 3844
  98.3 27.1 %copy-start.128 = (f32[2,160]{1,0:T(2,128)}, f32[2,160]{1,0:T(2,128)S(1)}, u32[]{:S(2)}) copy-start(f32[2,160]{1,0:T(2,128)S(1)} %fusion.303) | copy-start | bytes 3844
  122.3 14.0 copy-start.60
  154.3 124.9 %copy-start = (f32[2,288,768]{2,1,0:T(8,128)}, f32[2,288,768]{2,1,0:T(8,128)S(1)}, u32[]{:S(2)}) copy-start(f32[2,288,768]{2,1,0:T(8,128)S(1)} %get-tuple-element.104) | copy-start | bytes 5308420
  154.3 124.9 %copy-start.109 = (f32[2,288]{1,0:T(2,128)}, f32[2,288]{1,0:T(2,128)S(1)}, u32[]{:S(2)}) copy-start(f32[2,288]{1,0:T(2,128)S(1)} %broadcast_multiply_fusion.2) | copy-start | bytes 6916
  156.0 87.2 %reduce-scatter.24.cloned.1.call-start = ((), (), s32[]{:S(2)}) async-start(), calls=%async_computation.17 | async-start | bytes 1474560 | tf_op jit(solution)/shard_map/reduce_scatter | solution.py:201
  167.1 112.0 %reduce-scatter.30.cloned.1.call-start = ((), (), s32[]{:S(2)}) async-start(), calls=%async_computation.21 | async-start | bytes 2654208 | tf_op jit(solution)/shard_map/reduce_scatter | solution.py:207
  240.3 71.9 %all-gather.11.cloned.1.call-start = ((), (), s32[]{:S(2)}) async-start(), calls=%async_computation.22 | async-start | bytes 2654208 | tf_op jit(solution)/shard_map/all_gather | solution.py:220
  244.9 33.9 %copy-start.163 = (f32[2,160]{1,0:T(2,128)}, f32[2,160]{1,0:T(2,128)S(1)}, u32[]{:S(2)}) copy-start(f32[2,160]{1,0:T(2,128)S(1)} %multiply_reduce_fusion.16) | copy-start | bytes 3844
  281.3 12.3 copy-start.157
  281.3 101.3 %copy-start.121 = (f32[2,288]{1,0:T(2,128)}, f32[2,288]{1,0:T(2,128)S(1)}, u32[]{:S(2)}) copy-start(f32[2,288]{1,0:T(2,128)S(1)} %fusion.301) | copy-start | bytes 6916
  282.6 61.3 %reduce-scatter.26.cloned.1.call-start = ((), (), s32[]{:S(2)}) async-start(), calls=%async_computation.18 | async-start | bytes 1474560 | tf_op jit(solution)/shard_map/reduce_scatter | solution.py:227
  299.3 83.3 %reduce-scatter.32.cloned.1.call-start = ((), (), s32[]{:S(2)}) async-start(), calls=%async_computation.23 | async-start | bytes 2654208 | tf_op jit(solution)/shard_map/reduce_scatter | solution.py:233
  319.2 17.0 %copy-start.25 = (f32[2,576,1536]{2,1,0:T(8,128)}, f32[2,576,1536]{2,1,0:T(8,128)S(1)}, u32[]{:S(2)}) copy-start(f32[2,576,1536]{2,1,0:T(8,128)S(1)} %get-tuple-element.124) | copy-start | bytes 21233668
  343.9 60.5 %reduce-scatter.34.cloned.1.call-start = ((), (), s32[]{:S(2)}) async-start(), calls=%async_computation.24 | async-start | bytes 1474560 | tf_op jit(solution)/shard_map/reduce_scatter | solution.py:263
  345.4 27.8 %copy-start.37 = (f32[2,320,1536]{2,1,0:T(8,128)S(1)}, f32[2,320,1536]{2,1,0:T(8,128)}, u32[]{:S(2)}) copy-start(f32[2,320,1536]{2,1,0:T(8,128)} %get-tuple-element.108) | copy-start | bytes 11796484
  345.7 27.5 %copy-start.36 = (f32[2,320,1536]{2,1,0:T(8,128)S(1)}, f32[2,320,1536]{2,1,0:T(8,128)}, u32[]{:S(2)}) copy-start(f32[2,320,1536]{2,1,0:T(8,128)} %get-tuple-element.119) | copy-start | bytes 11796484
  346.3 33.0 %slice-start = ((s8[4718592]{0:T(1024)(128)(4,1)}), s8[4194304]{0:T(1024)(128)(4,1)S(1)}, s32[]{:S(2)}) async-start(s8[4718592]{0:T(1024)(128)(4,1)} %bitcast.478), calls=%async_computation.37 | async-start | bytes 8388608
  382.0 54.1 %all-gather.13.cloned.1.call-start = ((), (), s32[]{:S(2)}) async-start(), calls=%async_computation.26 | async-start | bytes 2654208 | tf_op jit(solution)/shard_map/all_gather | solution.py:252
  390.3 142.2 %reduce-scatter.38.cloned.1.call-start = ((), (), s32[]{:S(2)}) async-start(), calls=%async_computation.27 | async-start | bytes 2654208 | tf_op jit(solution)/shard_map/reduce_scatter | solution.py:266
  392.9 13.9 copy-start.164
  454.5 91.5 %reduce-scatter.36.cloned.1.call-start = ((), (), s32[]{:S(2)}) async-start(), calls=%async_computation.25 | async-start | bytes 1474560 | tf_op jit(solution)/shard_map/reduce_scatter | solution.py:303
  456.3 31.3 %copy-start.177 = (bf16[768]{0:T(1024)(128)(2,1)S(1)}, bf16[768]{0:T(1024)(128)(2,1)}, u32[]{:S(2)}) copy-start(bf16[768]{0:T(1024)(128)(2,1)} %get-tuple-element.62) | copy-start | bytes 4612
  456.3 32.0 %copy-start.57 = (bf16[2,320,384]{1,2,0:T(8,128)(2,1)S(1)}, bf16[2,320,384]{1,2,0:T(8,128)(2,1)}, u32[]{:S(2)}) copy-start(bf16[2,320,384]{1,2,0:T(8,128)(2,1)} %copy.239) | copy-start | bytes 1474564
  456.3 25.0 %copy-start.146 = (f32[2,160]{1,0:T(2,128)}, f32[2,160]{1,0:T(2,128)S(1)}, u32[]{:S(2)}) copy-start(f32[2,160]{1,0:T(2,128)S(1)} %negate_multiply_fusion.6) | copy-start | bytes 3844
  526.2 51.3 %all-gather.15.cloned.1.call-start = ((), (), s32[]{:S(2)}) async-start(), calls=%async_computation.28 | async-start | bytes 2654208 | tf_op jit(solution)/shard_map/all_gather | solution.py:278
  538.6 249.2 %reduce-scatter.40.cloned.1.call-start = ((), (), s32[]{:S(2)}) async-start(), calls=%async_computation.29 | async-start | bytes 2654208 | tf_op jit(solution)/shard_map/reduce_scatter | solution.py:309
  549.7 116.7 %copy-start.21 = (f32[2,160,768]{2,1,0:T(8,128)}, f32[2,160,768]{2,1,0:T(8,128)S(1)}, u32[]{:S(2)}) copy-start(f32[2,160,768]{2,1,0:T(8,128)S(1)} %get-tuple-element.92) | copy-start | bytes 2949124
  549.7 33.7 %copy-start.34 = (bf16[2,576,384]{1,2,0:T(8,128)(2,1)S(1)}, bf16[2,576,384]{1,2,0:T(8,128)(2,1)}, u32[]{:S(2)}) copy-start(bf16[2,576,384]{1,2,0:T(8,128)(2,1)} %copy.248) | copy-start | bytes 2654212
  549.7 116.6 %copy-start.165 = (f32[2,160]{1,0:T(2,128)}, f32[2,160]{1,0:T(2,128)S(1)}, u32[]{:S(2)}) copy-start(f32[2,160]{1,0:T(2,128)S(1)} %negate_multiply_fusion.5) | copy-start | bytes 3844
  603.9 58.9 %copy-start.38 = (bf16[2,6,64,576]{3,2,1,0:T(8,128)(2,1)}, bf16[2,6,64,576]{3,2,1,0:T(8,128)(2,1)S(1)}, u32[]{:S(2)}) copy-start(bf16[2,6,64,576]{3,2,1,0:T(8,128)(2,1)S(1)} %fusion.170) | copy-start | bytes 2654212
  666.3 24.8 %copy-start.92 = (bf16[2,6,64,320]{3,2,1,0:T(8,128)(2,1)S(1)}, bf16[2,6,64,320]{3,2,1,0:T(8,128)(2,1)}, u32[]{:S(2)}) copy-start(bf16[2,6,64,320]{3,2,1,0:T(8,128)(2,1)} %copy-done.91) | copy-start | bytes 1474564
  666.3 157.8 %all-gather.17.cloned.1.call-start = ((), (), s32[]{:S(2)}) async-start(), calls=%async_computation.30 | async-start | bytes 2654208 | tf_op jit(solution)/shard_map/all_gather | solution.py:324
  666.5 26.2 %copy-start.43 = (bf16[2,576,384]{1,2,0:T(8,128)(2,1)S(1)}, bf16[2,576,384]{1,2,0:T(8,128)(2,1)}, u32[]{:S(2)}) copy-start(bf16[2,576,384]{1,2,0:T(8,128)(2,1)} %copy-done.42) | copy-start | bytes 2654212
  697.9 35.7 %copy-start.82 = (bf16[2,320,768]{2,1,0:T(8,128)(2,1)S(1)}, bf16[2,320,768]{2,1,0:T(8,128)(2,1)}, u32[]{:S(2)}) copy-start(bf16[2,320,768]{2,1,0:T(8,128)(2,1)} %copy-done.80) | copy-start | bytes 2949124
  697.9 38.5 %copy-start.56 = (bf16[2,320,384]{1,2,0:T(8,128)(2,1)S(1)}, bf16[2,320,384]{1,2,0:T(8,128)(2,1)}, u32[]{:S(2)}) copy-start(bf16[2,320,384]{1,2,0:T(8,128)(2,1)} %copy-done.55) | copy-start | bytes 1474564
  736.4 34.9 %copy-start.95 = (bf16[2,6,64,320]{3,2,1,0:T(8,128)(2,1)S(1)}, bf16[2,6,64,320]{3,2,1,0:T(8,128)(2,1)}, u32[]{:S(2)}) copy-start(bf16[2,6,64,320]{3,2,1,0:T(8,128)(2,1)} %fusion.215) | copy-start | bytes 1474564
  794.7 181.6 %reduce-scatter.50.cloned.1.call-start = ((), (), s32[]{:S(2)}) async-start(), calls=%async_computation.35 | async-start | bytes 294912
  802.7 25.0 %copy-start.54 = (bf16[2,320,384]{1,2,0:T(8,128)(2,1)S(1)}, bf16[2,320,384]{1,2,0:T(8,128)(2,1)}, u32[]{:S(2)}) copy-start(bf16[2,320,384]{1,2,0:T(8,128)(2,1)} %copy-done.53) | copy-start | bytes 1474564
  804.2 173.0 %reduce-scatter.48.cloned.1.call-start = ((), (), s32[]{:S(2)}) async-start(), calls=%async_computation.34 | async-start | bytes 294912
  805.4 239.2 %reduce-scatter.42.cloned.1.call-start = ((), (), s32[]{:S(2)}) async-start(), calls=%async_computation.31 | async-start | bytes 1474560 | tf_op jit(solution)/shard_map/reduce_scatter | solution.py:354
  839.3 20.8 %copy-start.89 = (bf16[2,6,64,320]{3,2,1,0:T(8,128)(2,1)}, bf16[2,6,64,320]{3,2,1,0:T(8,128)(2,1)S(1)}, u32[]{:S(2)}) copy-start(bf16[2,6,64,320]{3,2,1,0:T(8,128)(2,1)S(1)} %fusion.209) | copy-start | bytes 1474564
  862.8 183.9 %reduce-scatter.44.cloned.1.call-start = ((), (), s32[]{:S(2)}) async-start(), calls=%async_computation.32 | async-start | bytes 2654208 | tf_op jit(solution)/shard_map/reduce_scatter | solution.py:360
  870.9 15.4 copy-start.77
  914.0 534.4 %all-reduce.9.cloned.1.call-start = ((), (), s32[]{:S(2)}) async-start(), calls=%async_computation.36 | async-start | bytes 56623104
  961.0 604.0 %reduce-scatter.46.cloned.1.call-start = ((), (), s32[]{:S(2)}) async-start(), calls=%async_computation.33 | async-start | bytes 10027008 | tf_op jit(solution)/shard_map/reduce_scatter | solution.py:132
  973.7 70.9 %copy-start.22 = (f32[2,160,768]{2,1,0:T(8,128)S(1)}, f32[2,160,768]{2,1,0:T(8,128)}, u32[]{:S(2)}) copy-start(f32[2,160,768]{2,1,0:T(8,128)} %copy-done.21) | copy-start | bytes 2949124
  973.7 70.9 %copy-start.166 = (f32[2,160]{1,0:T(2,128)S(1)}, f32[2,160]{1,0:T(2,128)}, u32[]{:S(2)}) copy-start(f32[2,160]{1,0:T(2,128)} %copy-done.165) | copy-start | bytes 3844
  973.7 73.0 %copy-start.14 = (f32[2,288,768]{2,1,0:T(8,128)S(1)}, f32[2,288,768]{2,1,0:T(8,128)}, u32[]{:S(2)}) copy-start(f32[2,288,768]{2,1,0:T(8,128)} %copy-done.13) | copy-start | bytes 5308420
  973.7 73.0 %copy-start.155 = (f32[2,288]{1,0:T(2,128)S(1)}, f32[2,288]{1,0:T(2,128)}, u32[]{:S(2)}) copy-start(f32[2,288]{1,0:T(2,128)} %copy-done.154) | copy-start | bytes 6916
  (153 other events, 702.7 us)
Sparse Core Ops, SparseCore 0:
  9.6 32.6 all-gather.6
  64.7 31.8 reduce-scatter.21
  98.9 53.3 reduce-scatter.27
  156.1 29.3 all-gather.8
  187.6 19.5 reduce-scatter.23
  240.4 38.7 reduce-scatter.29
  282.7 29.4 all-gather.10
  314.5 19.5 reduce-scatter.25
  344.0 38.5 reduce-scatter.31
  384.7 19.5 reduce-scatter.33
  406.5 29.4 all-gather.12
  454.6 37.0 reduce-scatter.37
  526.3 19.5 reduce-scatter.35
  548.0 29.4 all-gather.14
  666.4 34.0 reduce-scatter.39
  794.6 29.4 all-gather.16
  826.8 10.9 reduce-scatter.49
  840.4 10.9 reduce-scatter.47
  863.0 19.6 reduce-scatter.41
  914.1 28.2 reduce-scatter.43
  961.1 487.1 all-reduce.8
  1453.5 111.3 reduce-scatter.45
where the time goes:
time: 1580 us; the launch traced here: 1570 us
  waiting for transfers between devices  659 us (42%)
  matrix products  470 us (30%)
  blocking collectives  197 us (12%)
  other arithmetic  120 us (8%)
  local copies, waits for them, and re-layouts  106 us (7%)
  between operations  18.3 us (1%)
    unnamed x25, waiting for transfers between devices  400 us
    reduce_scatter x1, waiting for transfers between devices, reduce_ffn(): lax.psum_scatter(up_grads, 'dp', scatter_dimension=1, tiled=True)  111 us
    dot_general x4, matrix products, attend_backward(): jnp.einsum('bhqk,bkhe->bqhe', score_grad, split_heads(key_proj), preferre...  93.3 us
    dot_general x4, matrix products, attend_backward(): jnp.einsum('bhqk,bqhe->bkhe', score_grad, split_heads(queries), preferred...  91.5 us
    dot_general x20, matrix products, product(): jnp.einsum('brk,kn->brn', first_op, second_op, preferred_element_type=jnp...  72.4 us
    dot_general x20, matrix products, product_back(): jnp.einsum('brn,kn->brk', first_op, second_op, preferred_element_type=jnp...  68.5 us
    unnamed x1, blocking collectives  65 us
    dot_general x20, matrix products, weight_grad(): jnp.einsum('brk,brn->kn', first_op, second_op, preferred_element_type=jnp...  50.8 us
  transfers between devices with their start and end apart: 22, of which 13 were waited for; matrix products, arithmetic and copies ran while one was open for 34% of the time, Pallas kernels for 0%

commit v1 on v0

v1 whole, which is shorter than its diff:
```python
import math

import jax
import jax.numpy as jnp
from jax import lax
from jax.sharding import PartitionSpec as P

HD = 64
EPS = 1e-06
BF = jnp.bfloat16
F32 = jnp.float32
SWAP = [(0, 1), (1, 0)]


def norm_stats(tensor_in):
    row_mean = jnp.mean(tensor_in, axis=-1, keepdims=True)
    centered = tensor_in - row_mean
    spread = jnp.mean(centered * centered, axis=-1, keepdims=True)
    inv = lax.rsqrt(spread + EPS)
    return centered * inv, inv


def norm_back(normed, inv, gain, grad):
    t = grad * gain
    dh = inv * (t - jnp.mean(t, -1, keepdims=True) - normed * jnp.mean(t * normed, -1, keepdims=True))
    return dh, jnp.sum(grad * normed, 0), jnp.sum(grad, 0)


def dot(a, b):
    return jnp.dot(a, b, preferred_element_type=F32)


def dot_nt(a, b):
    return lax.dot_general(a, b, (((1,), (1,)), ((), ())), preferred_element_type=F32)


def dot_tn(a, b):
    return lax.dot_general(a, b, (((0,), (0,)), ((), ())), preferred_element_type=F32)


def heads(a):
    return a.reshape(a.shape[0], -1, HD)


def flat(a):
    return a.reshape(a.shape[0], -1)


def attend(q, k, v, allowed):
    raw = jnp.einsum("qhe,khe->hqk", heads(q), heads(k), preferred_element_type=F32)
    masked = jnp.where(allowed[None], raw * (1.0 / math.sqrt(HD)), -1e9)
    top = jnp.max(masked, -1, keepdims=True)
    ex = jnp.exp(masked - top)
    probs = (ex / jnp.sum(ex, -1, keepdims=True)).astype(BF)
    ctx = jnp.einsum("hqk,khe->qhe", probs, heads(v), preferred_element_type=F32)
    return flat(ctx).astype(BF), probs


def attend_back(q, k, v, probs, dctx):
    dh = heads(dctx)
    dprobs = jnp.einsum("qhe,khe->hqk", dh, heads(v), preferred_element_type=F32)
    dv = jnp.einsum("hqk,qhe->khe", probs, dh, preferred_element_type=F32)
    pf = probs.astype(F32)
    inner = jnp.sum(pf * dprobs, -1, keepdims=True)
    ds = (pf * (dprobs - inner) * (1.0 / math.sqrt(HD))).astype(BF)
    dq = jnp.einsum("hqk,khe->qhe", ds, heads(k), preferred_element_type=F32)
    dk = jnp.einsum("hqk,qhe->khe", ds, heads(q), preferred_element_type=F32)
    return flat(dq).astype(BF), flat(dk).astype(BF), flat(dv).astype(BF)


def gelu_pair(u):
    cdf = 0.5 * (1.0 + lax.erf(u * (1.0 / math.sqrt(2.0))))
    pdf = jnp.exp(-0.5 * u * u) * (1.0 / math.sqrt(2.0 * math.pi))
    return (u * cdf).astype(BF), cdf + u * pdf


def on_device(
    lang_input, visn_input, word_seg, region_seg, in_proj, out_proj, up_proj, down_proj,
    ln_gain, ln_bias, lang_cotan, visn_cotan,
):
    n_dp = lax.axis_size("dp")
    bits = n_dp.bit_length() - 1
    t = lax.axis_index("tensor")
    d = lax.axis_index("dp")

    def xor(value):
        return [(i, i ^ value) for i in range(n_dp)]

    def swap_row(x):
        own = lax.dynamic_index_in_dim(x, t, 0, keepdims=False)
        other = lax.dynamic_index_in_dim(x, 1 - t, 0, keepdims=False)
        return jnp.concatenate([own, lax.ppermute(other, "tensor", SWAP)], 0)

    def own_seg(seg):
        row = lax.dynamic_index_in_dim(seg, t, 0, keepdims=False)
        half = row.shape[0] // 2
        return jnp.where(t == 0, row, jnp.concatenate([row[half:], row[:half]]))

    piece = (d & 1) * 2 + ((d >> 1) & 1)

    def gather(w, axis):
        size = w.shape[axis] // 4
        a = lax.ppermute(lax.dynamic_slice_in_dim(w, piece * size, size, axis), "tensor", SWAP)
        b = lax.ppermute(a, "dp", xor(2))
        first = (d >> 1) & 1 == 0
        pair = jnp.where(first, jnp.concatenate([a, b], axis), jnp.concatenate([b, a], axis))
        other = lax.ppermute(pair, "dp", xor(1))
        low = d & 1 == 0
        return jnp.where(low, jnp.concatenate([pair, other], axis), jnp.concatenate([other, pair], axis))

    lang = swap_row(lang_input)
    visn = swap_row(visn_input)
    lw = lang.shape[0]
    lv = visn.shape[0]
    wseg = own_seg(word_seg)
    rseg = own_seg(region_seg)
    win = [(in_proj[s], gather(in_proj[s], 1)) for s in range(3)]
    wout = [(out_proj[s], gather(out_proj[s], 0)) for s in range(3)]
    wup = [(up_proj[s], gather(up_proj[s], 0)) for s in range(2)]
    wdown = [(down_proj[s], gather(down_proj[s], 0)) for s in range(2)]

    cross_mask = wseg[:, None] == rseg[None, :]
    word_mask = wseg[:, None] == wseg[None, :]
    region_mask = rseg[:, None] == rseg[None, :]

    def qkv(x, w):
        return [dot(x, w[i]).astype(BF) for i in range(3)]

    both = jnp.concatenate([lang, visn], 0)
    cq = [qkv(both, win[0][h]) for h in range(2)]
    cl = [attend(cq[h][0][:lw], cq[h][1][lw:], cq[h][2][lw:], cross_mask) for h in range(2)]
    cv = [attend(cq[h][0][lw:], cq[h][1][:lw], cq[h][2][:lw], cross_mask.T) for h in range(2)]
    cctx = [jnp.concatenate([cl[h][0], cv[h][0]], 0) for h in range(2)]
    h1 = both.astype(F32) + dot(cctx[0], wout[0][0]) + dot(cctx[1], wout[0][1])
    n1, i1 = norm_stats(h1)
    one = n1 * ln_gain[0] + ln_bias[0]
    one_low = one.astype(BF)
    streams = [(0, lw, word_mask), (lw, lw + lv, region_mask)]
    saved = []
    for j, (lo, hi, mask) in enumerate(streams):
        x1 = one_low[lo:hi]
        sq = [qkv(x1, win[1 + j][h]) for h in range(2)]
        sa = [attend(sq[h][0], sq[h][1], sq[h][2], mask) for h in range(2)]
        h2 = one[lo:hi] + dot(sa[0][0], wout[1 + j][0]) + dot(sa[1][0], wout[1 + j][1])
        n2, i2 = norm_stats(h2)
        two = n2 * ln_gain[1 + j] + ln_bias[1 + j]
        x2 = two.astype(BF)
        gel = [gelu_pair(dot(x2, wup[j][h])) for h in range(2)]
        h3 = two + dot(gel[0][0], wdown[j][0]) + dot(gel[1][0], wdown[j][1])
        n3, i3 = norm_stats(h3)
        three = n3 * ln_gain[3 + j] + ln_bias[3 + j]
        saved.append((x1, sq, sa, n2, i2, x2, gel, n3, i3, three.astype(BF)))

    def send_back(x, half):
        back = lax.ppermute(x[half:], "tensor", SWAP)
        mine = x[:half]
        back = back.astype(mine.dtype)
        return jnp.where(t == 0, jnp.stack([mine, back]), jnp.stack([back, mine]))

    lang_out = send_back(saved[0][9], lw // 2)
    visn_out = send_back(saved[1][9], lv // 2)

    def reduce(own, rem, order):
        pair = jnp.stack([own, rem])
        g = pair.astype(BF).reshape((2,) + (2,) * bits + (-1, own.shape[-1]))
        axes = [-1] + list(range(bits - 1, -1, -1))
        for b in order:
            if b < 0:
                g = g[0].astype(F32) + lax.ppermute(g[1], "tensor", SWAP).astype(F32)
                axes.remove(-1)
            else:
                ax = axes.index(b) if -1 not in axes else axes.index(b)
                bit = (d >> b) & 1
                send = lax.dynamic_index_in_dim(g, 1 - bit, ax, keepdims=False)
                keep = lax.dynamic_index_in_dim(g, bit, ax, keepdims=False)
                g = keep.astype(F32) + lax.ppermute(send, "dp", xor(1 << b)).astype(F32)
                axes.remove(b)
            if axes:
                g = g.astype(BF)
        return g

    rest = list(range(2, bits))
    y_first = [0, -1, 1] + rest
    x_first = [0, 1, -1] + rest

    dlang = swap_row(lang_cotan).astype(F32)
    dvisn = swap_row(visn_cotan).astype(F32)
    d_one = []
    up_g, down_g, in_g, out_g = [], [], [None], [None]
    gains = [None] * 5
    biases = [None] * 5
    for j, (lo, hi, mask) in enumerate(streams):
        x1, sq, sa, n2, i2, x2, gel, n3, i3, _ = saved[j]
        dh3, gains[3 + j], biases[3 + j] = norm_back(n3, i3, ln_gain[3 + j], (dlang, dvisn)[j])
        e = dh3.astype(BF)
        dx2 = dh3
        ups, downs = [], []
        for h in range(2):
            downs.append(dot_tn(e, gel[h][0]))
            du = (dot_nt(e, wdown[j][h]) * gel[h][1]).astype(BF)
            ups.append(dot_tn(x2, du))
            dx2 = dx2 + dot_nt(du, wup[j][h])
        order = (y_first, x_first)[j]
        down_g.append(reduce(downs[0], downs[1], order))
        up_g.append(reduce(ups[0], ups[1], order))
        dh2, gains[1 + j], biases[1 + j] = norm_back(n2, i2, ln_gain[1 + j], dx2)
        g2 = dh2.astype(BF)
        dx1 = dh2
        ins, outs = [], []
        for h in range(2):
            outs.append(dot_tn(g2, sa[h][0]))
            dctx = dot_nt(g2, wout[1 + j][h]).astype(BF)
            dqkv = attend_back(sq[h][0], sq[h][1], sq[h][2], sa[h][1], dctx)
            ins.append(jnp.concatenate([dot_tn(x1, g) for g in dqkv], 1))
            for i in range(3):
                dx1 = dx1 + dot_nt(dqkv[i], win[1 + j][h][i])
        out_g.append(reduce(outs[0], outs[1], order))
        in_g.append(reduce(ins[0], ins[1], order))
        d_one.append(dx1)

    d1 = jnp.concatenate(d_one, 0)
    dh1, gains[0], biases[0] = norm_back(n1, i1, ln_gain[0], d1)
    g1 = dh1.astype(BF)
    dx = dh1
    ins, outs = [], []
    for h in range(2):
        q, k, v = cq[h]
        outs.append(dot_tn(g1, cctx[h]))
        dctx = dot_nt(g1, wout[0][h]).astype(BF)
        ql, kv, vv = attend_back(q[:lw], k[lw:], v[lw:], cl[h][1], dctx[:lw])
        qv, kl, vl = attend_back(q[lw:], k[:lw], v[:lw], cv[h][1], dctx[lw:])
        dqkv = [jnp.concatenate(p, 0) for p in ((ql, qv), (kl, kv), (vl, vv))]
        ins.append(jnp.concatenate([dot_tn(both, g) for g in dqkv], 1))
        for i in range(3):
            dx = dx + dot_nt(dqkv[i], win[0][h][i])
    out_g[0] = reduce(outs[0], outs[1], y_first)
    in_g[0] = reduce(ins[0], ins[1], x_first)

    def return_grad(x):
        half = x.shape[0] // 2
        back = lax.ppermute(x[half:].astype(BF), "tensor", SWAP).astype(F32)
        return jnp.where(t == 0, jnp.stack([x[:half], back]), jnp.stack([back, x[:half]]))

    lang_grad = return_grad(dx[:lw])
    visn_grad = return_grad(dx[lw:])

    stats = lax.psum(jnp.stack(gains + biases), ("dp", "tensor"))
    width = stats.shape[1] // (n_dp * 2)
    stats = lax.dynamic_slice_in_dim(stats, (d * 2 + t) * width, width, 1)

    def split_in(g):
        return jnp.swapaxes(g.reshape(g.shape[0], 3, -1), 0, 1)

    return (
        lang_out,
        visn_out,
        lang_grad,
        visn_grad,
        jnp.stack([split_in(g) for g in in_g]),
        jnp.stack([g.T for g in out_g]),
        jnp.stack(up_g),
        jnp.stack([g.T for g in down_g]),
        stats[:5],
        stats[5:],
    )


def solution(mesh):
    rows = P("dp", "tensor", None)
    placed = (
        rows, rows, P("dp", None), P("dp", None),
        P(None, None, None, "tensor"), P(None, "tensor", None), P(None, None, "tensor"), P(None, "tensor", None),
        P(), P(), rows, rows,
    )
    return jax.shard_map(
        on_device,
        mesh=mesh,
        in_specs=placed,
        out_specs=(
            rows, rows, rows, rows,
            P(None, None, "dp", "tensor"), P(None, "tensor", "dp"), P(None, "dp", "tensor"), P(None, "tensor", "dp"),
            P(None, ("dp", "tensor")), P(None, ("dp", "tensor")),
        ),
        check_vma=False,
    )
```

time: 1580 us -> 1120 us (0.71)
  waiting for transfers between devices: 659 us -> 283 us
  blocking collectives: 197 us -> 41.3 us
  starting transfers between devices: 1.71 us -> 83.3 us
  matrix products: 470 us -> 429 us
  local copies, waits for them, and re-layouts: 106 us -> 137 us
    unnamed x25 -> x0, waiting for transfers between devices: 400 us -> none
    ppermute x0 -> x88, waiting for transfers between devices: none -> 283 us  [the longest x40 158 us: reduce(): g = keep.astype(F32) + lax.ppermute(send, 'dp', xor(1 << b)).astype(F32)]
    reduce_scatter x13 -> x0, waiting for transfers between devices: 141 us -> none  [the longest x1 111 us: reduce_ffn(): lax.psum_scatter(up_grads, 'dp', scatter_dimension=1, tiled=True)]
    all_gather x6 -> x0, blocking collectives: 132 us -> none  [the longest x1 24.7 us: on_device(): lax.all_gather(lang_two.astype(jnp.bfloat16), 'tensor', axis=1, tiled=True)]
    all_gather x6 -> x0, waiting for transfers between devices: 118 us -> none  [the longest x1 29.1 us: on_device(): lax.all_gather(visn_into3.astype(jnp.bfloat16), 'tensor', axis=1, tiled=T...]
    ppermute x0 -> x88, starting transfers between devices: none -> 83.3 us  [the longest x40 42.6 us: reduce(): g = keep.astype(F32) + lax.ppermute(send, 'dp', xor(1 << b)).astype(F32)]
    dot_general x84 -> x136, matrix products: 470 us -> 393 us  [the longest x32 76 us: dot_nt(): lax.dot_general(a, b, (((1,), (1,)), ((), ())), preferred_element_type=F32)]
    unnamed x1 -> x0, blocking collectives: 65 us -> none
  transfers between devices with their start and end apart: 22 -> 88, of which waited for: 13 -> 44; matrix products, arithmetic and copies ran while one was open for 34% -> 38% of each run, Pallas kernels for 0% -> 0%
where the time goes in v1:
time: 1120 us; the launch traced here: 1100 us
  matrix products  429 us (38%)
  waiting for transfers between devices  283 us (25%)
  local copies, waits for them, and re-layouts  137 us (12%)
  other arithmetic  125 us (11%)
  starting transfers between devices  83.3 us (7%)
  blocking collectives  41.3 us (4%)
    ppermute x40, waiting for transfers between devices, reduce(): g = keep.astype(F32) + lax.ppermute(send, 'dp', xor(1 << b)).astype(F32)  158 us
    dot_general x32, matrix products, dot_nt(): lax.dot_general(a, b, (((1,), (1,)), ((), ())), preferred_element_type=F32)  76 us
    dot_general x32, matrix products, dot_tn(): lax.dot_general(a, b, (((0,), (0,)), ((), ())), preferred_element_type=F32)  70.9 us
    dot_general x32, matrix products, dot(): return jnp.dot(a, b, preferred_element_type=F32)  66.3 us
    dot_general x8, matrix products, attend_back(): dq = jnp.einsum('hqk,khe->qhe', ds, heads(k), preferred_element_type=F32)  62.2 us
    dot_general x8, matrix products, attend_back(): dk = jnp.einsum('hqk,qhe->khe', ds, heads(q), preferred_element_type=F32)  61.3 us
    ppermute x10, waiting for transfers between devices, reduce(): g = g[0].astype(F32) + lax.ppermute(g[1], 'tensor', SWAP).astype(F32)  45 us
    ppermute x40, starting transfers between devices, reduce(): g = keep.astype(F32) + lax.ppermute(send, 'dp', xor(1 << b)).astype(F32)  42.6 us
  transfers between devices with their start and end apart: 88, of which 44 were waited for; matrix products, arithmetic and copies ran while one was open for 38% of the time, Pallas kernels for 0%

profile of v1, /device:TPU:0, one launch (start us, length us, event | category | flops | bytes accessed | tf_op | source)
XLA Modules:
  0.0 1103.7 jit_solution(7954263648566061824)
XLA Ops:
  19.7 4.1 fusion.465
  26.6 4.1 fusion.464
  61.9 5.2 fusion.470
  67.2 4.4 divide_convert_fusion.5
  71.6 4.1 fusion.469
  84.7 5.8 collective-permute-done.8
  93.4 6.6 collective-permute-done.21
  104.3 8.3 collective-permute-done.17
  114.0 8.0 collective-permute-done.30
  134.7 10.2 collective-permute-done.18
  146.5 11.1 %collective-permute-done.31 = bf16[384,768]{1,0:T(8,128)(2,1)S(1)} collective-permute-done((bf16[384,768]{1,0:T(8,128)(2,1)S(1)}, bf16[384,768]{1,0:T(8,128)(2,1)S(1)}, u32[]{:S(2)}, u32[]{:S(2)}) %collective-permute-start.31) | collective-permute-done | bytes 589856 | tf_op jit(solution)/shard_map/ppermute | solution.py:104
  159.0 10.2 collective-permute-done.15
  189.4 5.4 fusion.472
  199.9 4.2 fusion.471
  270.1 5.7 fusion.479
  275.8 4.3 divide_convert_fusion
  282.3 5.7 fusion.478
  288.0 4.3 divide_convert_fusion.1
  346.7 5.4 fusion.201
  362.0 4.7 fusion.198
  370.7 5.4 fusion.200
  376.2 4.2 convolution_convert_fusion.7
  380.4 5.0 fusion.199
  386.7 4.2 convolution_convert_fusion.2
  390.9 4.5 multiply_convert_fusion
  395.5 4.4 fusion.481
  423.1 5.8 fusion.61
  432.4 5.6 multiply_reduce_fusion.4
  455.2 4.7 convolution_convert_fusion.42
  459.9 4.9 fusion.488
  464.8 12.8 %fusion.192 = bf16[6,64,576]{2,1,0:T(8,128)(2,1)} fusion(bf16[576,6,64]{0,2,1:T(8,128)(2,1)} %bitcast.975, bf16[6,576,576]{1,2,0:T(8,128)(2,1)} %copy-done.3, f32[6,576,576]{1,2,0:T(8,128)} %fusion.488), kind=kOutput, calls=%fused_computation.403 | convolution fusion | flops 268963776 | bytes 12828672 | tf_op jit(solution)/shard_map/hqk,khe->qhe/dot_general | solution.py:66
  477.6 12.5 %fusion.193 = bf16[6,64,576]{2,1,0:T(8,128)(2,1)} fusion(bf16[576,6,64]{0,2,1:T(8,128)(2,1)} %bitcast.973, bf16[6,576,576]{1,2,0:T(8,128)(2,1)} %copy-done.3, f32[6,576,576]{1,2,0:T(8,128)} %fusion.488), kind=kOutput, calls=%fused_computation.404 | convolution fusion | flops 268963776 | bytes 12828672 | tf_op jit(solution)/shard_map/hqk,qhe->khe/dot_general | solution.py:67
  498.0 4.9 fusion.487
  502.9 12.1 %fusion.190 = bf16[6,64,576]{2,1,0:T(8,128)(2,1)} fusion(bf16[576,6,64]{0,2,1:T(8,128)(2,1)} %bitcast.971, bf16[6,576,576]{1,2,0:T(8,128)(2,1)} %copy-done.2, f32[6,576,576]{1,2,0:T(8,128)} %fusion.487), kind=kOutput, calls=%fused_computation.401 | convolution fusion | flops 268963776 | bytes 12828672 | tf_op jit(solution)/shard_map/hqk,khe->qhe/dot_general | solution.py:66
  515.0 12.2 %fusion.191 = bf16[6,64,576]{2,1,0:T(8,128)(2,1)} fusion(bf16[576,6,64]{0,2,1:T(8,128)(2,1)} %bitcast.969, bf16[6,576,576]{1,2,0:T(8,128)(2,1)} %copy-done.2, f32[6,576,576]{1,2,0:T(8,128)} %fusion.487), kind=kOutput, calls=%fused_computation.402 | convolution fusion | flops 268963776 | bytes 12828672 | tf_op jit(solution)/shard_map/hqk,qhe->khe/dot_general | solution.py:67
  568.5 6.2 fusion.204
  574.8 6.2 fusion.188
  587.4 7.4 fusion.205
  594.8 7.6 fusion.189
  608.1 5.5 fusion.202
  613.6 6.5 fusion.186
  626.0 7.0 fusion.203
  633.0 7.1 fusion.187
  715.0 41.3 %psum.7 = f32[10,768]{1,0:T(8,128)} all-reduce(f32[10,768]{1,0:T(8,128)} %stack.284), channel_id=1, replica_groups=mesh['dp'=16,'tensor'=2] {'dp','tensor'}, use_global_device_ids=true, to_apply=%region_55.56 | all-reduce | flops 7680 | bytes 61440 | tf_op jit(solution)/shard_map/psum | solution.py:247
  778.4 4.1 copy.171
  795.1 8.1 collective-permute-done.37
  804.6 4.8 collective-permute-done.33
  815.6 5.8 collective-permute-done.59
  822.2 7.2 collective-permute-done.54
  831.2 4.6 collective-permute-done.60
  836.8 4.5 collective-permute-done.65
  899.0 5.3 collective-permute-done.44
  908.0 17.1 %collective-permute-done.39 = bf16[2,2,2,48,1152]{4,3,2,1,0:T(8,128)(2,1)S(1)} collective-permute-done((bf16[2,2,2,48,1152]{4,3,2,1,0:T(8,128)(2,1)S(1)}, bf16[2,2,2,48,1152]{4,3,2,1,0:T(8,128)(2,1)S(1)}, u32[]{:S(2)}, u32[]{:S(2)}) %collective-permute-start.39) | collective-permute-done | bytes 884768 | tf_op jit(solution)/shard_map/ppermute | solution.py:176
  927.0 57.0 %collective-permute-done.45 = bf16[2,2,48,1152]{3,2,1,0:T(8,128)(2,1)S(1)} collective-permute-done((bf16[2,2,48,1152]{3,2,1,0:T(8,128)(2,1)S(1)}, bf16[2,2,48,1152]{3,2,1,0:T(8,128)(2,1)S(1)}, u32[]{:S(2)}, u32[]{:S(2)}) %collective-permute-start.45) | collective-permute-done | bytes 442400 | tf_op jit(solution)/shard_map/ppermute | solution.py:176
  985.0 9.9 collective-permute-done.50
  996.0 8.9 collective-permute-done.40
  1006.6 5.8 collective-permute-done.46
  1014.0 6.4 collective-permute-done.51
  1022.0 5.3 collective-permute-done.41
  1029.6 4.5 collective-permute-done.47
  1035.3 5.6 collective-permute-done.52
  1064.7 6.0 collective-permute-done.80
  1083.5 4.8 collective-permute-done.86
  1094.6 6.1 collective-permute-done.87
  (1017 shorter events, 597.7 us)
Async XLA Ops:
  2.7 51.6 %collective-permute-start = (bf16[160,768]{1,0:T(8,128)(2,1)}, bf16[160,768]{1,0:T(8,128)(2,1)}, u32[]{:S(2)}, u32[]{:S(2)}) collective-permute-start(bf16[160,768]{1,0:T(8,128)(2,1)} %get-tuple-element.100), channel_id=1, source_target_pairs={{0,1},{1,0},{2,3},{3,2},{4,5},{5,4},{6,7},{7,6},{8,9},{9,8},{10,11... | collective-permute-start | bytes 737288 | tf_op jit(solution)/shard_map/ppermute | solution.py:92
  7.8 47.3 %collective-permute-start.1 = (bf16[288,768]{1,0:T(8,128)(2,1)}, bf16[288,768]{1,0:T(8,128)(2,1)}, u32[]{:S(2)}, u32[]{:S(2)}) collective-permute-start(bf16[288,768]{1,0:T(8,128)(2,1)} %get-tuple-element.94), channel_id=1, source_target_pairs={{0,1},{1,0},{2,3},{3,2},{4,5},{5,4},{6,7},{7,6},{8,9},{9,8},{10,11... | collective-permute-start | bytes 1327112 | tf_op jit(solution)/shard_map/ppermute | solution.py:92
  8.6 30.4 %collective-permute-start.11 = (bf16[96,768]{1,0:T(8,128)(2,1)}, bf16[96,768]{1,0:T(8,128)(2,1)}, u32[]{:S(2)}, u32[]{:S(2)}) collective-permute-start(bf16[96,768]{1,0:T(8,128)(2,1)} %dynamic-slice_bitcast_fusion.37), channel_id=1, source_target_pairs={{0,1},{1,0},{2,3},{3,2},{4,5},{5,4},{6,7},{7,6},{8,9},{9,8},{10,11... | collective-permute-start | bytes 442376 | tf_op jit(solution)/shard_map/ppermute | solution.py:103
  10.6 30.5 %collective-permute-start.5 = (bf16[96,768]{1,0:T(8,128)(2,1)S(1)}, bf16[96,768]{1,0:T(8,128)(2,1)}, u32[]{:S(2)}, u32[]{:S(2)}) collective-permute-start(bf16[96,768]{1,0:T(8,128)(2,1)S(1)} %dynamic-slice_bitcast_fusion.38), channel_id=1, source_target_pairs={{0,1},{1,0},{2,3},{3,2},{4,5},{5,4},{6,7},{7,6},{8,9},{9,8},{10,11... | collective-permute-start | bytes 442376 | tf_op jit(solution)/shard_map/ppermute | solution.py:103
  10.8 31.6 %collective-permute-start.24 = (bf16[96,768]{1,0:T(8,128)(2,1)S(1)}, bf16[96,768]{1,0:T(8,128)(2,1)}, u32[]{:S(2)}, u32[]{:S(2)}) collective-permute-start(bf16[96,768]{1,0:T(8,128)(2,1)S(1)} %dynamic-slice_bitcast_fusion.36), channel_id=1, source_target_pairs={{0,1},{1,0},{2,3},{3,2},{4,5},{5,4},{6,7},{7,6},{8,9},{9,8},{10,11... | collective-permute-start | bytes 442376 | tf_op jit(solution)/shard_map/ppermute | solution.py:103
  42.3 59.8 %collective-permute-start.14 = (bf16[192,1536]{1,0:T(8,128)(2,1)}, bf16[192,1536]{1,0:T(8,128)(2,1)}, u32[]{:S(2)}, u32[]{:S(2)}) collective-permute-start(bf16[192,1536]{1,0:T(8,128)(2,1)} %dynamic-slice_bitcast_fusion.9), channel_id=1, source_target_pairs={{0,1},{1,0},{2,3},{3,2},{4,5},{5,4},{6,7},{7,6},{8,9},{9,8},{10,11... | collective-permute-start | bytes 1769480 | tf_op jit(solution)/shard_map/ppermute | solution.py:103
  48.7 54.0 %collective-permute-start.27 = (bf16[192,1536]{1,0:T(8,128)(2,1)}, bf16[192,1536]{1,0:T(8,128)(2,1)}, u32[]{:S(2)}, u32[]{:S(2)}) collective-permute-start(bf16[192,1536]{1,0:T(8,128)(2,1)} %dynamic-slice_bitcast_fusion.7), channel_id=1, source_target_pairs={{0,1},{1,0},{2,3},{3,2},{4,5},{5,4},{6,7},{7,6},{8,9},{9,8},{10,11... | collective-permute-start | bytes 1769480 | tf_op jit(solution)/shard_map/ppermute | solution.py:103
  51.3 32.6 %collective-permute-start.2 = (bf16[3,192,384]{2,1,0:T(8,128)(2,1)}, bf16[3,192,384]{2,1,0:T(8,128)(2,1)}, u32[]{:S(2)}, u32[]{:S(2)}) collective-permute-start(bf16[3,192,384]{2,1,0:T(8,128)(2,1)} %dynamic-slice_bitcast_fusion.15), channel_id=1, source_target_pairs={{0,1},{1,0},{2,3},{3,2},{4,5},{5,4},{6,7},{7,6},{8,9},{9,8},{10,11... | collective-permute-start | bytes 1327112 | tf_op jit(solution)/shard_map/ppermute | solution.py:103
  54.3 36.2 %collective-permute-start.8 = (bf16[3,192,384]{2,1,0:T(8,128)(2,1)}, bf16[3,192,384]{2,1,0:T(8,128)(2,1)}, u32[]{:S(2)}, u32[]{:S(2)}) collective-permute-start(bf16[3,192,384]{2,1,0:T(8,128)(2,1)} %dynamic-slice_bitcast_fusion.14), channel_id=1, source_target_pairs={{0,1},{1,0},{2,3},{3,2},{4,5},{5,4},{6,7},{7,6},{8,9},{9,8},{10,11... | collective-permute-start | bytes 1327112 | tf_op jit(solution)/shard_map/ppermute | solution.py:103
  55.1 44.9 %collective-permute-start.21 = (bf16[3,192,384]{2,1,0:T(8,128)(2,1)}, bf16[3,192,384]{2,1,0:T(8,128)(2,1)}, u32[]{:S(2)}, u32[]{:S(2)}) collective-permute-start(bf16[3,192,384]{2,1,0:T(8,128)(2,1)} %dynamic-slice_bitcast_fusion.13), channel_id=1, source_target_pairs={{0,1},{1,0},{2,3},{3,2},{4,5},{5,4},{6,7},{7,6},{8,9},{9,8},{10,11... | collective-permute-start | bytes 1327112 | tf_op jit(solution)/shard_map/ppermute | solution.py:103
  83.9 28.6 %collective-permute-start.17 = (bf16[384,768]{1,0:T(8,128)(2,1)}, bf16[384,768]{1,0:T(8,128)(2,1)S(1)}, u32[]{:S(2)}, u32[]{:S(2)}) collective-permute-start(bf16[384,768]{1,0:T(8,128)(2,1)} %dynamic-slice_bitcast_fusion.8), channel_id=1, source_target_pairs={{0,1},{1,0},{2,3},{3,2},{4,5},{5,4},{6,7},{7,6},{8,9},{9,8},{10,11... | collective-permute-start | bytes 1769480 | tf_op jit(solution)/shard_map/ppermute | solution.py:103
  90.5 31.5 %collective-permute-start.30 = (bf16[384,768]{1,0:T(8,128)(2,1)}, bf16[384,768]{1,0:T(8,128)(2,1)S(1)}, u32[]{:S(2)}, u32[]{:S(2)}) collective-permute-start(bf16[384,768]{1,0:T(8,128)(2,1)} %dynamic-slice_bitcast_fusion.6), channel_id=1, source_target_pairs={{0,1},{1,0},{2,3},{3,2},{4,5},{5,4},{6,7},{7,6},{8,9},{9,8},{10,11... | collective-permute-start | bytes 1769480 | tf_op jit(solution)/shard_map/ppermute | solution.py:103
  100.0 27.3 %collective-permute-start.3 = (bf16[3,192,384]{2,1,0:T(8,128)(2,1)}, bf16[3,192,384]{2,1,0:T(8,128)(2,1)S(1)}, u32[]{:S(2)}, u32[]{:S(2)}) collective-permute-start(bf16[3,192,384]{2,1,0:T(8,128)(2,1)} %collective-permute-done.2), channel_id=1, source_target_pairs={{0,4},{2,6},{4,0},{6,2},{8,12},{10,14},{12,8},{14,10},{16,20},{18,... | collective-permute-start | bytes 1327112 | tf_op jit(solution)/shard_map/ppermute | solution.py:104
  102.2 27.2 %collective-permute-start.9 = (bf16[3,192,384]{2,1,0:T(8,128)(2,1)}, bf16[3,192,384]{2,1,0:T(8,128)(2,1)S(1)}, u32[]{:S(2)}, u32[]{:S(2)}) collective-permute-start(bf16[3,192,384]{2,1,0:T(8,128)(2,1)} %collective-permute-done.8), channel_id=1, source_target_pairs={{0,4},{2,6},{4,0},{6,2},{8,12},{10,14},{12,8},{14,10},{16,20},{18,... | collective-permute-start | bytes 1327112 | tf_op jit(solution)/shard_map/ppermute | solution.py:104
  102.8 30.5 %collective-permute-start.22 = (bf16[3,192,384]{2,1,0:T(8,128)(2,1)}, bf16[3,192,384]{2,1,0:T(8,128)(2,1)S(1)}, u32[]{:S(2)}, u32[]{:S(2)}) collective-permute-start(bf16[3,192,384]{2,1,0:T(8,128)(2,1)} %collective-permute-done.21), channel_id=1, source_target_pairs={{0,4},{2,6},{4,0},{6,2},{8,12},{10,14},{12,8},{14,10},{16,20},{18,... | collective-permute-start | bytes 1327112 | tf_op jit(solution)/shard_map/ppermute | solution.py:104
  112.5 32.4 %collective-permute-start.18 = (bf16[384,768]{1,0:T(8,128)(2,1)S(1)}, bf16[384,768]{1,0:T(8,128)(2,1)S(1)}, u32[]{:S(2)}, u32[]{:S(2)}) collective-permute-start(bf16[384,768]{1,0:T(8,128)(2,1)S(1)} %collective-permute-done.17), channel_id=1, source_target_pairs={{0,4},{2,6},{4,0},{6,2},{8,12},{10,14},{12,8},{14,10},{16,20},{18,... | collective-permute-start | bytes 1769480 | tf_op jit(solution)/shard_map/ppermute | solution.py:104
  122.0 35.5 %collective-permute-start.31 = (bf16[384,768]{1,0:T(8,128)(2,1)S(1)}, bf16[384,768]{1,0:T(8,128)(2,1)S(1)}, u32[]{:S(2)}, u32[]{:S(2)}) collective-permute-start(bf16[384,768]{1,0:T(8,128)(2,1)S(1)} %collective-permute-done.30), channel_id=1, source_target_pairs={{0,4},{2,6},{4,0},{6,2},{8,12},{10,14},{12,8},{14,10},{16,20},{18,... | collective-permute-start | bytes 1769480 | tf_op jit(solution)/shard_map/ppermute | solution.py:104
  127.3 42.0 %collective-permute-start.15 = (bf16[192,1536]{1,0:T(8,128)(2,1)}, bf16[192,1536]{1,0:T(8,128)(2,1)S(1)}, u32[]{:S(2)}, u32[]{:S(2)}) collective-permute-start(bf16[192,1536]{1,0:T(8,128)(2,1)} %collective-permute-done.14), channel_id=1, source_target_pairs={{0,4},{2,6},{4,0},{6,2},{8,12},{10,14},{12,8},{14,10},{16,20},{18,... | collective-permute-start | bytes 1769480 | tf_op jit(solution)/shard_map/ppermute | solution.py:104
  129.3 46.2 %collective-permute-start.28 = (bf16[192,1536]{1,0:T(8,128)(2,1)}, bf16[192,1536]{1,0:T(8,128)(2,1)S(1)}, u32[]{:S(2)}, u32[]{:S(2)}) collective-permute-start(bf16[192,1536]{1,0:T(8,128)(2,1)} %collective-permute-done.27), channel_id=1, source_target_pairs={{0,4},{2,6},{4,0},{6,2},{8,12},{10,14},{12,8},{14,10},{16,20},{18,... | collective-permute-start | bytes 1769480 | tf_op jit(solution)/shard_map/ppermute | solution.py:104
  133.3 45.0 %collective-permute-start.4 = (bf16[3,384,384]{2,1,0:T(8,128)(2,1)S(1)}, bf16[3,384,384]{2,1,0:T(8,128)(2,1)S(1)}, u32[]{:S(2)}, u32[]{:S(2)}) collective-permute-start(bf16[3,384,384]{2,1,0:T(8,128)(2,1)S(1)} %maximum_select_fusion.13), channel_id=1, source_target_pairs={{0,2},{2,0},{4,6},{6,4},{8,10},{10,8},{12,14},{14,12},{16,18},{18,... | collective-permute-start | bytes 2654216 | tf_op jit(solution)/shard_map/ppermute | solution.py:107
  144.9 168.7 %collective-permute-start.34 = (bf16[160,768]{1,0:T(8,128)(2,1)}, bf16[160,768]{1,0:T(8,128)(2,1)}, u32[]{:S(2)}, u32[]{:S(2)}) collective-permute-start(bf16[160,768]{1,0:T(8,128)(2,1)} %get-tuple-element.96), channel_id=1, source_target_pairs={{0,1},{1,0},{2,3},{3,2},{4,5},{5,4},{6,7},{7,6},{8,9},{9,8},{10,11... | collective-permute-start | bytes 737288 | tf_op jit(solution)/shard_map/ppermute | solution.py:92
  157.5 245.6 %collective-permute-start.35 = (bf16[288,768]{1,0:T(8,128)(2,1)}, bf16[288,768]{1,0:T(8,128)(2,1)}, u32[]{:S(2)}, u32[]{:S(2)}) collective-permute-start(bf16[288,768]{1,0:T(8,128)(2,1)} %get-tuple-element.90), channel_id=1, source_target_pairs={{0,1},{1,0},{2,3},{3,2},{4,5},{5,4},{6,7},{7,6},{8,9},{9,8},{10,11... | collective-permute-start | bytes 1327112 | tf_op jit(solution)/shard_map/ppermute | solution.py:92
  169.2 126.6 %collective-permute-start.26 = (bf16[192,768]{1,0:T(8,128)(2,1)}, bf16[192,768]{1,0:T(8,128)(2,1)}, u32[]{:S(2)}, u32[]{:S(2)}) collective-permute-start(bf16[192,768]{1,0:T(8,128)(2,1)} %maximum_select_fusion.31), channel_id=1, source_target_pairs={{0,2},{2,0},{4,6},{6,4},{8,10},{10,8},{12,14},{14,12},{16,18},{18,... | collective-permute-start | bytes 884744 | tf_op jit(solution)/shard_map/ppermute | solution.py:107
  175.6 32.1 %collective-permute-start.7 = (bf16[192,768]{1,0:T(8,128)(2,1)}, bf16[192,768]{1,0:T(8,128)(2,1)}, u32[]{:S(2)}, u32[]{:S(2)}) collective-permute-start(bf16[192,768]{1,0:T(8,128)(2,1)} %maximum_select_fusion.29), channel_id=1, source_target_pairs={{0,2},{2,0},{4,6},{6,4},{8,10},{10,8},{12,14},{14,12},{16,18},{18,... | collective-permute-start | bytes 884744 | tf_op jit(solution)/shard_map/ppermute | solution.py:107
  178.2 87.5 %collective-permute-start.13 = (bf16[192,768]{1,0:T(8,128)(2,1)}, bf16[192,768]{1,0:T(8,128)(2,1)}, u32[]{:S(2)}, u32[]{:S(2)}) collective-permute-start(bf16[192,768]{1,0:T(8,128)(2,1)} %maximum_select_fusion.30), channel_id=1, source_target_pairs={{0,2},{2,0},{4,6},{6,4},{8,10},{10,8},{12,14},{14,12},{16,18},{18,... | collective-permute-start | bytes 884744 | tf_op jit(solution)/shard_map/ppermute | solution.py:107
  207.7 8.8 collective-permute-start.10
  216.5 8.8 collective-permute-start.23
  225.3 165.6 %collective-permute-start.29 = (bf16[384,1536]{1,0:T(8,128)(2,1)}, bf16[384,1536]{1,0:T(8,128)(2,1)}, u32[]{:S(2)}, u32[]{:S(2)}) collective-permute-start(bf16[384,1536]{1,0:T(8,128)(2,1)} %maximum_select_fusion.10), channel_id=1, source_target_pairs={{0,2},{2,0},{4,6},{6,4},{8,10},{10,8},{12,14},{14,12},{16,18},{18,... | collective-permute-start | bytes 3538952 | tf_op jit(solution)/shard_map/ppermute | solution.py:107
  265.8 42.7 %collective-permute-start.16 = (bf16[384,1536]{1,0:T(8,128)(2,1)}, bf16[384,1536]{1,0:T(8,128)(2,1)}, u32[]{:S(2)}, u32[]{:S(2)}) collective-permute-start(bf16[384,1536]{1,0:T(8,128)(2,1)} %maximum_select_fusion.8), channel_id=1, source_target_pairs={{0,2},{2,0},{4,6},{6,4},{8,10},{10,8},{12,14},{14,12},{16,18},{18,... | collective-permute-start | bytes 3538952 | tf_op jit(solution)/shard_map/ppermute | solution.py:107
  295.9 15.7 %collective-permute-start.19 = (bf16[768,768]{1,0:T(8,128)(2,1)S(1)}, bf16[768,768]{1,0:T(8,128)(2,1)S(1)}, u32[]{:S(2)}, u32[]{:S(2)}) collective-permute-start(bf16[768,768]{1,0:T(8,128)(2,1)S(1)} %copy-done.110), channel_id=1, source_target_pairs={{0,2},{2,0},{4,6},{6,4},{8,10},{10,8},{12,14},{14,12},{16,18},{18,... | collective-permute-start | bytes 3538952 | tf_op jit(solution)/shard_map/ppermute | solution.py:107
  308.5 87.0 %collective-permute-start.32 = (bf16[768,768]{1,0:T(8,128)(2,1)}, bf16[768,768]{1,0:T(8,128)(2,1)}, u32[]{:S(2)}, u32[]{:S(2)}) collective-permute-start(bf16[768,768]{1,0:T(8,128)(2,1)} %maximum_select_fusion.11), channel_id=1, source_target_pairs={{0,2},{2,0},{4,6},{6,4},{8,10},{10,8},{12,14},{14,12},{16,18},{18,... | collective-permute-start | bytes 3538952 | tf_op jit(solution)/shard_map/ppermute | solution.py:107
  658.9 133.4 %collective-permute-start.20 = (bf16[160,768]{1,0:T(8,128)(2,1)}, bf16[160,768]{1,0:T(8,128)(2,1)}, u32[]{:S(2)}, u32[]{:S(2)}) collective-permute-start(bf16[160,768]{1,0:T(8,128)(2,1)} %get-tuple-element.98), channel_id=1, source_target_pairs={{0,1},{1,0},{2,3},{3,2},{4,5},{5,4},{6,7},{7,6},{8,9},{9,8},{10,11... | collective-permute-start | bytes 737288 | tf_op jit(solution)/shard_map/ppermute | solution.py:155
  661.7 148.8 %collective-permute-start.58 = (bf16[2,2,2,2,48,384]{5,4,3,2,1,0:T(8,128)(2,1)}, bf16[2,2,2,2,48,384]{5,4,3,2,1,0:T(8,128)(2,1)}, u32[]{:S(2)}, u32[]{:S(2)}) collective-permute-start(bf16[2,2,2,2,48,384]{5,4,3,2,1,0:T(8,128)(2,1)} %fusion.233), channel_id=1, source_target_pairs={{0,2},{2,0},{4,6},{6,4},{8,10},{10,8},{12,14},{14,12},{16,18},{18,... | collective-permute-start | bytes 1769480 | tf_op jit(solution)/shard_map/ppermute | solution.py:176
  669.8 205.7 %collective-permute-start.43 = (bf16[2,2,2,2,48,1152]{5,4,3,2,1,0:T(8,128)(2,1)}, bf16[2,2,2,2,48,1152]{5,4,3,2,1,0:T(8,128)(2,1)}, u32[]{:S(2)}, u32[]{:S(2)}) collective-permute-start(bf16[2,2,2,2,48,1152]{5,4,3,2,1,0:T(8,128)(2,1)} %fusion.153), channel_id=1, source_target_pairs={{0,2},{2,0},{4,6},{6,4},{8,10},{10,8},{12,14},{14,12},{16,18},{18,... | collective-permute-start | bytes 5308424 | tf_op jit(solution)/shard_map/ppermute | solution.py:176
  679.5 207.6 %collective-permute-start.68 = (bf16[2,2,2,2,48,1536]{5,4,1,2,3,0:T(8,128)(2,1)}, bf16[2,2,2,2,48,1536]{5,4,1,2,3,0:T(8,128)(2,1)}, u32[]{:S(2)}, u32[]{:S(2)}) collective-permute-start(bf16[2,2,2,2,48,1536]{5,4,1,2,3,0:T(8,128)(2,1)} %bitcast.846), channel_id=1, source_target_pairs={{0,2},{2,0},{4,6},{6,4},{8,10},{10,8},{12,14},{14,12},{16,18},{18,... | collective-permute-start | bytes 7077896 | tf_op jit(solution)/shard_map/ppermute | solution.py:176
  790.0 13.2 %collective-permute-start.37 = (bf16[288,768]{1,0:T(8,128)(2,1)S(1)}, bf16[288,768]{1,0:T(8,128)(2,1)S(1)}, u32[]{:S(2)}, u32[]{:S(2)}) collective-permute-start(bf16[288,768]{1,0:T(8,128)(2,1)S(1)} %copy-done.158), channel_id=1, source_target_pairs={{0,1},{1,0},{2,3},{3,2},{4,5},{5,4},{6,7},{7,6},{8,9},{9,8},{10,11... | collective-permute-start | bytes 1327112 | tf_op jit(solution)/shard_map/ppermute | solution.py:241
  792.3 17.2 %collective-permute-start.33 = (bf16[288,768]{1,0:T(8,128)(2,1)S(1)}, bf16[288,768]{1,0:T(8,128)(2,1)S(1)}, u32[]{:S(2)}, u32[]{:S(2)}) collective-permute-start(bf16[288,768]{1,0:T(8,128)(2,1)S(1)} %get-tuple-element.92), channel_id=1, source_target_pairs={{0,1},{1,0},{2,3},{3,2},{4,5},{5,4},{6,7},{7,6},{8,9},{9,8},{10,11... | collective-permute-start | bytes 1327112 | tf_op jit(solution)/shard_map/ppermute | solution.py:155
  803.2 88.5 %collective-permute-start.78 = (bf16[2,2,2,2,48,1536]{5,4,1,2,3,0:T(8,128)(2,1)S(1)}, bf16[2,2,2,2,48,1536]{5,4,1,2,3,0:T(8,128)(2,1)S(1)}, u32[]{:S(2)}, u32[]{:S(2)}) collective-permute-start(bf16[2,2,2,2,48,1536]{5,4,1,2,3,0:T(8,128)(2,1)S(1)} %bitcast.918), channel_id=1, source_target_pairs={{0,2},{2,0},{4,6},{6,4},{8,10},{10,8},{12,14},{14,12},{16,18},{18,... | collective-permute-start | bytes 7077896 | tf_op jit(solution)/shard_map/ppermute | solution.py:176
  812.3 9.0 collective-permute-start.59
  813.4 16.1 %collective-permute-start.64 = (bf16[2,2,2,48,384]{4,3,1,2,0:T(8,128)(2,1)S(1)}, bf16[2,2,2,48,384]{4,3,1,2,0:T(8,128)(2,1)S(1)}, u32[]{:S(2)}, u32[]{:S(2)}) collective-permute-start(bf16[2,2,2,48,384]{4,3,1,2,0:T(8,128)(2,1)S(1)} %dynamic-slice_bitcast_fusion.22), channel_id=1, source_target_pairs={{0,4},{2,6},{4,0},{6,2},{8,12},{10,14},{12,8},{14,10},{16,20},{18,... | collective-permute-start | bytes 884744 | tf_op jit(solution)/shard_map/ppermute | solution.py:176
  829.4 48.8 %collective-permute-start.48 = (bf16[2,2,2,2,48,1152]{5,4,3,2,1,0:T(8,128)(2,1)S(1)}, bf16[2,2,2,2,48,1152]{5,4,3,2,1,0:T(8,128)(2,1)S(1)}, u32[]{:S(2)}, u32[]{:S(2)}) collective-permute-start(bf16[2,2,2,2,48,1152]{5,4,3,2,1,0:T(8,128)(2,1)S(1)} %fusion.149), channel_id=1, source_target_pairs={{0,2},{2,0},{4,6},{6,4},{8,10},{10,8},{12,14},{14,12},{16,18},{18,... | collective-permute-start | bytes 5308424 | tf_op jit(solution)/shard_map/ppermute | solution.py:176
  874.8 8.7 collective-permute-start.83
  878.2 17.1 %collective-permute-start.73 = (bf16[2,2,2,2,48,1536]{5,4,1,2,0,3:T(8,128)(2,1)S(1)}, bf16[2,2,2,2,48,1536]{5,4,1,2,0,3:T(8,128)(2,1)S(1)}, u32[]{:S(2)}, u32[]{:S(2)}) collective-permute-start(bf16[2,2,2,2,48,1536]{5,4,1,2,0,3:T(8,128)(2,1)S(1)} %bitcast.919), channel_id=1, source_target_pairs={{0,2},{2,0},{4,6},{6,4},{8,10},{10,8},{12,14},{14,12},{16,18},{18,... | collective-permute-start | bytes 7077896 | tf_op jit(solution)/shard_map/ppermute | solution.py:176
  881.8 22.5 %collective-permute-start.44 = (bf16[2,2,2,48,1152]{4,3,2,1,0:T(8,128)(2,1)S(1)}, bf16[2,2,2,48,1152]{4,3,2,1,0:T(8,128)(2,1)S(1)}, u32[]{:S(2)}, u32[]{:S(2)}) collective-permute-start(bf16[2,2,2,48,1152]{4,3,2,1,0:T(8,128)(2,1)S(1)} %slice_bitcast_fusion.4), channel_id=1, source_target_pairs={{0,1},{1,0},{2,3},{3,2},{4,5},{5,4},{6,7},{7,6},{8,9},{9,8},{10,11... | collective-permute-start | bytes 2654216 | tf_op jit(solution)/shard_map/ppermute | solution.py:169
  883.5 22.6 %collective-permute-start.49 = (bf16[2,2,2,48,1152]{4,3,2,1,0:T(8,128)(2,1)S(1)}, bf16[2,2,2,48,1152]{4,3,2,1,0:T(8,128)(2,1)S(1)}, u32[]{:S(2)}, u32[]{:S(2)}) collective-permute-start(bf16[2,2,2,48,1152]{4,3,2,1,0:T(8,128)(2,1)S(1)} %dynamic-slice_bitcast_fusion.2), channel_id=1, source_target_pairs={{0,4},{2,6},{4,0},{6,2},{8,12},{10,14},{12,8},{14,10},{16,20},{18,... | collective-permute-start | bytes 2654216 | tf_op jit(solution)/shard_map/ppermute | solution.py:176
  887.1 38.0 %collective-permute-start.39 = (bf16[2,2,2,48,1152]{4,3,2,1,0:T(8,128)(2,1)S(1)}, bf16[2,2,2,48,1152]{4,3,2,1,0:T(8,128)(2,1)S(1)}, u32[]{:S(2)}, u32[]{:S(2)}) collective-permute-start(bf16[2,2,2,48,1152]{4,3,2,1,0:T(8,128)(2,1)S(1)} %dynamic-slice_bitcast_fusion.3), channel_id=1, source_target_pairs={{0,4},{2,6},{4,0},{6,2},{8,12},{10,14},{12,8},{14,10},{16,20},{18,... | collective-permute-start | bytes 2654216 | tf_op jit(solution)/shard_map/ppermute | solution.py:176
  891.7 161.3 %collective-permute-start.69 = (bf16[2,2,2,48,1536]{4,3,0,1,2:T(8,128)(2,1)}, bf16[2,2,2,48,1536]{4,3,0,1,2:T(8,128)(2,1)S(1)}, u32[]{:S(2)}, u32[]{:S(2)}) collective-permute-start(bf16[2,2,2,48,1536]{4,3,0,1,2:T(8,128)(2,1)} %slice_bitcast_fusion.2), channel_id=1, source_target_pairs={{0,1},{1,0},{2,3},{3,2},{4,5},{5,4},{6,7},{7,6},{8,9},{9,8},{10,11... | collective-permute-start | bytes 3538952 | tf_op jit(solution)/shard_map/ppermute | solution.py:169
  895.3 159.8 %collective-permute-start.79 = (bf16[2,2,2,48,1536]{4,3,0,1,2:T(8,128)(2,1)}, bf16[2,2,2,48,1536]{4,3,0,1,2:T(8,128)(2,1)}, u32[]{:S(2)}, u32[]{:S(2)}) collective-permute-start(bf16[2,2,2,48,1536]{4,3,0,1,2:T(8,128)(2,1)} %slice_bitcast_fusion), channel_id=1, source_target_pairs={{0,1},{1,0},{2,3},{3,2},{4,5},{5,4},{6,7},{7,6},{8,9},{9,8},{10,11... | collective-permute-start | bytes 3538952 | tf_op jit(solution)/shard_map/ppermute | solution.py:169
  904.3 153.6 %collective-permute-start.84 = (bf16[2,2,2,48,1536]{4,3,1,2,0:T(8,128)(2,1)}, bf16[2,2,2,48,1536]{4,3,1,2,0:T(8,128)(2,1)}, u32[]{:S(2)}, u32[]{:S(2)}) collective-permute-start(bf16[2,2,2,48,1536]{4,3,1,2,0:T(8,128)(2,1)} %dynamic-slice_bitcast_fusion), channel_id=1, source_target_pairs={{0,4},{2,6},{4,0},{6,2},{8,12},{10,14},{12,8},{14,10},{16,20},{18,... | collective-permute-start | bytes 3538952 | tf_op jit(solution)/shard_map/ppermute | solution.py:176
  906.1 154.3 %collective-permute-start.74 = (bf16[2,2,2,48,1536]{4,3,1,2,0:T(8,128)(2,1)}, bf16[2,2,2,48,1536]{4,3,1,2,0:T(8,128)(2,1)}, u32[]{:S(2)}, u32[]{:S(2)}) collective-permute-start(bf16[2,2,2,48,1536]{4,3,1,2,0:T(8,128)(2,1)} %dynamic-slice_bitcast_fusion.1), channel_id=1, source_target_pairs={{0,4},{2,6},{4,0},{6,2},{8,12},{10,14},{12,8},{14,10},{16,20},{18,... | collective-permute-start | bytes 3538952 | tf_op jit(solution)/shard_map/ppermute | solution.py:176
  925.1 58.8 %collective-permute-start.45 = (bf16[2,2,48,1152]{3,2,1,0:T(8,128)(2,1)S(1)}, bf16[2,2,48,1152]{3,2,1,0:T(8,128)(2,1)S(1)}, u32[]{:S(2)}, u32[]{:S(2)}) collective-permute-start(bf16[2,2,48,1152]{3,2,1,0:T(8,128)(2,1)S(1)} %dynamic-slice_bitcast_fusion.10), channel_id=1, source_target_pairs={{0,4},{2,6},{4,0},{6,2},{8,12},{10,14},{12,8},{14,10},{16,20},{18,... | collective-permute-start | bytes 1327112 | tf_op jit(solution)/shard_map/ppermute | solution.py:176
  983.9 11.0 collective-permute-start.50
  994.9 10.0 collective-permute-start.40
  1053.3 11.1 %collective-permute-start.70 = (bf16[2,2,48,1536]{3,2,0,1:T(8,128)(2,1)S(1)}, bf16[2,2,48,1536]{3,2,0,1:T(8,128)(2,1)S(1)}, u32[]{:S(2)}, u32[]{:S(2)}) collective-permute-start(bf16[2,2,48,1536]{3,2,0,1:T(8,128)(2,1)S(1)} %dynamic-slice_bitcast_fusion.5), channel_id=1, source_target_pairs={{0,4},{2,6},{4,0},{6,2},{8,12},{10,14},{12,8},{14,10},{16,20},{18,... | collective-permute-start | bytes 1769480 | tf_op jit(solution)/shard_map/ppermute | solution.py:176
  1056.7 14.1 %collective-permute-start.80 = (bf16[2,2,48,1536]{3,2,0,1:T(8,128)(2,1)S(1)}, bf16[2,2,48,1536]{3,2,0,1:T(8,128)(2,1)S(1)}, u32[]{:S(2)}, u32[]{:S(2)}) collective-permute-start(bf16[2,2,48,1536]{3,2,0,1:T(8,128)(2,1)S(1)} %dynamic-slice_bitcast_fusion.4), channel_id=1, source_target_pairs={{0,4},{2,6},{4,0},{6,2},{8,12},{10,14},{12,8},{14,10},{16,20},{18,... | collective-permute-start | bytes 1769480 | tf_op jit(solution)/shard_map/ppermute | solution.py:176
  1059.6 11.5 %collective-permute-start.85 = (bf16[2,2,48,1536]{3,2,0,1:T(8,128)(2,1)S(1)}, bf16[2,2,48,1536]{3,2,0,1:T(8,128)(2,1)S(1)}, u32[]{:S(2)}, u32[]{:S(2)}) collective-permute-start(bf16[2,2,48,1536]{3,2,0,1:T(8,128)(2,1)S(1)} %slice_bitcast_fusion.7), channel_id=1, source_target_pairs={{0,1},{1,0},{2,3},{3,2},{4,5},{5,4},{6,7},{7,6},{8,9},{9,8},{10,11... | collective-permute-start | bytes 1769480 | tf_op jit(solution)/shard_map/ppermute | solution.py:169
  1062.1 14.6 %collective-permute-start.75 = (bf16[2,2,48,1536]{3,2,0,1:T(8,128)(2,1)S(1)}, bf16[2,2,48,1536]{3,2,0,1:T(8,128)(2,1)S(1)}, u32[]{:S(2)}, u32[]{:S(2)}) collective-permute-start(bf16[2,2,48,1536]{3,2,0,1:T(8,128)(2,1)S(1)} %slice_bitcast_fusion.9), channel_id=1, source_target_pairs={{0,1},{1,0},{2,3},{3,2},{4,5},{5,4},{6,7},{7,6},{8,9},{9,8},{10,11... | collective-permute-start | bytes 1769480 | tf_op jit(solution)/shard_map/ppermute | solution.py:169
  1064.6 14.8 %collective-permute-start.71 = (bf16[2,48,1536]{2,1,0:T(8,128)(2,1)S(1)}, bf16[2,48,1536]{2,1,0:T(8,128)(2,1)S(1)}, u32[]{:S(2)}, u32[]{:S(2)}) collective-permute-start(bf16[2,48,1536]{2,1,0:T(8,128)(2,1)S(1)} %dynamic-slice_bitcast_fusion.21), channel_id=1, source_target_pairs={{0,8},{2,10},{4,12},{6,14},{8,0},{10,2},{12,4},{14,6},{16,24},{18,... | collective-permute-start | bytes 884744 | tf_op jit(solution)/shard_map/ppermute | solution.py:176
  1071.0 11.8 %collective-permute-start.81 = (bf16[2,48,1536]{2,1,0:T(8,128)(2,1)S(1)}, bf16[2,48,1536]{2,1,0:T(8,128)(2,1)S(1)}, u32[]{:S(2)}, u32[]{:S(2)}) collective-permute-start(bf16[2,48,1536]{2,1,0:T(8,128)(2,1)S(1)} %dynamic-slice_bitcast_fusion.19), channel_id=1, source_target_pairs={{0,8},{2,10},{4,12},{6,14},{8,0},{10,2},{12,4},{14,6},{16,24},{18,... | collective-permute-start | bytes 884744 | tf_op jit(solution)/shard_map/ppermute | solution.py:176
  1071.2 17.0 %collective-permute-start.86 = (bf16[2,48,1536]{2,1,0:T(8,128)(2,1)S(1)}, bf16[2,48,1536]{2,1,0:T(8,128)(2,1)S(1)}, u32[]{:S(2)}, u32[]{:S(2)}) collective-permute-start(bf16[2,48,1536]{2,1,0:T(8,128)(2,1)S(1)} %dynamic-slice_bitcast_fusion.18), channel_id=1, source_target_pairs={{0,8},{2,10},{4,12},{6,14},{8,0},{10,2},{12,4},{14,6},{16,24},{18,... | collective-permute-start | bytes 884744 | tf_op jit(solution)/shard_map/ppermute | solution.py:176
  1076.9 17.0 %collective-permute-start.76 = (bf16[2,48,1536]{2,1,0:T(8,128)(2,1)S(1)}, bf16[2,48,1536]{2,1,0:T(8,128)(2,1)S(1)}, u32[]{:S(2)}, u32[]{:S(2)}) collective-permute-start(bf16[2,48,1536]{2,1,0:T(8,128)(2,1)S(1)} %dynamic-slice_bitcast_fusion.20), channel_id=1, source_target_pairs={{0,8},{2,10},{4,12},{6,14},{8,0},{10,2},{12,4},{14,6},{16,24},{18,... | collective-permute-start | bytes 884744 | tf_op jit(solution)/shard_map/ppermute | solution.py:176
  1079.5 15.0 %collective-permute-start.72 = (bf16[48,1536]{1,0:T(8,128)(2,1)S(1)}, bf16[48,1536]{1,0:T(8,128)(2,1)S(1)}, u32[]{:S(2)}, u32[]{:S(2)}) collective-permute-start(bf16[48,1536]{1,0:T(8,128)(2,1)S(1)} %dynamic-slice_bitcast_fusion.33), channel_id=1, source_target_pairs={{0,16},{2,18},{4,20},{6,22},{8,24},{10,26},{12,28},{14,30},{16,0},... | collective-permute-start | bytes 442376 | tf_op jit(solution)/shard_map/ppermute | solution.py:176
  1082.8 11.8 %collective-permute-start.82 = (bf16[48,1536]{1,0:T(8,128)(2,1)S(1)}, bf16[48,1536]{1,0:T(8,128)(2,1)S(1)}, u32[]{:S(2)}, u32[]{:S(2)}) collective-permute-start(bf16[48,1536]{1,0:T(8,128)(2,1)S(1)} %dynamic-slice_bitcast_fusion.31), channel_id=1, source_target_pairs={{0,16},{2,18},{4,20},{6,22},{8,24},{10,26},{12,28},{14,30},{16,0},... | collective-permute-start | bytes 442376 | tf_op jit(solution)/shard_map/ppermute | solution.py:176
  1088.4 12.4 %collective-permute-start.87 = (bf16[48,1536]{1,0:T(8,128)(2,1)S(1)}, bf16[48,1536]{1,0:T(8,128)(2,1)S(1)}, u32[]{:S(2)}, u32[]{:S(2)}) collective-permute-start(bf16[48,1536]{1,0:T(8,128)(2,1)S(1)} %dynamic-slice_bitcast_fusion.30), channel_id=1, source_target_pairs={{0,16},{2,18},{4,20},{6,22},{8,24},{10,26},{12,28},{14,30},{16,0},... | collective-permute-start | bytes 442376 | tf_op jit(solution)/shard_map/ppermute | solution.py:176
  (261 other events, 1670.0 us)

commit v2 on v1

v2 whole, which is shorter than its diff:
```python
import functools
import math

import jax
import jax.numpy as jnp
from jax import lax
from jax.experimental import pallas as pl
from jax.experimental.pallas import tpu as pltpu
from jax.sharding import PartitionSpec as P

HD = 64
EPS = 1e-06
BF = jnp.bfloat16
F32 = jnp.float32
SWAP = [(0, 1), (1, 0)]
LANES = 128
PAIR = 2
FAR = 2.0**30
VMEM = 56 * 1024 * 1024


def dot(a, b):
    return jnp.dot(a, b, preferred_element_type=F32)


def dot_nt(a, b):
    return lax.dot_general(a, b, (((1,), (1,)), ((), ())), preferred_element_type=F32)


def dot_tn(a, b):
    return lax.dot_general(a, b, (((0,), (0,)), ((), ())), preferred_element_type=F32)


def norm_stats(h):
    centered = h - jnp.mean(h, axis=-1, keepdims=True)
    inv = lax.rsqrt(jnp.mean(centered * centered, axis=-1, keepdims=True) + EPS)
    return centered * inv, inv


def norm_back(normed, inv, gain, grad):
    t = grad * gain
    return inv * (t - jnp.mean(t, -1, keepdims=True) - normed * jnp.mean(t * normed, -1, keepdims=True))


def gelu_pair(u):
    bell = jnp.exp(u * u * -0.5)
    t = 1.0 / (1.0 + (0.3275911 / math.sqrt(2.0)) * jnp.abs(u))
    poly = ((((1.061405429 * t - 1.453152027) * t + 1.421413741) * t - 0.284496736) * t + 0.254829592) * t
    tail = 0.5 * poly * bell
    cdf = jnp.where(u >= 0, 1.0 - tail, tail)
    return u * cdf, cdf + u * bell * (1.0 / math.sqrt(2.0 * math.pi))


def low_lanes(shape):
    return lax.broadcasted_iota(jnp.int32, shape, len(shape) - 1) < HD


def load_weights(j, slot, own, rem, buf, each):
    @pl.when(j < each)
    def _():
        for i in range(3):
            buf[:, i * LANES : (i + 1) * LANES] = own[i]

    @pl.when(j >= each)
    def _():
        rows = rem[0].shape[0] // 3
        for k in range(4):
            start = pl.multiple_of((slot ^ k) * rows, rows)
            for i in range(3):
                buf[pl.ds(start, rows), i * LANES : (i + 1) * LANES] = rem[k][i * rows : (i + 1) * rows]


def load_out(slot, rem, buf, base):
    rows = rem[0].shape[0] // 2
    cols = rem[0].shape[1]
    for k in range(4):
        start = pl.multiple_of(base + (slot ^ k) * rows, rows)
        buf[pl.ds(start, rows), :cols] = rem[k][:rows]
        buf[pl.ds(start, rows), cols:] = rem[k][rows:]


def load_row(own, recv, spans, buf):
    at = 0
    for n in spans:
        buf[2 * at : 2 * at + n, :] = own[at : at + n]
        buf[2 * at + n : 2 * (at + n), :] = recv[at : at + n]
        at += n


def const(shape, *lead):
    n = len(shape)
    return pl.BlockSpec(
        (None,) * len(lead) + tuple(shape), lambda *_: tuple(lead) + (0,) * n, pipeline_mode=pl.Buffered(1)
    )


def const_out(shape):
    return pl.BlockSpec(tuple(shape), lambda *_: (0,) * len(shape))


def params():
    return pltpu.CompilerParams(vmem_limit_bytes=VMEM)


CHEAP = pl.CostEstimate(flops=1, bytes_accessed=1, transcendentals=0)


def fwd_kernel(dirs, each, which, spans, slot_ref, *refs):
    first = spans is not None
    if first:
        x_own, x_recv = refs[:2]
        refs = refs[2:]
    else:
        x = refs[0]
        refs = refs[1:]
    qf, kf, own, r0, r1, r2, r3 = refs[:7]
    refs = refs[7:]
    if first:
        wo, w0, w1, w2, w3, gain, bias = refs[:7]
        refs = refs[7:]
    q_out, k_out, v_out, c_out = refs[:4]
    probs = refs[4 : 4 + len(dirs)]
    refs = refs[4 + len(dirs) :]
    if first:
        norms, refs = refs[: 3 * len(spans)], refs[3 * len(spans) :]
        buf, x, ctx_all, wobuf = refs
    else:
        (buf,) = refs
    j = pl.program_id(0)
    slot = slot_ref[which]

    if first:

        @pl.when(j == 0)
        def _():
            load_row(x_own, x_recv, spans, x)

    load_weights(j, slot, own, (r0, r1, r2, r3), buf, each)
    qkv = dot(x[...], buf[...])
    q = (qkv[:, :LANES] * (1.0 / math.sqrt(HD))).astype(BF)
    k = qkv[:, LANES : 2 * LANES].astype(BF)
    v = qkv[:, 2 * LANES :].astype(BF)
    q_out[...] = q
    k_out[...] = k
    v_out[...] = v
    for (q0, q1, k0, k1), p_out in zip(dirs, probs):
        q_all = jnp.concatenate([q[q0:q1], qf[q0:q1]], 1)
        keys = k[k0:k1]
        values = v[k0:k1]
        zero = jnp.zeros_like(keys)
        low = low_lanes(keys.shape)
        ctx = []
        for a in range(PAIR):
            k_all = jnp.concatenate([jnp.where(low if a == 0 else ~low, keys, zero), kf[k0:k1]], 1)
            scores = dot_nt(q_all, k_all)
            ex = jnp.exp(scores - jnp.max(scores, -1, keepdims=True))
            p = (ex * (1.0 / jnp.sum(ex, -1, keepdims=True))).astype(BF)
            p_out[a] = p
            ctx.append(dot(p, values))
        both = jnp.where(low_lanes(ctx[0].shape), ctx[0], ctx[1]).astype(BF)
        c_out[q0:q1, :] = both
        if first:
            ctx_all[j, q0:q1, :] = both

    if first:

        @pl.when(j == 2 * each - 1)
        def _():
            half = wo.shape[0]
            wobuf[:half, :] = wo[...]
            load_out(slot, (w0, w1, w2, w3), wobuf, half)
            full = jnp.concatenate([ctx_all[i] for i in range(2 * each)], 1)
            h = x[...].astype(F32) + dot(full, wobuf[...])
            normed, inv = norm_stats(h)
            one = (normed * gain[0:1, :] + bias[0:1, :]).astype(BF)
            at = 0
            for s, n in enumerate(spans):
                norms[3 * s][...] = normed[at : at + 2 * n]
                norms[3 * s + 1][...] = inv[at : at + 2 * n]
                norms[3 * s + 2][...] = one[at : at + 2 * n]
                at += 2 * n


def attention_forward(x, qf, kf, in_proj, pack, index, which, slot, dirs, first=None):
    tokens = qf.shape[0]
    width, half = in_proj.shape[2:]
    each = half // LANES
    pairs = 2 * each
    rows = 3 * width // 4
    col = pl.BlockSpec((tokens, LANES), lambda j, s: (0, j))
    own_spec = pl.BlockSpec((None, 3, width, LANES), lambda j, s: (index, 0, 0, jnp.minimum(j, each - 1)))
    rem_spec = pl.BlockSpec((rows, LANES), lambda j, s: (0, jnp.maximum(j - each, 0)))
    p_shapes = [(2 * pairs, q1 - q0, k1 - k0) for q0, q1, k0, k1 in dirs]
    full = jax.ShapeDtypeStruct((tokens, 2 * half), BF)
    xs = x if first else (x,)
    in_specs = [const(a.shape) for a in xs] + [const(qf.shape), const(kf.shape), own_spec] + [rem_spec] * 4
    out_specs = [col] * 4 + [pl.BlockSpec((PAIR,) + s[1:], lambda j, s: (j, 0, 0)) for s in p_shapes]
    out_shape = [full] * 4 + [jax.ShapeDtypeStruct(s, BF) for s in p_shapes]
    scratch = [pltpu.VMEM((width, 3 * LANES), BF)]
    extra = ()
    spans = None
    if first:
        out_proj, gains, biases, spans = first
        out_rows = width // 4
        tail = pl.BlockSpec((out_rows, half), lambda j, s: (rows // out_rows, 0), pipeline_mode=pl.Buffered(1))
        in_specs += [const((half, width), index)] + [tail] * 4 + [const(gains.shape)] * 2
        extra = (out_proj, *pack, gains, biases)
        for n in spans:
            for shape, kind in (((2 * n, width), F32), ((2 * n, 1), F32), ((2 * n, width), BF)):
                out_specs.append(const_out(shape))
                out_shape.append(jax.ShapeDtypeStruct(shape, kind))
        scratch += [
            pltpu.VMEM((tokens, width), BF),
            pltpu.VMEM((pairs, tokens, LANES), BF),
            pltpu.VMEM((2 * half, width), BF),
        ]
    return pl.pallas_call(
        functools.partial(fwd_kernel, dirs, each, which, spans),
        grid_spec=pltpu.PrefetchScalarGridSpec(
            num_scalar_prefetch=1, grid=(pairs,), in_specs=in_specs, out_specs=out_specs, scratch_shapes=scratch
        ),
        out_shape=out_shape,
        compiler_params=params(),
        cost_estimate=CHEAP,
        name="attention_forward",
    )(slot, *xs, qf, kf, in_proj, *pack, *extra)


def ffn_kernel(
    blocks, which, stream, spans, slot_ref, n1, ctx, wo, w0, w1, w2, w3, gain, bias, cot_own, cot_recv, perm,
    up_own, down_own, u0, u1, u2, u3, d0, d1, d2, d3,
    out_own, out_send, dh2_out, g2_out, stats, send, keep,
    wobuf, uall, dall, ubuf, dbuf, hidden, slope, acc, x2, x2t, et, e, n2, inv2,
):
    i = pl.program_id(0)
    each = blocks // 2
    b = lax.rem(i, blocks)
    half = wo.shape[0]
    tokens, width = n1.shape
    ln = 1 + stream
    last = 3 + stream

    @pl.when(i == 0)
    def _():
        cols = u0.shape[1]
        for k in range(4):
            u, d = (u0, u1, u2, u3)[k], (d0, d1, d2, d3)[k]
            uall[slot_ref[which[1]] ^ k] = u[...]
            at = slot_ref[which[2]] ^ k
            dall[at, :, :cols] = d[:cols, :]
            dall[at, :, cols:] = d[cols:, :]

    @pl.when(b < each)
    def _():
        ubuf[...] = up_own[...]
        dbuf[...] = down_own[...]

    @pl.when(b >= each)
    def _():
        ubuf[...] = uall[b - each]
        dbuf[...] = dall[b - each]

    @pl.when(i == 0)
    def _():
        wobuf[:half, :] = wo[...]
        load_out(slot_ref[which[0]], (w0, w1, w2, w3), wobuf, half)
        one = n1[...] * gain[0:1, :] + bias[0:1, :]
        h2 = one + dot(ctx[...], wobuf[...])
        normed, inv = norm_stats(h2)
        n2[...] = normed
        inv2[...] = inv
        two = normed * gain[ln : ln + 1, :] + bias[ln : ln + 1, :]
        acc[...] = two
        low = two.astype(BF)
        x2[...] = low
        x2t[...] = dot_nt(perm[...], low).astype(BF)

    @pl.when(i < blocks)
    def _():
        act, der = gelu_pair(dot(x2[...], ubuf[...]))
        act = act.astype(BF)
        hidden[b] = act
        slope[b] = der.astype(slope.dtype)
        acc[...] += dot(act, dbuf[...])

    @pl.when(i == blocks - 1)
    def _():
        normed, inv = norm_stats(acc[...])
        out = (normed * gain[last : last + 1, :] + bias[last : last + 1, :]).astype(BF)
        n = tokens // 2
        out_own[...] = out[:n]
        out_send[...] = out[n:]
        at = sum(spans[:stream])
        g = jnp.concatenate([cot_own[at : at + n], cot_recv[at : at + n]], 0).astype(F32)
        stats[0:1, :] = jnp.sum(g * normed, 0, keepdims=True)
        stats[1:2, :] = jnp.sum(g, 0, keepdims=True)
        dh3 = norm_back(normed, inv, gain[last : last + 1, :], g)
        acc[...] = dh3
        low = dh3.astype(BF)
        e[...] = low
        et[...] = dot_nt(perm[...], low).astype(BF)

    @pl.when(i >= blocks)
    def _():
        du = (dot_nt(e[...], dbuf[...]) * slope[b].astype(F32)).astype(BF)
        acc[...] += dot_nt(du, ubuf[...])
        rows = send.shape[1]
        up_grad = dot(x2t[...], du).astype(BF)
        keep[0] = up_grad[:rows]
        send[0] = up_grad[rows:]
        down_grad = dot(et[...], hidden[b]).astype(BF)
        keep[1] = down_grad[:rows]
        send[1] = down_grad[rows:]

    @pl.when(i == 2 * blocks - 1)
    def _():
        normed = n2[...]
        g = acc[...]
        stats[2:3, :] = jnp.sum(g * normed, 0, keepdims=True)
        stats[3:4, :] = jnp.sum(g, 0, keepdims=True)
        dh2 = norm_back(normed, inv2[...], gain[ln : ln + 1, :], g)
        dh2_out[...] = dh2
        g2_out[...] = dh2.astype(BF)


def feed_forward(
    n1, ctx, out_proj, wo_pack, gains, biases, cot_own, cot_recv, perm, up_proj, down_proj, up_pack, down_pack, which, slot, stream, spans
):
    tokens, width = n1.shape
    half = out_proj.shape[1]
    hid = up_proj.shape[2]
    block = up_pack[0].shape[1]
    each = hid // block
    blocks = 2 * each

    def own(i):
        return jnp.minimum(lax.rem(i, blocks), each - 1)

    def grad_map(i, s):
        b = jnp.maximum(i - blocks, 0)
        return (jnp.where(b < each, 0, 1), 0, 0, lax.rem(b, each))

    grad_spec = pl.BlockSpec((None, 2, width // 2, block), grad_map)
    grad_shape = jax.ShapeDtypeStruct((2, 2, width // 2, hid), BF)
    out_rows = width // 4
    tail = pl.BlockSpec((out_rows, half), lambda i, s: (3, 0), pipeline_mode=pl.Buffered(1))
    return pl.pallas_call(
        functools.partial(ffn_kernel, blocks, which, stream, spans),
        grid_spec=pltpu.PrefetchScalarGridSpec(
            num_scalar_prefetch=1,
            grid=(2 * blocks,),
            in_specs=[const((tokens, width)), const((tokens, width)), const((half, width), 1 + stream)]
            + [tail] * 4
            + [const(gains.shape)] * 2
            + [const(cot_own.shape)] * 2
            + [const((width, width))]
            + [
                pl.BlockSpec((None, width, block), lambda i, s: (stream, 0, own(i))),
                pl.BlockSpec((None, block, width), lambda i, s: (stream, own(i), 0)),
            ]
            + [const(up_pack[0].shape)] * 4
            + [const(down_pack[0].shape)] * 4,
            out_specs=[const_out((tokens // 2, width))] * 2
            + [const_out((tokens, width))] * 2
            + [const_out((4, width)), grad_spec, grad_spec],
            scratch_shapes=[
                pltpu.VMEM((2 * half, width), BF),
                pltpu.VMEM((4, width, block), BF),
                pltpu.VMEM((4, block, width), BF),
                pltpu.VMEM((width, block), BF),
                pltpu.VMEM((block, width), BF),
                pltpu.VMEM((blocks, tokens, block), BF),
                pltpu.VMEM((blocks, tokens, block), F32),
                pltpu.VMEM((tokens, width), F32),
                pltpu.VMEM((tokens, width), BF),
                pltpu.VMEM((width, tokens), BF),
                pltpu.VMEM((width, tokens), BF),
                pltpu.VMEM((tokens, width), BF),
                pltpu.VMEM((tokens, width), F32),
                pltpu.VMEM((tokens, 1), F32),
            ],
        ),
        out_shape=[
            jax.ShapeDtypeStruct((tokens // 2, width), BF),
            jax.ShapeDtypeStruct((tokens // 2, width), BF),
            jax.ShapeDtypeStruct((tokens, width), F32),
            jax.ShapeDtypeStruct((tokens, width), BF),
            jax.ShapeDtypeStruct((4, width), F32),
            grad_shape,
            grad_shape,
        ],
        compiler_params=params(),
        cost_estimate=CHEAP,
        name="feed_forward",
    )(slot, n1, ctx, out_proj, *wo_pack, gains, biases, cot_own, cot_recv, perm, up_proj, down_proj, *up_pack, *down_pack)


def bwd_kernel(dirs, each, which, spans, slot_ref, *refs):
    last = spans is not None
    n_in = 6 if last else 3
    sources, refs = refs[:n_in], refs[n_in:]
    perm, own, r0, r1, r2, r3, wo, w0, w1, w2, w3, q_in, k_in, v_in, c_in = refs[:15]
    refs = refs[15:]
    probs, refs = refs[: len(dirs)], refs[len(dirs) :]
    if last:
        dx_own, dx_send, send, keep = refs[:4]
        refs = refs[4:]
    else:
        n1, inv1, gain, dx_out, low_out, stats, send, keep = refs[:8]
        refs = refs[8:]
    buf, wobuf, xt, gt, dqkv, acc, g = refs
    j = pl.program_id(0)
    slot = slot_ref[which]
    load_weights(j, slot, own, (r0, r1, r2, r3), buf, each)

    @pl.when(j == 0)
    def _():
        half = wo.shape[0]
        wobuf[:half, :] = wo[...]
        load_out(slot, (w0, w1, w2, w3), wobuf, half)
        if last:
            x_own, x_recv, g_a, g_b, base_a, base_b = sources
            load_row(x_own, x_recv, spans, g)
            xt[...] = dot_nt(perm[...], g[...]).astype(BF)
            cut = g_a.shape[0]
            g[:cut, :] = g_a[...]
            g[cut:, :] = g_b[...]
            acc[:cut, :] = base_a[...]
            acc[cut:, :] = base_b[...]
        else:
            x, g_a, base = sources
            xt[...] = dot_nt(perm[...], x[...]).astype(BF)
            g[...] = g_a[...]
            acc[...] = base[...]
        gt[...] = dot_nt(perm[...], g[...]).astype(BF)

    dctx_all = dot_nt(g[...], wobuf[pl.ds(pl.multiple_of(j * LANES, LANES), LANES), :]).astype(BF)
    for (q0, q1, k0, k1), p_in in zip(dirs, probs):
        dctx = dctx_all[q0:q1]
        q = q_in[q0:q1, :]
        k = k_in[k0:k1, :]
        v = v_in[k0:k1, :]
        low = low_lanes(v.shape)
        zero = jnp.zeros_like(v)
        dq, dk, dv = [], [], []
        for a in range(PAIR):
            p = p_in[a]
            dp = dot_nt(dctx, jnp.where(low if a == 0 else ~low, v, zero))
            pf = p.astype(F32)
            ds = (pf * (dp - jnp.sum(pf * dp, -1, keepdims=True))).astype(BF)
            dq.append(dot(ds, k))
            dk.append(dot_tn(ds, q))
            dv.append(dot_tn(p, dctx))
        low_q = low_lanes(dq[0].shape)
        low_k = low_lanes(dk[0].shape)
        dqkv[q0:q1, :LANES] = (jnp.where(low_q, dq[0], dq[1]) * (1.0 / math.sqrt(HD))).astype(BF)
        dqkv[k0:k1, LANES : 2 * LANES] = jnp.where(low_k, dk[0], dk[1]).astype(BF)
        dqkv[k0:k1, 2 * LANES :] = jnp.where(low_k, dv[0], dv[1]).astype(BF)
    rows = send.shape[1]
    grads = dot(xt[...], dqkv[...]).astype(BF)
    for i in range(3):
        part = grads[:, i * LANES : (i + 1) * LANES]
        keep[i] = part[:rows]
        send[i] = part[rows:]
    out_grad = dot(gt[...], c_in[...]).astype(BF)
    keep[3] = out_grad[:rows]
    send[3] = out_grad[rows:]
    acc[...] += dot_nt(dqkv[...], buf[...])

    @pl.when(j == 2 * each - 1)
    def _():
        if last:
            at = 0
            for n in spans:
                dx_own[at : at + n, :] = acc[2 * at : 2 * at + n, :]
                dx_send[at : at + n, :] = acc[2 * at + n : 2 * (at + n), :].astype(BF)
                at += n
        else:
            total = acc[...]
            normed = n1[...]
            stats[0:1, :] = jnp.sum(total * normed, 0, keepdims=True)
            stats[1:2, :] = jnp.sum(total, 0, keepdims=True)
            dh = norm_back(normed, inv1[...], gain[0:1, :], total)
            dx_out[...] = dh
            low_out[...] = dh.astype(BF)


def attention_backward(sources, perm, in_proj, pack, index, which, out_proj, saved, norm, slot, dirs, spans=None):
    tokens = saved[0].shape[0]
    width, half = in_proj.shape[2:]
    each = half // LANES
    pairs = 2 * each
    rows = 3 * width // 4
    out_rows = width // 4
    col = pl.BlockSpec((tokens, LANES), lambda j, s: (0, j))
    own_spec = pl.BlockSpec((None, 3, width, LANES), lambda j, s: (index, 0, 0, jnp.minimum(j, each - 1)))
    rem_spec = pl.BlockSpec((rows, LANES), lambda j, s: (0, jnp.maximum(j - each, 0)))
    tail = pl.BlockSpec((out_rows, half), lambda j, s: (3, 0), pipeline_mode=pl.Buffered(1))
    p_shapes = [(2 * pairs, q1 - q0, k1 - k0) for q0, q1, k0, k1 in dirs]
    grad_spec = pl.BlockSpec(
        (None, 4, width // 2, LANES), lambda j, s: (jnp.where(j < each, 0, 1), 0, 0, lax.rem(j, each))
    )
    grad_shape = jax.ShapeDtypeStruct((2, 4, width // 2, half), BF)
    in_specs = [const(a.shape) for a in sources] + [const((width, width)), own_spec] + [rem_spec] * 4
    in_specs += [const((half, width), index)] + [tail] * 4
    in_specs += [col] * 4 + [pl.BlockSpec((PAIR,) + s[1:], lambda j, s: (j, 0, 0)) for s in p_shapes]
    if spans is None:
        in_specs += [const(a.shape) for a in norm]
        outs = [((tokens, width), F32), ((tokens, width), BF), ((2, width), F32)]
    else:
        outs = [((tokens // 2, width), F32), ((tokens // 2, width), BF)]
    return pl.pallas_call(
        functools.partial(bwd_kernel, dirs, each, which, spans),
        grid_spec=pltpu.PrefetchScalarGridSpec(
            num_scalar_prefetch=1,
            grid=(pairs,),
            in_specs=in_specs,
            out_specs=[const_out(s) for s, _ in outs] + [grad_spec, grad_spec],
            scratch_shapes=[
                pltpu.VMEM((width, 3 * LANES), BF),
                pltpu.VMEM((2 * half, width), BF),
                pltpu.VMEM((width, tokens), BF),
                pltpu.VMEM((width, tokens), BF),
                pltpu.VMEM((tokens, 3 * LANES), BF),
                pltpu.VMEM((tokens, width), F32),
                pltpu.VMEM((tokens, width), BF),
            ],
        ),
        out_shape=[jax.ShapeDtypeStruct(s, k) for s, k in outs] + [grad_shape, grad_shape],
        compiler_params=params(),
        cost_estimate=CHEAP,
        name="attention_backward",
    )(slot, *sources, perm, in_proj, *pack, out_proj, *pack, *saved, *(norm or ()))


def after(x, *deps):
    return lax.optimization_barrier((x,) + deps)[0]


def copies(pairs, sem):
    started = [pltpu.make_async_copy(a, b, sem.at[i]) for i, (a, b) in enumerate(pairs)]
    for c in started:
        c.start()
    for c in started:
        c.wait()


def attention_cuts(in_proj, out_proj, s, p, pack):
    rows = in_proj.shape[2] // 4
    cols = in_proj.shape[3]
    out_rows = out_proj.shape[1] // 4
    at = pl.multiple_of(p * rows, rows)
    out_at = pl.multiple_of(p * out_rows, out_rows)
    pairs = [(in_proj.at[s, i, pl.ds(at, rows), :], pack.at[pl.ds(i * rows, rows), :]) for i in range(3)]
    for c in range(2):
        pairs.append(
            (
                out_proj.at[s, pl.ds(out_at, out_rows), pl.ds(c * cols, cols)],
                pack.at[pl.ds(3 * rows + c * out_rows, out_rows), :],
            )
        )
    return pairs


def row_cuts(arrays, t, own, other):
    pairs = []
    at = 0
    for a in arrays:
        n = a.shape[1]
        pairs.append((a.at[t], own.at[pl.ds(at, n), :]))
        pairs.append((a.at[1 - t], other.at[pl.ds(at, n), :]))
        at += n
    return pairs


def first_cut_kernel(place, in_proj, out_proj, lang, visn, pack, own, other, sem):
    copies(
        attention_cuts(in_proj, out_proj, 0, place[0], pack) + row_cuts((lang, visn), place[2], own, other), sem
    )


def second_cut_kernel(
    place, in_proj, out_proj, up, down, lang, visn, self_l, self_v, up_l, up_v, down_l, down_v, own, other, sem
):
    px, pz = place[0], place[1]
    pairs = attention_cuts(in_proj, out_proj, 1, pz, self_l) + attention_cuts(in_proj, out_proj, 2, pz, self_v)
    cols = up_l.shape[1]
    for s, u, d in ((0, up_l, down_l), (1, up_v, down_v)):
        pairs.append((up.at[s, :, pl.ds(pl.multiple_of(px * cols, cols), cols)], u))
        for c in range(2):
            pairs.append(
                (
                    down.at[s, pl.ds(pl.multiple_of(pz * cols, cols), cols), pl.ds(c * cols, cols)],
                    d.at[pl.ds(c * cols, cols), :],
                )
            )
    copies(pairs + row_cuts((lang, visn), place[2], own, other), sem)


def cut_call(kernel, n_copies, shapes, place, *arrays):
    hbm = pl.BlockSpec(memory_space=pl.ANY)
    return pl.pallas_call(
        kernel,
        in_specs=[pl.BlockSpec(memory_space=pltpu.SMEM)] + [hbm] * len(arrays),
        out_specs=[pl.BlockSpec(memory_space=pltpu.VMEM)] * len(shapes),
        out_shape=[jax.ShapeDtypeStruct(s, BF) for s in shapes],
        scratch_shapes=[pltpu.SemaphoreType.DMA((n_copies,))],
        compiler_params=params(),
        cost_estimate=CHEAP,
        name="cut",
    )(place, *arrays)


class Chain:
    def __init__(self, terms, order, exchange):
        self.terms = list(terms)
        self.order = list(order)
        self.exchange = exchange

    def start(self, *deps):
        stage = self.order.pop(0)
        if stage < 0:
            out = sum(x[1].astype(F32) for x in self.terms)
            keep = [x[0] for x in self.terms]
        else:
            rows = self.terms[0].shape[-2] // 2
            out = sum(x[..., rows:, :].astype(F32) for x in self.terms)
            keep = [x[..., :rows, :] for x in self.terms]
        received = self.exchange(after(out.astype(BF), *deps), stage)
        self.terms = keep + [received]
        return received

    def total(self):
        while self.order:
            self.start()
        return sum(x.astype(F32) for x in self.terms)


def on_device(
    lang_input, visn_input, word_seg, region_seg, in_proj, out_proj, up_proj, down_proj,
    ln_gain, ln_bias, lang_cotan, visn_cotan,
):
    n_dp = lax.axis_size("dp")
    bits = n_dp.bit_length() - 1
    t = lax.axis_index("tensor")
    d = lax.axis_index("dp")
    width, half = in_proj.shape[2:]
    spans = (lang_input.shape[1], visn_input.shape[1])

    def exchange(x, stage):
        if stage < 0:
            return lax.ppermute(x, "tensor", SWAP)
        return lax.ppermute(x, "dp", [(i, i ^ (1 << stage)) for i in range(n_dp)])

    Y, C, X, Z = -1, 0, 1, 2
    rest = list(range(2, bits))
    y_first = [Y, X] + rest
    x_first = [X, Y] + rest
    SX, SZ = 0, 1

    def piece_of(hop):
        return (d & 1) * 2 + ((d >> hop) & 1)

    def own_seg(seg):
        row = lax.dynamic_index_in_dim(seg, t, 0, keepdims=False)
        n = row.shape[0] // 2
        return jnp.where(t == 0, row, jnp.concatenate([row[n:], row[:n]]))

    slot = jnp.stack([piece_of(X), piece_of(Z), t]).astype(jnp.int32)
    attn_pack = (width, half)
    rows_shape = (sum(spans), width)
    cross_piece, x_own, x_other = cut_call(
        first_cut_kernel, 9, [attn_pack, rows_shape, rows_shape], slot, in_proj, out_proj, lang_input, visn_input
    )
    cross_y = exchange(cross_piece, Y)
    self_l_piece, self_v_piece, up_l_piece, up_v_piece, down_l_piece, down_v_piece, cot_own, cot_other = cut_call(
        second_cut_kernel, 20, [attn_pack] * 6 + [rows_shape] * 2, after(slot, x_own),
        in_proj, out_proj, up_proj, down_proj, lang_cotan, visn_cotan,
    )
    seg = jnp.concatenate([own_seg(word_seg), own_seg(region_seg)])[:, None]
    lane = jnp.arange(LANES)[None, :]
    qf = jnp.where(lane == seg, -FAR, 0.0).astype(BF)
    kf = jnp.where((lane < 4) & (lane != seg), 1.0, 0.0).astype(BF)
    chunk = width // n_dp
    place = jnp.arange(width)
    order = sum((((place // chunk) >> (bits - 1 - b)) & 1) << b for b in range(bits)) ^ d
    perm = (place[None, :] == (order * chunk + place % chunk)[:, None]).astype(BF)
    qf, kf, perm = lax.optimization_barrier((qf, kf, perm))
    lw, lv = 2 * spans[0], 2 * spans[1]
    streams = ((0, lw), (lw, lw + lv))

    x_recv = exchange(after(x_other, cross_y, down_v_piece), Y)
    cross_x = exchange(cross_y, X)
    cross_pack = [cross_y, cross_x, exchange(cross_y, C), exchange(cross_x, C)]
    self_l_y = exchange(after(self_l_piece, x_recv), Y)
    up_l_y = exchange(after(up_l_piece, x_recv), Y)

    cross_dirs = ((0, lw, lw, lw + lv), (lw, lw + lv, 0, lw))
    f1 = attention_forward(
        (x_own, x_recv), qf, kf, in_proj, cross_pack, 0, SX, after(slot, perm), cross_dirs,
        (out_proj, ln_gain, ln_bias, spans),
    )
    cross, norms = f1[:6], (f1[6:9], f1[9:12])
    tok = norms[0][1]

    def self_forward(j, pack, slot_tied):
        lo, hi = streams[j]
        return attention_forward(
            norms[j][2], qf[lo:hi], kf[lo:hi], in_proj, pack, 1 + j, SZ, slot_tied, ((0, hi - lo, 0, hi - lo),)
        )

    def feed(j, ctx, wo_pack, up_pack, down_pack, slot_tied):
        return feed_forward(
            norms[j][0], ctx, out_proj, wo_pack, ln_gain, ln_bias, cot_own, cot_recv, perm, up_proj, down_proj,
            up_pack, down_pack, (SZ, SX, SZ), slot_tied, j, spans,
        )

    def self_back(j, ffn, saved, pack, slot_tied):
        n = streams[j][1] - streams[j][0]
        return attention_backward(
            (norms[j][2], ffn[3], ffn[2]), perm, in_proj, pack, 1 + j, SZ, out_proj, saved,
            (norms[j][0], norms[j][1], ln_gain), slot_tied, ((0, n, 0, n),),
        )

    self_l_z = exchange(after(self_l_y, tok), Z)
    up_l_x = exchange(after(up_l_y, tok), X)
    down_l_y = exchange(after(down_l_piece, tok), Y)
    self_l_pack = [self_l_y, self_l_z, exchange(after(self_l_y, tok), C), exchange(self_l_z, C)]
    up_l_pack = [up_l_y, up_l_x, exchange(after(up_l_y, self_l_z), C), exchange(after(up_l_x, self_l_z), C)]
    down_l_z = exchange(after(down_l_y, self_l_z), Z)
    cot_recv = exchange(after(cot_other, down_l_y), Y)
    self_l = self_forward(0, self_l_pack, after(slot, down_l_y, up_l_x))
    tok = self_l[3]
    down_l_pack = [down_l_y, down_l_z, exchange(after(down_l_y, tok), C), exchange(after(down_l_z, tok), C)]
    self_v_y = exchange(after(self_v_piece, tok, cot_recv), Y)
    up_v_y = exchange(after(up_v_piece, tok, cot_recv), Y)
    down_v_y = exchange(after(down_v_piece, tok, cot_recv), Y)

    ffn_l = feed(0, self_l[3], self_l_pack, up_l_pack, down_l_pack, after(slot, up_l_pack[3]))
    tok = ffn_l[4]
    fl_core = exchange(ffn_l[5], C)
    self_v_z = exchange(after(self_v_y, tok), Z)
    self_v_c = exchange(after(self_v_y, tok), C)
    out_l_recv = exchange(after(ffn_l[1], tok), Y)

    back_l = self_back(0, ffn_l, self_l, self_l_pack, after(slot, self_v_y, up_v_y, down_v_y))
    tok = back_l[2]
    self_v_pack = [self_v_y, self_v_z, self_v_c, exchange(after(self_v_z, tok), C)]
    up_v_x = exchange(after(up_v_y, tok), X)
    down_v_z = exchange(after(down_v_y, tok), Z)
    up_v_c = exchange(after(up_v_y, tok), C)
    down_v_c = exchange(after(down_v_y, tok), C)
    sl_core = exchange(back_l[3], C)

    self_v = self_forward(1, self_v_pack, after(slot, fl_core, out_l_recv, self_v_z))
    tok = self_v[3]
    up_v_pack = [up_v_y, up_v_x, up_v_c, exchange(after(up_v_x, tok), C)]
    down_v_pack = [down_v_y, down_v_z, down_v_c, exchange(after(down_v_z, tok), C)]
    fl = Chain([ffn_l[6], fl_core], y_first, exchange)
    sl = Chain([back_l[4], sl_core], x_first, exchange)
    fl_r = fl.start(tok)
    sl_r = sl.start(tok)

    ffn_v = feed(1, self_v[3], self_v_pack, up_v_pack, down_v_pack, after(slot, up_v_c, down_v_c, sl_core))
    tok = ffn_v[4]
    fv_core = exchange(ffn_v[5], C)
    out_v_recv = exchange(after(ffn_v[1], tok), Y)
    fl_r2 = fl.start(tok)
    sl_r2 = sl.start(tok)

    back_v = self_back(1, ffn_v, self_v, self_v_pack, after(slot, fl_r, sl_r))
    tok = back_v[2]
    gains = jnp.stack([back_l[2][0] + back_v[2][0], ffn_l[4][2], ffn_v[4][2], ffn_l[4][0], ffn_v[4][0]])
    biases = jnp.stack([back_l[2][1] + back_v[2][1], ffn_l[4][3], ffn_v[4][3], ffn_l[4][1], ffn_v[4][1]])
    stats = jnp.concatenate([gains, biases])
    fv_a = Chain([ffn_v[6][:, :1], fv_core[:, :1]], y_first, exchange)
    fv_b = Chain([ffn_v[6][:, 1:], fv_core[:, 1:]], x_first, exchange)
    sv_core = exchange(back_v[3], C)
    fv_ra = fv_a.start(tok)
    fv_rb = fv_b.start(tok)
    fl_r3 = fl.start(tok)
    sl_r3 = sl.start(tok)
    stats_r = exchange(after(stats, tok), C)

    last = attention_backward(
        (x_own, x_recv, back_l[1], back_v[1], back_l[0], back_v[0]), perm, in_proj, cross_pack, 0, SX, out_proj, cross,
        None, after(slot, fl_r2, sl_r2, fv_core, out_v_recv), cross_dirs, spans,
    )
    tok = last[0]
    x_core = exchange(last[2], C)
    grad_recv = exchange(after(last[1], x_core), Y)
    sv = Chain([back_v[4], sv_core], x_first, exchange)
    sv.start(tok)
    stats = stats + stats_r
    for stage in [Y] + list(range(1, bits)):
        stats = stats + exchange(after(stats, tok), stage)
    cx_a = Chain([last[3][:, :2], x_core[:, :2]], y_first, exchange)
    cx_b = Chain([last[3][:, 2:], x_core[:, 2:]], x_first, exchange)
    chains = [fv_a, fv_b, sv, fl, sl, cx_a, cx_b]
    while any(c.order for c in chains):
        for c in chains:
            if c.order:
                c.start()
    fv_a, fv_b, sv, fl, sl, cx_a, cx_b = [c.total() for c in chains]
    cx = jnp.concatenate([cx_a, cx_b], 0)
    fv = jnp.concatenate([fv_a, fv_b], 0)

    def whole(mine, back):
        back = back.astype(mine.dtype)
        return jnp.where(t == 0, jnp.stack([mine, back]), jnp.stack([back, mine]))

    cut_at = spans[0]
    attn = (cx, sl, sv)
    ffn = (fl, fv)
    share = stats.shape[1] // (n_dp * 2)
    stats = lax.dynamic_slice_in_dim(stats, (d * 2 + t) * share, share, 1)
    return (
        whole(ffn_l[0], out_l_recv),
        whole(ffn_v[0], out_v_recv),
        whole(last[0][:cut_at], grad_recv[:cut_at]),
        whole(last[0][cut_at:], grad_recv[cut_at:]),
        jnp.stack([g[:3] for g in attn]),
        jnp.stack([g[3].T for g in attn]),
        jnp.stack([g[0] for g in ffn]),
        jnp.stack([g[1].T for g in ffn]),
        stats[:5],
        stats[5:],
    )


def solution(mesh):
    rows = P("dp", "tensor", None)
    placed = (
        rows, rows, P("dp", None), P("dp", None),
        P(None, None, None, "tensor"), P(None, "tensor", None), P(None, None, "tensor"), P(None, "tensor", None),
        P(), P(), rows, rows,
    )
    return jax.shard_map(
        on_device,
        mesh=mesh,
        in_specs=placed,
        out_specs=(
            rows, rows, rows, rows,
            P(None, None, "dp", "tensor"), P(None, "tensor", "dp"), P(None, "dp", "tensor"), P(None, "tensor", "dp"),
            P(None, ("dp", "tensor")), P(None, ("dp", "tensor")),
        ),
        check_vma=False,
    )
```

time: 1120 us -> 655 us (0.58); the launches traced: 1100 us -> 652 us
  matrix products: 429 us -> 0 us
  Pallas kernels: 0 us -> 268 us
  local copies, waits for them, and re-layouts: 137 us -> 35.1 us
  other arithmetic: 125 us -> 38.1 us
  blocking collectives: 41.3 us -> 0 us
  waiting for transfers between devices: 283 us -> 243 us
  starting transfers between devices: 83.3 us -> 66.4 us
    dot_general x136 -> x0, matrix products: 393 us -> none  [the longest x32 76 us: dot_nt(): lax.dot_general(a, b, (((1,), (1,)), ((), ())), preferred_element_type=F32)]
    pallas_call x0 -> x10, Pallas kernels: none -> 268 us  [the longest x3 105 us: attention_backward(): pl.pallas_call(functools.partial(bwd_kernel, dirs, each, which, spans), g...]
    psum x1 -> x0, blocking collectives: 41.3 us -> none  [on_device(): stats = lax.psum(jnp.stack(gains + biases), ('dp', 'tensor'))]
    ppermute x88 -> x71, waiting for transfers between devices: 283 us -> 243 us  [the longest x51 144 us: exchange(): return lax.ppermute(x, 'dp', [(i, i ^ 1 << stage) for i in range(n_dp)])]
    sub x8 -> x0, matrix products: 36 us -> none  [attend(): ex = jnp.exp(masked - top)]
    convert_element_type x54 -> x30, other arithmetic: 52 us -> 25.2 us  [the longest x28 23 us: start(): received = self.exchange(after(out.astype(BF), *deps), stage)]
    convert_element_type x16 -> x0, local copies, waits for them, and re-layouts: 23.1 us -> none  [the longest x12 16.4 us: qkv(): return [dot(x, w[i]).astype(BF) for i in range(3)]]
    slice x46 -> x8, local copies, waits for them, and re-layouts: 26.5 us -> 3.43 us  [the longest x2 1.32 us: self_forward(): kf[lo:hi]]
  transfers between devices with their start and end apart: 88 -> 71, of which waited for: 44 -> 36; matrix products, arithmetic and copies ran while one was open for 38% -> 10% of each run, Pallas kernels for 0% -> 27%
where the time goes in v2:
time: 655 us; the launch traced here: 652 us
  Pallas kernels  268 us (41%)
  waiting for transfers between devices  243 us (37%)
  starting transfers between devices  66.4 us (10%)
  other arithmetic  38.1 us (6%)
  local copies, waits for them, and re-layouts  35.1 us (5%)
    ppermute x51, waiting for transfers between devices, exchange(): return lax.ppermute(x, 'dp', [(i, i ^ 1 << stage) for i in range(n_dp)])  144 us
    pallas_call x3, Pallas kernels, attention_backward(): pl.pallas_call(functools.partial(bwd_kernel, dirs, each, which, spans), g...  105 us
    ppermute x20, waiting for transfers between devices, exchange(): return lax.ppermute(x, 'tensor', SWAP)  98.7 us
    pallas_call x2, Pallas kernels, feed_forward(): pl.pallas_call(functools.partial(ffn_kernel, blocks, which, stream, spans...  94.1 us
    pallas_call x3, Pallas kernels, attention_forward(): pl.pallas_call(functools.partial(fwd_kernel, dirs, each, which, spans), g...  59.5 us
    ppermute x51, starting transfers between devices, exchange(): return lax.ppermute(x, 'dp', [(i, i ^ 1 << stage) for i in range(n_dp)])  40.5 us
    ppermute x20, starting transfers between devices, exchange(): return lax.ppermute(x, 'tensor', SWAP)  25.9 us
    convert_element_type x28, other arithmetic, start(): received = self.exchange(after(out.astype(BF), *deps), stage)  23 us
  transfers between devices with their start and end apart: 71, of which 36 were waited for; matrix products, arithmetic and copies ran while one was open for 10% of the time, Pallas kernels for 27%

profile of v2, /device:TPU:0, one launch (start us, length us, event | category | flops | bytes accessed | tf_op | source)
XLA Modules:
  0.0 652.4 jit_solution(14004529359165819811)
XLA Ops:
  1.3 3.6 cut.2
  4.9 3.0 collective-permute-start
  7.9 5.8 cut.3
  13.7 7.8 %collective-permute-done.refs_5_.refs_10_.refs_8_.refs_13_ = bf16[768,384]{1,0:T(8,128)(2,1)S(1)} collective-permute-done((bf16[768,384]{1,0:T(8,128)(2,1)}, bf16[768,384]{1,0:T(8,128)(2,1)S(1)}, u32[]{:S(2)}, u32[]{:S(2)}) %collective-permute-start) | collective-permute-done | bytes 589856 | tf_op jit(solution)/shard_map/ppermute | solution.py:652
  21.4 1.7 collective-permute-start.1
  23.2 1.6 collective-permute-start.3
  25.2 11.9 %collective-permute-done.3.refs_6_.refs_11_.refs_9_.refs_14_ = bf16[768,384]{1,0:T(8,128)(2,1)S(1)} collective-permute-done((bf16[768,384]{1,0:T(8,128)(2,1)S(1)}, bf16[768,384]{1,0:T(8,128)(2,1)S(1)}, u32[]{:S(2)}, u32[]{:S(2)}) %collective-permute-start.3) | collective-permute-done | bytes 589856 | tf_op jit(solution)/shard_map/ppermute | solution.py:653
  44.0 28.4 %attention_forward.3 = (bf16[896,768]{1,0:T(8,128)(2,1)}, bf16[896,768]{1,0:T(8,128)(2,1)}, bf16[896,768]{1,0:T(8,128)(2,1)}, bf16[896,768]{1,0:T(8,128)(2,1)}, ...) custom-call(s32[3]{0:T(128)} %pad_add_fusion.1.place.slot_ref, ...), custom_call_target="tpu_custom_call" | custom-call | flops 1 | bytes 1 | tf_op jit(solution)/shard_map/attention_forward/pallas_call | solution.py:217
  77.0 9.8 %collective-permute-done.8.refs_5_.w1.refs_6_.refs_11_ = bf16[768,384]{1,0:T(8,128)(2,1)S(1)} collective-permute-done((bf16[768,384]{1,0:T(8,128)(2,1)S(1)}, bf16[768,384]{1,0:T(8,128)(2,1)S(1)}, u32[]{:S(2)}, u32[]{:S(2)}) %collective-permute-start.8) | collective-permute-done | bytes 589856 | tf_op jit(solution)/shard_map/ppermute | solution.py:653
  92.1 12.4 %attention_forward.4 = (bf16[320,768]{1,0:T(8,128)(2,1)}, bf16[320,768]{1,0:T(8,128)(2,1)}, bf16[320,768]{1,0:T(8,128)(2,1)}, bf16[320,768]{1,0:T(8,128)(2,1)}, bf16[12,320,320]{2,1,0:T(8,128)(2,1)}) custom-call(s32[3]{0:T(128)} %pad_add_fusion.1.place.slot_ref, bf16[320,768]{1,0:T(8,128)(2,1)} %get-tuple-element.144.refs_0_, ...), custom_call_target="tpu_custom_call" | custom-call | flops 1 | bytes 1 | tf_op jit(solution)/shard_map/attention_forward/pallas_call | solution.py:217
  108.2 45.7 %feed_forward.2 = (bf16[160,768]{1,0:T(8,128)(2,1)}, bf16[160,768]{1,0:T(8,128)(2,1)}, f32[320,768]{1,0:T(8,128)}, bf16[320,768]{1,0:T(8,128)(2,1)}, f32[4,768]{...) custom-call(s32[3]{0:T(128)} %pad_add_fusion.1.place.slot_ref, ...), custom_call_target="tpu_custom_call" | custom-call | flops 1 | bytes 1 | tf_op jit(solution)/shard_map/feed_forward/pallas_call | solution.py:347
  157.6 12.7 %collective-permute-done.19.u0 = bf16[768,384]{1,0:T(8,128)(2,1)S(1)} collective-permute-done((bf16[768,384]{1,0:T(8,128)(2,1)S(1)}, bf16[768,384]{1,0:T(8,128)(2,1)S(1)}, u32[]{:S(2)}, u32[]{:S(2)}) %collective-permute-start.19) | collective-permute-done | bytes 589856 | tf_op jit(solution)/shard_map/ppermute | solution.py:652
  170.3 12.6 %collective-permute-done.20.refs_4_.w0.refs_5_.refs_10_ = bf16[768,384]{1,0:T(8,128)(2,1)S(1)} collective-permute-done((bf16[768,384]{1,0:T(8,128)(2,1)S(1)}, bf16[768,384]{1,0:T(8,128)(2,1)S(1)}, u32[]{:S(2)}, u32[]{:S(2)}) %collective-permute-start.20) | collective-permute-done | bytes 589856 | tf_op jit(solution)/shard_map/ppermute | solution.py:652
  183.0 12.1 %collective-permute-done.21.d0 = bf16[768,384]{1,0:T(8,128)(2,1)S(1)} collective-permute-done((bf16[768,384]{1,0:T(8,128)(2,1)S(1)}, bf16[768,384]{1,0:T(8,128)(2,1)S(1)}, u32[]{:S(2)}, u32[]{:S(2)}) %collective-permute-start.21) | collective-permute-done | bytes 589856 | tf_op jit(solution)/shard_map/ppermute | solution.py:652
  195.0 22.8 %attention_backward.3 = (f32[320,768]{1,0:T(8,128)}, bf16[320,768]{1,0:T(8,128)(2,1)}, f32[2,768]{1,0:T(2,128)}, bf16[2,4,384,384]{3,2,1,0:T(8,128)(2,1)}, bf16[2,4,384,384]{3,2,1,0:T(8,128)(2,1)}) custom-call(s32[3]{0:T(128)} %pad_add_fusion.1.place.slot_ref, bf16[320,768]{1,0:T(8,128)(2,1)} %get-tuple-element.144.refs_0_, ...), custom_call_target="tpu_custom_call" | custom-call | flops 1 | bytes 1 | tf_op jit(solution)/shard_map/attention_backward/pallas_call | solution.py:512
  222.7 2.0 slice_bitcast_fusion.1
  224.7 2.4 slice_bitcast_fusion.14
  227.1 7.9 %collective-permute-done.26.refs_5_.w1.refs_6_.refs_11_ = bf16[768,384]{1,0:T(8,128)(2,1)S(1)} collective-permute-done((bf16[768,384]{1,0:T(8,128)(2,1)S(1)}, bf16[768,384]{1,0:T(8,128)(2,1)S(1)}, u32[]{:S(2)}, u32[]{:S(2)}) %collective-permute-start.26) | collective-permute-done | bytes 589856 | tf_op jit(solution)/shard_map/ppermute | solution.py:653
  236.2 2.3 fusion
  240.8 18.7 %attention_forward.5 = (bf16[576,768]{1,0:T(8,128)(2,1)}, bf16[576,768]{1,0:T(8,128)(2,1)}, bf16[576,768]{1,0:T(8,128)(2,1)}, bf16[576,768]{1,0:T(8,128)(2,1)}, bf16[12,576,576]{2,1,0:T(8,128)(2,1)}) custom-call(s32[3]{0:T(128)} %pad_add_fusion.1.place.slot_ref, bf16[576,768]{1,0:T(8,128)(2,1)} %get-tuple-element.178.refs_0_, ...), custom_call_target="tpu_custom_call" | custom-call | flops 1 | bytes 1 | tf_op jit(solution)/shard_map/attention_forward/pallas_call | solution.py:217
  261.0 1.6 collective-permute-start.31
  263.5 1.9 slice_bitcast_fusion.10
  265.5 2.9 add_convert_fusion.4
  268.4 7.4 %collective-permute-done.31.d1 = bf16[768,384]{1,0:T(8,128)(2,1)S(1)} collective-permute-done((bf16[768,384]{1,0:T(8,128)(2,1)S(1)}, bf16[768,384]{1,0:T(8,128)(2,1)S(1)}, u32[]{:S(2)}, u32[]{:S(2)}) %collective-permute-start.31) | collective-permute-done | bytes 589856 | tf_op jit(solution)/shard_map/ppermute | solution.py:653
  277.0 1.8 slice_bitcast_fusion
  280.6 48.4 %feed_forward.3 = (bf16[288,768]{1,0:T(8,128)(2,1)}, bf16[288,768]{1,0:T(8,128)(2,1)}, f32[576,768]{1,0:T(8,128)}, bf16[576,768]{1,0:T(8,128)(2,1)}, f32[4,768]{...) custom-call(s32[3]{0:T(128)} %pad_add_fusion.1.place.slot_ref, ...), custom_call_target="tpu_custom_call" | custom-call | flops 1 | bytes 1 | tf_op jit(solution)/shard_map/feed_forward/pallas_call | solution.py:347
  329.7 1.9 slice_bitcast_fusion.12
  333.0 2.8 add_convert_fusion.5
  337.2 1.6 fusion.3
  338.8 1.6 collective-permute-start.37
  343.4 11.0 %collective-permute-done.37 = bf16[4,192,384]{2,1,0:T(8,128)(2,1)S(1)} collective-permute-done((bf16[4,192,384]{2,1,0:T(8,128)(2,1)S(1)}, bf16[4,192,384]{2,1,0:T(8,128)(2,1)S(1)}, u32[]{:S(2)}, u32[]{:S(2)}) %collective-permute-start.37) | collective-permute-done | bytes 589856 | tf_op jit(solution)/shard_map/ppermute | solution.py:652
  355.3 36.7 %attention_backward.4 = (f32[576,768]{1,0:T(8,128)}, bf16[576,768]{1,0:T(8,128)(2,1)}, f32[2,768]{1,0:T(2,128)}, bf16[2,4,384,384]{3,2,1,0:T(8,128)(2,1)}, bf16[2,4,384,384]{3,2,1,0:T(8,128)(2,1)}) custom-call(s32[3]{0:T(128)} %pad_add_fusion.1.place.slot_ref, bf16[576,768]{1,0:T(8,128)(2,1)} %get-tuple-element.178.refs_0_, ...), custom_call_target="tpu_custom_call" | custom-call | flops 1 | bytes 1 | tf_op jit(solution)/shard_map/attention_backward/pallas_call | solution.py:512
  393.4 2.7 concatenate.19
  396.1 1.6 collective-permute-start.49
  397.9 1.8 add_convert_fusion.8
  400.3 5.9 collective-permute-done.49
  407.2 2.7 collective-permute-start.50
  410.8 9.8 %collective-permute-done.50 = bf16[4,48,384]{2,1,0:T(8,128)(2,1)S(1)} collective-permute-done((bf16[4,48,384]{2,1,0:T(8,128)(2,1)S(1)}, bf16[4,48,384]{2,1,0:T(8,128)(2,1)S(1)}, u32[]{:S(2)}, u32[]{:S(2)}) %collective-permute-start.50) | collective-permute-done | bytes 147488 | tf_op jit(solution)/shard_map/ppermute | solution.py:653
  423.0 3.4 collective-permute-start.57
  427.8 11.8 %collective-permute-done.57 = bf16[2,48,1536]{2,1,0:T(8,128)(2,1)S(1)} collective-permute-done((bf16[2,48,1536]{2,1,0:T(8,128)(2,1)S(1)}, bf16[2,48,1536]{2,1,0:T(8,128)(2,1)S(1)}, u32[]{:S(2)}, u32[]{:S(2)}) %collective-permute-start.57) | collective-permute-done | bytes 294944 | tf_op jit(solution)/shard_map/ppermute | solution.py:653
  442.5 45.8 %attention_backward.5 = (f32[448,768]{1,0:T(8,128)}, bf16[448,768]{1,0:T(8,128)(2,1)}, bf16[2,4,384,384]{3,2,1,0:T(8,128)(2,1)}, bf16[2,4,384,384]{3,2,1,0:T(8,128)(2,1)}) custom-call(s32[3]{0:T(128)} %pad_add_fusion.1.place.slot_ref, bf16[448,768]{1,0:T(8,128)(2,1)} %get-tuple-element.121.refs_0_, bf16[448,768]{1,0:T(8,128)(2,1)} %copy-done.14, ...), custom_call_target="tpu_custom_call" | custom-call | flops 1 | bytes 1 | tf_op jit(solution)/shard_map/attention_backward/pallas_call | solution.py:512
  489.6 1.6 collective-permute-start.67
  492.3 1.5 add_convert_fusion.1
  493.9 1.7 fusion.2
  502.9 2.7 collective-permute-done.69
  507.9 2.9 collective-permute-done.70
  511.6 12.3 %collective-permute-done.58 = bf16[1,384,1536]{2,1,0:T(8,128)(2,1)S(1)} collective-permute-done((bf16[1,384,1536]{2,1,0:T(8,128)(2,1)S(1)}, bf16[1,384,1536]{2,1,0:T(8,128)(2,1)S(1)}, u32[]{:S(2)}, u32[]{:S(2)}) %collective-permute-start.58) | collective-permute-done | bytes 1179680 | tf_op jit(solution)/shard_map/ppermute | solution.py:652
  525.6 1.6 collective-permute-done.62
  529.8 22.8 %collective-permute-done.52 = bf16[2,4,192,384]{3,2,1,0:T(8,128)(2,1)S(1)} collective-permute-done((bf16[2,4,192,384]{3,2,1,0:T(8,128)(2,1)S(1)}, bf16[2,4,192,384]{3,2,1,0:T(8,128)(2,1)S(1)}, u32[]{:S(2)}, u32[]{:S(2)}) %collective-permute-start.52) | collective-permute-done | bytes 1179680 | tf_op jit(solution)/shard_map/ppermute | solution.py:653
  555.4 7.6 %collective-permute-done.59 = bf16[1,192,1536]{2,1,0:T(8,128)(2,1)S(1)} collective-permute-done((bf16[1,192,1536]{2,1,0:T(8,128)(2,1)S(1)}, bf16[1,192,1536]{2,1,0:T(8,128)(2,1)S(1)}, u32[]{:S(2)}, u32[]{:S(2)}) %collective-permute-start.59) | collective-permute-done | bytes 589856 | tf_op jit(solution)/shard_map/ppermute | solution.py:653
  563.4 2.1 collective-permute-start.64
  565.7 9.0 %collective-permute-done.60 = bf16[1,96,1536]{2,1,0:T(8,128)(2,1)S(1)} collective-permute-done((bf16[1,96,1536]{2,1,0:T(8,128)(2,1)S(1)}, bf16[1,96,1536]{2,1,0:T(8,128)(2,1)S(1)}, u32[]{:S(2)}, u32[]{:S(2)}) %collective-permute-start.60) | collective-permute-done | bytes 294944 | tf_op jit(solution)/shard_map/ppermute | solution.py:653
  575.6 10.2 %collective-permute-done.54 = bf16[4,96,384]{2,1,0:T(8,128)(2,1)S(1)} collective-permute-done((bf16[4,96,384]{2,1,0:T(8,128)(2,1)S(1)}, bf16[4,96,384]{2,1,0:T(8,128)(2,1)S(1)}, u32[]{:S(2)}, u32[]{:S(2)}) %collective-permute-start.54) | collective-permute-done | bytes 294944 | tf_op jit(solution)/shard_map/ppermute | solution.py:653
  586.7 2.3 collective-permute-start.65
  589.0 7.9 %collective-permute-done.55 = bf16[4,48,384]{2,1,0:T(8,128)(2,1)S(1)} collective-permute-done((bf16[4,48,384]{2,1,0:T(8,128)(2,1)S(1)}, bf16[4,48,384]{2,1,0:T(8,128)(2,1)S(1)}, u32[]{:S(2)}, u32[]{:S(2)}) %collective-permute-start.55) | collective-permute-done | bytes 147488 | tf_op jit(solution)/shard_map/ppermute | solution.py:653
  603.9 12.8 %collective-permute-done.41 = bf16[2,384,384]{2,1,0:T(8,128)(2,1)S(1)} collective-permute-done((bf16[2,384,384]{2,1,0:T(8,128)(2,1)S(1)}, bf16[2,384,384]{2,1,0:T(8,128)(2,1)S(1)}, u32[]{:S(2)}, u32[]{:S(2)}) %collective-permute-start.41) | collective-permute-done | bytes 589856 | tf_op jit(solution)/shard_map/ppermute | solution.py:652
  618.1 1.6 collective-permute-start.46
  619.7 11.7 %collective-permute-done.40 = bf16[448,768]{1,0:T(8,128)(2,1)S(1)} collective-permute-done((bf16[448,768]{1,0:T(8,128)(2,1)S(1)}, bf16[448,768]{1,0:T(8,128)(2,1)S(1)}, u32[]{:S(2)}, u32[]{:S(2)}) %collective-permute-start.40) | collective-permute-done | bytes 688160 | tf_op jit(solution)/shard_map/ppermute | solution.py:652
  633.9 2.2 collective-permute-done.46
  636.4 2.1 collective-permute-start.43
  638.4 3.5 collective-permute-done.47
  642.1 2.2 collective-permute-done.43
  645.1 3.0 collective-permute-done.48
  648.2 2.3 collective-permute-done.44
  (319 shorter events, 92.5 us)
Async XLA Ops:
  4.9 16.6 %collective-permute-start = (bf16[768,384]{1,0:T(8,128)(2,1)}, bf16[768,384]{1,0:T(8,128)(2,1)S(1)}, u32[]{:S(2)}, u32[]{:S(2)}) collective-permute-start(bf16[768,384]{1,0:T(8,128)(2,1)} %get-tuple-element.125), channel_id=1, source_target_pairs={{0,1},{1,0},{2,3},{3,2},{4,5},{5,4},{6,7},{7,6},{8,9},{9,8},{10,11... | collective-permute-start | bytes 1769480 | tf_op jit(solution)/shard_map/ppermute | solution.py:652
  21.4 16.6 %collective-permute-start.1 = (bf16[448,768]{1,0:T(8,128)(2,1)S(1)}, bf16[448,768]{1,0:T(8,128)(2,1)S(1)}, u32[]{:S(2)}, u32[]{:S(2)}) collective-permute-start(bf16[448,768]{1,0:T(8,128)(2,1)S(1)} %copy-done.60), channel_id=1, source_target_pairs={{0,1},{1,0},{2,3},{3,2},{4,5},{5,4},{6,7},{7,6},{8,9},{9,8},{10,11... | collective-permute-start | bytes 2064392 | tf_op jit(solution)/shard_map/ppermute | solution.py:652
  23.2 14.0 %collective-permute-start.3 = (bf16[768,384]{1,0:T(8,128)(2,1)S(1)}, bf16[768,384]{1,0:T(8,128)(2,1)S(1)}, u32[]{:S(2)}, u32[]{:S(2)}) collective-permute-start(bf16[768,384]{1,0:T(8,128)(2,1)S(1)} %collective-permute-done.refs_5_.refs_10_.refs_8_.refs_13_), channel_id=1, source_target_pairs={{0,4},{2,6},{4,0},{6,2},{8,12},{10,14},{12,8},{14,10},{16,20},{18,... | collective-permute-start | bytes 1769480 | tf_op jit(solution)/shard_map/ppermute | solution.py:653
  25.2 17.1 %collective-permute-start.4 = (bf16[768,384]{1,0:T(8,128)(2,1)S(1)}, bf16[768,384]{1,0:T(8,128)(2,1)S(1)}, u32[]{:S(2)}, u32[]{:S(2)}) collective-permute-start(bf16[768,384]{1,0:T(8,128)(2,1)S(1)} %collective-permute-done.refs_5_.refs_10_.refs_8_.refs_13_), channel_id=1, source_target_pairs={{0,2},{2,0},{4,6},{6,4},{8,10},{10,8},{12,14},{14,12},{16,18},{18,... | collective-permute-start | bytes 1769480 | tf_op jit(solution)/shard_map/ppermute | solution.py:653
  37.2 5.2 collective-permute-start.5
  38.1 34.4 %collective-permute-start.7 = (bf16[768,384]{1,0:T(8,128)(2,1)}, bf16[768,384]{1,0:T(8,128)(2,1)S(1)}, u32[]{:S(2)}, u32[]{:S(2)}) collective-permute-start(bf16[768,384]{1,0:T(8,128)(2,1)} %get-tuple-element.136), channel_id=1, source_target_pairs={{0,1},{1,0},{2,3},{3,2},{4,5},{5,4},{6,7},{7,6},{8,9},{9,8},{10,11... | collective-permute-start | bytes 1769480 | tf_op jit(solution)/shard_map/ppermute | solution.py:652
  41.7 33.8 %collective-permute-start.2 = (bf16[768,384]{1,0:T(8,128)(2,1)}, bf16[768,384]{1,0:T(8,128)(2,1)S(1)}, u32[]{:S(2)}, u32[]{:S(2)}) collective-permute-start(bf16[768,384]{1,0:T(8,128)(2,1)} %get-tuple-element.128), channel_id=1, source_target_pairs={{0,1},{1,0},{2,3},{3,2},{4,5},{5,4},{6,7},{7,6},{8,9},{9,8},{10,11... | collective-permute-start | bytes 1769480 | tf_op jit(solution)/shard_map/ppermute | solution.py:652
  72.5 14.4 %collective-permute-start.8 = (bf16[768,384]{1,0:T(8,128)(2,1)S(1)}, bf16[768,384]{1,0:T(8,128)(2,1)S(1)}, u32[]{:S(2)}, u32[]{:S(2)}) collective-permute-start(bf16[768,384]{1,0:T(8,128)(2,1)S(1)} %collective-permute-done.7.refs_4_.w0.refs_5_.refs_10_), channel_id=1, source_target_pairs={{0,8},{2,10},{4,12},{6,14},{8,0},{10,2},{12,4},{14,6},{16,24},{18,... | collective-permute-start | bytes 1769480 | tf_op jit(solution)/shard_map/ppermute | solution.py:653
  74.0 14.3 %collective-permute-start.10 = (bf16[768,384]{1,0:T(8,128)(2,1)}, bf16[768,384]{1,0:T(8,128)(2,1)S(1)}, u32[]{:S(2)}, u32[]{:S(2)}) collective-permute-start(bf16[768,384]{1,0:T(8,128)(2,1)} %get-tuple-element.142), channel_id=1, source_target_pairs={{0,1},{1,0},{2,3},{3,2},{4,5},{5,4},{6,7},{7,6},{8,9},{9,8},{10,11... | collective-permute-start | bytes 1769480 | tf_op jit(solution)/shard_map/ppermute | solution.py:652
  75.5 15.2 %collective-permute-start.6 = (bf16[768,384]{1,0:T(8,128)(2,1)S(1)}, bf16[768,384]{1,0:T(8,128)(2,1)S(1)}, u32[]{:S(2)}, u32[]{:S(2)}) collective-permute-start(bf16[768,384]{1,0:T(8,128)(2,1)S(1)} %collective-permute-done.2.u0), channel_id=1, source_target_pairs={{0,4},{2,6},{4,0},{6,2},{8,12},{10,14},{12,8},{14,10},{16,20},{18,... | collective-permute-start | bytes 1769480 | tf_op jit(solution)/shard_map/ppermute | solution.py:653
  77.0 13.7 %collective-permute-start.11 = (bf16[768,384]{1,0:T(8,128)(2,1)S(1)}, bf16[768,384]{1,0:T(8,128)(2,1)S(1)}, u32[]{:S(2)}, u32[]{:S(2)}) collective-permute-start(bf16[768,384]{1,0:T(8,128)(2,1)S(1)} %collective-permute-done.7.refs_4_.w0.refs_5_.refs_10_), channel_id=1, source_target_pairs={{0,2},{2,0},{4,6},{6,4},{8,10},{10,8},{12,14},{14,12},{16,18},{18,... | collective-permute-start | bytes 1769480 | tf_op jit(solution)/shard_map/ppermute | solution.py:653
  88.3 16.1 %collective-permute-start.15 = (bf16[768,384]{1,0:T(8,128)(2,1)S(1)}, bf16[768,384]{1,0:T(8,128)(2,1)S(1)}, u32[]{:S(2)}, u32[]{:S(2)}) collective-permute-start(bf16[768,384]{1,0:T(8,128)(2,1)S(1)} %collective-permute-done.10.d0), channel_id=1, source_target_pairs={{0,8},{2,10},{4,12},{6,14},{8,0},{10,2},{12,4},{14,6},{16,24},{18,... | collective-permute-start | bytes 1769480 | tf_op jit(solution)/shard_map/ppermute | solution.py:653
  88.8 17.2 %collective-permute-start.13 = (bf16[448,768]{1,0:T(8,128)(2,1)S(1)}, bf16[448,768]{1,0:T(8,128)(2,1)S(1)}, u32[]{:S(2)}, u32[]{:S(2)}) collective-permute-start(bf16[448,768]{1,0:T(8,128)(2,1)S(1)} %copy-done.59), channel_id=1, source_target_pairs={{0,1},{1,0},{2,3},{3,2},{4,5},{5,4},{6,7},{7,6},{8,9},{9,8},{10,11... | collective-permute-start | bytes 2064392 | tf_op jit(solution)/shard_map/ppermute | solution.py:652
  90.7 14.3 %collective-permute-start.9 = (bf16[768,384]{1,0:T(8,128)(2,1)S(1)}, bf16[768,384]{1,0:T(8,128)(2,1)S(1)}, u32[]{:S(2)}, u32[]{:S(2)}) collective-permute-start(bf16[768,384]{1,0:T(8,128)(2,1)S(1)} %collective-permute-done.6.u1), channel_id=1, source_target_pairs={{0,2},{2,0},{4,6},{6,4},{8,10},{10,8},{12,14},{14,12},{16,18},{18,... | collective-permute-start | bytes 1769480 | tf_op jit(solution)/shard_map/ppermute | solution.py:653
  90.7 14.3 %collective-permute-start.14 = (bf16[768,384]{1,0:T(8,128)(2,1)S(1)}, bf16[768,384]{1,0:T(8,128)(2,1)S(1)}, u32[]{:S(2)}, u32[]{:S(2)}) collective-permute-start(bf16[768,384]{1,0:T(8,128)(2,1)S(1)} %collective-permute-done.2.u0), channel_id=1, source_target_pairs={{0,2},{2,0},{4,6},{6,4},{8,10},{10,8},{12,14},{14,12},{16,18},{18,... | collective-permute-start | bytes 1769480 | tf_op jit(solution)/shard_map/ppermute | solution.py:653
  153.9 81.8 %collective-permute-start.25 = (bf16[2,2,384,1536]{3,2,1,0:T(8,128)(2,1)}, bf16[2,2,384,1536]{3,2,1,0:T(8,128)(2,1)}, u32[]{:S(2)}, u32[]{:S(2)}) collective-permute-start(bf16[2,2,384,1536]{3,2,1,0:T(8,128)(2,1)} %get-tuple-element.175), channel_id=1, source_target_pairs={{0,2},{2,0},{4,6},{6,4},{8,10},{10,8},{12,14},{14,12},{16,18},{18,... | collective-permute-start | bytes 14155784 | tf_op jit(solution)/shard_map/ppermute | solution.py:653
  154.2 16.1 %collective-permute-start.19 = (bf16[768,384]{1,0:T(8,128)(2,1)S(1)}, bf16[768,384]{1,0:T(8,128)(2,1)S(1)}, u32[]{:S(2)}, u32[]{:S(2)}) collective-permute-start(bf16[768,384]{1,0:T(8,128)(2,1)S(1)} %copy-done.63), channel_id=1, source_target_pairs={{0,1},{1,0},{2,3},{3,2},{4,5},{5,4},{6,7},{7,6},{8,9},{9,8},{10,11... | collective-permute-start | bytes 1769480 | tf_op jit(solution)/shard_map/ppermute | solution.py:652
  155.6 27.4 %collective-permute-start.20 = (bf16[768,384]{1,0:T(8,128)(2,1)S(1)}, bf16[768,384]{1,0:T(8,128)(2,1)S(1)}, u32[]{:S(2)}, u32[]{:S(2)}) collective-permute-start(bf16[768,384]{1,0:T(8,128)(2,1)S(1)} %copy-done.62), channel_id=1, source_target_pairs={{0,1},{1,0},{2,3},{3,2},{4,5},{5,4},{6,7},{7,6},{8,9},{9,8},{10,11... | collective-permute-start | bytes 1769480 | tf_op jit(solution)/shard_map/ppermute | solution.py:652
  156.2 38.8 %collective-permute-start.21 = (bf16[768,384]{1,0:T(8,128)(2,1)S(1)}, bf16[768,384]{1,0:T(8,128)(2,1)S(1)}, u32[]{:S(2)}, u32[]{:S(2)}) collective-permute-start(bf16[768,384]{1,0:T(8,128)(2,1)S(1)} %copy-done.61), channel_id=1, source_target_pairs={{0,1},{1,0},{2,3},{3,2},{4,5},{5,4},{6,7},{7,6},{8,9},{9,8},{10,11... | collective-permute-start | bytes 1769480 | tf_op jit(solution)/shard_map/ppermute | solution.py:652
  217.8 45.7 %collective-permute-start.24 = (bf16[2,4,384,384]{3,2,1,0:T(8,128)(2,1)}, bf16[2,4,384,384]{3,2,1,0:T(8,128)(2,1)}, u32[]{:S(2)}, u32[]{:S(2)}) collective-permute-start(bf16[2,4,384,384]{3,2,1,0:T(8,128)(2,1)} %get-tuple-element.172), channel_id=1, source_target_pairs={{0,2},{2,0},{4,6},{6,4},{8,10},{10,8},{12,14},{14,12},{16,18},{18,... | collective-permute-start | bytes 7077896 | tf_op jit(solution)/shard_map/ppermute | solution.py:653
  219.2 19.3 %collective-permute-start.27 = (bf16[768,384]{1,0:T(8,128)(2,1)S(1)}, bf16[768,384]{1,0:T(8,128)(2,1)S(1)}, u32[]{:S(2)}, u32[]{:S(2)}) collective-permute-start(bf16[768,384]{1,0:T(8,128)(2,1)S(1)} %collective-permute-done.20.refs_4_.w0.refs_5_.refs_10_), channel_id=1, source_target_pairs={{0,2},{2,0},{4,6},{6,4},{8,10},{10,8},{12,14},{14,12},{16,18},{18,... | collective-permute-start | bytes 1769480 | tf_op jit(solution)/shard_map/ppermute | solution.py:653
  219.7 15.2 %collective-permute-start.26 = (bf16[768,384]{1,0:T(8,128)(2,1)S(1)}, bf16[768,384]{1,0:T(8,128)(2,1)S(1)}, u32[]{:S(2)}, u32[]{:S(2)}) collective-permute-start(bf16[768,384]{1,0:T(8,128)(2,1)S(1)} %collective-permute-done.20.refs_4_.w0.refs_5_.refs_10_), channel_id=1, source_target_pairs={{0,8},{2,10},{4,12},{6,14},{8,0},{10,2},{12,4},{14,6},{16,24},{18,... | collective-permute-start | bytes 1769480 | tf_op jit(solution)/shard_map/ppermute | solution.py:653
  221.2 13.8 %collective-permute-start.18 = (bf16[160,768]{1,0:T(8,128)(2,1)}, bf16[160,768]{1,0:T(8,128)(2,1)S(1)}, u32[]{:S(2)}, u32[]{:S(2)}) collective-permute-start(bf16[160,768]{1,0:T(8,128)(2,1)} %get-tuple-element.156), channel_id=1, source_target_pairs={{0,1},{1,0},{2,3},{3,2},{4,5},{5,4},{6,7},{7,6},{8,9},{9,8},{10,11... | collective-permute-start | bytes 737288 | tf_op jit(solution)/shard_map/ppermute | solution.py:652
  235.0 26.0 %collective-permute-start.22 = (bf16[768,384]{1,0:T(8,128)(2,1)S(1)}, bf16[768,384]{1,0:T(8,128)(2,1)}, u32[]{:S(2)}, u32[]{:S(2)}) collective-permute-start(bf16[768,384]{1,0:T(8,128)(2,1)S(1)} %copy-done.30), channel_id=1, source_target_pairs={{0,2},{2,0},{4,6},{6,4},{8,10},{10,8},{12,14},{14,12},{16,18},{18,... | collective-permute-start | bytes 1769480 | tf_op jit(solution)/shard_map/ppermute | solution.py:653
  235.0 28.5 %collective-permute-start.23 = (bf16[768,384]{1,0:T(8,128)(2,1)S(1)}, bf16[768,384]{1,0:T(8,128)(2,1)}, u32[]{:S(2)}, u32[]{:S(2)}) collective-permute-start(bf16[768,384]{1,0:T(8,128)(2,1)S(1)} %copy-done.32), channel_id=1, source_target_pairs={{0,2},{2,0},{4,6},{6,4},{8,10},{10,8},{12,14},{14,12},{16,18},{18,... | collective-permute-start | bytes 1769480 | tf_op jit(solution)/shard_map/ppermute | solution.py:653
  238.5 37.3 %collective-permute-start.29 = (bf16[768,384]{1,0:T(8,128)(2,1)S(1)}, bf16[768,384]{1,0:T(8,128)(2,1)S(1)}, u32[]{:S(2)}, u32[]{:S(2)}) collective-permute-start(bf16[768,384]{1,0:T(8,128)(2,1)S(1)} %copy-done.30), channel_id=1, source_target_pairs={{0,4},{2,6},{4,0},{6,2},{8,12},{10,14},{12,8},{14,10},{16,20},{18,... | collective-permute-start | bytes 1769480 | tf_op jit(solution)/shard_map/ppermute | solution.py:653
  259.5 73.5 %collective-permute-start.34 = (bf16[2,384,1536]{2,1,0:T(8,128)(2,1)S(1)}, bf16[2,384,1536]{2,1,0:T(8,128)(2,1)}, u32[]{:S(2)}, u32[]{:S(2)}) collective-permute-start(bf16[2,384,1536]{2,1,0:T(8,128)(2,1)S(1)} %fusion), channel_id=1, source_target_pairs={{0,1},{1,0},{2,3},{3,2},{4,5},{5,4},{6,7},{7,6},{8,9},{9,8},{10,11... | collective-permute-start | bytes 7077896 | tf_op jit(solution)/shard_map/ppermute | solution.py:652
  261.0 14.8 %collective-permute-start.31 = (bf16[768,384]{1,0:T(8,128)(2,1)S(1)}, bf16[768,384]{1,0:T(8,128)(2,1)S(1)}, u32[]{:S(2)}, u32[]{:S(2)}) collective-permute-start(bf16[768,384]{1,0:T(8,128)(2,1)S(1)} %copy-done.32), channel_id=1, source_target_pairs={{0,8},{2,10},{4,12},{6,14},{8,0},{10,2},{12,4},{14,6},{16,24},{18,... | collective-permute-start | bytes 1769480 | tf_op jit(solution)/shard_map/ppermute | solution.py:653
  276.4 60.7 %collective-permute-start.36 = (bf16[2,4,192,384]{3,2,1,0:T(8,128)(2,1)}, bf16[2,4,192,384]{3,2,1,0:T(8,128)(2,1)}, u32[]{:S(2)}, u32[]{:S(2)}) collective-permute-start(bf16[2,4,192,384]{3,2,1,0:T(8,128)(2,1)} %add_convert_fusion.4), channel_id=1, source_target_pairs={{0,4},{2,6},{4,0},{6,2},{8,12},{10,14},{12,8},{14,10},{16,20},{18,... | collective-permute-start | bytes 3538952 | tf_op jit(solution)/shard_map/ppermute | solution.py:653
  329.0 12.1 %collective-permute-start.33 = (bf16[288,768]{1,0:T(8,128)(2,1)}, bf16[288,768]{1,0:T(8,128)(2,1)S(1)}, u32[]{:S(2)}, u32[]{:S(2)}) collective-permute-start(bf16[288,768]{1,0:T(8,128)(2,1)} %get-tuple-element.186), channel_id=1, source_target_pairs={{0,1},{1,0},{2,3},{3,2},{4,5},{5,4},{6,7},{7,6},{8,9},{9,8},{10,11... | collective-permute-start | bytes 1327112 | tf_op jit(solution)/shard_map/ppermute | solution.py:652
  331.6 110.9 %collective-permute-start.38 = (bf16[2,2,384,1536]{3,2,1,0:T(8,128)(2,1)}, bf16[2,2,384,1536]{3,2,1,0:T(8,128)(2,1)}, u32[]{:S(2)}, u32[]{:S(2)}) collective-permute-start(bf16[2,2,384,1536]{3,2,1,0:T(8,128)(2,1)} %get-tuple-element.193), channel_id=1, source_target_pairs={{0,2},{2,0},{4,6},{6,4},{8,10},{10,8},{12,14},{14,12},{16,18},{18,... | collective-permute-start | bytes 14155784 | tf_op jit(solution)/shard_map/ppermute | solution.py:653
  335.8 62.1 %collective-permute-start.35 = (bf16[2,192,1536]{2,1,0:T(8,128)(2,1)}, bf16[2,192,1536]{2,1,0:T(8,128)(2,1)}, u32[]{:S(2)}, u32[]{:S(2)}) collective-permute-start(bf16[2,192,1536]{2,1,0:T(8,128)(2,1)} %add_convert_fusion.5), channel_id=1, source_target_pairs={{0,4},{2,6},{4,0},{6,2},{8,12},{10,14},{12,8},{14,10},{16,20},{18,... | collective-permute-start | bytes 3538952 | tf_op jit(solution)/shard_map/ppermute | solution.py:653
  338.8 15.5 %collective-permute-start.37 = (bf16[4,192,384]{2,1,0:T(8,128)(2,1)S(1)}, bf16[4,192,384]{2,1,0:T(8,128)(2,1)S(1)}, u32[]{:S(2)}, u32[]{:S(2)}) collective-permute-start(bf16[4,192,384]{2,1,0:T(8,128)(2,1)S(1)} %fusion.3), channel_id=1, source_target_pairs={{0,1},{1,0},{2,3},{3,2},{4,5},{5,4},{6,7},{7,6},{8,9},{9,8},{10,11... | collective-permute-start | bytes 1769480 | tf_op jit(solution)/shard_map/ppermute | solution.py:652
  396.1 14.7 %collective-permute-start.66 = (f32[10,768]{1,0:T(8,128)}, f32[10,768]{1,0:T(8,128)S(1)}, u32[]{:S(2)}, u32[]{:S(2)}) collective-permute-start(f32[10,768]{1,0:T(8,128)} %concatenate.19), channel_id=1, source_target_pairs={{0,2},{2,0},{4,6},{6,4},{8,10},{10,8},{12,14},{14,12},{16,18},{18,... | collective-permute-start | bytes 92168 | tf_op jit(solution)/shard_map/ppermute | solution.py:653
  396.1 10.1 %collective-permute-start.49 = (bf16[4,96,384]{2,1,0:T(8,128)(2,1)}, bf16[4,96,384]{2,1,0:T(8,128)(2,1)S(1)}, u32[]{:S(2)}, u32[]{:S(2)}) collective-permute-start(bf16[4,96,384]{2,1,0:T(8,128)(2,1)} %add_convert_fusion.17), channel_id=1, source_target_pairs={{0,8},{2,10},{4,12},{6,14},{8,0},{10,2},{12,4},{14,6},{16,24},{18,... | collective-permute-start | bytes 884744 | tf_op jit(solution)/shard_map/ppermute | solution.py:653
  397.7 43.3 %collective-permute-start.51 = (bf16[2,4,384,384]{3,2,1,0:T(8,128)(2,1)}, bf16[2,4,384,384]{3,2,1,0:T(8,128)(2,1)S(1)}, u32[]{:S(2)}, u32[]{:S(2)}) collective-permute-start(bf16[2,4,384,384]{3,2,1,0:T(8,128)(2,1)} %get-tuple-element.221), channel_id=1, source_target_pairs={{0,2},{2,0},{4,6},{6,4},{8,10},{10,8},{12,14},{14,12},{16,18},{18,... | collective-permute-start | bytes 7077896 | tf_op jit(solution)/shard_map/ppermute | solution.py:653
  399.7 22.0 %collective-permute-start.56 = (bf16[2,96,1536]{2,1,0:T(8,128)(2,1)S(1)}, bf16[2,96,1536]{2,1,0:T(8,128)(2,1)S(1)}, u32[]{:S(2)}, u32[]{:S(2)}) collective-permute-start(bf16[2,96,1536]{2,1,0:T(8,128)(2,1)S(1)} %add_convert_fusion.8), channel_id=1, source_target_pairs={{0,8},{2,10},{4,12},{6,14},{8,0},{10,2},{12,4},{14,6},{16,24},{18,... | collective-permute-start | bytes 1769480 | tf_op jit(solution)/shard_map/ppermute | solution.py:653
  407.2 13.4 %collective-permute-start.50 = (bf16[4,48,384]{2,1,0:T(8,128)(2,1)S(1)}, bf16[4,48,384]{2,1,0:T(8,128)(2,1)S(1)}, u32[]{:S(2)}, u32[]{:S(2)}) collective-permute-start(bf16[4,48,384]{2,1,0:T(8,128)(2,1)S(1)} %add_convert_fusion.23), channel_id=1, source_target_pairs={{0,16},{2,18},{4,20},{6,22},{8,24},{10,26},{12,28},{14,30},{16,0},... | collective-permute-start | bytes 442376 | tf_op jit(solution)/shard_map/ppermute | solution.py:653
  423.0 16.6 %collective-permute-start.57 = (bf16[2,48,1536]{2,1,0:T(8,128)(2,1)S(1)}, bf16[2,48,1536]{2,1,0:T(8,128)(2,1)S(1)}, u32[]{:S(2)}, u32[]{:S(2)}) collective-permute-start(bf16[2,48,1536]{2,1,0:T(8,128)(2,1)S(1)} %add_convert_fusion.15), channel_id=1, source_target_pairs={{0,16},{2,18},{4,20},{6,22},{8,24},{10,26},{12,28},{14,30},{16,0},... | collective-permute-start | bytes 884744 | tf_op jit(solution)/shard_map/ppermute | solution.py:653
  489.6 7.1 %collective-permute-start.67 = (f32[10,768]{1,0:T(8,128)S(1)}, f32[10,768]{1,0:T(8,128)S(1)}, u32[]{:S(2)}, u32[]{:S(2)}) collective-permute-start(f32[10,768]{1,0:T(8,128)S(1)} %add.549), channel_id=1, source_target_pairs={{0,1},{1,0},{2,3},{3,2},{4,5},{5,4},{6,7},{7,6},{8,9},{9,8},{10,11... | collective-permute-start | bytes 92168 | tf_op jit(solution)/shard_map/ppermute | solution.py:652
  496.7 4.7 collective-permute-start.68
  497.4 26.4 %collective-permute-start.58 = (bf16[1,384,1536]{2,1,0:T(8,128)(2,1)S(1)}, bf16[1,384,1536]{2,1,0:T(8,128)(2,1)S(1)}, u32[]{:S(2)}, u32[]{:S(2)}) collective-permute-start(bf16[1,384,1536]{2,1,0:T(8,128)(2,1)S(1)} %fusion.2), channel_id=1, source_target_pairs={{0,1},{1,0},{2,3},{3,2},{4,5},{5,4},{6,7},{7,6},{8,9},{9,8},{10,11... | collective-permute-start | bytes 3538952 | tf_op jit(solution)/shard_map/ppermute | solution.py:652
  498.4 28.9 %collective-permute-start.62 = (bf16[2,1,192,1536]{3,2,1,0:T(8,128)(2,1)S(1)}, bf16[2,1,192,1536]{3,2,1,0:T(8,128)(2,1)S(1)}, u32[]{:S(2)}, u32[]{:S(2)}) collective-permute-start(bf16[2,1,192,1536]{3,2,1,0:T(8,128)(2,1)S(1)} %add_convert_fusion.1), channel_id=1, source_target_pairs={{0,4},{2,6},{4,0},{6,2},{8,12},{10,14},{12,8},{14,10},{16,20},{18,... | collective-permute-start | bytes 3538952 | tf_op jit(solution)/shard_map/ppermute | solution.py:653
  499.5 53.1 %collective-permute-start.52 = (bf16[2,4,192,384]{3,2,1,0:T(8,128)(2,1)S(1)}, bf16[2,4,192,384]{3,2,1,0:T(8,128)(2,1)S(1)}, u32[]{:S(2)}, u32[]{:S(2)}) collective-permute-start(bf16[2,4,192,384]{3,2,1,0:T(8,128)(2,1)S(1)} %add_convert_fusion.3), channel_id=1, source_target_pairs={{0,4},{2,6},{4,0},{6,2},{8,12},{10,14},{12,8},{14,10},{16,20},{18,... | collective-permute-start | bytes 3538952 | tf_op jit(solution)/shard_map/ppermute | solution.py:653
  500.4 99.9 %collective-permute-start.39 = (bf16[2,4,384,384]{3,2,1,0:T(8,128)(2,1)S(1)}, bf16[2,4,384,384]{3,2,1,0:T(8,128)(2,1)S(1)}, u32[]{:S(2)}, u32[]{:S(2)}) collective-permute-start(bf16[2,4,384,384]{3,2,1,0:T(8,128)(2,1)S(1)} %copy-done.57), channel_id=1, source_target_pairs={{0,2},{2,0},{4,6},{6,4},{8,10},{10,8},{12,14},{14,12},{16,18},{18,... | collective-permute-start | bytes 7077896 | tf_op jit(solution)/shard_map/ppermute | solution.py:653
  505.6 5.3 collective-permute-start.70
  524.1 38.9 %collective-permute-start.59 = (bf16[1,192,1536]{2,1,0:T(8,128)(2,1)S(1)}, bf16[1,192,1536]{2,1,0:T(8,128)(2,1)S(1)}, u32[]{:S(2)}, u32[]{:S(2)}) collective-permute-start(bf16[1,192,1536]{2,1,0:T(8,128)(2,1)S(1)} %add_convert_fusion.7), channel_id=1, source_target_pairs={{0,4},{2,6},{4,0},{6,2},{8,12},{10,14},{12,8},{14,10},{16,20},{18,... | collective-permute-start | bytes 1769480 | tf_op jit(solution)/shard_map/ppermute | solution.py:653
  528.6 34.6 %collective-permute-start.63 = (bf16[1,192,1536]{2,1,0:T(8,128)(2,1)S(1)}, bf16[1,192,1536]{2,1,0:T(8,128)(2,1)S(1)}, u32[]{:S(2)}, u32[]{:S(2)}) collective-permute-start(bf16[1,192,1536]{2,1,0:T(8,128)(2,1)S(1)} %fusion.6), channel_id=1, source_target_pairs={{0,1},{1,0},{2,3},{3,2},{4,5},{5,4},{6,7},{7,6},{8,9},{9,8},{10,11... | collective-permute-start | bytes 1769480 | tf_op jit(solution)/shard_map/ppermute | solution.py:652
  554.0 11.4 %collective-permute-start.53 = (bf16[4,192,384]{2,1,0:T(8,128)(2,1)S(1)}, bf16[4,192,384]{2,1,0:T(8,128)(2,1)S(1)}, u32[]{:S(2)}, u32[]{:S(2)}) collective-permute-start(bf16[4,192,384]{2,1,0:T(8,128)(2,1)S(1)} %fusion.5), channel_id=1, source_target_pairs={{0,1},{1,0},{2,3},{3,2},{4,5},{5,4},{6,7},{7,6},{8,9},{9,8},{10,11... | collective-permute-start | bytes 1769480 | tf_op jit(solution)/shard_map/ppermute | solution.py:652
  563.1 11.6 %collective-permute-start.60 = (bf16[1,96,1536]{2,1,0:T(8,128)(2,1)S(1)}, bf16[1,96,1536]{2,1,0:T(8,128)(2,1)S(1)}, u32[]{:S(2)}, u32[]{:S(2)}) collective-permute-start(bf16[1,96,1536]{2,1,0:T(8,128)(2,1)S(1)} %add_convert_fusion.14), channel_id=1, source_target_pairs={{0,8},{2,10},{4,12},{6,14},{8,0},{10,2},{12,4},{14,6},{16,24},{18,... | collective-permute-start | bytes 884744 | tf_op jit(solution)/shard_map/ppermute | solution.py:653
  563.4 23.2 %collective-permute-start.64 = (bf16[1,96,1536]{2,1,0:T(8,128)(2,1)S(1)}, bf16[1,96,1536]{2,1,0:T(8,128)(2,1)S(1)}, u32[]{:S(2)}, u32[]{:S(2)}) collective-permute-start(bf16[1,96,1536]{2,1,0:T(8,128)(2,1)S(1)} %add_convert_fusion.13), channel_id=1, source_target_pairs={{0,8},{2,10},{4,12},{6,14},{8,0},{10,2},{12,4},{14,6},{16,24},{18,... | collective-permute-start | bytes 884744 | tf_op jit(solution)/shard_map/ppermute | solution.py:653
  565.6 20.2 %collective-permute-start.54 = (bf16[4,96,384]{2,1,0:T(8,128)(2,1)S(1)}, bf16[4,96,384]{2,1,0:T(8,128)(2,1)S(1)}, u32[]{:S(2)}, u32[]{:S(2)}) collective-permute-start(bf16[4,96,384]{2,1,0:T(8,128)(2,1)S(1)} %add_convert_fusion.16), channel_id=1, source_target_pairs={{0,8},{2,10},{4,12},{6,14},{8,0},{10,2},{12,4},{14,6},{16,24},{18,... | collective-permute-start | bytes 884744 | tf_op jit(solution)/shard_map/ppermute | solution.py:653
  574.8 22.2 %collective-permute-start.61 = (bf16[1,48,1536]{2,1,0:T(8,128)(2,1)S(1)}, bf16[1,48,1536]{2,1,0:T(8,128)(2,1)S(1)}, u32[]{:S(2)}, u32[]{:S(2)}) collective-permute-start(bf16[1,48,1536]{2,1,0:T(8,128)(2,1)S(1)} %add_convert_fusion.21), channel_id=1, source_target_pairs={{0,16},{2,18},{4,20},{6,22},{8,24},{10,26},{12,28},{14,30},{16,0},... | collective-permute-start | bytes 442376 | tf_op jit(solution)/shard_map/ppermute | solution.py:653
  585.9 11.0 %collective-permute-start.55 = (bf16[4,48,384]{2,1,0:T(8,128)(2,1)S(1)}, bf16[4,48,384]{2,1,0:T(8,128)(2,1)S(1)}, u32[]{:S(2)}, u32[]{:S(2)}) collective-permute-start(bf16[4,48,384]{2,1,0:T(8,128)(2,1)S(1)} %add_convert_fusion.22), channel_id=1, source_target_pairs={{0,16},{2,18},{4,20},{6,22},{8,24},{10,26},{12,28},{14,30},{16,0},... | collective-permute-start | bytes 442376 | tf_op jit(solution)/shard_map/ppermute | solution.py:653
  586.7 12.5 %collective-permute-start.65 = (bf16[1,48,1536]{2,1,0:T(8,128)(2,1)S(1)}, bf16[1,48,1536]{2,1,0:T(8,128)(2,1)S(1)}, u32[]{:S(2)}, u32[]{:S(2)}) collective-permute-start(bf16[1,48,1536]{2,1,0:T(8,128)(2,1)S(1)} %add_convert_fusion.20), channel_id=1, source_target_pairs={{0,16},{2,18},{4,20},{6,22},{8,24},{10,26},{12,28},{14,30},{16,0},... | collective-permute-start | bytes 442376 | tf_op jit(solution)/shard_map/ppermute | solution.py:653
  600.4 16.3 %collective-permute-start.41 = (bf16[2,384,384]{2,1,0:T(8,128)(2,1)S(1)}, bf16[2,384,384]{2,1,0:T(8,128)(2,1)S(1)}, u32[]{:S(2)}, u32[]{:S(2)}) collective-permute-start(bf16[2,384,384]{2,1,0:T(8,128)(2,1)S(1)} %fusion.4), channel_id=1, source_target_pairs={{0,1},{1,0},{2,3},{3,2},{4,5},{5,4},{6,7},{7,6},{8,9},{9,8},{10,11... | collective-permute-start | bytes 1769480 | tf_op jit(solution)/shard_map/ppermute | solution.py:652
  601.8 16.2 %collective-permute-start.45 = (bf16[2,2,192,384]{3,2,1,0:T(8,128)(2,1)S(1)}, bf16[2,2,192,384]{3,2,1,0:T(8,128)(2,1)S(1)}, u32[]{:S(2)}, u32[]{:S(2)}) collective-permute-start(bf16[2,2,192,384]{3,2,1,0:T(8,128)(2,1)S(1)} %add_convert_fusion.10), channel_id=1, source_target_pairs={{0,4},{2,6},{4,0},{6,2},{8,12},{10,14},{12,8},{14,10},{16,20},{18,... | collective-permute-start | bytes 1769480 | tf_op jit(solution)/shard_map/ppermute | solution.py:653
  603.3 28.2 %collective-permute-start.40 = (bf16[448,768]{1,0:T(8,128)(2,1)S(1)}, bf16[448,768]{1,0:T(8,128)(2,1)S(1)}, u32[]{:S(2)}, u32[]{:S(2)}) collective-permute-start(bf16[448,768]{1,0:T(8,128)(2,1)S(1)} %copy-done.58), channel_id=1, source_target_pairs={{0,1},{1,0},{2,3},{3,2},{4,5},{5,4},{6,7},{7,6},{8,9},{9,8},{10,11... | collective-permute-start | bytes 2064392 | tf_op jit(solution)/shard_map/ppermute | solution.py:652
  616.9 19.4 %collective-permute-start.42 = (bf16[2,192,384]{2,1,0:T(8,128)(2,1)S(1)}, bf16[2,192,384]{2,1,0:T(8,128)(2,1)S(1)}, u32[]{:S(2)}, u32[]{:S(2)}) collective-permute-start(bf16[2,192,384]{2,1,0:T(8,128)(2,1)S(1)} %add_convert_fusion.19), channel_id=1, source_target_pairs={{0,4},{2,6},{4,0},{6,2},{8,12},{10,14},{12,8},{14,10},{16,20},{18,... | collective-permute-start | bytes 884744 | tf_op jit(solution)/shard_map/ppermute | solution.py:653
  618.1 18.0 %collective-permute-start.46 = (bf16[2,192,384]{2,1,0:T(8,128)(2,1)S(1)}, bf16[2,192,384]{2,1,0:T(8,128)(2,1)S(1)}, u32[]{:S(2)}, u32[]{:S(2)}) collective-permute-start(bf16[2,192,384]{2,1,0:T(8,128)(2,1)S(1)} %fusion.9), channel_id=1, source_target_pairs={{0,1},{1,0},{2,3},{3,2},{4,5},{5,4},{6,7},{7,6},{8,9},{9,8},{10,11... | collective-permute-start | bytes 884744 | tf_op jit(solution)/shard_map/ppermute | solution.py:652
  636.2 5.8 collective-permute-start.47
  636.4 8.0 %collective-permute-start.43 = (bf16[2,96,384]{2,1,0:T(8,128)(2,1)S(1)}, bf16[2,96,384]{2,1,0:T(8,128)(2,1)S(1)}, u32[]{:S(2)}, u32[]{:S(2)}) collective-permute-start(bf16[2,96,384]{2,1,0:T(8,128)(2,1)S(1)} %add_convert_fusion.25), channel_id=1, source_target_pairs={{0,8},{2,10},{4,12},{6,14},{8,0},{10,2},{12,4},{14,6},{16,24},{18,... | collective-permute-start | bytes 442376 | tf_op jit(solution)/shard_map/ppermute | solution.py:653
  642.0 6.1 collective-permute-start.48
  644.4 6.1 collective-permute-start.44
  (73 other events, 1059.3 us)

commit v3 on v2

--- a/solution.py
+++ b/solution.py
@@ -16,7 +16,9 @@
 LANES = 128
 PAIR = 2
 FAR = 2.0**30
-VMEM = 56 * 1024 * 1024
+MIB = 1024 * 1024
+ATTENTION_VMEM = 56 * MIB
+FFN_VMEM = (56 * MIB, 56 * MIB)
 
 
 def dot(a, b):
@@ -25,10 +27,6 @@
 
 def dot_nt(a, b):
     return lax.dot_general(a, b, (((1,), (1,)), ((), ())), preferred_element_type=F32)
-
-
-def dot_tn(a, b):
-    return lax.dot_general(a, b, (((0,), (0,)), ((), ())), preferred_element_type=F32)
 
 
 def norm_stats(h):
@@ -98,11 +96,41 @@
     return pl.BlockSpec(tuple(shape), lambda *_: (0,) * len(shape))
 
 
-def params():
-    return pltpu.CompilerParams(vmem_limit_bytes=VMEM)
-
-
-CHEAP = pl.CostEstimate(flops=1, bytes_accessed=1, transcendentals=0)
+def params(limit=ATTENTION_VMEM):
+    return pltpu.CompilerParams(vmem_limit_bytes=limit)
+
+
+PLAN = {
+    "stats_fl": (3, 5),
+    "fl_core": (2, 4),
+    "out_l": (3, 5),
+    "stats_bl": (4, 5),
+    "sl_core": (3, 5),
+    "fl_1": (4, None),
+    "sl_1": (4, 6),
+    "stats_fv": (5, 7),
+    "fv_core": (5, 7),
+    "out_v": (5, 7),
+    "fl_a2": (5, 7),
+    "fl_b2": (5, None),
+    "sl_2": (5, 8),
+    "svr_core": (6, 8),
+    "fv_1": (6, 8),
+    "fl_3": (6, 7),
+    "sl_3": (6, 7),
+    "stats_bv": (7, 8),
+    "svo_core": (7, 9),
+    "fv_a2": (7, 9),
+    "fv_b2": (7, None),
+    "fl_4": (7, 9),
+    "sl_4": (7, 9),
+    "xr_core": (8, None),
+    "sv_1": (8, None),
+    "fv_3": (8, None),
+    "stats_y": (8, None),
+}
+WEIGHTS = (1000000000, 1000000000, 100000000000, 100000000000, 100000000000, 30000000000, 10000000000, 1, 5000000000, 100000000000)
+WORK = iter(())
 
 
 def fwd_kernel(dirs, each, which, spans, slot_ref, *refs):
@@ -221,47 +249,53 @@
         ),
         out_shape=out_shape,
         compiler_params=params(),
-        cost_estimate=CHEAP,
+        cost_estimate=pl.CostEstimate(flops=next(WORK), bytes_accessed=1, transcendentals=0),
         name="attention_forward",
     )(slot, *xs, qf, kf, in_proj, *pack, *extra)
 
 
 def ffn_kernel(
-    blocks, which, stream, spans, slot_ref, n1, ctx, wo, w0, w1, w2, w3, gain, bias, cot_own, cot_recv, perm,
-    up_own, down_own, u0, u1, u2, u3, d0, d1, d2, d3,
+    blocks, which, stream, spans, packs_at, slot_ref, n1, ctx, wo, w0, w1, w2, w3, gain, bias, cot_own, cot_recv, perm,
+    up, down, u0, u1, u2, u3, d0, d1, d2, d3,
     out_own, out_send, dh2_out, g2_out, stats, send, keep,
-    wobuf, uall, dall, ubuf, dbuf, hidden, slope, acc, x2, x2t, et, e, n2, inv2,
+    wobuf, uall, dall, hidden, slope, acc, x2, x2t, et, e, n2, inv2, sem,
 ):
     i = pl.program_id(0)
     each = blocks // 2
     b = lax.rem(i, blocks)
     half = wo.shape[0]
     tokens, width = n1.shape
+    block = uall.shape[2]
+    piece = u0.shape[1]
+    per = block // piece
     ln = 1 + stream
     last = 3 + stream
 
+    def fetches(*wanted):
+        own, rem = [], []
+        for k in range(each):
+            at = pl.ds(k * block, block)
+            own.append([(up.at[stream, :, at], uall.at[k]), (down.at[stream, at, :], dall.at[k])])
+        for k, (u, d) in enumerate(((u0, d0), (u1, d1), (u2, d2), (u3, d3))):
+            q = slot_ref[which[1]] ^ k
+            at = pl.ds(pl.multiple_of(lax.rem(q, per) * piece, piece), piece)
+            rem.append((u.at[pl.ds(packs_at[0] * width, width), :], uall.at[each + q // per, :, at]))
+            q = slot_ref[which[2]] ^ k
+            at = pl.ds(pl.multiple_of(lax.rem(q, per) * piece, piece), piece)
+            for c in range(width // piece):
+                rows = pl.ds(packs_at[1] * width + c * piece, piece)
+                rem.append((d.at[rows, :], dall.at[each + q // per, at, pl.ds(c * piece, piece)]))
+        groups, n = own + [rem], 0
+        for k, group in enumerate(groups):
+            if k in wanted:
+                for m, (src, dst) in enumerate(group):
+                    yield pltpu.make_async_copy(src, dst, sem.at[n + m])
+            n += len(group)
+
     @pl.when(i == 0)
     def _():
-        cols = u0.shape[1]
-        for k in range(4):
-            u, d = (u0, u1, u2, u3)[k], (d0, d1, d2, d3)[k]
-            uall[slot_ref[which[1]] ^ k] = u[...]
-            at = slot_ref[which[2]] ^ k
-            dall[at, :, :cols] = d[:cols, :]
-            dall[at, :, cols:] = d[cols:, :]
-
-    @pl.when(b < each)
-    def _():
-        ubuf[...] = up_own[...]
-        dbuf[...] = down_own[...]
-
-    @pl.when(b >= each)
-    def _():
-        ubuf[...] = uall[b - each]
-        dbuf[...] = dall[b - each]
-
-    @pl.when(i == 0)
-    def _():
+        for copy in fetches(*range(each + 1)):
+            copy.start()
         wobuf[:half, :] = wo[...]
         load_out(slot_ref[which[0]], (w0, w1, w2, w3), wobuf, half)
         one = n1[...] * gain[0:1, :] + bias[0:1, :]
@@ -275,13 +309,20 @@
         x2[...] = low
         x2t[...] = dot_nt(perm[...], low).astype(BF)
 
+    for k in range(each + 1):
+
+        @pl.when(i == k)
+        def _(k=k):
+            for copy in fetches(k):
+                copy.wait()
+
     @pl.when(i < blocks)
     def _():
-        act, der = gelu_pair(dot(x2[...], ubuf[...]))
+        act, der = gelu_pair(dot(x2[...], uall[b]))
         act = act.astype(BF)
         hidden[b] = act
         slope[b] = der.astype(slope.dtype)
-        acc[...] += dot(act, dbuf[...])
+        acc[...] += dot(act, dall[b])
 
     @pl.when(i == blocks - 1)
     def _():
@@ -302,8 +343,8 @@
 
     @pl.when(i >= blocks)
     def _():
-        du = (dot_nt(e[...], dbuf[...]) * slope[b].astype(F32)).astype(BF)
-        acc[...] += dot_nt(du, ubuf[...])
+        du = (dot_nt(e[...], dall[b]) * slope[b].astype(F32)).astype(BF)
+        acc[...] += dot_nt(du, uall[b])
         rows = send.shape[1]
         up_grad = dot(x2t[...], du).astype(BF)
         keep[0] = up_grad[:rows]
@@ -326,26 +367,25 @@
 def feed_forward(
     n1, ctx, out_proj, wo_pack, gains, biases, cot_own, cot_recv, perm, up_proj, down_proj, up_pack, down_pack, which, slot, stream, spans
 ):
+    (up_pack, up_at), (down_pack, down_at) = up_pack, down_pack
     tokens, width = n1.shape
     half = out_proj.shape[1]
     hid = up_proj.shape[2]
-    block = up_pack[0].shape[1]
+    block = 2 * up_pack[0].shape[1]
     each = hid // block
     blocks = 2 * each
 
-    def own(i):
-        return jnp.minimum(lax.rem(i, blocks), each - 1)
-
     def grad_map(i, s):
         b = jnp.maximum(i - blocks, 0)
-        return (jnp.where(b < each, 0, 1), 0, 0, lax.rem(b, each))
+        return (b // each, 0, 0, lax.rem(b, each))
 
     grad_spec = pl.BlockSpec((None, 2, width // 2, block), grad_map)
     grad_shape = jax.ShapeDtypeStruct((2, 2, width // 2, hid), BF)
     out_rows = width // 4
     tail = pl.BlockSpec((out_rows, half), lambda i, s: (3, 0), pipeline_mode=pl.Buffered(1))
+    hbm = pl.BlockSpec(memory_space=pl.ANY)
     return pl.pallas_call(
-        functools.partial(ffn_kernel, blocks, which, stream, spans),
+        functools.partial(ffn_kernel, blocks, which, stream, spans, (up_at, down_at)),
         grid_spec=pltpu.PrefetchScalarGridSpec(
             num_scalar_prefetch=1,
             grid=(2 * blocks,),
@@ -354,21 +394,14 @@
             + [const(gains.shape)] * 2
             + [const(cot_own.shape)] * 2
             + [const((width, width))]
-            + [
-                pl.BlockSpec((None, width, block), lambda i, s: (stream, 0, own(i))),
-                pl.BlockSpec((None, block, width), lambda i, s: (stream, own(i), 0)),
-            ]
-            + [const(up_pack[0].shape)] * 4
-            + [const(down_pack[0].shape)] * 4,
+            + [hbm] * 10,
             out_specs=[const_out((tokens // 2, width))] * 2
             + [const_out((tokens, width))] * 2
             + [const_out((4, width)), grad_spec, grad_spec],
             scratch_shapes=[
                 pltpu.VMEM((2 * half, width), BF),
-                pltpu.VMEM((4, width, block), BF),
-                pltpu.VMEM((4, block, width), BF),
-                pltpu.VMEM((width, block), BF),
-                pltpu.VMEM((block, width), BF),
+                pltpu.VMEM((blocks, width, block), BF),
+                pltpu.VMEM((blocks, block, width), BF),
                 pltpu.VMEM((blocks, tokens, block), BF),
                 pltpu.VMEM((blocks, tokens, block), F32),
                 pltpu.VMEM((tokens, width), F32),
@@ -378,6 +411,7 @@
                 pltpu.VMEM((tokens, width), BF),
                 pltpu.VMEM((tokens, width), F32),
                 pltpu.VMEM((tokens, 1), F32),
+                pltpu.SemaphoreType.DMA((2 * each + 12,)),
             ],
         ),
         out_shape=[
@@ -389,37 +423,83 @@
             grad_shape,
             grad_shape,
         ],
-        compiler_params=params(),
-        cost_estimate=CHEAP,
+        compiler_params=params(FFN_VMEM[stream]),
+        cost_estimate=pl.CostEstimate(flops=next(WORK), bytes_accessed=1, transcendentals=0),
         name="feed_forward",
     )(slot, n1, ctx, out_proj, *wo_pack, gains, biases, cot_own, cot_recv, perm, up_proj, down_proj, *up_pack, *down_pack)
 
 
-def bwd_kernel(dirs, each, which, spans, slot_ref, *refs):
-    last = spans is not None
-    n_in = 6 if last else 3
-    sources, refs = refs[:n_in], refs[n_in:]
-    perm, own, r0, r1, r2, r3, wo, w0, w1, w2, w3, q_in, k_in, v_in, c_in = refs[:15]
-    refs = refs[15:]
+def bwd_kernel(dirs, each, which, spans, half_of, norm, slot_ref, *refs):
+    first = half_of != 0
+    cross = spans is not None
+    if cross and first:
+        x_own, x_recv, g_a, g_b, base_a, base_b = refs[:6]
+        refs = refs[6:]
+    elif first:
+        x, g_a, base = refs[:3]
+        refs = refs[3:]
+    else:
+        g_in, base, xt, gt = refs[:4]
+        refs = refs[4:]
+    if first:
+        perm, refs = refs[0], refs[1:]
+    own, wo = None, None
+    rem, w_rem = (), ()
+    if half_of != 1:
+        own, wo, refs = refs[0], refs[1], refs[2:]
+    if half_of != 0:
+        rem, w_rem, refs = refs[:4], refs[4:8], refs[8:]
+    q_in, k_in, v_in, c_in = refs[:4]
+    refs = refs[4:]
     probs, refs = refs[: len(dirs)], refs[len(dirs) :]
-    if last:
-        dx_own, dx_send, send, keep = refs[:4]
+    if norm:
+        n1, inv1, gain, dx_out, low_out, stats = refs[:6]
+        refs = refs[6:]
+    elif cross and half_of != 1:
+        dx_own, dx_send = refs[:2]
+        refs = refs[2:]
+    else:
+        dx_out, g_out, xt, gt = refs[:4]
         refs = refs[4:]
+    send, keep, buf, wobuf, dqkv, acc = refs[:6]
+    if half_of is None:
+        xt, gt = refs[6:8]
+        g = refs[8]
+    elif first:
+        g = g_out
     else:
-        n1, inv1, gain, dx_out, low_out, stats, send, keep = refs[:8]
-        refs = refs[8:]
-    buf, wobuf, xt, gt, dqkv, acc, g = refs
+        g = g_in
     j = pl.program_id(0)
     slot = slot_ref[which]
-    load_weights(j, slot, own, (r0, r1, r2, r3), buf, each)
+    width = wobuf.shape[1]
+    count = each * (2 if half_of is None else 1)
+
+    if half_of != 1:
+
+        @pl.when(j < each)
+        def _():
+            for i in range(3):
+                buf[:, i * LANES : (i + 1) * LANES] = own[i]
+
+    if half_of != 0:
+
+        @pl.when(j >= count - each)
+        def _():
+            rows = rem[0].shape[0] // 3
+            for k in range(4):
+                start = pl.multiple_of((slot ^ k) * rows, rows)
+                for i in range(3):
+                    buf[pl.ds(start, rows), i * LANES : (i + 1) * LANES] = rem[k][i * rows : (i + 1) * rows]
 
     @pl.when(j == 0)
     def _():
-        half = wo.shape[0]
-        wobuf[:half, :] = wo[...]
-        load_out(slot, (w0, w1, w2, w3), wobuf, half)
-        if last:
-            x_own, x_recv, g_a, g_b, base_a, base_b = sources
+        base_row = 0
+        if half_of != 1:
+            wobuf[: wo.shape[0], :] = wo[...]
+            base_row = wo.shape[0]
+        if half_of != 0:
+            load_out(slot, w_rem, wobuf, base_row)
+        if cross and first:
             load_row(x_own, x_recv, spans, g)
             xt[...] = dot_nt(perm[...], g[...]).astype(BF)
             cut = g_a.shape[0]
@@ -427,14 +507,18 @@
             g[cut:, :] = g_b[...]
             acc[:cut, :] = base_a[...]
             acc[cut:, :] = base_b[...]
-        else:
-            x, g_a, base = sources
+        elif first:
             xt[...] = dot_nt(perm[...], x[...]).astype(BF)
             g[...] = g_a[...]
             acc[...] = base[...]
-        gt[...] = dot_nt(perm[...], g[...]).astype(BF)
-
-    dctx_all = dot_nt(g[...], wobuf[pl.ds(pl.multiple_of(j * LANES, LANES), LANES), :]).astype(BF)
+        else:
+            acc[...] = base[...]
+        if first:
+            gt[...] = dot_nt(perm[...], g[...]).astype(BF)
+
+    wo_rows = wobuf[pl.ds(pl.multiple_of(j * LANES, LANES), LANES), :]
+    dctx_all = dot_nt(g[...], wo_rows).astype(BF)
+    dctx_t_all = dot_nt(wo_rows, g[...]).astype(BF)
     for (q0, q1, k0, k1), p_in in zip(dirs, probs):
         dctx = dctx_all[q0:q1]
         q = q_in[q0:q1, :]
@@ -442,6 +526,8 @@
         v = v_in[k0:k1, :]
         low = low_lanes(v.shape)
         zero = jnp.zeros_like(v)
+        dctx_t = dctx_t_all[:, q0:q1]
+        q_t = q.astype(F32).T.astype(BF)
         dq, dk, dv = [], [], []
         for a in range(PAIR):
             p = p_in[a]
@@ -449,13 +535,12 @@
             pf = p.astype(F32)
             ds = (pf * (dp - jnp.sum(pf * dp, -1, keepdims=True))).astype(BF)
             dq.append(dot(ds, k))
-            dk.append(dot_tn(ds, q))
-            dv.append(dot_tn(p, dctx))
+            dk.append(dot(q_t[a * HD : (a + 1) * HD], ds))
+            dv.append(dot(dctx_t[a * HD : (a + 1) * HD], p))
         low_q = low_lanes(dq[0].shape)
-        low_k = low_lanes(dk[0].shape)
         dqkv[q0:q1, :LANES] = (jnp.where(low_q, dq[0], dq[1]) * (1.0 / math.sqrt(HD))).astype(BF)
-        dqkv[k0:k1, LANES : 2 * LANES] = jnp.where(low_k, dk[0], dk[1]).astype(BF)
-        dqkv[k0:k1, 2 * LANES :] = jnp.where(low_k, dv[0], dv[1]).astype(BF)
+        dqkv[k0:k1, LANES : 2 * LANES] = jnp.concatenate(dk, 0).T.astype(BF)
+        dqkv[k0:k1, 2 * LANES :] = jnp.concatenate(dv, 0).T.astype(BF)
     rows = send.shape[1]
     grads = dot(xt[...], dqkv[...]).astype(BF)
     for i in range(3):
@@ -467,15 +552,9 @@
     send[3] = out_grad[rows:]
     acc[...] += dot_nt(dqkv[...], buf[...])
 
-    @pl.when(j == 2 * each - 1)
+    @pl.when(j == count - 1)
     def _():
-        if last:
-            at = 0
-            for n in spans:
-                dx_own[at : at + n, :] = acc[2 * at : 2 * at + n, :]
-                dx_send[at : at + n, :] = acc[2 * at + n : 2 * (at + n), :].astype(BF)
-                at += n
-        else:
+        if norm:
             total = acc[...]
             normed = n1[...]
             stats[0:1, :] = jnp.sum(total * normed, 0, keepdims=True)
@@ -483,58 +562,81 @@
             dh = norm_back(normed, inv1[...], gain[0:1, :], total)
             dx_out[...] = dh
             low_out[...] = dh.astype(BF)
-
-
-def attention_backward(sources, perm, in_proj, pack, index, which, out_proj, saved, norm, slot, dirs, spans=None):
+        elif cross and half_of != 1:
+            at = 0
+            for n in spans:
+                dx_own[at : at + n, :] = acc[2 * at : 2 * at + n, :]
+                dx_send[at : at + n, :] = acc[2 * at + n : 2 * (at + n), :].astype(BF)
+                at += n
+        else:
+            dx_out[...] = acc[...]
+
+
+def attention_backward(sources, perm, in_proj, pack, index, which, out_proj, saved, norm, slot, dirs, half_of=None, spans=None):
     tokens = saved[0].shape[0]
     width, half = in_proj.shape[2:]
     each = half // LANES
-    pairs = 2 * each
     rows = 3 * width // 4
     out_rows = width // 4
-    col = pl.BlockSpec((tokens, LANES), lambda j, s: (0, j))
-    own_spec = pl.BlockSpec((None, 3, width, LANES), lambda j, s: (index, 0, 0, jnp.minimum(j, each - 1)))
-    rem_spec = pl.BlockSpec((rows, LANES), lambda j, s: (0, jnp.maximum(j - each, 0)))
+    count = 2 * each if half_of is None else each
+    shift = each if half_of == 1 else 0
+    col = pl.BlockSpec((tokens, LANES), lambda j, s: (0, j + shift))
     tail = pl.BlockSpec((out_rows, half), lambda j, s: (3, 0), pipeline_mode=pl.Buffered(1))
-    p_shapes = [(2 * pairs, q1 - q0, k1 - k0) for q0, q1, k0, k1 in dirs]
-    grad_spec = pl.BlockSpec(
-        (None, 4, width // 2, LANES), lambda j, s: (jnp.where(j < each, 0, 1), 0, 0, lax.rem(j, each))
-    )
-    grad_shape = jax.ShapeDtypeStruct((2, 4, width // 2, half), BF)
-    in_specs = [const(a.shape) for a in sources] + [const((width, width)), own_spec] + [rem_spec] * 4
-    in_specs += [const((half, width), index)] + [tail] * 4
-    in_specs += [col] * 4 + [pl.BlockSpec((PAIR,) + s[1:], lambda j, s: (j, 0, 0)) for s in p_shapes]
-    if spans is None:
+    p_shapes = [(PAIR, q1 - q0, k1 - k0) for q0, q1, k0, k1 in dirs]
+    first = half_of != 0
+    args = list(sources)
+    in_specs = [const(a.shape) for a in sources]
+    if first:
+        args.append(perm)
+        in_specs.append(const((width, width)))
+    if half_of != 1:
+        args += [in_proj, out_proj]
+        in_specs += [
+            pl.BlockSpec((None, 3, width, LANES), lambda j, s: (index, 0, 0, jnp.minimum(j, each - 1))),
+            const((half, width), index),
+        ]
+    if half_of != 0:
+        args += [*pack, *pack]
+        in_specs += [pl.BlockSpec((rows, LANES), lambda j, s: (0, jnp.maximum(j + shift - each, 0)))] * 4 + [tail] * 4
+    args += list(saved)
+    in_specs += [col] * 4 + [pl.BlockSpec(s, lambda j, s: (j + shift, 0, 0)) for s in p_shapes]
+    if norm:
+        args += list(norm)
         in_specs += [const(a.shape) for a in norm]
         outs = [((tokens, width), F32), ((tokens, width), BF), ((2, width), F32)]
+    elif spans is not None and half_of != 1:
+        outs = [((tokens // 2, width), F32), ((tokens // 2, width), BF)]
     else:
-        outs = [((tokens // 2, width), F32), ((tokens // 2, width), BF)]
+        outs = [((tokens, width), F32), ((tokens, width), BF), ((width, tokens), BF), ((width, tokens), BF)]
+    scratch = [
+        pltpu.VMEM((width, 3 * LANES), BF),
+        pltpu.VMEM((half if half_of is not None else 2 * half, width), BF),
+        pltpu.VMEM((tokens, 3 * LANES), BF),
+        pltpu.VMEM((tokens, width), F32),
+    ]
+    if half_of is None:
+        grad_spec = pl.BlockSpec(
+            (None, 4, width // 2, LANES), lambda j, s: (jnp.where(j < each, 0, 1), 0, 0, lax.rem(j, each))
+        )
+        grad_shape = jax.ShapeDtypeStruct((2, 4, width // 2, half), BF)
+        scratch += [pltpu.VMEM((width, tokens), BF)] * 2 + [pltpu.VMEM((tokens, width), BF)]
+    else:
+        grad_spec = pl.BlockSpec((4, width // 2, LANES), lambda j, s: (0, 0, j))
+        grad_shape = jax.ShapeDtypeStruct((4, width // 2, half), BF)
     return pl.pallas_call(
-        functools.partial(bwd_kernel, dirs, each, which, spans),
+        functools.partial(bwd_kernel, dirs, each, which, spans, half_of, bool(norm)),
         grid_spec=pltpu.PrefetchScalarGridSpec(
             num_scalar_prefetch=1,
-            grid=(pairs,),
+            grid=(count,),
             in_specs=in_specs,
             out_specs=[const_out(s) for s, _ in outs] + [grad_spec, grad_spec],
-            scratch_shapes=[
-                pltpu.VMEM((width, 3 * LANES), BF),
-                pltpu.VMEM((2 * half, width), BF),
-                pltpu.VMEM((width, tokens), BF),
-                pltpu.VMEM((width, tokens), BF),
-                pltpu.VMEM((tokens, 3 * LANES), BF),
-                pltpu.VMEM((tokens, width), F32),
-                pltpu.VMEM((tokens, width), BF),
-            ],
+            scratch_shapes=scratch,
         ),
         out_shape=[jax.ShapeDtypeStruct(s, k) for s, k in outs] + [grad_shape, grad_shape],
         compiler_params=params(),
-        cost_estimate=CHEAP,
+        cost_estimate=pl.CostEstimate(flops=next(WORK), bytes_accessed=1, transcendentals=0),
         name="attention_backward",
-    )(slot, *sources, perm, in_proj, *pack, out_proj, *pack, *saved, *(norm or ()))
-
-
-def after(x, *deps):
-    return lax.optimization_barrier((x,) + deps)[0]
+    )(slot, *args)
 
 
 def copies(pairs, sem):
@@ -580,17 +682,18 @@
 
 
 def second_cut_kernel(
-    place, in_proj, out_proj, up, down, lang, visn, self_l, self_v, up_l, up_v, down_l, down_v, own, other, sem
+    place, in_proj, out_proj, up, down, lang, visn, self_l, self_v, up_l, down_l, ffn_v, own, other, sem
 ):
     px, pz = place[0], place[1]
     pairs = attention_cuts(in_proj, out_proj, 1, pz, self_l) + attention_cuts(in_proj, out_proj, 2, pz, self_v)
     cols = up_l.shape[1]
-    for s, u, d in ((0, up_l, down_l), (1, up_v, down_v)):
+    rows = up_l.shape[0]
+    for s, u, d, p in ((0, up_l, down_l, pz), (1, ffn_v.at[pl.ds(0, rows)], ffn_v.at[pl.ds(rows, rows)], px)):
         pairs.append((up.at[s, :, pl.ds(pl.multiple_of(px * cols, cols), cols)], u))
         for c in range(2):
             pairs.append(
                 (
-                    down.at[s, pl.ds(pl.multiple_of(pz * cols, cols), cols), pl.ds(c * cols, cols)],
+                    down.at[s, pl.ds(pl.multiple_of(p * cols, cols), cols), pl.ds(c * cols, cols)],
                     d.at[pl.ds(c * cols, cols), :],
                 )
             )
@@ -606,40 +709,79 @@
         out_shape=[jax.ShapeDtypeStruct(s, BF) for s in shapes],
         scratch_shapes=[pltpu.SemaphoreType.DMA((n_copies,))],
         compiler_params=params(),
-        cost_estimate=CHEAP,
+        cost_estimate=pl.CostEstimate(flops=1, bytes_accessed=1, transcendentals=0),
         name="cut",
     )(place, *arrays)
 
 
+def after(x, *deps):
+    return lax.optimization_barrier((x,) + deps)[0]
+
+
+def total_of(terms):
+    return sum(x.astype(F32) for x in terms)
+
+
 class Chain:
-    def __init__(self, terms, order, exchange):
-        self.terms = list(terms)
+    def __init__(self, parts, order, exchange):
+        self.parts = [(list(own), list(rem)) for own, rem in parts]
         self.order = list(order)
         self.exchange = exchange
+        self.received = None
+
+    def absorb(self, *deps):
+        if self.received is None:
+            return
+        received = after(self.received, *deps) if deps else self.received
+        self.received = None
+        at = 0
+        for own, rem in self.parts:
+            n = own[0].shape[-3]
+            got = lax.slice_in_dim(received, at, at + n, axis=received.ndim - 3)
+            at += n
+            if rem:
+                own.append(got[0])
+                rem.append(got[1])
+            else:
+                own.append(got)
 
     def start(self, *deps):
+        self.absorb()
         stage = self.order.pop(0)
-        if stage < 0:
-            out = sum(x[1].astype(F32) for x in self.terms)
-            keep = [x[0] for x in self.terms]
-        else:
-            rows = self.terms[0].shape[-2] // 2
-            out = sum(x[..., rows:, :].astype(F32) for x in self.terms)
-            keep = [x[..., :rows, :] for x in self.terms]
-        received = self.exchange(after(out.astype(BF), *deps), stage)
-        self.terms = keep + [received]
-        return received
-
-    def total(self):
-        while self.order:
-            self.start()
-        return sum(x.astype(F32) for x in self.terms)
+        halved = stage >= 0
+        sent, kept = [], []
+        for own, rem in self.parts:
+            if halved:
+                rows = own[0].shape[-2] // 2
+                out = [total_of([x[..., rows:, :] for x in side]).astype(BF) for side in (own, rem) if side]
+                kept.append(tuple([x[..., :rows, :] for x in side] for side in (own, rem)))
+            else:
+                out = [total_of(rem).astype(BF)]
+                kept.append((own, []))
+            sent.append(out)
+        whole = [jnp.stack(out) if len(out) > 1 else out[0] for out in sent]
+        whole = jnp.concatenate(whole, whole[0].ndim - 3) if len(whole) > 1 else whole[0]
+        self.parts = kept
+        self.received = self.exchange(after(whole, *deps), stage)
+        return self.received
+
+    def total(self, *deps):
+        self.absorb(*deps)
+        return [total_of(own) for own, _ in self.parts]
+
+
+def joined(*chains):
+    for c in chains:
+        c.absorb()
+    return Chain([p for c in chains for p in c.parts], chains[0].order, chains[0].exchange)
 
 
 def on_device(
     lang_input, visn_input, word_seg, region_seg, in_proj, out_proj, up_proj, down_proj,
     ln_gain, ln_bias, lang_cotan, visn_cotan,
 ):
+    global WORK
+    WORK = iter(WEIGHTS)
     n_dp = lax.axis_size("dp")
     bits = n_dp.bit_length() - 1
     t = lax.axis_index("tensor")
@@ -656,6 +798,7 @@
     rest = list(range(2, bits))
     y_first = [Y, X] + rest
     x_first = [X, Y] + rest
+    z_first = [Z, X, Y] + rest[1:]
     SX, SZ = 0, 1
 
     def piece_of(hop):
@@ -673,8 +816,8 @@
         first_cut_kernel, 9, [attn_pack, rows_shape, rows_shape], slot, in_proj, out_proj, lang_input, visn_input
     )
     cross_y = exchange(cross_piece, Y)
-    self_l_piece, self_v_piece, up_l_piece, up_v_piece, down_l_piece, down_v_piece, cot_own, cot_other = cut_call(
-        second_cut_kernel, 20, [attn_pack] * 6 + [rows_shape] * 2, after(slot, x_own),
+    self_l_piece, self_v_piece, up_l_piece, down_l_piece, ffn_v_piece, cot_own, cot_other = cut_call(
+        second_cut_kernel, 20, [attn_pack] * 4 + [(2 * width, half)] + [rows_shape] * 2, after(slot, x_own),
         in_proj, out_proj, up_proj, down_proj, lang_cotan, visn_cotan,
     )
     seg = jnp.concatenate([own_seg(word_seg), own_seg(region_seg)])[:, None]
@@ -683,13 +826,18 @@
     kf = jnp.where((lane < 4) & (lane != seg), 1.0, 0.0).astype(BF)
     chunk = width // n_dp
     place = jnp.arange(width)
-    order = sum((((place // chunk) >> (bits - 1 - b)) & 1) << b for b in range(bits)) ^ d
-    perm = (place[None, :] == (order * chunk + place % chunk)[:, None]).astype(BF)
-    qf, kf, perm = lax.optimization_barrier((qf, kf, perm))
+
+    def permutation(halvings):
+        order = sum((((place // chunk) >> (bits - 1 - i)) & 1) << b for i, b in enumerate(halvings)) ^ d
+        return (place[None, :] == (order * chunk + place % chunk)[:, None]).astype(BF)
+
+    perm = permutation([C, X, Z] + rest[1:])
+    perm_z = permutation([C, Z, X] + rest[1:])
+    qf, kf, perm, perm_z = lax.optimization_barrier((qf, kf, perm, perm_z))
     lw, lv = 2 * spans[0], 2 * spans[1]
     streams = ((0, lw), (lw, lw + lv))
 
-    x_recv = exchange(after(x_other, cross_y, down_v_piece), Y)
+    x_recv = exchange(after(x_other, cross_y, ffn_v_piece), Y)
     cross_x = exchange(cross_y, X)
     cross_pack = [cross_y, cross_x, exchange(cross_y, C), exchange(cross_x, C)]
     self_l_y = exchange(after(self_l_piece, x_recv), Y)
@@ -709,17 +857,17 @@
             norms[j][2], qf[lo:hi], kf[lo:hi], in_proj, pack, 1 + j, SZ, slot_tied, ((0, hi - lo, 0, hi - lo),)
         )
 
-    def feed(j, ctx, wo_pack, up_pack, down_pack, slot_tied):
+    def feed(j, ctx, wo_pack, up_pack, down_pack, which, slot_tied):
         return feed_forward(
             norms[j][0], ctx, out_proj, wo_pack, ln_gain, ln_bias, cot_own, cot_recv, perm, up_proj, down_proj,
-            up_pack, down_pack, (SZ, SX, SZ), slot_tied, j, spans,
+            up_pack, down_pack, which, slot_tied, j, spans,
         )
 
-    def self_back(j, ffn, saved, pack, slot_tied):
+    def self_back(j, sources, saved, pack, slot_tied, half_of=None):
         n = streams[j][1] - streams[j][0]
+        norm = None if half_of == 1 else (norms[j][0], norms[j][1], ln_gain)
         return attention_backward(
-            (norms[j][2], ffn[3], ffn[2]), perm, in_proj, pack, 1 + j, SZ, out_proj, saved,
-            (norms[j][0], norms[j][1], ln_gain), slot_tied, ((0, n, 0, n),),
+            sources, perm_z if j == 0 else perm, in_proj, pack, 1 + j, SZ, out_proj, saved, norm, slot_tied, ((0, n, 0, n),), half_of
         )
 
     self_l_z = exchange(after(self_l_y, tok), Z)
@@ -730,80 +878,158 @@
     down_l_z = exchange(after(down_l_y, self_l_z), Z)
     cot_recv = exchange(after(cot_other, down_l_y), Y)
     self_l = self_forward(0, self_l_pack, after(slot, down_l_y, up_l_x))
+
     tok = self_l[3]
     down_l_pack = [down_l_y, down_l_z, exchange(after(down_l_y, tok), C), exchange(after(down_l_z, tok), C)]
     self_v_y = exchange(after(self_v_piece, tok, cot_recv), Y)
-    up_v_y = exchange(after(up_v_piece, tok, cot_recv), Y)
-    down_v_y = exchange(after(down_v_piece, tok, cot_recv), Y)
-
-    ffn_l = feed(0, self_l[3], self_l_pack, up_l_pack, down_l_pack, after(slot, up_l_pack[3]))
+    ffn_v_y = exchange(after(ffn_v_piece, tok, cot_recv), Y)
+    ffn_l = feed(0, self_l[3], self_l_pack, (up_l_pack, 0), (down_l_pack, 0), (SZ, SX, SZ), after(slot, up_l_pack[3]))
+
+    def ffn_chains(ffn, core):
+        keep = ffn[6]
+        made = []
+        for i, stages in enumerate((y_first[:2], x_first[:2])):
+            made.append(Chain([([keep[0, i : i + 1], core[0, i : i + 1]], [keep[1, i : i + 1], core[1, i : i + 1]])], stages, exchange))
+        return made
+
+    def self_chains(own, own_core, rem, rem_core):
+        made = []
+        for i, stages in ((0, y_first[:2]), (2, x_first[:2])):
+            made.append(Chain([([own[i : i + 2], own_core[i : i + 2]], [rem[i : i + 2], rem_core[i : i + 2]])], stages, exchange))
+        return made
+
+    def rejoin(*chains):
+        both = joined(*chains)
+        both.order = list(rest)
+        return both
+
+    toks = {2: ffn_l[4]}
+    ties = {k: [] for k in range(12)}
+    have = {"ffn_l": ffn_l}
+
+    def plain(source, pick, stage):
+        return lambda dep: exchange(after(pick(have[source]), dep), stage)
+
+    def chain(name, make=None):
+        def run(dep):
+            if make is not None:
+                made = make()
+                if isinstance(made, tuple) or isinstance(made, list):
+                    for key, c in zip(name.split(), made):
+                        have[key] = c
+                    return [c.start(dep) for c in made]
+                have[name] = made
+            return have[name].start(dep)
+        return run
+
+    sl_parts = lambda: Chain([([have["back_l"][4][0], have["sl_core"][0]], [have["back_l"][4][1], have["sl_core"][1]])], z_first, exchange)
+    tasks = [
+        ("stats_fl", plain("ffn_l", lambda f: f[4], C)),
+        ("fl_core", plain("ffn_l", lambda f: f[5], C)),
+        ("out_l", plain("ffn_l", lambda f: f[1], Y)),
+        ("stats_bl", plain("back_l", lambda f: f[2], C)),
+        ("sl_core", plain("back_l", lambda f: f[3], C)),
+        ("fl_1", chain("fl_a fl_b", lambda: ffn_chains(have["ffn_l"], have["fl_core"]))),
+        ("sl_1", chain("sl", sl_parts)),
+        ("stats_fv", plain("ffn_v", lambda f: f[4], C)),
+        ("fv_core", plain("ffn_v", lambda f: f[5], C)),
+        ("out_v", plain("ffn_v", lambda f: f[1], Y)),
+        ("fl_a2", chain("fl_a")),
+        ("fl_b2", chain("fl_b")),
+        ("sl_2", chain("sl")),
+        ("svr_core", plain("bva", lambda f: f[4], C)),
+        ("fv_1", chain("fv_a fv_b", lambda: ffn_chains(have["ffn_v"], have["fv_core"]))),
+        ("fl_3", chain("fl", lambda: rejoin(have["fl_a"], have["fl_b"]))),
+        ("sl_3", chain("sl")),
+        ("stats_bv", plain("bvb", lambda f: f[2], C)),
+        ("svo_core", plain("bvb", lambda f: f[3], C)),
+        ("fv_a2", chain("fv_a")),
+        ("fv_b2", chain("fv_b")),
+        ("fl_4", chain("fl")),
+        ("sl_4", chain("sl")),
+        ("xr_core", plain("xa", lambda f: f[4], C)),
+        ("sv_1", chain("sv_a sv_b", lambda: self_chains(have["bvb"][4], have["svo_core"], have["bva"][5], have["svr_core"]))),
+        ("fv_3", chain("fv", lambda: rejoin(have["fv_a"], have["fv_b"]))),
+        ("stats_y", lambda dep: exchange(after(stats_c(), dep), Y)),
+    ]
+
+    def stats_c():
+        rows = [(have[a][i], have[b]) for a, i, b in (("ffn_l", 4, "stats_fl"), ("ffn_v", 4, "stats_fv"), ("back_l", 2, "stats_bl"), ("bvb", 2, "stats_bv"))]
+        a, b, c, e = [x + y for x, y in rows]
+        return jnp.concatenate([c[:1] + e[:1], a[2:3], b[2:3], a[:1], b[:1], c[1:] + e[1:], a[3:4], b[3:4], a[1:2], b[1:2]])
+
+    def boundary(i, kernel=None, tok=None):
+        if kernel is not None:
+            have[kernel[0]] = kernel[1]
+            toks[i] = tok
+        for name, run in tasks:
+            begin, end = PLAN[name]
+            if begin == i:
+                got = run(toks[i])
+                have[name] = got
+                if end is not None:
+                    ties[end] += got if isinstance(got, list) else [got]
+
+    boundary(2)
     tok = ffn_l[4]
-    fl_core = exchange(ffn_l[5], C)
     self_v_z = exchange(after(self_v_y, tok), Z)
     self_v_c = exchange(after(self_v_y, tok), C)
-    out_l_recv = exchange(after(ffn_l[1], tok), Y)
-
-    back_l = self_back(0, ffn_l, self_l, self_l_pack, after(slot, self_v_y, up_v_y, down_v_y))
+    ffn_v_x = exchange(after(ffn_v_y, tok), X)
+    ffn_v_c = exchange(after(ffn_v_y, tok), C)
+    back_l = self_back(0, (norms[0][2], ffn_l[3], ffn_l[2]), self_l, self_l_pack, after(slot, self_v_y, ffn_v_y, *ties[3]))
+
     tok = back_l[2]
+    boundary(3, ("back_l", back_l), tok)
     self_v_pack = [self_v_y, self_v_z, self_v_c, exchange(after(self_v_z, tok), C)]
-    up_v_x = exchange(after(up_v_y, tok), X)
-    down_v_z = exchange(after(down_v_y, tok), Z)
-    up_v_c = exchange(after(up_v_y, tok), C)
-    down_v_c = exchange(after(down_v_y, tok), C)
-    sl_core = exchange(back_l[3], C)
-
-    self_v = self_forward(1, self_v_pack, after(slot, fl_core, out_l_recv, self_v_z))
-    tok = self_v[3]
-    up_v_pack = [up_v_y, up_v_x, up_v_c, exchange(after(up_v_x, tok), C)]
-    down_v_pack = [down_v_y, down_v_z, down_v_c, exchange(after(down_v_z, tok), C)]
-    fl = Chain([ffn_l[6], fl_core], y_first, exchange)
-    sl = Chain([back_l[4], sl_core], x_first, exchange)
-    fl_r = fl.start(tok)
-    sl_r = sl.start(tok)
-
-    ffn_v = feed(1, self_v[3], self_v_pack, up_v_pack, down_v_pack, after(slot, up_v_c, down_v_c, sl_core))
-    tok = ffn_v[4]
-    fv_core = exchange(ffn_v[5], C)
-    out_v_recv = exchange(after(ffn_v[1], tok), Y)
-    fl_r2 = fl.start(tok)
-    sl_r2 = sl.start(tok)
-
-    back_v = self_back(1, ffn_v, self_v, self_v_pack, after(slot, fl_r, sl_r))
-    tok = back_v[2]
-    gains = jnp.stack([back_l[2][0] + back_v[2][0], ffn_l[4][2], ffn_v[4][2], ffn_l[4][0], ffn_v[4][0]])
-    biases = jnp.stack([back_l[2][1] + back_v[2][1], ffn_l[4][3], ffn_v[4][3], ffn_l[4][1], ffn_v[4][1]])
-    stats = jnp.concatenate([gains, biases])
-    fv_a = Chain([ffn_v[6][:, :1], fv_core[:, :1]], y_first, exchange)
-    fv_b = Chain([ffn_v[6][:, 1:], fv_core[:, 1:]], x_first, exchange)
-    sv_core = exchange(back_v[3], C)
-    fv_ra = fv_a.start(tok)
-    fv_rb = fv_b.start(tok)
-    fl_r3 = fl.start(tok)
-    sl_r3 = sl.start(tok)
-    stats_r = exchange(after(stats, tok), C)
-
-    last = attention_backward(
-        (x_own, x_recv, back_l[1], back_v[1], back_l[0], back_v[0]), perm, in_proj, cross_pack, 0, SX, out_proj, cross,
-        None, after(slot, fl_r2, sl_r2, fv_core, out_v_recv), cross_dirs, spans,
+    ffn_v_pack = [ffn_v_y, ffn_v_x, ffn_v_c, exchange(after(ffn_v_x, tok), C)]
+    self_v = self_forward(1, self_v_pack, after(slot, self_v_z, ffn_v_x, *ties[4]))
+
+    boundary(4, ("self_v", self_v), self_v[3])
+    ffn_v = feed(
+        1, self_v[3], self_v_pack, (ffn_v_pack, 0), (ffn_v_pack, 1), (SZ, SX, SX), after(slot, ffn_v_pack[3], *ties[5])
     )
-    tok = last[0]
-    x_core = exchange(last[2], C)
-    grad_recv = exchange(after(last[1], x_core), Y)
-    sv = Chain([back_v[4], sv_core], x_first, exchange)
-    sv.start(tok)
-    stats = stats + stats_r
-    for stage in [Y] + list(range(1, bits)):
-        stats = stats + exchange(after(stats, tok), stage)
-    cx_a = Chain([last[3][:, :2], x_core[:, :2]], y_first, exchange)
-    cx_b = Chain([last[3][:, 2:], x_core[:, 2:]], x_first, exchange)
-    chains = [fv_a, fv_b, sv, fl, sl, cx_a, cx_b]
-    while any(c.order for c in chains):
-        for c in chains:
-            if c.order:
-                c.start()
-    fv_a, fv_b, sv, fl, sl, cx_a, cx_b = [c.total() for c in chains]
-    cx = jnp.concatenate([cx_a, cx_b], 0)
-    fv = jnp.concatenate([fv_a, fv_b], 0)
+    boundary(5, ("ffn_v", ffn_v), ffn_v[4])
+    bva = self_back(1, (norms[1][2], ffn_v[3], ffn_v[2]), self_v, self_v_pack, after(slot, *ties[6]), 1)
+    boundary(6, ("bva", bva), bva[0])
+    bvb = self_back(1, (bva[1], bva[0], bva[2], bva[3]), self_v, self_v_pack, after(slot, *ties[7]), 0)
+    boundary(7, ("bvb", bvb), bvb[2])
+    xa = attention_backward(
+        (x_own, x_recv, back_l[1], bvb[1], back_l[0], bvb[0]), perm, in_proj, cross_pack, 0, SX, out_proj, cross,
+        None, after(slot, *ties[8]), cross_dirs, 1, spans,
+    )
+    boundary(8, ("xa", xa), xa[0])
+    xb = attention_backward(
+        (xa[1], xa[0], xa[2], xa[3]), perm, in_proj, cross_pack, 0, SX, out_proj, cross,
+        None, after(slot, *ties[9]), cross_dirs, 0, spans,
+    )
+
+    tok = xb[0]
+    fl, sl, fv, sv_a, sv_b = [have[k] for k in ("fl", "sl", "fv", "sv_a", "sv_b")]
+    out_l_recv, out_v_recv = have["out_l"], have["out_v"]
+    stats = stats_c() + have["stats_y"]
+    xo_core = exchange(xb[2], C)
+    grad_recv = exchange(after(xb[1], tok), Y)
+    got = [c.start(tok, *have["sv_1"]) for c in (sv_a, sv_b)] + [fv.start(tok)]
+    if sl.order:
+        sl.start(tok)
+    if fl.order:
+        fl.start(tok)
+    cx_a, cx_b = self_chains(xb[3], xo_core, xa[5], have["xr_core"])
+    got = [cx_a.start(tok), cx_b.start(tok)]
+    sv = rejoin(sv_a, sv_b)
+    sv.start(*got)
+    stats = stats + exchange(after(stats, *got), X)
+    got = [cx_a.start(*got), cx_b.start(*got)]
+    cx = rejoin(cx_a, cx_b)
+    sv.start(*got)
+    for stage in rest:
+        tied = got
+        got = [cx.start(*tied)]
+        stats = stats + exchange(after(stats, *tied), stage)
+    for c in (sv, fv, fl, sl):
+        while c.order:
+            c.start(*got)
+    fl, sl, fv, sv, cx = [jnp.concatenate(c.total(xb[0]), 0) for c in (fl, sl, fv, sv, cx)]
 
     def whole(mine, back):
         back = back.astype(mine.dtype)
@@ -817,8 +1043,8 @@
     return (
         whole(ffn_l[0], out_l_recv),
         whole(ffn_v[0], out_v_recv),
-        whole(last[0][:cut_at], grad_recv[:cut_at]),
-        whole(last[0][cut_at:], grad_recv[cut_at:]),
+        whole(xb[0][:cut_at], grad_recv[:cut_at]),
+        whole(xb[0][cut_at:], grad_recv[cut_at:]),
         jnp.stack([g[:3] for g in attn]),
         jnp.stack([g[3].T for g in attn]),
         jnp.stack([g[0] for g in ffn]),

time: 655 us -> 548 us (0.84)
  waiting for transfers between devices: 243 us -> 117 us
  other arithmetic: 38.1 us -> 64.5 us
  Pallas kernels: 268 us -> 259 us
    ppermute x51, waiting for transfers between devices: 144 us -> 79.8 us  [exchange(): return lax.ppermute(x, 'dp', [(i, i ^ 1 << stage) for i in range(n_dp)])]
    ppermute x20 -> x21, waiting for transfers between devices: 98.7 us -> 37.1 us  [exchange(): return lax.ppermute(x, 'tensor', SWAP)]
    pallas_call x2, Pallas kernels: 94.1 us -> 64.9 us  [feed_forward(): pl.pallas_call(functools.partial(ffn_kernel, blocks, which, stream, spans...]
    pallas_call x3 -> x5, Pallas kernels: 105 us -> 126 us  [attention_backward(): pl.pallas_call(functools.partial(bwd_kernel, dirs, each, which, spans, ha...]
    convert_element_type x29 -> x26, other arithmetic: 24.3 us -> 36.6 us  [the longest x15 18.4 us: start(): total_of([x[..., rows:, :] for x in side]).astype(BF)]
    another operation x0 -> x16, other arithmetic: none -> 10.1 us  [start(): whole = [jnp.stack(out) if len(out) > 1 else out[0] for out in sent]]
    squeeze x18 -> x12, local copies, waits for them, and re-layouts: 17.3 us -> 18.6 us  [the longest x2 7.22 us: ffn_chains(): keep[0, i:i + 1]]
    ppermute x20 -> x21, starting transfers between devices: 25.9 us -> 25.8 us  [exchange(): return lax.ppermute(x, 'tensor', SWAP)]
  transfers between devices with their start and end apart: 71 -> 72, of which waited for: 36 -> 25; matrix products, arithmetic and copies ran while one was open for 10% -> 17% of each run, Pallas kernels for 27% -> 47%
where the time goes in v3:
time: 548 us; the launch traced here: 545 us
  Pallas kernels  259 us (47%)
  waiting for transfers between devices  117 us (21%)
  starting transfers between devices  65.1 us (12%)
  other arithmetic  64.5 us (12%)
  local copies, waits for them, and re-layouts  37.4 us (7%)
    pallas_call x5, Pallas kernels, attention_backward(): pl.pallas_call(functools.partial(bwd_kernel, dirs, each, which, spans, ha...  126 us
    ppermute x51, waiting for transfers between devices, exchange(): return lax.ppermute(x, 'dp', [(i, i ^ 1 << stage) for i in range(n_dp)])  79.8 us
    pallas_call x2, Pallas kernels, feed_forward(): pl.pallas_call(functools.partial(ffn_kernel, blocks, which, stream, spans...  64.9 us
    pallas_call x3, Pallas kernels, attention_forward(): pl.pallas_call(functools.partial(fwd_kernel, dirs, each, which, spans), g...  59.7 us
    ppermute x51, starting transfers between devices, exchange(): return lax.ppermute(x, 'dp', [(i, i ^ 1 << stage) for i in range(n_dp)])  39.3 us
    ppermute x21, waiting for transfers between devices, exchange(): return lax.ppermute(x, 'tensor', SWAP)  37.1 us
    ppermute x21, starting transfers between devices, exchange(): return lax.ppermute(x, 'tensor', SWAP)  25.8 us
    convert_element_type x15, other arithmetic, start(): total_of([x[..., rows:, :] for x in side]).astype(BF)  18.4 us
  transfers between devices with their start and end apart: 72, of which 25 were waited for; matrix products, arithmetic and copies ran while one was open for 17% of the time, Pallas kernels for 47%

profile of v3, /device:TPU:0, one launch (start us, length us, event | category | flops | bytes accessed | tf_op | source)
XLA Modules:
  0.0 545.4 jit_solution(1593028001464919859)
XLA Ops:
  1.2 3.6 cut.2
  4.9 3.0 collective-permute-start
  7.9 5.7 %cut.3 = (bf16[768,384]{1,0:T(8,128)(2,1)}, bf16[768,384]{1,0:T(8,128)(2,1)}, bf16[768,384]{1,0:T(8,128)(2,1)}, bf16[768,384]{1,0:T(8,128)(2,1)}, bf16[1536,384]...) custom-call(s32[3]{0:T(128)} %pad_add_fusion.1.place.slot_ref, bf16[3,3,768,384]{3,2,1,0:T(8,128)(2,1)} %refs_4_.7, ...), custom_call_target="tpu_custom_call" | custom-call | flops 1 | bytes 1 | tf_op jit(solution)/shard_map/cut/pallas_call | solution.py:705
  14.0 7.5 %collective-permute-done.refs_5_.refs_10_.refs_7_.refs_11_ = bf16[768,384]{1,0:T(8,128)(2,1)S(1)} collective-permute-done((bf16[768,384]{1,0:T(8,128)(2,1)}, bf16[768,384]{1,0:T(8,128)(2,1)S(1)}, u32[]{:S(2)}, u32[]{:S(2)}) %collective-permute-start) | collective-permute-done | bytes 589856 | tf_op jit(solution)/shard_map/ppermute | solution.py:794
  21.4 1.7 collective-permute-start.1
  23.2 1.5 collective-permute-start.3
  26.1 10.9 %collective-permute-done.3.refs_6_.refs_11_.refs_8_.refs_12_ = bf16[768,384]{1,0:T(8,128)(2,1)S(1)} collective-permute-done((bf16[768,384]{1,0:T(8,128)(2,1)S(1)}, bf16[768,384]{1,0:T(8,128)(2,1)S(1)}, u32[]{:S(2)}, u32[]{:S(2)}) %collective-permute-start.3) | collective-permute-done | bytes 589856 | tf_op jit(solution)/shard_map/ppermute | solution.py:795
  44.1 28.4 %attention_forward.3 = (bf16[896,768]{1,0:T(8,128)(2,1)}, bf16[896,768]{1,0:T(8,128)(2,1)}, bf16[896,768]{1,0:T(8,128)(2,1)}, bf16[896,768]{1,0:T(8,128)(2,1)}, ...) custom-call(s32[3]{0:T(128)} %pad_add_fusion.1.place.slot_ref, ...), custom_call_target="tpu_custom_call" | custom-call | flops 1000000000 | bytes 1 | tf_op jit(solution)/shard_map/attention_forward/pallas_call | solution.py:245
  72.5 1.5 collective-permute-start.8
  74.1 1.5 collective-permute-start.10
  75.6 1.5 collective-permute-start.6
  77.1 9.8 %collective-permute-done.8.refs_5_.w1.refs_7_.refs_11_ = bf16[768,384]{1,0:T(8,128)(2,1)S(1)} collective-permute-done((bf16[768,384]{1,0:T(8,128)(2,1)S(1)}, bf16[768,384]{1,0:T(8,128)(2,1)S(1)}, u32[]{:S(2)}, u32[]{:S(2)}) %collective-permute-start.8) | collective-permute-done | bytes 589856 | tf_op jit(solution)/shard_map/ppermute | solution.py:795
  89.2 1.5 slice.1010.refs_1_
  90.8 1.5 slice.1011.refs_2_
  93.6 12.6 %attention_forward.4 = (bf16[320,768]{1,0:T(8,128)(2,1)}, bf16[320,768]{1,0:T(8,128)(2,1)}, bf16[320,768]{1,0:T(8,128)(2,1)}, bf16[320,768]{1,0:T(8,128)(2,1)}, bf16[12,320,320]{2,1,0:T(8,128)(2,1)}) custom-call(s32[3]{0:T(128)} %pad_add_fusion.1.place.slot_ref, bf16[320,768]{1,0:T(8,128)(2,1)} %get-tuple-element.188.refs_0_, ...), custom_call_target="tpu_custom_call" | custom-call | flops 1000000000 | bytes 1 | tf_op jit(solution)/shard_map/attention_forward/pallas_call | solution.py:245
  110.2 26.3 %feed_forward.2 = (bf16[160,768]{1,0:T(8,128)(2,1)}, bf16[160,768]{1,0:T(8,128)(2,1)}, f32[320,768]{1,0:T(8,128)}, bf16[320,768]{1,0:T(8,128)(2,1)}, f32[4,768]{...) custom-call(s32[3]{0:T(128)} %pad_add_fusion.1.place.slot_ref, ...), custom_call_target="tpu_custom_call" | custom-call | flops 99999997952 | bytes 1 | tf_op jit(solution)/shard_map/feed_forward/pallas_call | solution.py:387
  136.7 11.0 %collective-permute-done.19.u0.d0 = bf16[1536,384]{1,0:T(8,128)(2,1)} collective-permute-done((bf16[1536,384]{1,0:T(8,128)(2,1)S(1)}, bf16[1536,384]{1,0:T(8,128)(2,1)}, u32[]{:S(2)}, u32[]{:S(2)}) %collective-permute-start.19) | collective-permute-done | bytes 1179680 | tf_op jit(solution)/shard_map/ppermute | solution.py:794
  147.7 33.5 %attention_backward.5 = (f32[320,768]{1,0:T(8,128)}, bf16[320,768]{1,0:T(8,128)(2,1)}, f32[2,768]{1,0:T(2,128)}, bf16[2,4,384,384]{3,2,1,0:T(8,128)(2,1)}, bf16[2,4,384,384]{3,2,1,0:T(8,128)(2,1)}) custom-call(s32[3]{0:T(128)} %pad_add_fusion.1.place.slot_ref, bf16[320,768]{1,0:T(8,128)(2,1)} %get-tuple-element.188.refs_0_, ...), custom_call_target="tpu_custom_call" | custom-call | flops 99999997952 | bytes 1 | tf_op jit(solution)/shard_map/attention_backward/pallas_call | solution.py:626
  182.7 1.5 collective-permute-start.25
  185.6 3.5 slice_bitcast_fusion.14
  189.2 1.5 collective-permute-start.20
  190.7 7.7 %collective-permute-done.25.refs_5_.w1.refs_9_ = bf16[768,384]{1,0:T(8,128)(2,1)S(1)} collective-permute-done((bf16[768,384]{1,0:T(8,128)(2,1)S(1)}, bf16[768,384]{1,0:T(8,128)(2,1)S(1)}, u32[]{:S(2)}, u32[]{:S(2)}) %collective-permute-start.25) | collective-permute-done | bytes 589856 | tf_op jit(solution)/shard_map/ppermute | solution.py:795
  201.5 10.9 %collective-permute-done.21.u1.d1 = bf16[1536,384]{1,0:T(8,128)(2,1)S(1)} collective-permute-done((bf16[1536,384]{1,0:T(8,128)(2,1)}, bf16[1536,384]{1,0:T(8,128)(2,1)S(1)}, u32[]{:S(2)}, u32[]{:S(2)}) %collective-permute-start.21) | collective-permute-done | bytes 1179680 | tf_op jit(solution)/shard_map/ppermute | solution.py:795
  213.0 1.9 slice_bitcast_fusion.4
  218.4 18.7 %attention_forward.5 = (bf16[576,768]{1,0:T(8,128)(2,1)}, bf16[576,768]{1,0:T(8,128)(2,1)}, bf16[576,768]{1,0:T(8,128)(2,1)}, bf16[576,768]{1,0:T(8,128)(2,1)}, bf16[12,576,576]{2,1,0:T(8,128)(2,1)}) custom-call(s32[3]{0:T(128)} %pad_add_fusion.1.place.slot_ref, bf16[576,768]{1,0:T(8,128)(2,1)} %get-tuple-element.222.refs_0_, ...), custom_call_target="tpu_custom_call" | custom-call | flops 99999997952 | bytes 1 | tf_op jit(solution)/shard_map/attention_forward/pallas_call | solution.py:245
  237.3 2.9 fusion.2
  240.2 1.5 collective-permute-start.34
  241.7 3.3 slice_bitcast_fusion.6
  250.2 38.6 %feed_forward.3 = (bf16[288,768]{1,0:T(8,128)(2,1)}, bf16[288,768]{1,0:T(8,128)(2,1)}, f32[576,768]{1,0:T(8,128)}, bf16[576,768]{1,0:T(8,128)(2,1)}, f32[4,768]{...) custom-call(s32[3]{0:T(128)} %pad_add_fusion.1.place.slot_ref, ...), custom_call_target="tpu_custom_call" | custom-call | flops 30000001024 | bytes 1 | tf_op jit(solution)/shard_map/feed_forward/pallas_call | solution.py:387
  289.4 3.7 slice_bitcast_fusion.9
  294.3 6.6 %collective-permute-done.31 = bf16[288,768]{1,0:T(8,128)(2,1)S(1)} collective-permute-done((bf16[288,768]{1,0:T(8,128)(2,1)}, bf16[288,768]{1,0:T(8,128)(2,1)S(1)}, u32[]{:S(2)}, u32[]{:S(2)}) %collective-permute-start.31) | collective-permute-done | bytes 442400 | tf_op jit(solution)/shard_map/ppermute | solution.py:794
  302.1 2.3 add_convert_fusion.11
  304.9 2.1 fusion.5
  308.9 1.6 fusion.18
  314.0 21.1 %attention_backward.6 = (f32[576,768]{1,0:T(8,128)}, bf16[576,768]{1,0:T(8,128)(2,1)}, bf16[768,576]{1,0:T(8,128)(2,1)}, bf16[768,576]{1,0:T(8,128)(2,1)}, bf16[...) custom-call(s32[3]{0:T(128)} %pad_add_fusion.1.place.slot_ref, bf16[576,768]{1,0:T(8,128)(2,1)} %get-tuple-element.222.refs_0_, ...), custom_call_target="tpu_custom_call" | custom-call | flops 10000000000 | bytes 1 | tf_op jit(solution)/shard_map/attention_backward/pallas_call | solution.py:626
  336.4 1.5 fusion.14
  337.9 1.6 collective-permute-start.41
  344.5 2.8 collective-permute-done.41
  347.3 1.9 add_convert_fusion.30
  351.2 2.6 fusion.3
  353.8 1.5 collective-permute-start.43
  359.8 1.6 add_convert_fusion.32
  361.4 19.8 %attention_backward.7 = (f32[576,768]{1,0:T(8,128)}, bf16[576,768]{1,0:T(8,128)(2,1)}, f32[2,768]{1,0:T(2,128)}, bf16[4,384,384]{2,1,0:T(8,128)(2,1)}, bf16[4,384,384]{2,1,0:T(8,128)(2,1)}) custom-call(s32[3]{0:T(128)} %pad_add_fusion.1.place.slot_ref, bf16[576,768]{1,0:T(8,128)(2,1)} %get-tuple-element.254.refs_0_, f32[576,768]{1,0:T(8,128)} %get-tuple-element.249.refs_1_, ...), custom_call_target="tpu_custom_call" | custom-call | flops 1 | bytes 1 | tf_op jit(solution)/shard_map/attention_backward/pallas_call | solution.py:626
  382.6 2.6 collective-permute-start.45
  386.8 2.6 concatenate.56
  389.4 2.4 add_convert_fusion.6
  391.9 1.5 collective-permute-start.44
  393.4 27.6 %attention_backward.8 = (f32[896,768]{1,0:T(8,128)}, bf16[896,768]{1,0:T(8,128)(2,1)}, bf16[768,896]{1,0:T(8,128)(2,1)}, bf16[768,896]{1,0:T(8,128)(2,1)}, bf16[...) custom-call(s32[3]{0:T(128)} %pad_add_fusion.1.place.slot_ref, bf16[448,768]{1,0:T(8,128)(2,1)} %get-tuple-element.165.refs_0_, ...), custom_call_target="tpu_custom_call" | custom-call | flops 5000000000 | bytes 1 | tf_op jit(solution)/shard_map/attention_backward/pallas_call | solution.py:626
  421.6 2.1 fusion.4
  428.0 23.5 %attention_backward.9 = (f32[448,768]{1,0:T(8,128)}, bf16[448,768]{1,0:T(8,128)(2,1)}, bf16[4,384,384]{2,1,0:T(8,128)(2,1)}, bf16[4,384,384]{2,1,0:T(8,128)(2,1)}) custom-call(s32[3]{0:T(128)} %pad_add_fusion.1.place.slot_ref, bf16[896,768]{1,0:T(8,128)(2,1)} %get-tuple-element.282.refs_0_, f32[896,768]{1,0:T(8,128)} %get-tuple-element.283.refs_1_, ...), custom_call_target="tpu_custom_call" | custom-call | flops 99999997952 | bytes 1 | tf_op jit(solution)/shard_map/attention_backward/pallas_call | solution.py:626
  460.2 1.5 add_bitcast_fusion.1
  463.1 6.5 %collective-permute-done.60 = bf16[2,2,192,384]{3,2,1,0:T(8,128)(2,1)S(1)} collective-permute-done((bf16[2,2,192,384]{3,2,1,0:T(8,128)(2,1)S(1)}, bf16[2,2,192,384]{3,2,1,0:T(8,128)(2,1)S(1)}, u32[]{:S(2)}, u32[]{:S(2)}) %collective-permute-start.60) | collective-permute-done | bytes 589856 | tf_op jit(solution)/shard_map/ppermute | solution.py:795
  471.4 2.7 collective-permute-done.66
  476.6 2.6 collective-permute-start.67
  484.8 1.6 collective-permute-done.62
  487.6 4.2 collective-permute-done.67
  493.0 4.9 collective-permute-done.53
  501.2 11.1 %collective-permute-done.54 = bf16[2,2,192,384]{3,2,1,0:T(8,128)(2,1)S(1)} collective-permute-done((bf16[2,2,192,384]{3,2,1,0:T(8,128)(2,1)S(1)}, bf16[2,2,192,384]{3,2,1,0:T(8,128)(2,1)S(1)}, u32[]{:S(2)}, u32[]{:S(2)}) %collective-permute-start.54) | collective-permute-done | bytes 589856 | tf_op jit(solution)/shard_map/ppermute | solution.py:795
  517.8 3.2 collective-permute-done.69
  522.3 2.6 collective-permute-start.64
  527.1 2.9 collective-permute-done.70
  531.1 3.0 collective-permute-done.57
  534.3 3.0 collective-permute-start.58
  537.2 4.6 collective-permute-done.71
  (383 shorter events, 100.6 us)
Async XLA Ops:
  4.9 16.6 %collective-permute-start = (bf16[768,384]{1,0:T(8,128)(2,1)}, bf16[768,384]{1,0:T(8,128)(2,1)S(1)}, u32[]{:S(2)}, u32[]{:S(2)}) collective-permute-start(bf16[768,384]{1,0:T(8,128)(2,1)} %get-tuple-element.169), channel_id=1, source_target_pairs={{0,1},{1,0},{2,3},{3,2},{4,5},{5,4},{6,7},{7,6},{8,9},{9,8},{10,11... | collective-permute-start | bytes 1769480 | tf_op jit(solution)/shard_map/ppermute | solution.py:794
  21.4 16.6 %collective-permute-start.1 = (bf16[448,768]{1,0:T(8,128)(2,1)S(1)}, bf16[448,768]{1,0:T(8,128)(2,1)S(1)}, u32[]{:S(2)}, u32[]{:S(2)}) collective-permute-start(bf16[448,768]{1,0:T(8,128)(2,1)S(1)} %copy-done.74), channel_id=1, source_target_pairs={{0,1},{1,0},{2,3},{3,2},{4,5},{5,4},{6,7},{7,6},{8,9},{9,8},{10,11... | collective-permute-start | bytes 2064392 | tf_op jit(solution)/shard_map/ppermute | solution.py:794
  23.2 13.9 %collective-permute-start.3 = (bf16[768,384]{1,0:T(8,128)(2,1)S(1)}, bf16[768,384]{1,0:T(8,128)(2,1)S(1)}, u32[]{:S(2)}, u32[]{:S(2)}) collective-permute-start(bf16[768,384]{1,0:T(8,128)(2,1)S(1)} %collective-permute-done.refs_5_.refs_10_.refs_7_.refs_11_), channel_id=1, source_target_pairs={{0,4},{2,6},{4,0},{6,2},{8,12},{10,14},{12,8},{14,10},{16,20},{18,... | collective-permute-start | bytes 1769480 | tf_op jit(solution)/shard_map/ppermute | solution.py:795
  26.1 16.3 %collective-permute-start.4 = (bf16[768,384]{1,0:T(8,128)(2,1)S(1)}, bf16[768,384]{1,0:T(8,128)(2,1)S(1)}, u32[]{:S(2)}, u32[]{:S(2)}) collective-permute-start(bf16[768,384]{1,0:T(8,128)(2,1)S(1)} %collective-permute-done.refs_5_.refs_10_.refs_7_.refs_11_), channel_id=1, source_target_pairs={{0,2},{2,0},{4,6},{6,4},{8,10},{10,8},{12,14},{14,12},{16,18},{18,... | collective-permute-start | bytes 1769480 | tf_op jit(solution)/shard_map/ppermute | solution.py:795
  37.1 5.4 collective-permute-start.5
  38.1 34.5 %collective-permute-start.7 = (bf16[768,384]{1,0:T(8,128)(2,1)S(1)}, bf16[768,384]{1,0:T(8,128)(2,1)S(1)}, u32[]{:S(2)}, u32[]{:S(2)}) collective-permute-start(bf16[768,384]{1,0:T(8,128)(2,1)S(1)} %copy-done.83), channel_id=1, source_target_pairs={{0,1},{1,0},{2,3},{3,2},{4,5},{5,4},{6,7},{7,6},{8,9},{9,8},{10,11... | collective-permute-start | bytes 1769480 | tf_op jit(solution)/shard_map/ppermute | solution.py:794
  41.8 33.8 %collective-permute-start.2 = (bf16[768,384]{1,0:T(8,128)(2,1)S(1)}, bf16[768,384]{1,0:T(8,128)(2,1)S(1)}, u32[]{:S(2)}, u32[]{:S(2)}) collective-permute-start(bf16[768,384]{1,0:T(8,128)(2,1)S(1)} %copy-done.82), channel_id=1, source_target_pairs={{0,1},{1,0},{2,3},{3,2},{4,5},{5,4},{6,7},{7,6},{8,9},{9,8},{10,11... | collective-permute-start | bytes 1769480 | tf_op jit(solution)/shard_map/ppermute | solution.py:794
  72.5 14.4 %collective-permute-start.8 = (bf16[768,384]{1,0:T(8,128)(2,1)S(1)}, bf16[768,384]{1,0:T(8,128)(2,1)S(1)}, u32[]{:S(2)}, u32[]{:S(2)}) collective-permute-start(bf16[768,384]{1,0:T(8,128)(2,1)S(1)} %collective-permute-done.7.refs_4_.w0.refs_6_.refs_10_), channel_id=1, source_target_pairs={{0,8},{2,10},{4,12},{6,14},{8,0},{10,2},{12,4},{14,6},{16,24},{18,... | collective-permute-start | bytes 1769480 | tf_op jit(solution)/shard_map/ppermute | solution.py:795
  74.1 14.1 %collective-permute-start.10 = (bf16[768,384]{1,0:T(8,128)(2,1)S(1)}, bf16[768,384]{1,0:T(8,128)(2,1)S(1)}, u32[]{:S(2)}, u32[]{:S(2)}) collective-permute-start(bf16[768,384]{1,0:T(8,128)(2,1)S(1)} %copy-done.80), channel_id=1, source_target_pairs={{0,1},{1,0},{2,3},{3,2},{4,5},{5,4},{6,7},{7,6},{8,9},{9,8},{10,11... | collective-permute-start | bytes 1769480 | tf_op jit(solution)/shard_map/ppermute | solution.py:794
  75.6 16.7 %collective-permute-start.6 = (bf16[768,384]{1,0:T(8,128)(2,1)S(1)}, bf16[768,384]{1,0:T(8,128)(2,1)S(1)}, u32[]{:S(2)}, u32[]{:S(2)}) collective-permute-start(bf16[768,384]{1,0:T(8,128)(2,1)S(1)} %collective-permute-done.2.u0), channel_id=1, source_target_pairs={{0,4},{2,6},{4,0},{6,2},{8,12},{10,14},{12,8},{14,10},{16,20},{18,... | collective-permute-start | bytes 1769480 | tf_op jit(solution)/shard_map/ppermute | solution.py:795
  77.1 15.2 %collective-permute-start.11 = (bf16[768,384]{1,0:T(8,128)(2,1)S(1)}, bf16[768,384]{1,0:T(8,128)(2,1)S(1)}, u32[]{:S(2)}, u32[]{:S(2)}) collective-permute-start(bf16[768,384]{1,0:T(8,128)(2,1)S(1)} %collective-permute-done.7.refs_4_.w0.refs_6_.refs_10_), channel_id=1, source_target_pairs={{0,2},{2,0},{4,6},{6,4},{8,10},{10,8},{12,14},{14,12},{16,18},{18,... | collective-permute-start | bytes 1769480 | tf_op jit(solution)/shard_map/ppermute | solution.py:795
  86.9 6.0 %collective-permute-start.12 = (bf16[768,384]{1,0:T(8,128)(2,1)S(1)}, bf16[768,384]{1,0:T(8,128)(2,1)S(1)}, u32[]{:S(2)}, u32[]{:S(2)}) collective-permute-start(bf16[768,384]{1,0:T(8,128)(2,1)S(1)} %collective-permute-done.8.refs_5_.w1.refs_7_.refs_11_), channel_id=1, source_target_pairs={{0,2},{2,0},{4,6},{6,4},{8,10},{10,8},{12,14},{14,12},{16,18},{18,... | collective-permute-start | bytes 1769480 | tf_op jit(solution)/shard_map/ppermute | solution.py:795
  88.2 18.3 %collective-permute-start.15 = (bf16[768,384]{1,0:T(8,128)(2,1)S(1)}, bf16[768,384]{1,0:T(8,128)(2,1)}, u32[]{:S(2)}, u32[]{:S(2)}) collective-permute-start(bf16[768,384]{1,0:T(8,128)(2,1)S(1)} %collective-permute-done.10.d0), channel_id=1, source_target_pairs={{0,8},{2,10},{4,12},{6,14},{8,0},{10,2},{12,4},{14,6},{16,24},{18,... | collective-permute-start | bytes 1769480 | tf_op jit(solution)/shard_map/ppermute | solution.py:795
  88.6 18.2 %collective-permute-start.13 = (bf16[448,768]{1,0:T(8,128)(2,1)S(1)}, bf16[448,768]{1,0:T(8,128)(2,1)S(1)}, u32[]{:S(2)}, u32[]{:S(2)}) collective-permute-start(bf16[448,768]{1,0:T(8,128)(2,1)S(1)} %copy-done.72), channel_id=1, source_target_pairs={{0,1},{1,0},{2,3},{3,2},{4,5},{5,4},{6,7},{7,6},{8,9},{9,8},{10,11... | collective-permute-start | bytes 2064392 | tf_op jit(solution)/shard_map/ppermute | solution.py:794
  92.3 14.5 %collective-permute-start.9 = (bf16[768,384]{1,0:T(8,128)(2,1)S(1)}, bf16[768,384]{1,0:T(8,128)(2,1)}, u32[]{:S(2)}, u32[]{:S(2)}) collective-permute-start(bf16[768,384]{1,0:T(8,128)(2,1)S(1)} %collective-permute-done.6.u1), channel_id=1, source_target_pairs={{0,2},{2,0},{4,6},{6,4},{8,10},{10,8},{12,14},{14,12},{16,18},{18,... | collective-permute-start | bytes 1769480 | tf_op jit(solution)/shard_map/ppermute | solution.py:795
  92.4 16.6 %collective-permute-start.14 = (bf16[768,384]{1,0:T(8,128)(2,1)S(1)}, bf16[768,384]{1,0:T(8,128)(2,1)}, u32[]{:S(2)}, u32[]{:S(2)}) collective-permute-start(bf16[768,384]{1,0:T(8,128)(2,1)S(1)} %collective-permute-done.2.u0), channel_id=1, source_target_pairs={{0,2},{2,0},{4,6},{6,4},{8,10},{10,8},{12,14},{14,12},{16,18},{18,... | collective-permute-start | bytes 1769480 | tf_op jit(solution)/shard_map/ppermute | solution.py:795
  106.8 29.9 %collective-permute-start.18 = (bf16[768,384]{1,0:T(8,128)(2,1)S(1)}, bf16[768,384]{1,0:T(8,128)(2,1)S(1)}, u32[]{:S(2)}, u32[]{:S(2)}) collective-permute-start(bf16[768,384]{1,0:T(8,128)(2,1)S(1)} %copy-done.77), channel_id=1, source_target_pairs={{0,1},{1,0},{2,3},{3,2},{4,5},{5,4},{6,7},{7,6},{8,9},{9,8},{10,11... | collective-permute-start | bytes 1769480 | tf_op jit(solution)/shard_map/ppermute | solution.py:794
  108.3 39.4 %collective-permute-start.19 = (bf16[1536,384]{1,0:T(8,128)(2,1)S(1)}, bf16[1536,384]{1,0:T(8,128)(2,1)}, u32[]{:S(2)}, u32[]{:S(2)}) collective-permute-start(bf16[1536,384]{1,0:T(8,128)(2,1)S(1)} %copy-done.66), channel_id=1, source_target_pairs={{0,1},{1,0},{2,3},{3,2},{4,5},{5,4},{6,7},{7,6},{8,9},{9,8},{10,11... | collective-permute-start | bytes 3538952 | tf_op jit(solution)/shard_map/ppermute | solution.py:794
  136.5 80.9 %collective-permute-start.26 = (bf16[2,2,384,1536]{3,2,1,0:T(8,128)(2,1)}, bf16[2,2,384,1536]{3,2,1,0:T(8,128)(2,1)}, u32[]{:S(2)}, u32[]{:S(2)}) collective-permute-start(bf16[2,2,384,1536]{3,2,1,0:T(8,128)(2,1)} %get-tuple-element.220), channel_id=1, source_target_pairs={{0,2},{2,0},{4,6},{6,4},{8,10},{10,8},{12,14},{14,12},{16,18},{18,... | collective-permute-start | bytes 14155784 | tf_op jit(solution)/shard_map/ppermute | solution.py:795
  181.2 31.2 %collective-permute-start.24 = (bf16[2,4,384,384]{3,2,1,0:T(8,128)(2,1)}, bf16[2,4,384,384]{3,2,1,0:T(8,128)(2,1)}, u32[]{:S(2)}, u32[]{:S(2)}) collective-permute-start(bf16[2,4,384,384]{3,2,1,0:T(8,128)(2,1)} %get-tuple-element.217), channel_id=1, source_target_pairs={{0,2},{2,0},{4,6},{6,4},{8,10},{10,8},{12,14},{14,12},{16,18},{18,... | collective-permute-start | bytes 7077896 | tf_op jit(solution)/shard_map/ppermute | solution.py:795
  182.7 15.7 %collective-permute-start.25 = (bf16[768,384]{1,0:T(8,128)(2,1)S(1)}, bf16[768,384]{1,0:T(8,128)(2,1)S(1)}, u32[]{:S(2)}, u32[]{:S(2)}) collective-permute-start(bf16[768,384]{1,0:T(8,128)(2,1)S(1)} %collective-permute-done.18.refs_4_.w0.refs_8_), channel_id=1, source_target_pairs={{0,8},{2,10},{4,12},{6,14},{8,0},{10,2},{12,4},{14,6},{16,24},{18,... | collective-permute-start | bytes 1769480 | tf_op jit(solution)/shard_map/ppermute | solution.py:795
  184.2 28.3 %collective-permute-start.21 = (bf16[1536,384]{1,0:T(8,128)(2,1)}, bf16[1536,384]{1,0:T(8,128)(2,1)S(1)}, u32[]{:S(2)}, u32[]{:S(2)}) collective-permute-start(bf16[1536,384]{1,0:T(8,128)(2,1)} %collective-permute-done.19.u0.d0), channel_id=1, source_target_pairs={{0,4},{2,6},{4,0},{6,2},{8,12},{10,14},{12,8},{14,10},{16,20},{18,... | collective-permute-start | bytes 3538952 | tf_op jit(solution)/shard_map/ppermute | solution.py:795
  189.2 11.2 %collective-permute-start.20 = (bf16[160,768]{1,0:T(8,128)(2,1)S(1)}, bf16[160,768]{1,0:T(8,128)(2,1)S(1)}, u32[]{:S(2)}, u32[]{:S(2)}) collective-permute-start(bf16[160,768]{1,0:T(8,128)(2,1)S(1)} %copy-done.88), channel_id=1, source_target_pairs={{0,1},{1,0},{2,3},{3,2},{4,5},{5,4},{6,7},{7,6},{8,9},{9,8},{10,11... | collective-permute-start | bytes 737288 | tf_op jit(solution)/shard_map/ppermute | solution.py:794
  199.6 17.8 %collective-permute-start.27 = (bf16[768,384]{1,0:T(8,128)(2,1)S(1)}, bf16[768,384]{1,0:T(8,128)(2,1)S(1)}, u32[]{:S(2)}, u32[]{:S(2)}) collective-permute-start(bf16[768,384]{1,0:T(8,128)(2,1)S(1)} %collective-permute-done.18.refs_4_.w0.refs_8_), channel_id=1, source_target_pairs={{0,2},{2,0},{4,6},{6,4},{8,10},{10,8},{12,14},{14,12},{16,18},{18,... | collective-permute-start | bytes 1769480 | tf_op jit(solution)/shard_map/ppermute | solution.py:795
  200.3 48.8 %collective-permute-start.30 = (bf16[1536,384]{1,0:T(8,128)(2,1)}, bf16[1536,384]{1,0:T(8,128)(2,1)S(1)}, u32[]{:S(2)}, u32[]{:S(2)}) collective-permute-start(bf16[1536,384]{1,0:T(8,128)(2,1)} %collective-permute-done.19.u0.d0), channel_id=1, source_target_pairs={{0,2},{2,0},{4,6},{6,4},{8,10},{10,8},{12,14},{14,12},{16,18},{18,... | collective-permute-start | bytes 3538952 | tf_op jit(solution)/shard_map/ppermute | solution.py:795
  212.5 36.2 %collective-permute-start.22 = (bf16[1536,384]{1,0:T(8,128)(2,1)S(1)}, bf16[1536,384]{1,0:T(8,128)(2,1)S(1)}, u32[]{:S(2)}, u32[]{:S(2)}) collective-permute-start(bf16[1536,384]{1,0:T(8,128)(2,1)S(1)} %collective-permute-done.21.u1.d1), channel_id=1, source_target_pairs={{0,2},{2,0},{4,6},{6,4},{8,10},{10,8},{12,14},{14,12},{16,18},{18,... | collective-permute-start | bytes 3538952 | tf_op jit(solution)/shard_map/ppermute | solution.py:795
  237.1 12.0 %collective-permute-start.29 = (f32[2,768]{1,0:T(2,128)S(1)}, f32[2,768]{1,0:T(2,128)S(1)}, u32[]{:S(2)}, u32[]{:S(2)}) collective-permute-start(f32[2,768]{1,0:T(2,128)S(1)} %copy-done.64), channel_id=1, source_target_pairs={{0,2},{2,0},{4,6},{6,4},{8,10},{10,8},{12,14},{14,12},{16,18},{18,... | collective-permute-start | bytes 18440 | tf_op jit(solution)/shard_map/ppermute | solution.py:795
  240.2 61.8 %collective-permute-start.34 = (bf16[1,384,1536]{2,1,0:T(8,128)(2,1)}, bf16[1,384,1536]{2,1,0:T(8,128)(2,1)}, u32[]{:S(2)}, u32[]{:S(2)}) collective-permute-start(bf16[1,384,1536]{2,1,0:T(8,128)(2,1)} %fusion.2), channel_id=1, source_target_pairs={{0,1},{1,0},{2,3},{3,2},{4,5},{5,4},{6,7},{7,6},{8,9},{9,8},{10,11... | collective-permute-start | bytes 3538952 | tf_op jit(solution)/shard_map/ppermute | solution.py:794
  247.2 57.7 %collective-permute-start.36 = (bf16[2,1,192,1536]{3,2,1,0:T(8,128)(2,1)}, bf16[2,1,192,1536]{3,2,1,0:T(8,128)(2,1)}, u32[]{:S(2)}, u32[]{:S(2)}) collective-permute-start(bf16[2,1,192,1536]{3,2,1,0:T(8,128)(2,1)} %pad_maximum_fusion), channel_id=1, source_target_pairs={{0,4},{2,6},{4,0},{6,2},{8,12},{10,14},{12,8},{14,10},{16,20},{18,... | collective-permute-start | bytes 3538952 | tf_op jit(solution)/shard_map/ppermute | solution.py:795
  248.7 58.8 %collective-permute-start.38 = (bf16[2,4,192,384]{3,2,1,0:T(8,128)(2,1)}, bf16[2,4,192,384]{3,2,1,0:T(8,128)(2,1)}, u32[]{:S(2)}, u32[]{:S(2)}) collective-permute-start(bf16[2,4,192,384]{3,2,1,0:T(8,128)(2,1)} %pad_maximum_fusion.1), channel_id=1, source_target_pairs={{0,8},{2,10},{4,12},{6,14},{8,0},{10,2},{12,4},{14,6},{16,24},{18,... | collective-permute-start | bytes 3538952 | tf_op jit(solution)/shard_map/ppermute | solution.py:795
  288.8 12.2 %collective-permute-start.31 = (bf16[288,768]{1,0:T(8,128)(2,1)}, bf16[288,768]{1,0:T(8,128)(2,1)S(1)}, u32[]{:S(2)}, u32[]{:S(2)}) collective-permute-start(bf16[288,768]{1,0:T(8,128)(2,1)} %get-tuple-element.231), channel_id=1, source_target_pairs={{0,1},{1,0},{2,3},{3,2},{4,5},{5,4},{6,7},{7,6},{8,9},{9,8},{10,11... | collective-permute-start | bytes 1327112 | tf_op jit(solution)/shard_map/ppermute | solution.py:794
  293.2 58.0 %collective-permute-start.33 = (bf16[2,2,384,1536]{3,2,1,0:T(8,128)(2,1)}, bf16[2,2,384,1536]{3,2,1,0:T(8,128)(2,1)S(1)}, u32[]{:S(2)}, u32[]{:S(2)}) collective-permute-start(bf16[2,2,384,1536]{3,2,1,0:T(8,128)(2,1)} %get-tuple-element.234), channel_id=1, source_target_pairs={{0,2},{2,0},{4,6},{6,4},{8,10},{10,8},{12,14},{14,12},{16,18},{18,... | collective-permute-start | bytes 14155784 | tf_op jit(solution)/shard_map/ppermute | solution.py:795
  304.3 35.2 %collective-permute-start.35 = (bf16[1,192,1536]{2,1,0:T(8,128)(2,1)}, bf16[1,192,1536]{2,1,0:T(8,128)(2,1)}, u32[]{:S(2)}, u32[]{:S(2)}) collective-permute-start(bf16[1,192,1536]{2,1,0:T(8,128)(2,1)} %add_convert_fusion.11), channel_id=1, source_target_pairs={{0,4},{2,6},{4,0},{6,2},{8,12},{10,14},{12,8},{14,10},{16,20},{18,... | collective-permute-start | bytes 1769480 | tf_op jit(solution)/shard_map/ppermute | solution.py:795
  307.0 33.9 %collective-permute-start.37 = (bf16[1,192,1536]{2,1,0:T(8,128)(2,1)}, bf16[1,192,1536]{2,1,0:T(8,128)(2,1)}, u32[]{:S(2)}, u32[]{:S(2)}) collective-permute-start(bf16[1,192,1536]{2,1,0:T(8,128)(2,1)} %fusion.5), channel_id=1, source_target_pairs={{0,1},{1,0},{2,3},{3,2},{4,5},{5,4},{6,7},{7,6},{8,9},{9,8},{10,11... | collective-permute-start | bytes 1769480 | tf_op jit(solution)/shard_map/ppermute | solution.py:794
  312.5 23.8 %collective-permute-start.40 = (bf16[2,4,96,384]{3,2,1,0:T(8,128)(2,1)}, bf16[2,4,96,384]{3,2,1,0:T(8,128)(2,1)}, u32[]{:S(2)}, u32[]{:S(2)}) collective-permute-start(bf16[2,4,96,384]{3,2,1,0:T(8,128)(2,1)} %pad_maximum_fusion.5), channel_id=1, source_target_pairs={{0,4},{2,6},{4,0},{6,2},{8,12},{10,14},{12,8},{14,10},{16,20},{18,... | collective-permute-start | bytes 1769480 | tf_op jit(solution)/shard_map/ppermute | solution.py:795
  335.1 14.1 %collective-permute-start.47 = (bf16[4,384,384]{2,1,0:T(8,128)(2,1)}, bf16[4,384,384]{2,1,0:T(8,128)(2,1)S(1)}, u32[]{:S(2)}, u32[]{:S(2)}) collective-permute-start(bf16[4,384,384]{2,1,0:T(8,128)(2,1)} %get-tuple-element.268), channel_id=1, source_target_pairs={{0,2},{2,0},{4,6},{6,4},{8,10},{10,8},{12,14},{14,12},{16,18},{18,... | collective-permute-start | bytes 3538952 | tf_op jit(solution)/shard_map/ppermute | solution.py:795
  337.9 9.4 %collective-permute-start.41 = (bf16[4,96,384]{2,1,0:T(8,128)(2,1)S(1)}, bf16[4,96,384]{2,1,0:T(8,128)(2,1)S(1)}, u32[]{:S(2)}, u32[]{:S(2)}) collective-permute-start(bf16[4,96,384]{2,1,0:T(8,128)(2,1)S(1)} %fusion.14), channel_id=1, source_target_pairs={{0,1},{1,0},{2,3},{3,2},{4,5},{5,4},{6,7},{7,6},{8,9},{9,8},{10,11... | collective-permute-start | bytes 884744 | tf_op jit(solution)/shard_map/ppermute | solution.py:794
  342.1 17.7 %collective-permute-start.39 = (bf16[2,96,1536]{2,1,0:T(8,128)(2,1)S(1)}, bf16[2,96,1536]{2,1,0:T(8,128)(2,1)S(1)}, u32[]{:S(2)}, u32[]{:S(2)}) collective-permute-start(bf16[2,96,1536]{2,1,0:T(8,128)(2,1)S(1)} %pad_maximum_fusion.4), channel_id=1, source_target_pairs={{0,8},{2,10},{4,12},{6,14},{8,0},{10,2},{12,4},{14,6},{16,24},{18,... | collective-permute-start | bytes 1769480 | tf_op jit(solution)/shard_map/ppermute | solution.py:795
  353.8 35.6 %collective-permute-start.43 = (bf16[1,384,1536]{2,1,0:T(8,128)(2,1)}, bf16[1,384,1536]{2,1,0:T(8,128)(2,1)}, u32[]{:S(2)}, u32[]{:S(2)}) collective-permute-start(bf16[1,384,1536]{2,1,0:T(8,128)(2,1)} %fusion.3), channel_id=1, source_target_pairs={{0,1},{1,0},{2,3},{3,2},{4,5},{5,4},{6,7},{7,6},{8,9},{9,8},{10,11... | collective-permute-start | bytes 3538952 | tf_op jit(solution)/shard_map/ppermute | solution.py:794
  359.2 34.2 %collective-permute-start.48 = (bf16[2,1,192,1536]{3,2,1,0:T(8,128)(2,1)}, bf16[2,1,192,1536]{3,2,1,0:T(8,128)(2,1)}, u32[]{:S(2)}, u32[]{:S(2)}) collective-permute-start(bf16[2,1,192,1536]{3,2,1,0:T(8,128)(2,1)} %pad_maximum_fusion.2), channel_id=1, source_target_pairs={{0,4},{2,6},{4,0},{6,2},{8,12},{10,14},{12,8},{14,10},{16,20},{18,... | collective-permute-start | bytes 3538952 | tf_op jit(solution)/shard_map/ppermute | solution.py:795
  382.1 45.9 %collective-permute-start.42 = (bf16[4,384,384]{2,1,0:T(8,128)(2,1)}, bf16[4,384,384]{2,1,0:T(8,128)(2,1)}, u32[]{:S(2)}, u32[]{:S(2)}) collective-permute-start(bf16[4,384,384]{2,1,0:T(8,128)(2,1)} %get-tuple-element.260), channel_id=1, source_target_pairs={{0,2},{2,0},{4,6},{6,4},{8,10},{10,8},{12,14},{14,12},{16,18},{18,... | collective-permute-start | bytes 3538952 | tf_op jit(solution)/shard_map/ppermute | solution.py:795
  382.6 44.6 %collective-permute-start.45 = (bf16[2,48,1536]{2,1,0:T(8,128)(2,1)}, bf16[2,48,1536]{2,1,0:T(8,128)(2,1)}, u32[]{:S(2)}, u32[]{:S(2)}) collective-permute-start(bf16[2,48,1536]{2,1,0:T(8,128)(2,1)} %pad_maximum_fusion.11), channel_id=1, source_target_pairs={{0,16},{2,18},{4,20},{6,22},{8,24},{10,26},{12,28},{14,30},{16,0},... | collective-permute-start | bytes 884744 | tf_op jit(solution)/shard_map/ppermute | solution.py:795
  385.2 42.0 %collective-permute-start.46 = (bf16[4,48,384]{2,1,0:T(8,128)(2,1)}, bf16[4,48,384]{2,1,0:T(8,128)(2,1)}, u32[]{:S(2)}, u32[]{:S(2)}) collective-permute-start(bf16[4,48,384]{2,1,0:T(8,128)(2,1)} %add_convert_fusion.30), channel_id=1, source_target_pairs={{0,16},{2,18},{4,20},{6,22},{8,24},{10,26},{12,28},{14,30},{16,0},... | collective-permute-start | bytes 442376 | tf_op jit(solution)/shard_map/ppermute | solution.py:795
  391.9 36.1 %collective-permute-start.44 = (bf16[1,192,1536]{2,1,0:T(8,128)(2,1)}, bf16[1,192,1536]{2,1,0:T(8,128)(2,1)S(1)}, u32[]{:S(2)}, u32[]{:S(2)}) collective-permute-start(bf16[1,192,1536]{2,1,0:T(8,128)(2,1)} %add_convert_fusion.6), channel_id=1, source_target_pairs={{0,4},{2,6},{4,0},{6,2},{8,12},{10,14},{12,8},{14,10},{16,20},{18,... | collective-permute-start | bytes 1769480 | tf_op jit(solution)/shard_map/ppermute | solution.py:795
  425.2 27.3 %collective-permute-start.59 = (bf16[2,384,384]{2,1,0:T(8,128)(2,1)S(1)}, bf16[2,384,384]{2,1,0:T(8,128)(2,1)S(1)}, u32[]{:S(2)}, u32[]{:S(2)}) collective-permute-start(bf16[2,384,384]{2,1,0:T(8,128)(2,1)S(1)} %copy-done.50), channel_id=1, source_target_pairs={{0,1},{1,0},{2,3},{3,2},{4,5},{5,4},{6,7},{7,6},{8,9},{9,8},{10,11... | collective-permute-start | bytes 1769480 | tf_op jit(solution)/shard_map/ppermute | solution.py:794
  427.1 49.5 %collective-permute-start.52 = (bf16[4,384,384]{2,1,0:T(8,128)(2,1)}, bf16[4,384,384]{2,1,0:T(8,128)(2,1)}, u32[]{:S(2)}, u32[]{:S(2)}) collective-permute-start(bf16[4,384,384]{2,1,0:T(8,128)(2,1)} %get-tuple-element.293), channel_id=1, source_target_pairs={{0,2},{2,0},{4,6},{6,4},{8,10},{10,8},{12,14},{14,12},{16,18},{18,... | collective-permute-start | bytes 3538952 | tf_op jit(solution)/shard_map/ppermute | solution.py:795
  427.2 30.2 %collective-permute-start.65 = (bf16[1,192,1536]{2,1,0:T(8,128)(2,1)}, bf16[1,192,1536]{2,1,0:T(8,128)(2,1)}, u32[]{:S(2)}, u32[]{:S(2)}) collective-permute-start(bf16[1,192,1536]{2,1,0:T(8,128)(2,1)} %fusion.4), channel_id=1, source_target_pairs={{0,1},{1,0},{2,3},{3,2},{4,5},{5,4},{6,7},{7,6},{8,9},{9,8},{10,11... | collective-permute-start | bytes 1769480 | tf_op jit(solution)/shard_map/ppermute | solution.py:794
  454.2 15.4 %collective-permute-start.60 = (bf16[2,2,192,384]{3,2,1,0:T(8,128)(2,1)S(1)}, bf16[2,2,192,384]{3,2,1,0:T(8,128)(2,1)S(1)}, u32[]{:S(2)}, u32[]{:S(2)}) collective-permute-start(bf16[2,2,192,384]{3,2,1,0:T(8,128)(2,1)S(1)} %pad_maximum_fusion.7), channel_id=1, source_target_pairs={{0,4},{2,6},{4,0},{6,2},{8,12},{10,14},{12,8},{14,10},{16,20},{18,... | collective-permute-start | bytes 1769480 | tf_op jit(solution)/shard_map/ppermute | solution.py:795
  458.7 15.4 %collective-permute-start.66 = (bf16[2,96,1536]{2,1,0:T(8,128)(2,1)S(1)}, bf16[2,96,1536]{2,1,0:T(8,128)(2,1)S(1)}, u32[]{:S(2)}, u32[]{:S(2)}) collective-permute-start(bf16[2,96,1536]{2,1,0:T(8,128)(2,1)S(1)} %pad_maximum_fusion.8), channel_id=1, source_target_pairs={{0,8},{2,10},{4,12},{6,14},{8,0},{10,2},{12,4},{14,6},{16,24},{18,... | collective-permute-start | bytes 1769480 | tf_op jit(solution)/shard_map/ppermute | solution.py:795
  461.7 19.8 %collective-permute-start.50 = (bf16[448,768]{1,0:T(8,128)(2,1)S(1)}, bf16[448,768]{1,0:T(8,128)(2,1)S(1)}, u32[]{:S(2)}, u32[]{:S(2)}) collective-permute-start(bf16[448,768]{1,0:T(8,128)(2,1)S(1)} %copy-done.73), channel_id=1, source_target_pairs={{0,1},{1,0},{2,3},{3,2},{4,5},{5,4},{6,7},{7,6},{8,9},{9,8},{10,11... | collective-permute-start | bytes 2064392 | tf_op jit(solution)/shard_map/ppermute | solution.py:794
  463.1 34.8 %collective-permute-start.51 = (bf16[4,384,384]{2,1,0:T(8,128)(2,1)S(1)}, bf16[4,384,384]{2,1,0:T(8,128)(2,1)S(1)}, u32[]{:S(2)}, u32[]{:S(2)}) collective-permute-start(bf16[4,384,384]{2,1,0:T(8,128)(2,1)S(1)} %copy-done.67), channel_id=1, source_target_pairs={{0,2},{2,0},{4,6},{6,4},{8,10},{10,8},{12,14},{14,12},{16,18},{18,... | collective-permute-start | bytes 3538952 | tf_op jit(solution)/shard_map/ppermute | solution.py:795
  469.7 15.1 %collective-permute-start.61 = (bf16[2,192,384]{2,1,0:T(8,128)(2,1)S(1)}, bf16[2,192,384]{2,1,0:T(8,128)(2,1)S(1)}, u32[]{:S(2)}, u32[]{:S(2)}) collective-permute-start(bf16[2,192,384]{2,1,0:T(8,128)(2,1)S(1)} %get-tuple-element.306), channel_id=1, source_target_pairs={{0,4},{2,6},{4,0},{6,2},{8,12},{10,14},{12,8},{14,10},{16,20},{18,... | collective-permute-start | bytes 884744 | tf_op jit(solution)/shard_map/ppermute | solution.py:795
  474.0 12.4 %collective-permute-start.62 = (bf16[2,192,384]{2,1,0:T(8,128)(2,1)S(1)}, bf16[2,192,384]{2,1,0:T(8,128)(2,1)S(1)}, u32[]{:S(2)}, u32[]{:S(2)}) collective-permute-start(bf16[2,192,384]{2,1,0:T(8,128)(2,1)S(1)} %fusion.12), channel_id=1, source_target_pairs={{0,1},{1,0},{2,3},{3,2},{4,5},{5,4},{6,7},{7,6},{8,9},{9,8},{10,11... | collective-permute-start | bytes 884744 | tf_op jit(solution)/shard_map/ppermute | solution.py:794
  476.6 15.1 %collective-permute-start.67 = (bf16[2,48,1536]{2,1,0:T(8,128)(2,1)S(1)}, bf16[2,48,1536]{2,1,0:T(8,128)(2,1)S(1)}, u32[]{:S(2)}, u32[]{:S(2)}) collective-permute-start(bf16[2,48,1536]{2,1,0:T(8,128)(2,1)S(1)} %pad_maximum_fusion.14), channel_id=1, source_target_pairs={{0,16},{2,18},{4,20},{6,22},{8,24},{10,26},{12,28},{14,30},{16,0},... | collective-permute-start | bytes 884744 | tf_op jit(solution)/shard_map/ppermute | solution.py:795
  481.5 16.3 %collective-permute-start.53 = (bf16[2,384,384]{2,1,0:T(8,128)(2,1)S(1)}, bf16[2,384,384]{2,1,0:T(8,128)(2,1)S(1)}, u32[]{:S(2)}, u32[]{:S(2)}) collective-permute-start(bf16[2,384,384]{2,1,0:T(8,128)(2,1)S(1)} %add_convert_fusion.3), channel_id=1, source_target_pairs={{0,1},{1,0},{2,3},{3,2},{4,5},{5,4},{6,7},{7,6},{8,9},{9,8},{10,11... | collective-permute-start | bytes 1769480 | tf_op jit(solution)/shard_map/ppermute | solution.py:794
  498.1 14.2 %collective-permute-start.54 = (bf16[2,2,192,384]{3,2,1,0:T(8,128)(2,1)S(1)}, bf16[2,2,192,384]{3,2,1,0:T(8,128)(2,1)S(1)}, u32[]{:S(2)}, u32[]{:S(2)}) collective-permute-start(bf16[2,2,192,384]{3,2,1,0:T(8,128)(2,1)S(1)} %pad_maximum_fusion.6), channel_id=1, source_target_pairs={{0,4},{2,6},{4,0},{6,2},{8,12},{10,14},{12,8},{14,10},{16,20},{18,... | collective-permute-start | bytes 1769480 | tf_op jit(solution)/shard_map/ppermute | solution.py:795
  512.4 8.7 %collective-permute-start.63 = (bf16[4,96,384]{2,1,0:T(8,128)(2,1)S(1)}, bf16[4,96,384]{2,1,0:T(8,128)(2,1)S(1)}, u32[]{:S(2)}, u32[]{:S(2)}) collective-permute-start(bf16[4,96,384]{2,1,0:T(8,128)(2,1)S(1)} %pad_maximum_fusion.13), channel_id=1, source_target_pairs={{0,8},{2,10},{4,12},{6,14},{8,0},{10,2},{12,4},{14,6},{16,24},{18,... | collective-permute-start | bytes 884744 | tf_op jit(solution)/shard_map/ppermute | solution.py:795
  513.3 8.8 %collective-permute-start.55 = (bf16[2,192,384]{2,1,0:T(8,128)(2,1)S(1)}, bf16[2,192,384]{2,1,0:T(8,128)(2,1)S(1)}, u32[]{:S(2)}, u32[]{:S(2)}) collective-permute-start(bf16[2,192,384]{2,1,0:T(8,128)(2,1)S(1)} %get-tuple-element.296), channel_id=1, source_target_pairs={{0,4},{2,6},{4,0},{6,2},{8,12},{10,14},{12,8},{14,10},{16,20},{18,... | collective-permute-start | bytes 884744 | tf_op jit(solution)/shard_map/ppermute | solution.py:795
  515.5 6.8 %collective-permute-start.56 = (bf16[2,192,384]{2,1,0:T(8,128)(2,1)S(1)}, bf16[2,192,384]{2,1,0:T(8,128)(2,1)S(1)}, u32[]{:S(2)}, u32[]{:S(2)}) collective-permute-start(bf16[2,192,384]{2,1,0:T(8,128)(2,1)S(1)} %fusion.13), channel_id=1, source_target_pairs={{0,1},{1,0},{2,3},{3,2},{4,5},{5,4},{6,7},{7,6},{8,9},{9,8},{10,11... | collective-permute-start | bytes 884744 | tf_op jit(solution)/shard_map/ppermute | solution.py:794
  522.3 7.7 %collective-permute-start.64 = (bf16[4,48,384]{2,1,0:T(8,128)(2,1)S(1)}, bf16[4,48,384]{2,1,0:T(8,128)(2,1)S(1)}, u32[]{:S(2)}, u32[]{:S(2)}) collective-permute-start(bf16[4,48,384]{2,1,0:T(8,128)(2,1)S(1)} %pad_maximum_fusion.19), channel_id=1, source_target_pairs={{0,16},{2,18},{4,20},{6,22},{8,24},{10,26},{12,28},{14,30},{16,0},... | collective-permute-start | bytes 442376 | tf_op jit(solution)/shard_map/ppermute | solution.py:795
  524.9 5.1 collective-permute-start.70
  526.1 8.0 %collective-permute-start.57 = (bf16[4,96,384]{2,1,0:T(8,128)(2,1)S(1)}, bf16[4,96,384]{2,1,0:T(8,128)(2,1)S(1)}, u32[]{:S(2)}, u32[]{:S(2)}) collective-permute-start(bf16[4,96,384]{2,1,0:T(8,128)(2,1)S(1)} %pad_maximum_fusion.12), channel_id=1, source_target_pairs={{0,8},{2,10},{4,12},{6,14},{8,0},{10,2},{12,4},{14,6},{16,24},{18,... | collective-permute-start | bytes 884744 | tf_op jit(solution)/shard_map/ppermute | solution.py:795
  534.1 7.7 %collective-permute-start.71 = (f32[10,768]{1,0:T(8,128)S(1)}, f32[10,768]{1,0:T(8,128)S(1)}, u32[]{:S(2)}, u32[]{:S(2)}) collective-permute-start(f32[10,768]{1,0:T(8,128)S(1)} %add.741), channel_id=1, source_target_pairs={{0,16},{2,18},{4,20},{6,22},{8,24},{10,26},{12,28},{14,30},{16,0},... | collective-permute-start | bytes 92168 | tf_op jit(solution)/shard_map/ppermute | solution.py:795
  534.3 9.2 %collective-permute-start.58 = (bf16[4,48,384]{2,1,0:T(8,128)(2,1)S(1)}, bf16[4,48,384]{2,1,0:T(8,128)(2,1)S(1)}, u32[]{:S(2)}, u32[]{:S(2)}) collective-permute-start(bf16[4,48,384]{2,1,0:T(8,128)(2,1)S(1)} %pad_maximum_fusion.18), channel_id=1, source_target_pairs={{0,16},{2,18},{4,20},{6,22},{8,24},{10,26},{12,28},{14,30},{16,0},... | collective-permute-start | bytes 442376 | tf_op jit(solution)/shard_map/ppermute | solution.py:795
  (97 other events, 1036.6 us)

commit v4 on v3

--- a/solution.py
+++ b/solution.py
@@ -100,37 +100,9 @@
     return pltpu.CompilerParams(vmem_limit_bytes=limit)
 
 
-PLAN = {
-    "stats_fl": (3, 5),
-    "fl_core": (2, 4),
-    "out_l": (3, 5),
-    "stats_bl": (4, 5),
-    "sl_core": (3, 5),
-    "fl_1": (4, None),
-    "sl_1": (4, 6),
-    "stats_fv": (5, 7),
-    "fv_core": (5, 7),
-    "out_v": (5, 7),
-    "fl_a2": (5, 7),
-    "fl_b2": (5, None),
-    "sl_2": (5, 8),
-    "svr_core": (6, 8),
-    "fv_1": (6, 8),
-    "fl_3": (6, 7),
-    "sl_3": (6, 7),
-    "stats_bv": (7, 8),
-    "svo_core": (7, 9),
-    "fv_a2": (7, 9),
-    "fv_b2": (7, None),
-    "fl_4": (7, 9),
-    "sl_4": (7, 9),
-    "xr_core": (8, None),
-    "sv_1": (8, None),
-    "fv_3": (8, None),
-    "stats_y": (8, None),
-}
-WEIGHTS = (1000000000, 1000000000, 100000000000, 100000000000, 100000000000, 30000000000, 10000000000, 1, 5000000000, 100000000000)
+WEIGHTS = (100000000000, 100000000000, 100000000000, 100000000000, 100000000000, 100000000000, 100000000000, 100000000000, 100000000000, 100000000000)
 WORK = iter(())
+ADD_WORK = 1
 
 
 def fwd_kernel(dirs, each, which, spans, slot_ref, *refs):
@@ -279,11 +251,11 @@
         for k, (u, d) in enumerate(((u0, d0), (u1, d1), (u2, d2), (u3, d3))):
             q = slot_ref[which[1]] ^ k
             at = pl.ds(pl.multiple_of(lax.rem(q, per) * piece, piece), piece)
-            rem.append((u.at[pl.ds(packs_at[0] * width, width), :], uall.at[each + q // per, :, at]))
+            rem.append((u.at[pl.ds(packs_at[0][k] * width, width), :], uall.at[each + q // per, :, at]))
             q = slot_ref[which[2]] ^ k
             at = pl.ds(pl.multiple_of(lax.rem(q, per) * piece, piece), piece)
             for c in range(width // piece):
-                rows = pl.ds(packs_at[1] * width + c * piece, piece)
+                rows = pl.ds(packs_at[1][k] * width + c * piece, piece)
                 rem.append((d.at[rows, :], dall.at[each + q // per, at, pl.ds(c * piece, piece)]))
         groups, n = own + [rem], 0
         for k, group in enumerate(groups):
@@ -345,13 +317,10 @@
     def _():
         du = (dot_nt(e[...], dall[b]) * slope[b].astype(F32)).astype(BF)
         acc[...] += dot_nt(du, uall[b])
-        rows = send.shape[1]
-        up_grad = dot(x2t[...], du).astype(BF)
-        keep[0] = up_grad[:rows]
-        send[0] = up_grad[rows:]
-        down_grad = dot(et[...], hidden[b]).astype(BF)
-        keep[1] = down_grad[:rows]
-        send[1] = down_grad[rows:]
+        rows = width // 2
+        for m, grad in enumerate((dot(x2t[...], du).astype(BF), dot(et[...], hidden[b]).astype(BF))):
+            keep[m * rows : (m + 1) * rows, :] = grad[:rows]
+            send[m * rows : (m + 1) * rows, :] = grad[rows:]
 
     @pl.when(i == 2 * blocks - 1)
     def _():
@@ -367,7 +336,8 @@
 def feed_forward(
     n1, ctx, out_proj, wo_pack, gains, biases, cot_own, cot_recv, perm, up_proj, down_proj, up_pack, down_pack, which, slot, stream, spans
 ):
-    (up_pack, up_at), (down_pack, down_at) = up_pack, down_pack
+    up_pack, up_at = zip(*up_pack)
+    down_pack, down_at = zip(*down_pack)
     tokens, width = n1.shape
     half = out_proj.shape[1]
     hid = up_proj.shape[2]
@@ -377,10 +347,10 @@
 
     def grad_map(i, s):
         b = jnp.maximum(i - blocks, 0)
-        return (b // each, 0, 0, lax.rem(b, each))
-
-    grad_spec = pl.BlockSpec((None, 2, width // 2, block), grad_map)
-    grad_shape = jax.ShapeDtypeStruct((2, 2, width // 2, hid), BF)
+        return (b // each, lax.rem(b, each))
+
+    grad_specs = [pl.BlockSpec((width, block), grad_map)] * 2
+    grad_shape = jax.ShapeDtypeStruct((2 * width, hid), BF)
     out_rows = width // 4
     tail = pl.BlockSpec((out_rows, half), lambda i, s: (3, 0), pipeline_mode=pl.Buffered(1))
     hbm = pl.BlockSpec(memory_space=pl.ANY)
@@ -397,7 +367,8 @@
             + [hbm] * 10,
             out_specs=[const_out((tokens // 2, width))] * 2
             + [const_out((tokens, width))] * 2
-            + [const_out((4, width)), grad_spec, grad_spec],
+            + [const_out((4, width))]
+            + grad_specs,
             scratch_shapes=[
                 pltpu.VMEM((2 * half, width), BF),
                 pltpu.VMEM((blocks, width, block), BF),
@@ -420,9 +391,8 @@
             jax.ShapeDtypeStruct((tokens, width), F32),
             jax.ShapeDtypeStruct((tokens, width), BF),
             jax.ShapeDtypeStruct((4, width), F32),
-            grad_shape,
-            grad_shape,
-        ],
+        ]
+        + [grad_shape] * 2,
         compiler_params=params(FFN_VMEM[stream]),
         cost_estimate=pl.CostEstimate(flops=next(WORK), bytes_accessed=1, transcendentals=0),
         name="feed_forward",
@@ -432,17 +402,12 @@
 def bwd_kernel(dirs, each, which, spans, half_of, norm, slot_ref, *refs):
     first = half_of != 0
     cross = spans is not None
-    if cross and first:
-        x_own, x_recv, g_a, g_b, base_a, base_b = refs[:6]
-        refs = refs[6:]
-    elif first:
-        x, g_a, base = refs[:3]
-        refs = refs[3:]
-    else:
-        g_in, base, xt, gt = refs[:4]
-        refs = refs[4:]
+    n_g = 2 if cross else 1
+    gs, bases, refs = refs[:n_g], refs[n_g : 2 * n_g if first else n_g + 1], refs[2 * n_g if first else n_g + 1 :]
+    n_x = n_g if first else 2
+    xs, refs = refs[:n_x], refs[n_x:]
     if first:
-        perm, refs = refs[0], refs[1:]
+        perm_in, refs = refs[0], refs[1:]
     own, wo = None, None
     rem, w_rem = (), ()
     if half_of != 1:
@@ -453,26 +418,71 @@
     refs = refs[4:]
     probs, refs = refs[: len(dirs)], refs[len(dirs) :]
     if norm:
-        n1, inv1, gain, dx_out, low_out, stats = refs[:6]
+        n1_in, inv1, gain, dx_out, low_out, stats = refs[:6]
         refs = refs[6:]
     elif cross and half_of != 1:
         dx_own, dx_send = refs[:2]
         refs = refs[2:]
     else:
-        dx_out, g_out, xt, gt = refs[:4]
-        refs = refs[4:]
-    send, keep, buf, wobuf, dqkv, acc = refs[:6]
-    if half_of is None:
-        xt, gt = refs[6:8]
-        g = refs[8]
-    elif first:
-        g = g_out
-    else:
-        g = g_in
+        dx_out, xt_out, gt_out = refs[:3]
+        refs = refs[3:]
+    n_grads = 4 if cross else 2
+    grad_refs, refs = refs[:n_grads], refs[n_grads:]
+    buf, wobuf, dqkv, acc, g, xt, gt, sem = refs[:8]
+    refs = refs[8:]
+    if first:
+        xbuf, perm, refs = refs[0], refs[1], refs[2:]
+    if norm:
+        (n1,) = refs
     j = pl.program_id(0)
     slot = slot_ref[which]
-    width = wobuf.shape[1]
+    tokens = g.shape[0]
     count = each * (2 if half_of is None else 1)
+
+    def fetches(kind):
+        pairs = []
+        if kind == 0:
+            if not first:
+                pairs = [(xs[0], xt), (xs[1], gt)]
+            else:
+                pairs = [(perm_in, perm)]
+                if cross:
+                    at = 0
+                    for n in spans:
+                        for i, x in enumerate(xs):
+                            pairs.append((x.at[pl.ds(at, n), :], xbuf.at[pl.ds(2 * at + i * n, n), :]))
+                        at += n
+                else:
+                    pairs.append((xs[0], xbuf))
+        elif kind == 1:
+            at = 0
+            for base in bases:
+                n = base.shape[0]
+                pairs.append((base, acc.at[pl.ds(at, n), :]))
+                at += n
+        elif norm:
+            pairs = [(n1_in, n1)]
+        shift = (0, 6, 8)[kind]
+        return [pltpu.make_async_copy(a, b, sem.at[shift + i]) for i, (a, b) in enumerate(pairs)]
+
+    def results():
+        return [pltpu.make_async_copy(xt, xt_out, sem.at[9]), pltpu.make_async_copy(gt, gt_out, sem.at[10])]
+
+    @pl.when(j == 0)
+    def _():
+        for kind in range(3):
+            for copy in fetches(kind):
+                copy.start()
+        base_row = 0
+        if half_of != 1:
+            wobuf[: wo.shape[0], :] = wo[...]
+            base_row = wo.shape[0]
+        if half_of != 0:
+            load_out(slot, w_rem, wobuf, base_row)
+        at = 0
+        for part in gs:
+            g[at : at + part.shape[0], :] = part[...]
+            at += part.shape[0]
 
     if half_of != 1:
 
@@ -490,31 +500,6 @@
                 start = pl.multiple_of((slot ^ k) * rows, rows)
                 for i in range(3):
                     buf[pl.ds(start, rows), i * LANES : (i + 1) * LANES] = rem[k][i * rows : (i + 1) * rows]
-
-    @pl.when(j == 0)
-    def _():
-        base_row = 0
-        if half_of != 1:
-            wobuf[: wo.shape[0], :] = wo[...]
-            base_row = wo.shape[0]
-        if half_of != 0:
-            load_out(slot, w_rem, wobuf, base_row)
-        if cross and first:
-            load_row(x_own, x_recv, spans, g)
-            xt[...] = dot_nt(perm[...], g[...]).astype(BF)
-            cut = g_a.shape[0]
-            g[:cut, :] = g_a[...]
-            g[cut:, :] = g_b[...]
-            acc[:cut, :] = base_a[...]
-            acc[cut:, :] = base_b[...]
-        elif first:
-            xt[...] = dot_nt(perm[...], x[...]).astype(BF)
-            g[...] = g_a[...]
-            acc[...] = base[...]
-        else:
-            acc[...] = base[...]
-        if first:
-            gt[...] = dot_nt(perm[...], g[...]).astype(BF)
 
     wo_rows = wobuf[pl.ds(pl.multiple_of(j * LANES, LANES), LANES), :]
     dctx_all = dot_nt(g[...], wo_rows).astype(BF)
@@ -541,19 +526,40 @@
         dqkv[q0:q1, :LANES] = (jnp.where(low_q, dq[0], dq[1]) * (1.0 / math.sqrt(HD))).astype(BF)
         dqkv[k0:k1, LANES : 2 * LANES] = jnp.concatenate(dk, 0).T.astype(BF)
         dqkv[k0:k1, 2 * LANES :] = jnp.concatenate(dv, 0).T.astype(BF)
-    rows = send.shape[1]
-    grads = dot(xt[...], dqkv[...]).astype(BF)
-    for i in range(3):
-        part = grads[:, i * LANES : (i + 1) * LANES]
-        keep[i] = part[:rows]
-        send[i] = part[rows:]
-    out_grad = dot(gt[...], c_in[...]).astype(BF)
-    keep[3] = out_grad[:rows]
-    send[3] = out_grad[rows:]
+
+    @pl.when(j == 0)
+    def _():
+        for copy in fetches(0):
+            copy.wait()
+        if first:
+            xt[...] = dot_nt(perm[...], xbuf[...]).astype(BF)
+            gt[...] = dot_nt(perm[...], g[...]).astype(BF)
+            if half_of == 1:
+                for copy in results():
+                    copy.start()
+        for copy in fetches(1):
+            copy.wait()
+
+    made = dot(xt[...], dqkv[...]).astype(BF)
+    made = [made[:, i * LANES : (i + 1) * LANES] for i in range(3)] + [dot(gt[...], c_in[...]).astype(BF)]
+
+    def store(targets):
+        arrays = len(targets) // 2
+        per = 4 // arrays
+        for i, grad in enumerate(made):
+            send, keep = targets[2 * (i // per) : 2 * (i // per) + 2]
+            rows, cols = keep.shape
+            at = pl.ds(pl.multiple_of(i % per * (cols // per) + lax.rem(j, each) * LANES, LANES), LANES)
+            keep[:, at] = grad[:rows]
+            send[:, at] = grad[rows:]
+
+    store(grad_refs)
     acc[...] += dot_nt(dqkv[...], buf[...])
 
     @pl.when(j == count - 1)
     def _():
+        for copy in fetches(2):
+            copy.wait()
         if norm:
             total = acc[...]
             normed = n1[...]
@@ -570,6 +576,9 @@
                 at += n
         else:
             dx_out[...] = acc[...]
+        if half_of == 1:
+            for copy in results():
+                copy.wait()
 
 
 def attention_backward(sources, perm, in_proj, pack, index, which, out_proj, saved, norm, slot, dirs, half_of=None, spans=None):
@@ -582,13 +591,15 @@
     shift = each if half_of == 1 else 0
     col = pl.BlockSpec((tokens, LANES), lambda j, s: (0, j + shift))
     tail = pl.BlockSpec((out_rows, half), lambda j, s: (3, 0), pipeline_mode=pl.Buffered(1))
+    hbm = pl.BlockSpec(memory_space=pl.ANY)
     p_shapes = [(PAIR, q1 - q0, k1 - k0) for q0, q1, k0, k1 in dirs]
     first = half_of != 0
+    n_g = 1 if spans is None else 2
     args = list(sources)
-    in_specs = [const(a.shape) for a in sources]
+    in_specs = [const(a.shape) for a in sources[:n_g]] + [hbm] * (len(sources) - n_g)
     if first:
         args.append(perm)
-        in_specs.append(const((width, width)))
+        in_specs.append(hbm)
     if half_of != 1:
         args += [in_proj, out_proj]
         in_specs += [
@@ -602,37 +613,43 @@
     in_specs += [col] * 4 + [pl.BlockSpec(s, lambda j, s: (j + shift, 0, 0)) for s in p_shapes]
     if norm:
         args += list(norm)
-        in_specs += [const(a.shape) for a in norm]
+        in_specs += [hbm] + [const(a.shape) for a in norm[1:]]
         outs = [((tokens, width), F32), ((tokens, width), BF), ((2, width), F32)]
     elif spans is not None and half_of != 1:
         outs = [((tokens // 2, width), F32), ((tokens // 2, width), BF)]
     else:
-        outs = [((tokens, width), F32), ((tokens, width), BF), ((width, tokens), BF), ((width, tokens), BF)]
+        outs = [((tokens, width), F32), ((width, tokens), BF), ((width, tokens), BF)]
+    out_specs = [const_out(s) for s, _ in outs]
+    if half_of == 1:
+        out_specs[1:] = [hbm] * 2
     scratch = [
         pltpu.VMEM((width, 3 * LANES), BF),
         pltpu.VMEM((half if half_of is not None else 2 * half, width), BF),
         pltpu.VMEM((tokens, 3 * LANES), BF),
         pltpu.VMEM((tokens, width), F32),
+        pltpu.VMEM((tokens, width), BF),
+        pltpu.VMEM((width, tokens), BF),
+        pltpu.VMEM((width, tokens), BF),
+        pltpu.SemaphoreType.DMA((11,)),
     ]
+    if first:
+        scratch += [pltpu.VMEM((tokens, width), BF), pltpu.VMEM((width, width), BF)]
+    if norm:
+        scratch.append(pltpu.VMEM((tokens, width), F32))
+    grad_shape = jax.ShapeDtypeStruct((width // 2, (4 if spans is None else 2) * half), BF)
+    grad_specs = [pl.BlockSpec(grad_shape.shape, lambda j, s: (j // each, 0))] * (2 if spans is None else 4)
     if half_of is None:
-        grad_spec = pl.BlockSpec(
-            (None, 4, width // 2, LANES), lambda j, s: (jnp.where(j < each, 0, 1), 0, 0, lax.rem(j, each))
-        )
-        grad_shape = jax.ShapeDtypeStruct((2, 4, width // 2, half), BF)
-        scratch += [pltpu.VMEM((width, tokens), BF)] * 2 + [pltpu.VMEM((tokens, width), BF)]
-    else:
-        grad_spec = pl.BlockSpec((4, width // 2, LANES), lambda j, s: (0, 0, j))
-        grad_shape = jax.ShapeDtypeStruct((4, width // 2, half), BF)
+        grad_shape = jax.ShapeDtypeStruct((width, 4 * half), BF)
     return pl.pallas_call(
         functools.partial(bwd_kernel, dirs, each, which, spans, half_of, bool(norm)),
         grid_spec=pltpu.PrefetchScalarGridSpec(
             num_scalar_prefetch=1,
             grid=(count,),
             in_specs=in_specs,
-            out_specs=[const_out(s) for s, _ in outs] + [grad_spec, grad_spec],
+            out_specs=out_specs + grad_specs,
             scratch_shapes=scratch,
         ),
-        out_shape=[jax.ShapeDtypeStruct(s, k) for s, k in outs] + [grad_shape, grad_shape],
+        out_shape=[jax.ShapeDtypeStruct(s, k) for s, k in outs] + [grad_shape] * len(grad_specs),
         compiler_params=params(),
         cost_estimate=pl.CostEstimate(flops=next(WORK), bytes_accessed=1, transcendentals=0),
         name="attention_backward",
@@ -688,12 +705,12 @@
     pairs = attention_cuts(in_proj, out_proj, 1, pz, self_l) + attention_cuts(in_proj, out_proj, 2, pz, self_v)
     cols = up_l.shape[1]
     rows = up_l.shape[0]
-    for s, u, d, p in ((0, up_l, down_l, pz), (1, ffn_v.at[pl.ds(0, rows)], ffn_v.at[pl.ds(rows, rows)], px)):
+    for s, u, d in ((0, up_l, down_l), (1, ffn_v.at[pl.ds(0, rows)], ffn_v.at[pl.ds(rows, rows)])):
         pairs.append((up.at[s, :, pl.ds(pl.multiple_of(px * cols, cols), cols)], u))
         for c in range(2):
             pairs.append(
                 (
-                    down.at[s, pl.ds(pl.multiple_of(p * cols, cols), cols), pl.ds(c * cols, cols)],
+                    down.at[s, pl.ds(pl.multiple_of(pz * cols, cols), cols), pl.ds(c * cols, cols)],
                     d.at[pl.ds(c * cols, cols), :],
                 )
             )
@@ -718,62 +735,113 @@
     return lax.optimization_barrier((x,) + deps)[0]
 
 
-def total_of(terms):
-    return sum(x.astype(F32) for x in terms)
-
-
-class Chain:
-    def __init__(self, parts, order, exchange):
-        self.parts = [(list(own), list(rem)) for own, rem in parts]
+def add_kernel(plan, n_in, *refs):
+    ins, outs = refs[:n_in], refs[n_in:]
+    for out, pieces in zip(outs, plan):
+        for at, rows, terms in pieces:
+            total = ins[terms[0]][...].astype(F32)
+            for k in terms[1:]:
+                total += ins[k][...].astype(F32)
+            out[at : at + rows, :] = total.astype(out.dtype)
+
+
+def add_up(outputs, kind):
+    if all(rows % 16 == 0 for _, pieces in outputs for rows, _ in pieces):
+        arrays, specs, plan, shapes = [], [], [], []
+        for wide, pieces in outputs:
+            at, laid = 0, []
+            for rows, terms in pieces:
+                where = []
+                for array, start, col in terms:
+                    where.append(len(arrays))
+                    arrays.append(array)
+                    specs.append(
+                        pl.BlockSpec(
+                            (rows, wide), lambda *_, i=start // rows, j=col: (i, j), pipeline_mode=pl.Buffered(1)
+                        )
+                    )
+                laid.append((at, rows, where))
+                at += rows
+            plan.append(laid)
+            shapes.append((at, wide))
+        return pl.pallas_call(
+            functools.partial(add_kernel, plan, len(arrays)),
+            grid=(1,),
+            in_specs=specs,
+            out_specs=[pl.BlockSpec(s, lambda *_: (0, 0), pipeline_mode=pl.Buffered(1)) for s in shapes],
+            out_shape=[jax.ShapeDtypeStruct(s, kind) for s in shapes],
+            compiler_params=params(),
+            cost_estimate=pl.CostEstimate(flops=ADD_WORK, bytes_accessed=1, transcendentals=0),
+            name="add_up",
+        )(*arrays)
+    return [
+        jnp.concatenate(
+            [
+                sum(a[s : s + rows, c * wide : (c + 1) * wide].astype(F32) for a, s, c in terms).astype(kind)
+                for rows, terms in pieces
+            ]
+        )
+        for wide, pieces in outputs
+    ]
+
+
+class Sum:
+    def __init__(self, own, rem, rows, order, wide, col=0):
+        self.wide = wide
+        self.own = [(a, row, col) for a, row in own]
+        self.rem = [(a, row, col) for a, row in rem]
+        self.rows = rows
         self.order = list(order)
-        self.exchange = exchange
-        self.received = None
-
-    def absorb(self, *deps):
-        if self.received is None:
-            return
-        received = after(self.received, *deps) if deps else self.received
-        self.received = None
+
+
+def send_all(sums, exchange, *deps):
+    ways = {}
+    for s in sums:
+        ways.setdefault((s.order.pop(0), s.wide), []).append(s)
+    outputs, filed = [], []
+    for (stage, wide), group in ways.items():
+        pieces = []
+        for s in group:
+            if stage < 0:
+                pieces.append((s.rows, s.rem, s, s.own))
+                s.rem = []
+            else:
+                half = s.rows // 2
+                for side in (s.own, s.rem):
+                    if side:
+                        pieces.append((half, [(a, start + half, c) for a, start, c in side], s, side))
+        pieces.sort(key=lambda p: -p[0])
+        outputs.append((wide, [(rows, terms) for rows, terms, _, _ in pieces]))
+        filed.append((stage, group, pieces))
+    made = add_up(outputs, BF)
+    exchange.made = made
+    arrived = []
+    for (stage, group, pieces), buffer in zip(filed, made):
+        got = exchange(after(buffer, *deps), stage)
+        arrived.append(got)
         at = 0
-        for own, rem in self.parts:
-            n = own[0].shape[-3]
-            got = lax.slice_in_dim(received, at, at + n, axis=received.ndim - 3)
-            at += n
-            if rem:
-                own.append(got[0])
-                rem.append(got[1])
-            else:
-                own.append(got)
-
-    def start(self, *deps):
-        self.absorb()
-        stage = self.order.pop(0)
-        halved = stage >= 0
-        sent, kept = [], []
-        for own, rem in self.parts:
-            if halved:
-                rows = own[0].shape[-2] // 2
-                out = [total_of([x[..., rows:, :] for x in side]).astype(BF) for side in (own, rem) if side]
-                kept.append(tuple([x[..., :rows, :] for x in side] for side in (own, rem)))
-            else:
-                out = [total_of(rem).astype(BF)]
-                kept.append((own, []))
-            sent.append(out)
-        whole = [jnp.stack(out) if len(out) > 1 else out[0] for out in sent]
-        whole = jnp.concatenate(whole, whole[0].ndim - 3) if len(whole) > 1 else whole[0]
-        self.parts = kept
-        self.received = self.exchange(after(whole, *deps), stage)
-        return self.received
-
-    def total(self, *deps):
-        self.absorb(*deps)
-        return [total_of(own) for own, _ in self.parts]
-
-
-def joined(*chains):
-    for c in chains:
-        c.absorb()
-    return Chain([p for c in chains for p in c.parts], chains[0].order, chains[0].exchange)
+        for rows, _, _, side in pieces:
+            side.append((got, at, 0))
+            at += rows
+        if stage >= 0:
+            for s in group:
+                s.rows //= 2
+    return arrived
+
+
+def finish(named, *deps):
+    tied = {}
+
+    def late(array):
+        if id(array) not in tied:
+            tied[id(array)] = after(array, *deps)
+        return tied[id(array)]
+
+    outputs = []
+    for s in named.values():
+        *early, (last, row, col) = s.own
+        outputs.append((s.wide, [(s.rows, early + [(late(last), row, col)])]))
+    return dict(zip(named, add_up(outputs, F32)))
 
 
 def on_device(
@@ -838,7 +906,7 @@
     streams = ((0, lw), (lw, lw + lv))
 
     x_recv = exchange(after(x_other, cross_y, ffn_v_piece), Y)
-    cross_x = exchange(cross_y, X)
+    cross_x = exchange(after(cross_y, ffn_v_piece), X)
     cross_pack = [cross_y, cross_x, exchange(cross_y, C), exchange(cross_x, C)]
     self_l_y = exchange(after(self_l_piece, x_recv), Y)
     up_l_y = exchange(after(up_l_piece, x_recv), Y)
@@ -879,176 +947,140 @@
     cot_recv = exchange(after(cot_other, down_l_y), Y)
     self_l = self_forward(0, self_l_pack, after(slot, down_l_y, up_l_x))
 
+    def cores(sends, *deps):
+        return [exchange(after(x, *deps) if deps else x, C) for x in sends]
+
     tok = self_l[3]
     down_l_pack = [down_l_y, down_l_z, exchange(after(down_l_y, tok), C), exchange(after(down_l_z, tok), C)]
     self_v_y = exchange(after(self_v_piece, tok, cot_recv), Y)
     ffn_v_y = exchange(after(ffn_v_piece, tok, cot_recv), Y)
-    ffn_l = feed(0, self_l[3], self_l_pack, (up_l_pack, 0), (down_l_pack, 0), (SZ, SX, SZ), after(slot, up_l_pack[3]))
-
-    def ffn_chains(ffn, core):
-        keep = ffn[6]
-        made = []
-        for i, stages in enumerate((y_first[:2], x_first[:2])):
-            made.append(Chain([([keep[0, i : i + 1], core[0, i : i + 1]], [keep[1, i : i + 1], core[1, i : i + 1]])], stages, exchange))
-        return made
-
-    def self_chains(own, own_core, rem, rem_core):
-        made = []
-        for i, stages in ((0, y_first[:2]), (2, x_first[:2])):
-            made.append(Chain([([own[i : i + 2], own_core[i : i + 2]], [rem[i : i + 2], rem_core[i : i + 2]])], stages, exchange))
-        return made
-
-    def rejoin(*chains):
-        both = joined(*chains)
-        both.order = list(rest)
-        return both
-
-    toks = {2: ffn_l[4]}
-    ties = {k: [] for k in range(12)}
-    have = {"ffn_l": ffn_l}
-
-    def plain(source, pick, stage):
-        return lambda dep: exchange(after(pick(have[source]), dep), stage)
-
-    def chain(name, make=None):
-        def run(dep):
-            if make is not None:
-                made = make()
-                if isinstance(made, tuple) or isinstance(made, list):
-                    for key, c in zip(name.split(), made):
-                        have[key] = c
-                    return [c.start(dep) for c in made]
-                have[name] = made
-            return have[name].start(dep)
-        return run
-
-    sl_parts = lambda: Chain([([have["back_l"][4][0], have["sl_core"][0]], [have["back_l"][4][1], have["sl_core"][1]])], z_first, exchange)
-    tasks = [
-        ("stats_fl", plain("ffn_l", lambda f: f[4], C)),
-        ("fl_core", plain("ffn_l", lambda f: f[5], C)),
-        ("out_l", plain("ffn_l", lambda f: f[1], Y)),
-        ("stats_bl", plain("back_l", lambda f: f[2], C)),
-        ("sl_core", plain("back_l", lambda f: f[3], C)),
-        ("fl_1", chain("fl_a fl_b", lambda: ffn_chains(have["ffn_l"], have["fl_core"]))),
-        ("sl_1", chain("sl", sl_parts)),
-        ("stats_fv", plain("ffn_v", lambda f: f[4], C)),
-        ("fv_core", plain("ffn_v", lambda f: f[5], C)),
-        ("out_v", plain("ffn_v", lambda f: f[1], Y)),
-        ("fl_a2", chain("fl_a")),
-        ("fl_b2", chain("fl_b")),
-        ("sl_2", chain("sl")),
-        ("svr_core", plain("bva", lambda f: f[4], C)),
-        ("fv_1", chain("fv_a fv_b", lambda: ffn_chains(have["ffn_v"], have["fv_core"]))),
-        ("fl_3", chain("fl", lambda: rejoin(have["fl_a"], have["fl_b"]))),
-        ("sl_3", chain("sl")),
-        ("stats_bv", plain("bvb", lambda f: f[2], C)),
-        ("svo_core", plain("bvb", lambda f: f[3], C)),
-        ("fv_a2", chain("fv_a")),
-        ("fv_b2", chain("fv_b")),
-        ("fl_4", chain("fl")),
-        ("sl_4", chain("sl")),
-        ("xr_core", plain("xa", lambda f: f[4], C)),
-        ("sv_1", chain("sv_a sv_b", lambda: self_chains(have["bvb"][4], have["svo_core"], have["bva"][5], have["svr_core"]))),
-        ("fv_3", chain("fv", lambda: rejoin(have["fv_a"], have["fv_b"]))),
-        ("stats_y", lambda dep: exchange(after(stats_c(), dep), Y)),
-    ]
-
-    def stats_c():
-        rows = [(have[a][i], have[b]) for a, i, b in (("ffn_l", 4, "stats_fl"), ("ffn_v", 4, "stats_fv"), ("back_l", 2, "stats_bl"), ("bvb", 2, "stats_bv"))]
-        a, b, c, e = [x + y for x, y in rows]
-        return jnp.concatenate([c[:1] + e[:1], a[2:3], b[2:3], a[:1], b[:1], c[1:] + e[1:], a[3:4], b[3:4], a[1:2], b[1:2]])
-
-    def boundary(i, kernel=None, tok=None):
-        if kernel is not None:
-            have[kernel[0]] = kernel[1]
-            toks[i] = tok
-        for name, run in tasks:
-            begin, end = PLAN[name]
-            if begin == i:
-                got = run(toks[i])
-                have[name] = got
-                if end is not None:
-                    ties[end] += got if isinstance(got, list) else [got]
-
-    boundary(2)
+    ffn_l = feed(0, self_l[3], self_l_pack, [(a, 0) for a in up_l_pack], [(a, 0) for a in down_l_pack], (SZ, SX, SZ), after(slot, up_l_pack[3]))
+
     tok = ffn_l[4]
+    near_fl = exchange(ffn_l[4], C)
+    core_fl = exchange(ffn_l[5], C)
     self_v_z = exchange(after(self_v_y, tok), Z)
     self_v_c = exchange(after(self_v_y, tok), C)
-    ffn_v_x = exchange(after(ffn_v_y, tok), X)
+    out_l_recv = exchange(after(ffn_l[1], tok), Y)
+    back_l = self_back(0, (ffn_l[3], ffn_l[2], norms[0][2]), self_l, self_l_pack, after(slot, self_v_y, near_fl))
+
+    tok = back_l[2]
+    near_bl = exchange(back_l[2], C)
+    core_sl = exchange(back_l[3], C)
+    self_v_pack = [self_v_y, self_v_z, self_v_c, exchange(after(self_v_z, tok), C)]
+    up_v_x = exchange(after(ffn_v_y[:width], tok), X)
+    down_v_z = exchange(after(ffn_v_y[width:], tok), Z)
     ffn_v_c = exchange(after(ffn_v_y, tok), C)
-    back_l = self_back(0, (norms[0][2], ffn_l[3], ffn_l[2]), self_l, self_l_pack, after(slot, self_v_y, ffn_v_y, *ties[3]))
-
-    tok = back_l[2]
-    boundary(3, ("back_l", back_l), tok)
-    self_v_pack = [self_v_y, self_v_z, self_v_c, exchange(after(self_v_z, tok), C)]
-    ffn_v_pack = [ffn_v_y, ffn_v_x, ffn_v_c, exchange(after(ffn_v_x, tok), C)]
-    self_v = self_forward(1, self_v_pack, after(slot, self_v_z, ffn_v_x, *ties[4]))
-
-    boundary(4, ("self_v", self_v), self_v[3])
+    self_v = self_forward(1, self_v_pack, after(slot, self_v_z, ffn_v_y, out_l_recv, near_bl, core_fl))
+
+    tok = self_v[3]
+    up_v_pack = [(ffn_v_y, 0), (up_v_x, 0), (ffn_v_c, 0), (exchange(after(up_v_x, tok), C), 0)]
+    down_v_pack = [(ffn_v_y, 1), (down_v_z, 0), (ffn_v_c, 1), (exchange(after(down_v_z, tok), C), 0)]
+    rows = width // 2
+    hid = up_proj.shape[2]
+
+    def part(arrays, i):
+        return [(a, i * rows) for a in arrays]
+
+    ful, fdl = [
+        Sum(part((ffn_l[6], core_fl), i), part((ffn_l[6], core_fl), 2 + i), rows, way, hid)
+        for i, way in enumerate((y_first, x_first))
+    ]
+    sl = Sum(part((back_l[4], core_sl), 0), part((back_l[4], core_sl), 1), rows, [Z, X] + rest[1:] + [Y], hid)
+    got4 = send_all([ful, fdl, sl], exchange, tok)
     ffn_v = feed(
-        1, self_v[3], self_v_pack, (ffn_v_pack, 0), (ffn_v_pack, 1), (SZ, SX, SX), after(slot, ffn_v_pack[3], *ties[5])
+        1, self_v[3], self_v_pack, up_v_pack, down_v_pack, (SZ, SX, SZ), after(slot, up_v_x, down_v_z)
     )
-    boundary(5, ("ffn_v", ffn_v), ffn_v[4])
-    bva = self_back(1, (norms[1][2], ffn_v[3], ffn_v[2]), self_v, self_v_pack, after(slot, *ties[6]), 1)
-    boundary(6, ("bva", bva), bva[0])
-    bvb = self_back(1, (bva[1], bva[0], bva[2], bva[3]), self_v, self_v_pack, after(slot, *ties[7]), 0)
-    boundary(7, ("bvb", bvb), bvb[2])
+
+    tok = ffn_v[4]
+    near_fv = exchange(ffn_v[4], C)
+    core_fv = exchange(ffn_v[5], C)
+    got5 = send_all([ful, fdl, sl], exchange, tok)
+    out_v_recv = exchange(after(ffn_v[1], tok), Y)
+    bva = self_back(1, (ffn_v[3], ffn_v[2], norms[1][2]), self_v, self_v_pack, after(slot, near_fv, *got4), 1)
+
+    tok = bva[0]
+    core_svr = exchange(bva[3], C)
+    fuv, fdv = [
+        Sum(part((ffn_v[6], core_fv), i), part((ffn_v[6], core_fv), 2 + i), rows, way, hid)
+        for i, way in enumerate((y_first, x_first))
+    ]
+    got6 = send_all([fuv, fdv, ful, fdl, sl], exchange, tok)
+    bvb = self_back(1, (ffn_v[3], bva[0], bva[1], bva[2]), self_v, self_v_pack, after(slot, out_v_recv, *got5, core_fv), 0)
+
+    tok = bvb[2]
+    near_bv = exchange(bvb[2], C)
+    core_svo = exchange(bvb[3], C)
+    sv = Sum(part((bvb[4], core_svo), 0), part((bva[4], core_svr), 0), rows, y_first, hid)
+    got7 = send_all([sv, fuv, ful, fdl], exchange, tok)
     xa = attention_backward(
-        (x_own, x_recv, back_l[1], bvb[1], back_l[0], bvb[0]), perm, in_proj, cross_pack, 0, SX, out_proj, cross,
-        None, after(slot, *ties[8]), cross_dirs, 1, spans,
+        (back_l[1], bvb[1], back_l[0], bvb[0], x_own, x_recv), perm, in_proj, cross_pack, 0, SX, out_proj, cross,
+        None, after(slot, *got6), cross_dirs, 1, spans,
     )
-    boundary(8, ("xa", xa), xa[0])
+
+    tok = xa[0]
+    near = [
+        a + b for a, b in ((ffn_l[4], near_fl), (ffn_v[4], near_fv), (back_l[2], near_bl), (bvb[2], near_bv))
+    ]
+    a, b, c, e = near
+    stats = jnp.concatenate([c[:1] + e[:1], a[2:3], b[2:3], a[:1], b[:1], c[1:] + e[1:], a[3:4], b[3:4], a[1:2], b[1:2]])
+    core_xr = cores(xa[3:7:2])
+    got8 = send_all([sv, fuv, fdv, sl], exchange, tok)
     xb = attention_backward(
-        (xa[1], xa[0], xa[2], xa[3]), perm, in_proj, cross_pack, 0, SX, out_proj, cross,
-        None, after(slot, *ties[9]), cross_dirs, 0, spans,
+        (back_l[1], bvb[1], xa[0], xa[1], xa[2]), perm, in_proj, cross_pack, 0, SX, out_proj, cross,
+        None, after(slot, near_bv, *got7), cross_dirs, 0, spans,
     )
 
     tok = xb[0]
-    fl, sl, fv, sv_a, sv_b = [have[k] for k in ("fl", "sl", "fv", "sv_a", "sv_b")]
-    out_l_recv, out_v_recv = have["out_l"], have["out_v"]
-    stats = stats_c() + have["stats_y"]
-    xo_core = exchange(xb[2], C)
-    grad_recv = exchange(after(xb[1], tok), Y)
-    got = [c.start(tok, *have["sv_1"]) for c in (sv_a, sv_b)] + [fv.start(tok)]
-    if sl.order:
-        sl.start(tok)
-    if fl.order:
-        fl.start(tok)
-    cx_a, cx_b = self_chains(xb[3], xo_core, xa[5], have["xr_core"])
-    got = [cx_a.start(tok), cx_b.start(tok)]
-    sv = rejoin(sv_a, sv_b)
-    sv.start(*got)
-    stats = stats + exchange(after(stats, *got), X)
-    got = [cx_a.start(*got), cx_b.start(*got)]
-    cx = rejoin(cx_a, cx_b)
-    sv.start(*got)
-    for stage in rest:
-        tied = got
-        got = [cx.start(*tied)]
-        stats = stats + exchange(after(stats, *tied), stage)
-    for c in (sv, fv, fl, sl):
-        while c.order:
-            c.start(*got)
-    fl, sl, fv, sv, cx = [jnp.concatenate(c.total(xb[0]), 0) for c in (fl, sl, fv, sv, cx)]
+    core_xo = cores(xb[2:6:2])
+    cxs = [
+        Sum(part((xb[3 + 2 * i], core_xo[i]), 0), part((xa[4 + 2 * i], core_xr[i]), 0), rows, way, hid // 2)
+        for i, way in enumerate((y_first, x_first))
+    ]
+    others = [sv, fuv, fdv, sl, ful, fdl]
+    first = send_all([s for s in others if s.order], exchange, tok)
+    for s in cxs:
+        s.own[-1] = (after(s.own[-1][0], *exchange.made), 0, 0)
+    tied = core_xo
+    grad_recv = None
+    beside = first
+    for stage in range(1, bits):
+        got = send_all(cxs, exchange, *tied)
+        left = [s for s in others if s.order]
+        if left and stage > 1:
+            beside = send_all(left, exchange, *tied)
+        stats = stats + exchange(after(stats, *tied), Y if stage == 1 else stage - 1)
+        if grad_recv is None and stage > 1:
+            grad_recv = exchange(after(xb[1], *tied), Y)
+        tied = got + beside
+    got = send_all(cxs, exchange, *tied)
+    stats = stats + exchange(after(stats, *tied), bits - 1)
+    while any(s.order for s in others):
+        send_all([s for s in others if s.order], exchange, *tied)
+    sums = finish({"ful": ful, "fdl": fdl, "sl": sl}, xb[0])
+    sums |= finish({"fuv": fuv, "fdv": fdv, "sv": sv}, *tied)
+    sums |= finish({"cxa": cxs[0], "cxb": cxs[1]})
 
     def whole(mine, back):
         back = back.astype(mine.dtype)
         return jnp.where(t == 0, jnp.stack([mine, back]), jnp.stack([back, mine]))
 
     cut_at = spans[0]
-    attn = (cx, sl, sv)
-    ffn = (fl, fv)
     share = stats.shape[1] // (n_dp * 2)
     stats = lax.dynamic_slice_in_dim(stats, (d * 2 + t) * share, share, 1)
+    attn = [
+        jnp.concatenate(g, 1).reshape(-1, 4, half)
+        for g in ((sums["cxa"], sums["cxb"]), (sums["sl"],), (sums["sv"],))
+    ]
     return (
         whole(ffn_l[0], out_l_recv),
         whole(ffn_v[0], out_v_recv),
         whole(xb[0][:cut_at], grad_recv[:cut_at]),
         whole(xb[0][cut_at:], grad_recv[cut_at:]),
-        jnp.stack([g[:3] for g in attn]),
-        jnp.stack([g[3].T for g in attn]),
-        jnp.stack([g[0] for g in ffn]),
-        jnp.stack([g[1].T for g in ffn]),
+        jnp.stack([jnp.swapaxes(g[:, :3], 0, 1) for g in attn]),
+        jnp.stack([g[:, 3].T for g in attn]),
+        jnp.stack([sums["ful"], sums["fuv"]]),
+        jnp.stack([sums["fdl"].T, sums["fdv"].T]),
         stats[:5],
         stats[5:],
     )

time: 548 us -> 466 us (0.85)
  waiting for transfers between devices: 117 us -> 63 us
  other arithmetic: 64.5 us -> 15.4 us
  Pallas kernels: 259 us -> 289 us
  local copies, waits for them, and re-layouts: 37.4 us -> 27.8 us
    pallas_call x0 -> x14, Pallas kernels: none -> 45 us  [add_up(): pl.pallas_call(functools.partial(add_kernel, plan, len(arrays)), grid=(1,...]
    ppermute x51 -> x53, waiting for transfers between devices: 79.8 us -> 42.5 us  [exchange(): return lax.ppermute(x, 'dp', [(i, i ^ 1 << stage) for i in range(n_dp)])]
    convert_element_type x24 -> x0, other arithmetic: 34 us -> none  [the longest x15 18.4 us: start(): total_of([x[..., rows:, :] for x in side]).astype(BF)]
    squeeze x12 -> x0, local copies, waits for them, and re-layouts: 18.6 us -> none  [the longest x2 7.22 us: ffn_chains(): keep[0, i:i + 1]]
    ppermute x21 -> x19, waiting for transfers between devices: 37.1 us -> 20.5 us  [exchange(): return lax.ppermute(x, 'tensor', SWAP)]
    pallas_call x5, Pallas kernels: 126 us -> 110 us  [attention_backward(): pl.pallas_call(functools.partial(bwd_kernel, dirs, each, which, spans, ha...]
    another operation x24 -> x4, other arithmetic: 16.2 us -> 4.33 us  [the longest x1 1.89 us: on_device(): jnp.stack([sums['fdl'].T, sums['fdv'].T])]
    unnamed x178 -> x174, local copies, waits for them, and re-layouts: 8.53 us -> 19.4 us
  transfers between devices with their start and end apart: 72 -> 72, of which waited for: 25 -> 15; matrix products, arithmetic and copies ran while one was open for 17% -> 4% of each run, Pallas kernels for 47% -> 61%
where the time goes in v4:
time: 466 us; the launch traced here: 458 us
  Pallas kernels  289 us (62%)
  waiting for transfers between devices  63 us (14%)
  starting transfers between devices  61.2 us (13%)
  local copies, waits for them, and re-layouts  27.8 us (6%)
  other arithmetic  15.4 us (3%)
    pallas_call x5, Pallas kernels, attention_backward(): pl.pallas_call(functools.partial(bwd_kernel, dirs, each, which, spans, ha...  110 us
    pallas_call x2, Pallas kernels, feed_forward(): pl.pallas_call(functools.partial(ffn_kernel, blocks, which, stream, spans...  64.8 us
    pallas_call x3, Pallas kernels, attention_forward(): pl.pallas_call(functools.partial(fwd_kernel, dirs, each, which, spans), g...  59.7 us
    pallas_call x14, Pallas kernels, add_up(): pl.pallas_call(functools.partial(add_kernel, plan, len(arrays)), grid=(1,...  45 us
    ppermute x53, waiting for transfers between devices, exchange(): return lax.ppermute(x, 'dp', [(i, i ^ 1 << stage) for i in range(n_dp)])  42.5 us
    ppermute x53, starting transfers between devices, exchange(): return lax.ppermute(x, 'dp', [(i, i ^ 1 << stage) for i in range(n_dp)])  38.8 us
    ppermute x19, starting transfers between devices, exchange(): return lax.ppermute(x, 'tensor', SWAP)  22.4 us
    ppermute x19, waiting for transfers between devices, exchange(): return lax.ppermute(x, 'tensor', SWAP)  20.5 us
  transfers between devices with their start and end apart: 72, of which 15 were waited for; matrix products, arithmetic and copies ran while one was open for 4% of the time, Pallas kernels for 61%

profile of v4, /device:TPU:0, one launch (start us, length us, event | category | flops | bytes accessed | tf_op | source)
XLA Modules:
  0.0 458.5 jit_solution(14434766222794868653)
XLA Ops:
  1.3 3.6 cut.2
  4.9 3.0 collective-permute-start
  8.0 5.7 %cut.3 = (bf16[768,384]{1,0:T(8,128)(2,1)}, bf16[768,384]{1,0:T(8,128)(2,1)}, bf16[768,384]{1,0:T(8,128)(2,1)}, bf16[768,384]{1,0:T(8,128)(2,1)}, bf16[1536,384]...) custom-call(s32[3]{0:T(128)} %pad_add_fusion.1.place.slot_ref, bf16[3,3,768,384]{3,2,1,0:T(8,128)(2,1)} %refs_5_.5, ...), custom_call_target="tpu_custom_call" | custom-call | flops 1 | bytes 1 | tf_op jit(solution)/shard_map/cut/pallas_call | solution.py:722
  13.9 7.6 %collective-permute-done.refs_5_.refs_10_.refs_7_.refs_11_ = bf16[768,384]{1,0:T(8,128)(2,1)S(1)} collective-permute-done((bf16[768,384]{1,0:T(8,128)(2,1)}, bf16[768,384]{1,0:T(8,128)(2,1)S(1)}, u32[]{:S(2)}, u32[]{:S(2)}) %collective-permute-start) | collective-permute-done | bytes 589856 | tf_op jit(solution)/shard_map/ppermute | solution.py:862
  21.5 1.7 collective-permute-start.3
  23.5 1.6 collective-permute-start.1
  26.0 10.0 %collective-permute-done.3.refs_6_.refs_11_.refs_8_.refs_12_ = bf16[768,384]{1,0:T(8,128)(2,1)S(1)} collective-permute-done((bf16[768,384]{1,0:T(8,128)(2,1)S(1)}, bf16[768,384]{1,0:T(8,128)(2,1)S(1)}, u32[]{:S(2)}, u32[]{:S(2)}) %collective-permute-start.3) | collective-permute-done | bytes 589856 | tf_op jit(solution)/shard_map/ppermute | solution.py:863
  39.6 1.5 collective-permute-start.2
  43.2 28.4 %attention_forward.3 = (bf16[896,768]{1,0:T(8,128)(2,1)}, bf16[896,768]{1,0:T(8,128)(2,1)}, bf16[896,768]{1,0:T(8,128)(2,1)}, bf16[896,768]{1,0:T(8,128)(2,1)}, ...) custom-call(s32[3]{0:T(128)} %pad_add_fusion.1.place.slot_ref, ...), custom_call_target="tpu_custom_call" | custom-call | flops 99999997952 | bytes 1 | tf_op jit(solution)/shard_map/attention_forward/pallas_call | solution.py:217
  71.6 1.6 collective-permute-start.8
  73.3 1.5 collective-permute-start.10
  75.4 10.7 %collective-permute-done.8.refs_5_.w1.refs_7_.refs_11_ = bf16[768,384]{1,0:T(8,128)(2,1)S(1)} collective-permute-done((bf16[768,384]{1,0:T(8,128)(2,1)S(1)}, bf16[768,384]{1,0:T(8,128)(2,1)S(1)}, u32[]{:S(2)}, u32[]{:S(2)}) %collective-permute-start.8) | collective-permute-done | bytes 589856 | tf_op jit(solution)/shard_map/ppermute | solution.py:863
  86.0 1.6 slice.122.refs_1_
  87.6 1.5 slice.123.refs_2_
  89.1 1.5 collective-permute-start.13
  90.6 1.6 collective-permute-start.15
  93.6 12.5 %attention_forward.4 = (bf16[320,768]{1,0:T(8,128)(2,1)}, bf16[320,768]{1,0:T(8,128)(2,1)}, bf16[320,768]{1,0:T(8,128)(2,1)}, bf16[320,768]{1,0:T(8,128)(2,1)}, bf16[12,320,320]{2,1,0:T(8,128)(2,1)}) custom-call(s32[3]{0:T(128)} %pad_add_fusion.1.place.slot_ref, bf16[320,768]{1,0:T(8,128)(2,1)} %get-tuple-element.211.refs_0_.refs_2_, ...), custom_call_target="tpu_custom_call" | custom-call | flops 99999997952 | bytes 1 | tf_op jit(solution)/shard_map/attention_forward/pallas_call | solution.py:217
  107.0 1.4 collective-permute-start.20
  109.9 26.7 %feed_forward.2 = (bf16[160,768]{1,0:T(8,128)(2,1)}, bf16[160,768]{1,0:T(8,128)(2,1)}, f32[320,768]{1,0:T(8,128)}, bf16[320,768]{1,0:T(8,128)(2,1)}, f32[4,768]{...) custom-call(s32[3]{0:T(128)} %pad_add_fusion.1.place.slot_ref, ...), custom_call_target="tpu_custom_call" | custom-call | flops 99999997952 | bytes 1 | tf_op jit(solution)/shard_map/feed_forward/pallas_call | solution.py:357
  139.8 22.3 %attention_backward.5 = (f32[320,768]{1,0:T(8,128)}, bf16[320,768]{1,0:T(8,128)(2,1)}, f32[2,768]{1,0:T(2,128)}, bf16[768,1536]{1,0:T(8,128)(2,1)}, bf16[768,1536]{1,0:T(8,128)(2,1)}) custom-call(s32[3]{0:T(128)} %pad_add_fusion.1.place.slot_ref, bf16[320,768]{1,0:T(8,128)(2,1)} %get-tuple-element.228.refs_0_, f32[320,768]{1,0:T(8,128)} %get-tuple-element.229.refs_1_, ...), custom_call_target="tpu_custom_call" | custom-call | flops 99999997952 | bytes 1 | tf_op jit(solution)/shard_map/attention_backward/pallas_call | solution.py:643
  163.5 1.5 collective-permute-start.18
  167.6 4.5 collective-permute-done.18
  172.8 1.5 collective-permute-start.22
  174.3 18.8 %attention_forward.5 = (bf16[576,768]{1,0:T(8,128)(2,1)}, bf16[576,768]{1,0:T(8,128)(2,1)}, bf16[576,768]{1,0:T(8,128)(2,1)}, bf16[576,768]{1,0:T(8,128)(2,1)}, bf16[12,576,576]{2,1,0:T(8,128)(2,1)}) custom-call(s32[3]{0:T(128)} %pad_add_fusion.1.place.slot_ref, bf16[576,768]{1,0:T(8,128)(2,1)} %get-tuple-element.243.refs_0_.refs_2_, ...), custom_call_target="tpu_custom_call" | custom-call | flops 99999997952 | bytes 1 | tf_op jit(solution)/shard_map/attention_forward/pallas_call | solution.py:217
  195.2 5.0 %add_up.14 = (bf16[384,1536]{1,0:T(8,128)(2,1)}, bf16[384,1536]{1,0:T(8,128)(2,1)}, bf16[384,1536]{1,0:T(8,128)(2,1)}) custom-call(bf16[1536,1536]{1,0:T(8,128)(2,1)} %get-tuple-element.253.refs_0_.refs_2_.refs_4_.refs_9_.refs_6_.refs_10_.refs_5_, bf16[1536,1536]{1,0:T(8,128)(2,1)} %copy-done, ...), custom_call_target="tpu_custom_call" | custom-call | flops 1 | bytes 1 | tf_op jit(solution)/shard_map/add_up/pallas_call | solution.py:767
  202.1 1.5 collective-permute-start.34
  204.7 38.1 %feed_forward.3 = (bf16[288,768]{1,0:T(8,128)(2,1)}, bf16[288,768]{1,0:T(8,128)(2,1)}, f32[576,768]{1,0:T(8,128)}, bf16[576,768]{1,0:T(8,128)(2,1)}, f32[4,768]{...) custom-call(s32[3]{0:T(128)} %pad_add_fusion.1.place.slot_ref, ...), custom_call_target="tpu_custom_call" | custom-call | flops 99999997952 | bytes 1 | tf_op jit(solution)/shard_map/feed_forward/pallas_call | solution.py:357
  247.2 4.2 add_up.15
  251.4 1.5 collective-permute-start.38
  252.9 1.4 collective-permute-start.37
  254.4 20.4 %attention_backward.6 = (f32[576,768]{1,0:T(8,128)}, bf16[768,576]{1,0:T(8,128)(2,1)}, bf16[768,576]{1,0:T(8,128)(2,1)}, bf16[384,1536]{1,0:T(8,128)(2,1)}, bf16[384,1536]{1,0:T(8,128)(2,1)}) custom-call(s32[3]{0:T(128)} %pad_add_fusion.1.place.slot_ref, bf16[576,768]{1,0:T(8,128)(2,1)} %get-tuple-element.268.refs_0_, ...), custom_call_target="tpu_custom_call" | custom-call | flops 99999997952 | bytes 1 | tf_op jit(solution)/shard_map/attention_backward/pallas_call | solution.py:643
  274.8 5.8 %collective-permute-done.37.refs_9_.refs_17_.refs_21_.refs_8_.refs_13_.refs_3_.refs_15_ = bf16[384,1536]{1,0:T(8,128)(2,1)S(1)} collective-permute-done((bf16[384,1536]{1,0:T(8,128)(2,1)}, bf16[384,1536]{1,0:T(8,128)(2,1)S(1)}, u32[]{:S(2)}, u32[]{:S(2)}) %collective-permute-start.37) | collective-permute-done | bytes 1179680 | tf_op jit(solution)/shard_map/ppermute | solution.py:863
  281.6 1.5 copy-done.1
  283.2 5.3 %add_up.16 = (bf16[384,1536]{1,0:T(8,128)(2,1)}, bf16[384,1536]{1,0:T(8,128)(2,1)}, bf16[192,1536]{1,0:T(8,128)(2,1)}, bf16[96,1536]{1,0:T(8,128)(2,1)}) custom-call(bf16[1536,1536]{1,0:T(8,128)(2,1)} %get-tuple-element.282.refs_0_.refs_2_.refs_4_.refs_3_.refs_7_.refs_8_.refs_5_.refs_6_, bf16[1536,1536]{1,0:T(8,128)(2,1)} %copy-done.1, ...), custom_call_target="tpu_custom_call" | custom-call | flops 1 | bytes 1 | tf_op jit(solution)/shard_map/add_up/pallas_call | solution.py:767
  288.4 2.6 collective-permute-start.49
  291.0 1.4 collective-permute-start.48
  293.7 19.8 %attention_backward.7 = (f32[576,768]{1,0:T(8,128)}, bf16[576,768]{1,0:T(8,128)(2,1)}, f32[2,768]{1,0:T(2,128)}, bf16[384,1536]{1,0:T(8,128)(2,1)}, bf16[384,1536]{1,0:T(8,128)(2,1)}) custom-call(s32[3]{0:T(128)} %pad_add_fusion.1.place.slot_ref, bf16[576,768]{1,0:T(8,128)(2,1)} %get-tuple-element.268.refs_0_, f32[576,768]{1,0:T(8,128)} %get-tuple-element.275.refs_1_, ...), custom_call_target="tpu_custom_call" | custom-call | flops 99999997952 | bytes 1 | tf_op jit(solution)/shard_map/attention_backward/pallas_call | solution.py:643
  314.1 3.4 collective-permute-done.48.refs_9_.refs_6_.refs_7_.refs_8_
  317.5 1.6 collective-permute-done.43.refs_4_.refs_5_.refs_10_.refs_2_
  320.2 4.1 add_up.17
  325.9 25.2 %attention_backward.8 = (f32[896,768]{1,0:T(8,128)}, bf16[768,896]{1,0:T(8,128)(2,1)}, bf16[768,896]{1,0:T(8,128)(2,1)}, bf16[384,768]{1,0:T(8,128)(2,1)}, bf16[...) custom-call(s32[3]{0:T(128)} %pad_add_fusion.1.place.slot_ref, ...), custom_call_target="tpu_custom_call" | custom-call | flops 99999997952 | bytes 1 | tf_op jit(solution)/shard_map/attention_backward/pallas_call | solution.py:643
  352.8 4.0 add_up.18
  358.2 1.5 collective-permute-start.54
  359.7 1.4 collective-permute-start.53
  361.1 22.8 %attention_backward.9 = (f32[448,768]{1,0:T(8,128)}, bf16[448,768]{1,0:T(8,128)(2,1)}, bf16[384,768]{1,0:T(8,128)(2,1)}, bf16[384,768]{1,0:T(8,128)(2,1)}, bf16[...) custom-call(s32[3]{0:T(128)} %pad_add_fusion.1.place.slot_ref, bf16[320,768]{1,0:T(8,128)(2,1)} %get-tuple-element.294.refs_0_, ...), custom_call_target="tpu_custom_call" | custom-call | flops 99999997952 | bytes 1 | tf_op jit(solution)/shard_map/attention_backward/pallas_call | solution.py:643
  386.3 2.9 add_up.19
  391.3 2.9 add_up.20
  396.3 2.6 collective-permute-start.61
  399.0 9.3 %collective-permute-done.60.refs_4_.refs_9_.refs_10_.refs_16_ = bf16[192,1536]{1,0:T(8,128)(2,1)S(1)} collective-permute-done((bf16[192,1536]{1,0:T(8,128)(2,1)}, bf16[192,1536]{1,0:T(8,128)(2,1)S(1)}, u32[]{:S(2)}, u32[]{:S(2)}) %collective-permute-start.60) | collective-permute-done | bytes 589856 | tf_op jit(solution)/shard_map/ppermute | solution.py:863
  409.1 2.3 add_up.23
  412.7 2.4 add_up.21
  417.1 1.6 collective-permute-start.68
  418.7 2.2 maximum_select_fusion.2
  420.9 3.8 collective-permute-done.68
  426.9 2.2 add_up.22
  429.2 2.0 collective-permute-start.66
  431.5 2.9 add_up.26
  436.1 1.7 collective-permute-done.70
  437.8 1.6 collective-permute-start.71
  439.4 1.9 add_up.24
  442.8 2.8 add_up.27
  445.6 1.9 pad_maximum_fusion.2
  449.3 1.7 collective-permute-done.62
  453.4 2.0 add_up.25
  (330 shorter events, 60.8 us)
Async XLA Ops:
  4.9 16.6 %collective-permute-start = (bf16[768,384]{1,0:T(8,128)(2,1)}, bf16[768,384]{1,0:T(8,128)(2,1)S(1)}, u32[]{:S(2)}, u32[]{:S(2)}) collective-permute-start(bf16[768,384]{1,0:T(8,128)(2,1)} %get-tuple-element.191), channel_id=1, source_target_pairs={{0,1},{1,0},{2,3},{3,2},{4,5},{5,4},{6,7},{7,6},{8,9},{9,8},{10,11... | collective-permute-start | bytes 1769480 | tf_op jit(solution)/shard_map/ppermute | solution.py:862
  21.5 14.5 %collective-permute-start.3 = (bf16[768,384]{1,0:T(8,128)(2,1)S(1)}, bf16[768,384]{1,0:T(8,128)(2,1)S(1)}, u32[]{:S(2)}, u32[]{:S(2)}) collective-permute-start(bf16[768,384]{1,0:T(8,128)(2,1)S(1)} %collective-permute-done.refs_5_.refs_10_.refs_7_.refs_11_), channel_id=1, source_target_pairs={{0,4},{2,6},{4,0},{6,2},{8,12},{10,14},{12,8},{14,10},{16,20},{18,... | collective-permute-start | bytes 1769480 | tf_op jit(solution)/shard_map/ppermute | solution.py:863
  23.5 16.1 %collective-permute-start.1 = (bf16[448,768]{1,0:T(8,128)(2,1)S(1)}, bf16[448,768]{1,0:T(8,128)(2,1)S(1)}, u32[]{:S(2)}, u32[]{:S(2)}) collective-permute-start(bf16[448,768]{1,0:T(8,128)(2,1)S(1)} %copy-done.59), channel_id=1, source_target_pairs={{0,1},{1,0},{2,3},{3,2},{4,5},{5,4},{6,7},{7,6},{8,9},{9,8},{10,11... | collective-permute-start | bytes 2064392 | tf_op jit(solution)/shard_map/ppermute | solution.py:862
  26.0 15.6 %collective-permute-start.4 = (bf16[768,384]{1,0:T(8,128)(2,1)S(1)}, bf16[768,384]{1,0:T(8,128)(2,1)S(1)}, u32[]{:S(2)}, u32[]{:S(2)}) collective-permute-start(bf16[768,384]{1,0:T(8,128)(2,1)S(1)} %collective-permute-done.refs_5_.refs_10_.refs_7_.refs_11_), channel_id=1, source_target_pairs={{0,2},{2,0},{4,6},{6,4},{8,10},{10,8},{12,14},{14,12},{16,18},{18,... | collective-permute-start | bytes 1769480 | tf_op jit(solution)/shard_map/ppermute | solution.py:863
  39.6 35.2 %collective-permute-start.2 = (bf16[768,384]{1,0:T(8,128)(2,1)S(1)}, bf16[768,384]{1,0:T(8,128)(2,1)S(1)}, u32[]{:S(2)}, u32[]{:S(2)}) collective-permute-start(bf16[768,384]{1,0:T(8,128)(2,1)S(1)} %copy-done.71), channel_id=1, source_target_pairs={{0,1},{1,0},{2,3},{3,2},{4,5},{5,4},{6,7},{7,6},{8,9},{9,8},{10,11... | collective-permute-start | bytes 1769480 | tf_op jit(solution)/shard_map/ppermute | solution.py:862
  41.1 30.5 %collective-permute-start.7 = (bf16[768,384]{1,0:T(8,128)(2,1)S(1)}, bf16[768,384]{1,0:T(8,128)(2,1)S(1)}, u32[]{:S(2)}, u32[]{:S(2)}) collective-permute-start(bf16[768,384]{1,0:T(8,128)(2,1)S(1)} %copy-done.73), channel_id=1, source_target_pairs={{0,1},{1,0},{2,3},{3,2},{4,5},{5,4},{6,7},{7,6},{8,9},{9,8},{10,11... | collective-permute-start | bytes 1769480 | tf_op jit(solution)/shard_map/ppermute | solution.py:862
  71.6 14.4 %collective-permute-start.8 = (bf16[768,384]{1,0:T(8,128)(2,1)S(1)}, bf16[768,384]{1,0:T(8,128)(2,1)S(1)}, u32[]{:S(2)}, u32[]{:S(2)}) collective-permute-start(bf16[768,384]{1,0:T(8,128)(2,1)S(1)} %collective-permute-done.7.refs_4_.w0.refs_6_.refs_10_), channel_id=1, source_target_pairs={{0,8},{2,10},{4,12},{6,14},{8,0},{10,2},{12,4},{14,6},{16,24},{18,... | collective-permute-start | bytes 1769480 | tf_op jit(solution)/shard_map/ppermute | solution.py:863
  73.3 15.8 %collective-permute-start.10 = (bf16[768,384]{1,0:T(8,128)(2,1)S(1)}, bf16[768,384]{1,0:T(8,128)(2,1)S(1)}, u32[]{:S(2)}, u32[]{:S(2)}) collective-permute-start(bf16[768,384]{1,0:T(8,128)(2,1)S(1)} %copy-done.67), channel_id=1, source_target_pairs={{0,1},{1,0},{2,3},{3,2},{4,5},{5,4},{6,7},{7,6},{8,9},{9,8},{10,11... | collective-permute-start | bytes 1769480 | tf_op jit(solution)/shard_map/ppermute | solution.py:862
  74.8 15.8 %collective-permute-start.6 = (bf16[768,384]{1,0:T(8,128)(2,1)S(1)}, bf16[768,384]{1,0:T(8,128)(2,1)S(1)}, u32[]{:S(2)}, u32[]{:S(2)}) collective-permute-start(bf16[768,384]{1,0:T(8,128)(2,1)S(1)} %collective-permute-done.2.u0), channel_id=1, source_target_pairs={{0,4},{2,6},{4,0},{6,2},{8,12},{10,14},{12,8},{14,10},{16,20},{18,... | collective-permute-start | bytes 1769480 | tf_op jit(solution)/shard_map/ppermute | solution.py:863
  75.4 16.9 %collective-permute-start.11 = (bf16[768,384]{1,0:T(8,128)(2,1)S(1)}, bf16[768,384]{1,0:T(8,128)(2,1)S(1)}, u32[]{:S(2)}, u32[]{:S(2)}) collective-permute-start(bf16[768,384]{1,0:T(8,128)(2,1)S(1)} %collective-permute-done.7.refs_4_.w0.refs_6_.refs_10_), channel_id=1, source_target_pairs={{0,2},{2,0},{4,6},{6,4},{8,10},{10,8},{12,14},{14,12},{16,18},{18,... | collective-permute-start | bytes 1769480 | tf_op jit(solution)/shard_map/ppermute | solution.py:863
  86.0 6.7 %collective-permute-start.12 = (bf16[768,384]{1,0:T(8,128)(2,1)S(1)}, bf16[768,384]{1,0:T(8,128)(2,1)S(1)}, u32[]{:S(2)}, u32[]{:S(2)}) collective-permute-start(bf16[768,384]{1,0:T(8,128)(2,1)S(1)} %collective-permute-done.8.refs_5_.w1.refs_7_.refs_11_), channel_id=1, source_target_pairs={{0,2},{2,0},{4,6},{6,4},{8,10},{10,8},{12,14},{14,12},{16,18},{18,... | collective-permute-start | bytes 1769480 | tf_op jit(solution)/shard_map/ppermute | solution.py:863
  89.1 17.8 %collective-permute-start.13 = (bf16[448,768]{1,0:T(8,128)(2,1)S(1)}, bf16[448,768]{1,0:T(8,128)(2,1)S(1)}, u32[]{:S(2)}, u32[]{:S(2)}) collective-permute-start(bf16[448,768]{1,0:T(8,128)(2,1)S(1)} %copy-done.58), channel_id=1, source_target_pairs={{0,1},{1,0},{2,3},{3,2},{4,5},{5,4},{6,7},{7,6},{8,9},{9,8},{10,11... | collective-permute-start | bytes 2064392 | tf_op jit(solution)/shard_map/ppermute | solution.py:862
  90.6 15.5 %collective-permute-start.15 = (bf16[768,384]{1,0:T(8,128)(2,1)S(1)}, bf16[768,384]{1,0:T(8,128)(2,1)S(1)}, u32[]{:S(2)}, u32[]{:S(2)}) collective-permute-start(bf16[768,384]{1,0:T(8,128)(2,1)S(1)} %collective-permute-done.10.d0), channel_id=1, source_target_pairs={{0,8},{2,10},{4,12},{6,14},{8,0},{10,2},{12,4},{14,6},{16,24},{18,... | collective-permute-start | bytes 1769480 | tf_op jit(solution)/shard_map/ppermute | solution.py:863
  92.2 16.2 %collective-permute-start.14 = (bf16[768,384]{1,0:T(8,128)(2,1)S(1)}, bf16[768,384]{1,0:T(8,128)(2,1)S(1)}, u32[]{:S(2)}, u32[]{:S(2)}) collective-permute-start(bf16[768,384]{1,0:T(8,128)(2,1)S(1)} %collective-permute-done.2.u0), channel_id=1, source_target_pairs={{0,2},{2,0},{4,6},{6,4},{8,10},{10,8},{12,14},{14,12},{16,18},{18,... | collective-permute-start | bytes 1769480 | tf_op jit(solution)/shard_map/ppermute | solution.py:863
  92.2 16.2 %collective-permute-start.9 = (bf16[768,384]{1,0:T(8,128)(2,1)S(1)}, bf16[768,384]{1,0:T(8,128)(2,1)}, u32[]{:S(2)}, u32[]{:S(2)}) collective-permute-start(bf16[768,384]{1,0:T(8,128)(2,1)S(1)} %collective-permute-done.6.u1), channel_id=1, source_target_pairs={{0,2},{2,0},{4,6},{6,4},{8,10},{10,8},{12,14},{14,12},{16,18},{18,... | collective-permute-start | bytes 1769480 | tf_op jit(solution)/shard_map/ppermute | solution.py:863
  107.0 30.4 %collective-permute-start.20 = (bf16[768,384]{1,0:T(8,128)(2,1)S(1)}, bf16[768,384]{1,0:T(8,128)(2,1)}, u32[]{:S(2)}, u32[]{:S(2)}) collective-permute-start(bf16[768,384]{1,0:T(8,128)(2,1)S(1)} %copy-done.64), channel_id=1, source_target_pairs={{0,1},{1,0},{2,3},{3,2},{4,5},{5,4},{6,7},{7,6},{8,9},{9,8},{10,11... | collective-permute-start | bytes 1769480 | tf_op jit(solution)/shard_map/ppermute | solution.py:862
  136.8 28.2 %collective-permute-start.19 = (bf16[1536,384]{1,0:T(8,128)(2,1)S(1)}, bf16[1536,384]{1,0:T(8,128)(2,1)}, u32[]{:S(2)}, u32[]{:S(2)}) collective-permute-start(bf16[1536,384]{1,0:T(8,128)(2,1)S(1)} %copy-done.55), channel_id=1, source_target_pairs={{0,1},{1,0},{2,3},{3,2},{4,5},{5,4},{6,7},{7,6},{8,9},{9,8},{10,11... | collective-permute-start | bytes 3538952 | tf_op jit(solution)/shard_map/ppermute | solution.py:862
  137.4 24.7 %collective-permute-start.24 = (bf16[768,384]{1,0:T(8,128)(2,1)}, bf16[768,384]{1,0:T(8,128)(2,1)}, u32[]{:S(2)}, u32[]{:S(2)}) collective-permute-start(bf16[768,384]{1,0:T(8,128)(2,1)} %collective-permute-done.20.refs_4_.w0.refs_8_), channel_id=1, source_target_pairs={{0,8},{2,10},{4,12},{6,14},{8,0},{10,2},{12,4},{14,6},{16,24},{18,... | collective-permute-start | bytes 1769480 | tf_op jit(solution)/shard_map/ppermute | solution.py:863
  138.7 35.7 %collective-permute-start.27 = (bf16[768,384]{1,0:T(8,128)(2,1)}, bf16[768,384]{1,0:T(8,128)(2,1)}, u32[]{:S(2)}, u32[]{:S(2)}) collective-permute-start(bf16[768,384]{1,0:T(8,128)(2,1)} %collective-permute-done.20.refs_4_.w0.refs_8_), channel_id=1, source_target_pairs={{0,2},{2,0},{4,6},{6,4},{8,10},{10,8},{12,14},{14,12},{16,18},{18,... | collective-permute-start | bytes 1769480 | tf_op jit(solution)/shard_map/ppermute | solution.py:863
  138.7 34.2 %collective-permute-start.26 = (bf16[1536,1536]{1,0:T(8,128)(2,1)}, bf16[1536,1536]{1,0:T(8,128)(2,1)S(1)}, u32[]{:S(2)}, u32[]{:S(2)}) collective-permute-start(bf16[1536,1536]{1,0:T(8,128)(2,1)} %get-tuple-element.241), channel_id=1, source_target_pairs={{0,2},{2,0},{4,6},{6,4},{8,10},{10,8},{12,14},{14,12},{16,18},{18,... | collective-permute-start | bytes 14155784 | tf_op jit(solution)/shard_map/ppermute | solution.py:863
  162.1 12.2 %collective-permute-start.28 = (bf16[768,384]{1,0:T(8,128)(2,1)}, bf16[768,384]{1,0:T(8,128)(2,1)}, u32[]{:S(2)}, u32[]{:S(2)}) collective-permute-start(bf16[768,384]{1,0:T(8,128)(2,1)} %collective-permute-done.24.refs_5_.w1.refs_9_), channel_id=1, source_target_pairs={{0,2},{2,0},{4,6},{6,4},{8,10},{10,8},{12,14},{14,12},{16,18},{18,... | collective-permute-start | bytes 1769480 | tf_op jit(solution)/shard_map/ppermute | solution.py:863
  163.5 8.6 %collective-permute-start.18 = (bf16[160,768]{1,0:T(8,128)(2,1)}, bf16[160,768]{1,0:T(8,128)(2,1)S(1)}, u32[]{:S(2)}, u32[]{:S(2)}) collective-permute-start(bf16[160,768]{1,0:T(8,128)(2,1)} %get-tuple-element.223), channel_id=1, source_target_pairs={{0,1},{1,0},{2,3},{3,2},{4,5},{5,4},{6,7},{7,6},{8,9},{9,8},{10,11... | collective-permute-start | bytes 737288 | tf_op jit(solution)/shard_map/ppermute | solution.py:862
  167.2 26.6 %collective-permute-start.33 = (bf16[768,1536]{1,0:T(8,128)(2,1)}, bf16[768,1536]{1,0:T(8,128)(2,1)S(1)}, u32[]{:S(2)}, u32[]{:S(2)}) collective-permute-start(bf16[768,1536]{1,0:T(8,128)(2,1)} %get-tuple-element.255), channel_id=1, source_target_pairs={{0,2},{2,0},{4,6},{6,4},{8,10},{10,8},{12,14},{14,12},{16,18},{18,... | collective-permute-start | bytes 7077896 | tf_op jit(solution)/shard_map/ppermute | solution.py:863
  172.1 21.0 %collective-permute-start.23 = (bf16[768,384]{1,0:T(8,128)(2,1)S(1)}, bf16[768,384]{1,0:T(8,128)(2,1)}, u32[]{:S(2)}, u32[]{:S(2)}) collective-permute-start(bf16[768,384]{1,0:T(8,128)(2,1)S(1)} %get-tuple-element.237), channel_id=1, source_target_pairs={{0,8},{2,10},{4,12},{6,14},{8,0},{10,2},{12,4},{14,6},{16,24},{18,... | collective-permute-start | bytes 1769480 | tf_op jit(solution)/shard_map/ppermute | solution.py:863
  172.8 20.9 %collective-permute-start.22 = (bf16[768,384]{1,0:T(8,128)(2,1)S(1)}, bf16[768,384]{1,0:T(8,128)(2,1)}, u32[]{:S(2)}, u32[]{:S(2)}) collective-permute-start(bf16[768,384]{1,0:T(8,128)(2,1)S(1)} %get-tuple-element.236), channel_id=1, source_target_pairs={{0,4},{2,6},{4,0},{6,2},{8,12},{10,14},{12,8},{14,10},{16,20},{18,... | collective-permute-start | bytes 1769480 | tf_op jit(solution)/shard_map/ppermute | solution.py:863
  174.3 27.8 %collective-permute-start.29 = (bf16[1536,384]{1,0:T(8,128)(2,1)}, bf16[1536,384]{1,0:T(8,128)(2,1)}, u32[]{:S(2)}, u32[]{:S(2)}) collective-permute-start(bf16[1536,384]{1,0:T(8,128)(2,1)} %collective-permute-done.19.u0.d0), channel_id=1, source_target_pairs={{0,2},{2,0},{4,6},{6,4},{8,10},{10,8},{12,14},{14,12},{16,18},{18,... | collective-permute-start | bytes 3538952 | tf_op jit(solution)/shard_map/ppermute | solution.py:863
  193.1 10.5 %collective-permute-start.31 = (bf16[768,384]{1,0:T(8,128)(2,1)}, bf16[768,384]{1,0:T(8,128)(2,1)S(1)}, u32[]{:S(2)}, u32[]{:S(2)}) collective-permute-start(bf16[768,384]{1,0:T(8,128)(2,1)} %collective-permute-done.23.d1), channel_id=1, source_target_pairs={{0,2},{2,0},{4,6},{6,4},{8,10},{10,8},{12,14},{14,12},{16,18},{18,... | collective-permute-start | bytes 1769480 | tf_op jit(solution)/shard_map/ppermute | solution.py:863
  193.7 10.0 %collective-permute-start.30 = (bf16[768,384]{1,0:T(8,128)(2,1)}, bf16[768,384]{1,0:T(8,128)(2,1)S(1)}, u32[]{:S(2)}, u32[]{:S(2)}) collective-permute-start(bf16[768,384]{1,0:T(8,128)(2,1)} %collective-permute-done.22.u1), channel_id=1, source_target_pairs={{0,2},{2,0},{4,6},{6,4},{8,10},{10,8},{12,14},{14,12},{16,18},{18,... | collective-permute-start | bytes 1769480 | tf_op jit(solution)/shard_map/ppermute | solution.py:863
  200.2 44.5 %collective-permute-start.36 = (bf16[384,1536]{1,0:T(8,128)(2,1)}, bf16[384,1536]{1,0:T(8,128)(2,1)S(1)}, u32[]{:S(2)}, u32[]{:S(2)}) collective-permute-start(bf16[384,1536]{1,0:T(8,128)(2,1)} %get-tuple-element.261), channel_id=1, source_target_pairs={{0,4},{2,6},{4,0},{6,2},{8,12},{10,14},{12,8},{14,10},{16,20},{18,... | collective-permute-start | bytes 3538952 | tf_op jit(solution)/shard_map/ppermute | solution.py:863
  200.8 43.9 %collective-permute-start.35 = (bf16[384,1536]{1,0:T(8,128)(2,1)}, bf16[384,1536]{1,0:T(8,128)(2,1)S(1)}, u32[]{:S(2)}, u32[]{:S(2)}) collective-permute-start(bf16[384,1536]{1,0:T(8,128)(2,1)} %get-tuple-element.259), channel_id=1, source_target_pairs={{0,8},{2,10},{4,12},{6,14},{8,0},{10,2},{12,4},{14,6},{16,24},{18,... | collective-permute-start | bytes 3538952 | tf_op jit(solution)/shard_map/ppermute | solution.py:863
  202.1 42.7 %collective-permute-start.34 = (bf16[384,1536]{1,0:T(8,128)(2,1)}, bf16[384,1536]{1,0:T(8,128)(2,1)S(1)}, u32[]{:S(2)}, u32[]{:S(2)}) collective-permute-start(bf16[384,1536]{1,0:T(8,128)(2,1)} %get-tuple-element.257), channel_id=1, source_target_pairs={{0,1},{1,0},{2,3},{3,2},{4,5},{5,4},{6,7},{7,6},{8,9},{9,8},{10,11... | collective-permute-start | bytes 3538952 | tf_op jit(solution)/shard_map/ppermute | solution.py:862
  242.9 37.8 %collective-permute-start.39 = (bf16[1536,1536]{1,0:T(8,128)(2,1)}, bf16[1536,1536]{1,0:T(8,128)(2,1)S(1)}, u32[]{:S(2)}, u32[]{:S(2)}) collective-permute-start(bf16[1536,1536]{1,0:T(8,128)(2,1)} %get-tuple-element.266), channel_id=1, source_target_pairs={{0,2},{2,0},{4,6},{6,4},{8,10},{10,8},{12,14},{14,12},{16,18},{18,... | collective-permute-start | bytes 14155784 | tf_op jit(solution)/shard_map/ppermute | solution.py:863
  244.2 30.6 %collective-permute-start.32 = (bf16[288,768]{1,0:T(8,128)(2,1)}, bf16[288,768]{1,0:T(8,128)(2,1)}, u32[]{:S(2)}, u32[]{:S(2)}) collective-permute-start(bf16[288,768]{1,0:T(8,128)(2,1)} %get-tuple-element.252), channel_id=1, source_target_pairs={{0,1},{1,0},{2,3},{3,2},{4,5},{5,4},{6,7},{7,6},{8,9},{9,8},{10,11... | collective-permute-start | bytes 1327112 | tf_op jit(solution)/shard_map/ppermute | solution.py:862
  251.4 23.4 %collective-permute-start.38 = (bf16[192,1536]{1,0:T(8,128)(2,1)}, bf16[192,1536]{1,0:T(8,128)(2,1)S(1)}, u32[]{:S(2)}, u32[]{:S(2)}) collective-permute-start(bf16[192,1536]{1,0:T(8,128)(2,1)} %get-tuple-element.265), channel_id=1, source_target_pairs={{0,1},{1,0},{2,3},{3,2},{4,5},{5,4},{6,7},{7,6},{8,9},{9,8},{10,11... | collective-permute-start | bytes 1769480 | tf_op jit(solution)/shard_map/ppermute | solution.py:862
  252.9 27.7 %collective-permute-start.37 = (bf16[384,1536]{1,0:T(8,128)(2,1)}, bf16[384,1536]{1,0:T(8,128)(2,1)S(1)}, u32[]{:S(2)}, u32[]{:S(2)}) collective-permute-start(bf16[384,1536]{1,0:T(8,128)(2,1)} %get-tuple-element.263), channel_id=1, source_target_pairs={{0,4},{2,6},{4,0},{6,2},{8,12},{10,14},{12,8},{14,10},{16,20},{18,... | collective-permute-start | bytes 3538952 | tf_op jit(solution)/shard_map/ppermute | solution.py:863
  274.7 44.4 %collective-permute-start.42 = (bf16[384,1536]{1,0:T(8,128)(2,1)}, bf16[384,1536]{1,0:T(8,128)(2,1)}, u32[]{:S(2)}, u32[]{:S(2)}) collective-permute-start(bf16[384,1536]{1,0:T(8,128)(2,1)} %get-tuple-element.281), channel_id=1, source_target_pairs={{0,2},{2,0},{4,6},{6,4},{8,10},{10,8},{12,14},{14,12},{16,18},{18,... | collective-permute-start | bytes 3538952 | tf_op jit(solution)/shard_map/ppermute | solution.py:863
  288.4 25.1 %collective-permute-start.49 = (bf16[96,1536]{1,0:T(8,128)(2,1)}, bf16[96,1536]{1,0:T(8,128)(2,1)S(1)}, u32[]{:S(2)}, u32[]{:S(2)}) collective-permute-start(bf16[96,1536]{1,0:T(8,128)(2,1)} %get-tuple-element.299), channel_id=1, source_target_pairs={{0,16},{2,18},{4,20},{6,22},{8,24},{10,26},{12,28},{14,30},{16,0},... | collective-permute-start | bytes 884744 | tf_op jit(solution)/shard_map/ppermute | solution.py:863
  291.0 26.5 %collective-permute-start.48 = (bf16[384,1536]{1,0:T(8,128)(2,1)}, bf16[384,1536]{1,0:T(8,128)(2,1)S(1)}, u32[]{:S(2)}, u32[]{:S(2)}) collective-permute-start(bf16[384,1536]{1,0:T(8,128)(2,1)} %get-tuple-element.297), channel_id=1, source_target_pairs={{0,4},{2,6},{4,0},{6,2},{8,12},{10,14},{12,8},{14,10},{16,20},{18,... | collective-permute-start | bytes 3538952 | tf_op jit(solution)/shard_map/ppermute | solution.py:863
  292.5 21.1 %collective-permute-start.44 = (bf16[192,1536]{1,0:T(8,128)(2,1)}, bf16[192,1536]{1,0:T(8,128)(2,1)S(1)}, u32[]{:S(2)}, u32[]{:S(2)}) collective-permute-start(bf16[192,1536]{1,0:T(8,128)(2,1)} %get-tuple-element.286), channel_id=1, source_target_pairs={{0,8},{2,10},{4,12},{6,14},{8,0},{10,2},{12,4},{14,6},{16,24},{18,... | collective-permute-start | bytes 1769480 | tf_op jit(solution)/shard_map/ppermute | solution.py:863
  293.2 25.9 %collective-permute-start.43 = (bf16[384,1536]{1,0:T(8,128)(2,1)}, bf16[384,1536]{1,0:T(8,128)(2,1)S(1)}, u32[]{:S(2)}, u32[]{:S(2)}) collective-permute-start(bf16[384,1536]{1,0:T(8,128)(2,1)} %get-tuple-element.284), channel_id=1, source_target_pairs={{0,1},{1,0},{2,3},{3,2},{4,5},{5,4},{6,7},{7,6},{8,9},{9,8},{10,11... | collective-permute-start | bytes 3538952 | tf_op jit(solution)/shard_map/ppermute | solution.py:862
  313.5 37.6 %collective-permute-start.41 = (f32[2,768]{1,0:T(2,128)}, f32[2,768]{1,0:T(2,128)S(1)}, u32[]{:S(2)}, u32[]{:S(2)}) collective-permute-start(f32[2,768]{1,0:T(2,128)} %get-tuple-element.279), channel_id=1, source_target_pairs={{0,2},{2,0},{4,6},{6,4},{8,10},{10,8},{12,14},{14,12},{16,18},{18,... | collective-permute-start | bytes 18440 | tf_op jit(solution)/shard_map/ppermute | solution.py:863
  313.6 37.6 %collective-permute-start.52 = (bf16[384,1536]{1,0:T(8,128)(2,1)}, bf16[384,1536]{1,0:T(8,128)(2,1)S(1)}, u32[]{:S(2)}, u32[]{:S(2)}) collective-permute-start(bf16[384,1536]{1,0:T(8,128)(2,1)} %get-tuple-element.319), channel_id=1, source_target_pairs={{0,2},{2,0},{4,6},{6,4},{8,10},{10,8},{12,14},{14,12},{16,18},{18,... | collective-permute-start | bytes 3538952 | tf_op jit(solution)/shard_map/ppermute | solution.py:863
  324.3 26.8 %collective-permute-start.47 = (bf16[96,1536]{1,0:T(8,128)(2,1)}, bf16[96,1536]{1,0:T(8,128)(2,1)S(1)}, u32[]{:S(2)}, u32[]{:S(2)}) collective-permute-start(bf16[96,1536]{1,0:T(8,128)(2,1)} %get-tuple-element.292), channel_id=1, source_target_pairs={{0,16},{2,18},{4,20},{6,22},{8,24},{10,26},{12,28},{14,30},{16,0},... | collective-permute-start | bytes 884744 | tf_op jit(solution)/shard_map/ppermute | solution.py:863
  324.7 26.4 %collective-permute-start.46 = (bf16[192,1536]{1,0:T(8,128)(2,1)}, bf16[192,1536]{1,0:T(8,128)(2,1)S(1)}, u32[]{:S(2)}, u32[]{:S(2)}) collective-permute-start(bf16[192,1536]{1,0:T(8,128)(2,1)} %get-tuple-element.290), channel_id=1, source_target_pairs={{0,4},{2,6},{4,0},{6,2},{8,12},{10,14},{12,8},{14,10},{16,20},{18,... | collective-permute-start | bytes 1769480 | tf_op jit(solution)/shard_map/ppermute | solution.py:863
  325.3 25.8 %collective-permute-start.45 = (bf16[384,1536]{1,0:T(8,128)(2,1)}, bf16[384,1536]{1,0:T(8,128)(2,1)S(1)}, u32[]{:S(2)}, u32[]{:S(2)}) collective-permute-start(bf16[384,1536]{1,0:T(8,128)(2,1)} %get-tuple-element.288), channel_id=1, source_target_pairs={{0,1},{1,0},{2,3},{3,2},{4,5},{5,4},{6,7},{7,6},{8,9},{9,8},{10,11... | collective-permute-start | bytes 3538952 | tf_op jit(solution)/shard_map/ppermute | solution.py:862
  356.9 27.6 %collective-permute-start.55 = (bf16[96,1536]{1,0:T(8,128)(2,1)}, bf16[96,1536]{1,0:T(8,128)(2,1)S(1)}, u32[]{:S(2)}, u32[]{:S(2)}) collective-permute-start(bf16[96,1536]{1,0:T(8,128)(2,1)} %get-tuple-element.325), channel_id=1, source_target_pairs={{0,8},{2,10},{4,12},{6,14},{8,0},{10,2},{12,4},{14,6},{16,24},{18,... | collective-permute-start | bytes 884744 | tf_op jit(solution)/shard_map/ppermute | solution.py:863
  358.2 26.9 %collective-permute-start.54 = (bf16[240,1536]{1,0:T(8,128)(2,1)}, bf16[240,1536]{1,0:T(8,128)(2,1)S(1)}, u32[]{:S(2)}, u32[]{:S(2)}) collective-permute-start(bf16[240,1536]{1,0:T(8,128)(2,1)} %get-tuple-element.323), channel_id=1, source_target_pairs={{0,1},{1,0},{2,3},{3,2},{4,5},{5,4},{6,7},{7,6},{8,9},{9,8},{10,11... | collective-permute-start | bytes 2211848 | tf_op jit(solution)/shard_map/ppermute | solution.py:862
  359.7 25.0 %collective-permute-start.53 = (bf16[192,1536]{1,0:T(8,128)(2,1)}, bf16[192,1536]{1,0:T(8,128)(2,1)S(1)}, u32[]{:S(2)}, u32[]{:S(2)}) collective-permute-start(bf16[192,1536]{1,0:T(8,128)(2,1)} %get-tuple-element.321), channel_id=1, source_target_pairs={{0,4},{2,6},{4,0},{6,2},{8,12},{10,14},{12,8},{14,10},{16,20},{18,... | collective-permute-start | bytes 1769480 | tf_op jit(solution)/shard_map/ppermute | solution.py:863
  383.9 6.1 %collective-permute-start.51 = (bf16[384,768]{1,0:T(8,128)(2,1)}, bf16[384,768]{1,0:T(8,128)(2,1)S(1)}, u32[]{:S(2)}, u32[]{:S(2)}) collective-permute-start(bf16[384,768]{1,0:T(8,128)(2,1)} %get-tuple-element.317), channel_id=1, source_target_pairs={{0,2},{2,0},{4,6},{6,4},{8,10},{10,8},{12,14},{14,12},{16,18},{18,... | collective-permute-start | bytes 1769480 | tf_op jit(solution)/shard_map/ppermute | solution.py:863
  384.6 9.5 %collective-permute-start.57 = (bf16[384,768]{1,0:T(8,128)(2,1)}, bf16[384,768]{1,0:T(8,128)(2,1)S(1)}, u32[]{:S(2)}, u32[]{:S(2)}) collective-permute-start(bf16[384,768]{1,0:T(8,128)(2,1)} %get-tuple-element.332), channel_id=1, source_target_pairs={{0,2},{2,0},{4,6},{6,4},{8,10},{10,8},{12,14},{14,12},{16,18},{18,... | collective-permute-start | bytes 1769480 | tf_op jit(solution)/shard_map/ppermute | solution.py:863
  389.2 19.0 %collective-permute-start.60 = (bf16[192,1536]{1,0:T(8,128)(2,1)}, bf16[192,1536]{1,0:T(8,128)(2,1)S(1)}, u32[]{:S(2)}, u32[]{:S(2)}) collective-permute-start(bf16[192,1536]{1,0:T(8,128)(2,1)} %get-tuple-element.336), channel_id=1, source_target_pairs={{0,8},{2,10},{4,12},{6,14},{8,0},{10,2},{12,4},{14,6},{16,24},{18,... | collective-permute-start | bytes 1769480 | tf_op jit(solution)/shard_map/ppermute | solution.py:863
  394.1 17.3 %collective-permute-start.59 = (bf16[384,768]{1,0:T(8,128)(2,1)}, bf16[384,768]{1,0:T(8,128)(2,1)S(1)}, u32[]{:S(2)}, u32[]{:S(2)}) collective-permute-start(bf16[384,768]{1,0:T(8,128)(2,1)} %get-tuple-element.335), channel_id=1, source_target_pairs={{0,4},{2,6},{4,0},{6,2},{8,12},{10,14},{12,8},{14,10},{16,20},{18,... | collective-permute-start | bytes 1769480 | tf_op jit(solution)/shard_map/ppermute | solution.py:863
  394.8 16.7 %collective-permute-start.58 = (bf16[384,768]{1,0:T(8,128)(2,1)}, bf16[384,768]{1,0:T(8,128)(2,1)S(1)}, u32[]{:S(2)}, u32[]{:S(2)}) collective-permute-start(bf16[384,768]{1,0:T(8,128)(2,1)} %get-tuple-element.333), channel_id=1, source_target_pairs={{0,1},{1,0},{2,3},{3,2},{4,5},{5,4},{6,7},{7,6},{8,9},{9,8},{10,11... | collective-permute-start | bytes 1769480 | tf_op jit(solution)/shard_map/ppermute | solution.py:862
  396.3 15.1 %collective-permute-start.61 = (bf16[48,1536]{1,0:T(8,128)(2,1)S(1)}, bf16[48,1536]{1,0:T(8,128)(2,1)S(1)}, u32[]{:S(2)}, u32[]{:S(2)}) collective-permute-start(bf16[48,1536]{1,0:T(8,128)(2,1)S(1)} %copy-done.83), channel_id=1, source_target_pairs={{0,16},{2,18},{4,20},{6,22},{8,24},{10,26},{12,28},{14,30},{16,0},... | collective-permute-start | bytes 442376 | tf_op jit(solution)/shard_map/ppermute | solution.py:863
  411.5 17.7 %collective-permute-start.65 = (bf16[96,1536]{1,0:T(8,128)(2,1)}, bf16[96,1536]{1,0:T(8,128)(2,1)S(1)}, u32[]{:S(2)}, u32[]{:S(2)}) collective-permute-start(bf16[96,1536]{1,0:T(8,128)(2,1)} %add_up.23), channel_id=1, source_target_pairs={{0,16},{2,18},{4,20},{6,22},{8,24},{10,26},{12,28},{14,30},{16,0},... | collective-permute-start | bytes 884744 | tf_op jit(solution)/shard_map/ppermute | solution.py:863
  415.1 10.4 %collective-permute-start.64 = (bf16[192,768]{1,0:T(8,128)(2,1)}, bf16[192,768]{1,0:T(8,128)(2,1)S(1)}, u32[]{:S(2)}, u32[]{:S(2)}) collective-permute-start(bf16[192,768]{1,0:T(8,128)(2,1)} %get-tuple-element.344), channel_id=1, source_target_pairs={{0,1},{1,0},{2,3},{3,2},{4,5},{5,4},{6,7},{7,6},{8,9},{9,8},{10,11... | collective-permute-start | bytes 884744 | tf_op jit(solution)/shard_map/ppermute | solution.py:862
  415.6 9.9 %collective-permute-start.63 = (bf16[192,768]{1,0:T(8,128)(2,1)}, bf16[192,768]{1,0:T(8,128)(2,1)S(1)}, u32[]{:S(2)}, u32[]{:S(2)}) collective-permute-start(bf16[192,768]{1,0:T(8,128)(2,1)} %get-tuple-element.342), channel_id=1, source_target_pairs={{0,4},{2,6},{4,0},{6,2},{8,12},{10,14},{12,8},{14,10},{16,20},{18,... | collective-permute-start | bytes 884744 | tf_op jit(solution)/shard_map/ppermute | solution.py:863
  417.1 7.6 %collective-permute-start.68 = (f32[10,768]{1,0:T(8,128)S(1)}, f32[10,768]{1,0:T(8,128)S(1)}, u32[]{:S(2)}, u32[]{:S(2)}) collective-permute-start(f32[10,768]{1,0:T(8,128)S(1)} %concatenate.19), channel_id=1, source_target_pairs={{0,1},{1,0},{2,3},{3,2},{4,5},{5,4},{6,7},{7,6},{8,9},{9,8},{10,11... | collective-permute-start | bytes 92168 | tf_op jit(solution)/shard_map/ppermute | solution.py:862
  424.7 6.5 %collective-permute-start.69 = (f32[10,768]{1,0:T(8,128)S(1)}, f32[10,768]{1,0:T(8,128)S(1)}, u32[]{:S(2)}, u32[]{:S(2)}) collective-permute-start(f32[10,768]{1,0:T(8,128)S(1)} %add.147), channel_id=1, source_target_pairs={{0,4},{2,6},{4,0},{6,2},{8,12},{10,14},{12,8},{14,10},{16,20},{18,... | collective-permute-start | bytes 92168 | tf_op jit(solution)/shard_map/ppermute | solution.py:863
  429.2 8.7 %collective-permute-start.66 = (bf16[192,768]{1,0:T(8,128)(2,1)}, bf16[192,768]{1,0:T(8,128)(2,1)S(1)}, u32[]{:S(2)}, u32[]{:S(2)}) collective-permute-start(bf16[192,768]{1,0:T(8,128)(2,1)} %add_up.22), channel_id=1, source_target_pairs={{0,8},{2,10},{4,12},{6,14},{8,0},{10,2},{12,4},{14,6},{16,24},{18,... | collective-permute-start | bytes 884744 | tf_op jit(solution)/shard_map/ppermute | solution.py:863
  431.3 6.5 %collective-permute-start.70 = (f32[10,768]{1,0:T(8,128)S(1)}, f32[10,768]{1,0:T(8,128)S(1)}, u32[]{:S(2)}, u32[]{:S(2)}) collective-permute-start(f32[10,768]{1,0:T(8,128)S(1)} %add.148), channel_id=1, source_target_pairs={{0,8},{2,10},{4,12},{6,14},{8,0},{10,2},{12,4},{14,6},{16,24},{18,... | collective-permute-start | bytes 92168 | tf_op jit(solution)/shard_map/ppermute | solution.py:863
  435.5 15.5 %collective-permute-start.62 = (bf16[448,768]{1,0:T(8,128)(2,1)}, bf16[448,768]{1,0:T(8,128)(2,1)S(1)}, u32[]{:S(2)}, u32[]{:S(2)}) collective-permute-start(bf16[448,768]{1,0:T(8,128)(2,1)} %get-tuple-element.338), channel_id=1, source_target_pairs={{0,1},{1,0},{2,3},{3,2},{4,5},{5,4},{6,7},{7,6},{8,9},{9,8},{10,11... | collective-permute-start | bytes 2064392 | tf_op jit(solution)/shard_map/ppermute | solution.py:862
  437.8 10.8 %collective-permute-start.71 = (f32[10,768]{1,0:T(8,128)S(1)}, f32[10,768]{1,0:T(8,128)S(1)}, u32[]{:S(2)}, u32[]{:S(2)}) collective-permute-start(f32[10,768]{1,0:T(8,128)S(1)} %add.149), channel_id=1, source_target_pairs={{0,16},{2,18},{4,20},{6,22},{8,24},{10,26},{12,28},{14,30},{16,0},... | collective-permute-start | bytes 92168 | tf_op jit(solution)/shard_map/ppermute | solution.py:863
  441.4 11.0 %collective-permute-start.67 = (bf16[96,768]{1,0:T(8,128)(2,1)}, bf16[96,768]{1,0:T(8,128)(2,1)S(1)}, u32[]{:S(2)}, u32[]{:S(2)}) collective-permute-start(bf16[96,768]{1,0:T(8,128)(2,1)} %add_up.24), channel_id=1, source_target_pairs={{0,16},{2,18},{4,20},{6,22},{8,24},{10,26},{12,28},{14,30},{16,0},... | collective-permute-start | bytes 442376 | tf_op jit(solution)/shard_map/ppermute | solution.py:863
  (92 other events, 633.5 us)

commit v5 on v4

--- a/solution.py
+++ b/solution.py
@@ -100,6 +100,7 @@
     return pltpu.CompilerParams(vmem_limit_bytes=limit)
 
 
+ADD_STEPS = 2
 WEIGHTS = (100000000000, 100000000000, 100000000000, 100000000000, 100000000000, 100000000000, 100000000000, 100000000000, 100000000000, 100000000000)
 WORK = iter(())
 ADD_WORK = 1
@@ -757,7 +758,7 @@
                     arrays.append(array)
                     specs.append(
                         pl.BlockSpec(
-                            (rows, wide), lambda *_, i=start // rows, j=col: (i, j), pipeline_mode=pl.Buffered(1)
+                            (rows, wide // ADD_STEPS), lambda c, i=start // rows, j=col * ADD_STEPS: (i, j + c)
                         )
                     )
                 laid.append((at, rows, where))
@@ -766,9 +767,9 @@
             shapes.append((at, wide))
         return pl.pallas_call(
             functools.partial(add_kernel, plan, len(arrays)),
-            grid=(1,),
+            grid=(ADD_STEPS,),
             in_specs=specs,
-            out_specs=[pl.BlockSpec(s, lambda *_: (0, 0), pipeline_mode=pl.Buffered(1)) for s in shapes],
+            out_specs=[pl.BlockSpec((s[0], s[1] // ADD_STEPS), lambda c: (0, c)) for s in shapes],
             out_shape=[jax.ShapeDtypeStruct(s, kind) for s in shapes],
             compiler_params=params(),
             cost_estimate=pl.CostEstimate(flops=ADD_WORK, bytes_accessed=1, transcendentals=0),
@@ -844,6 +845,27 @@
     return dict(zip(named, add_up(outputs, F32)))
 
 
+def send_last(sums, across, bits, *deps):
+    outputs = []
+    for k in (1, 2, 3):
+        pieces = []
+        for s in sums:
+            quarter = s.rows // 4
+            pieces.append((quarter, [(a, start + k * quarter, c) for a, start, c in s.own]))
+        outputs.append((sums[0].wide, pieces))
+    made = add_up(outputs, BF)
+    arrived = []
+    for k, buffer in zip((1, 2, 3), made):
+        got = across(after(buffer, *deps), (k & 1) << (bits - 1) | (k >> 1) << (bits - 2))
+        arrived.append(got)
+        for i, s in enumerate(sums):
+            s.own.append((got, i * (s.rows // 4), 0))
+    for s in sums:
+        s.rows //= 4
+        s.order = []
+    return arrived
+
+
 def on_device(
     lang_input, visn_input, word_seg, region_seg, in_proj, out_proj, up_proj, down_proj,
     ln_gain, ln_bias, lang_cotan, visn_cotan,
@@ -862,6 +884,9 @@
             return lax.ppermute(x, "tensor", SWAP)
         return lax.ppermute(x, "dp", [(i, i ^ (1 << stage)) for i in range(n_dp)])
 
+    def across(x, value):
+        return lax.ppermute(x, "dp", [(i, i ^ value) for i in range(n_dp)])
+
     Y, C, X, Z = -1, 0, 1, 2
     rest = list(range(2, bits))
     y_first = [Y, X] + rest
@@ -888,10 +913,15 @@
         second_cut_kernel, 20, [attn_pack] * 4 + [(2 * width, half)] + [rows_shape] * 2, after(slot, x_own),
         in_proj, out_proj, up_proj, down_proj, lang_cotan, visn_cotan,
     )
-    seg = jnp.concatenate([own_seg(word_seg), own_seg(region_seg)])[:, None]
     lane = jnp.arange(LANES)[None, :]
-    qf = jnp.where(lane == seg, -FAR, 0.0).astype(BF)
-    kf = jnp.where((lane < 4) & (lane != seg), 1.0, 0.0).astype(BF)
+
+    def features(seg):
+        seg = seg[:, None]
+        query = jnp.where(lane == seg, -FAR, 0.0).astype(BF)
+        return query, jnp.where((lane < 4) & (lane != seg), 1.0, 0.0).astype(BF)
+
+    segs = [own_seg(word_seg), own_seg(region_seg)]
+    masks = [features(x) for x in (*segs, jnp.concatenate(segs))]
     chunk = width // n_dp
     place = jnp.arange(width)
 
@@ -901,7 +931,7 @@
 
     perm = permutation([C, X, Z] + rest[1:])
     perm_z = permutation([C, Z, X] + rest[1:])
-    qf, kf, perm, perm_z = lax.optimization_barrier((qf, kf, perm, perm_z))
+    masks, perm, perm_z = lax.optimization_barrier((masks, perm, perm_z))
     lw, lv = 2 * spans[0], 2 * spans[1]
     streams = ((0, lw), (lw, lw + lv))
 
@@ -913,7 +943,7 @@
 
     cross_dirs = ((0, lw, lw, lw + lv), (lw, lw + lv, 0, lw))
     f1 = attention_forward(
-        (x_own, x_recv), qf, kf, in_proj, cross_pack, 0, SX, after(slot, perm), cross_dirs,
+        (x_own, x_recv), *masks[2], in_proj, cross_pack, 0, SX, after(slot, perm), cross_dirs,
         (out_proj, ln_gain, ln_bias, spans),
     )
     cross, norms = f1[:6], (f1[6:9], f1[9:12])
@@ -922,7 +952,7 @@
     def self_forward(j, pack, slot_tied):
         lo, hi = streams[j]
         return attention_forward(
-            norms[j][2], qf[lo:hi], kf[lo:hi], in_proj, pack, 1 + j, SZ, slot_tied, ((0, hi - lo, 0, hi - lo),)
+            norms[j][2], *masks[j], in_proj, pack, 1 + j, SZ, slot_tied, ((0, hi - lo, 0, hi - lo),)
         )
 
     def feed(j, ctx, wo_pack, up_pack, down_pack, which, slot_tied):
@@ -1044,7 +1074,7 @@
     tied = core_xo
     grad_recv = None
     beside = first
-    for stage in range(1, bits):
+    for stage in range(1, bits - 1):
         got = send_all(cxs, exchange, *tied)
         left = [s for s in others if s.order]
         if left and stage > 1:
@@ -1053,8 +1083,10 @@
         if grad_recv is None and stage > 1:
             grad_recv = exchange(after(xb[1], *tied), Y)
         tied = got + beside
-    got = send_all(cxs, exchange, *tied)
-    stats = stats + exchange(after(stats, *tied), bits - 1)
+    got = send_last(cxs, across, bits, *tied)
+    stats = stats + exchange(after(stats, *tied), bits - 2 if bits > 3 else Y)
+    far = after(stats, *tied)
+    stats = stats + across(far, 1 << (bits - 1))
     while any(s.order for s in others):
         send_all([s for s in others if s.order], exchange, *tied)
     sums = finish({"ful": ful, "fdl": fdl, "sl": sl}, xb[0])

time: 466 us -> 461 us (0.989)
    ppermute x53 -> x50, starting transfers between devices: 38.8 us -> 32.4 us  [exchange(): return lax.ppermute(x, 'dp', [(i, i ^ 1 << stage) for i in range(n_dp)])]
    ppermute x0 -> x4, waiting for transfers between devices: none -> 5.91 us  [across(): return lax.ppermute(x, 'dp', [(i, i ^ value) for i in range(n_dp)])]
    ppermute x0 -> x4, starting transfers between devices: none -> 4.92 us  [across(): return lax.ppermute(x, 'dp', [(i, i ^ value) for i in range(n_dp)])]
    ppermute x19, waiting for transfers between devices: 20.5 us -> 15.7 us  [exchange(): return lax.ppermute(x, 'tensor', SWAP)]
    ppermute x53 -> x50, waiting for transfers between devices: 42.5 us -> 37.9 us  [exchange(): return lax.ppermute(x, 'dp', [(i, i ^ 1 << stage) for i in range(n_dp)])]
    pallas_call x14 -> x13, Pallas kernels: 45 us -> 40.5 us  [add_up(): pl.pallas_call(functools.partial(add_kernel, plan, len(arrays)), grid=(AD...]
    unnamed x174 -> x160, local copies, waits for them, and re-layouts: 19.4 us -> 19.1 us
  transfers between devices with their start and end apart: 72 -> 73, of which waited for: 15 -> 17; matrix products, arithmetic and copies ran while one was open for 4% -> 5% of each run, Pallas kernels for 61% -> 61%
where the time goes in v5:
time: 461 us; the launch traced here: 453 us
  Pallas kernels  285 us (62%)
  starting transfers between devices  63 us (14%)
  waiting for transfers between devices  59.6 us (13%)
  local copies, waits for them, and re-layouts  24 us (5%)
  other arithmetic  20 us (4%)
    pallas_call x5, Pallas kernels, attention_backward(): pl.pallas_call(functools.partial(bwd_kernel, dirs, each, which, spans, ha...  110 us
    pallas_call x2, Pallas kernels, feed_forward(): pl.pallas_call(functools.partial(ffn_kernel, blocks, which, stream, spans...  64.6 us
    pallas_call x3, Pallas kernels, attention_forward(): pl.pallas_call(functools.partial(fwd_kernel, dirs, each, which, spans), g...  60 us
    pallas_call x13, Pallas kernels, add_up(): pl.pallas_call(functools.partial(add_kernel, plan, len(arrays)), grid=(AD...  40.5 us
    ppermute x50, waiting for transfers between devices, exchange(): return lax.ppermute(x, 'dp', [(i, i ^ 1 << stage) for i in range(n_dp)])  37.9 us
    ppermute x50, starting transfers between devices, exchange(): return lax.ppermute(x, 'dp', [(i, i ^ 1 << stage) for i in range(n_dp)])  32.4 us
    ppermute x19, starting transfers between devices, exchange(): return lax.ppermute(x, 'tensor', SWAP)  25.6 us
    unnamed x160, local copies, waits for them, and re-layouts  19.1 us
  transfers between devices with their start and end apart: 73, of which 17 were waited for; matrix products, arithmetic and copies ran while one was open for 5% of the time, Pallas kernels for 61%

profile of v5, /device:TPU:0, one launch (start us, length us, event | category | flops | bytes accessed | tf_op | source)
XLA Modules:
  0.0 453.1 jit_solution(17302486005617211272)
XLA Ops:
  1.3 3.6 cut.2
  4.9 3.0 collective-permute-start
  8.0 5.7 %cut.3 = (bf16[768,384]{1,0:T(8,128)(2,1)}, bf16[768,384]{1,0:T(8,128)(2,1)}, bf16[768,384]{1,0:T(8,128)(2,1)}, bf16[768,384]{1,0:T(8,128)(2,1)}, bf16[1536,384]...) custom-call(s32[3]{0:T(128)} %pad_add_fusion.1.place.slot_ref, bf16[3,3,768,384]{3,2,1,0:T(8,128)(2,1)} %refs_5_.5, ...), custom_call_target="tpu_custom_call" | custom-call | flops 1 | bytes 1 | tf_op jit(solution)/shard_map/cut/pallas_call | solution.py:723
  14.9 6.6 %collective-permute-done.refs_5_.refs_10_.refs_7_.refs_11_ = bf16[768,384]{1,0:T(8,128)(2,1)S(1)} collective-permute-done((bf16[768,384]{1,0:T(8,128)(2,1)}, bf16[768,384]{1,0:T(8,128)(2,1)S(1)}, u32[]{:S(2)}, u32[]{:S(2)}) %collective-permute-start) | collective-permute-done | bytes 589856 | tf_op jit(solution)/shard_map/ppermute | solution.py:884
  21.5 1.7 collective-permute-start.3
  24.3 1.6 collective-permute-start.1
  26.7 9.3 %collective-permute-done.3.refs_6_.refs_11_.refs_8_.refs_12_ = bf16[768,384]{1,0:T(8,128)(2,1)S(1)} collective-permute-done((bf16[768,384]{1,0:T(8,128)(2,1)S(1)}, bf16[768,384]{1,0:T(8,128)(2,1)S(1)}, u32[]{:S(2)}, u32[]{:S(2)}) %collective-permute-start.3) | collective-permute-done | bytes 589856 | tf_op jit(solution)/shard_map/ppermute | solution.py:885
  38.7 1.8 collective-permute-done.1.refs_1_.refs_5_
  40.4 1.5 collective-permute-start.2
  44.1 28.4 %attention_forward.3 = (bf16[896,768]{1,0:T(8,128)(2,1)}, bf16[896,768]{1,0:T(8,128)(2,1)}, bf16[896,768]{1,0:T(8,128)(2,1)}, bf16[896,768]{1,0:T(8,128)(2,1)}, ...) custom-call(s32[3]{0:T(128)} %pad_add_fusion.1.place.slot_ref, ...), custom_call_target="tpu_custom_call" | custom-call | flops 99999997952 | bytes 1 | tf_op jit(solution)/shard_map/attention_forward/pallas_call | solution.py:218
  72.5 1.6 collective-permute-start.8
  74.1 1.5 collective-permute-start.10
  76.2 9.8 %collective-permute-done.8.refs_5_.w1.refs_7_.refs_11_ = bf16[768,384]{1,0:T(8,128)(2,1)S(1)} collective-permute-done((bf16[768,384]{1,0:T(8,128)(2,1)S(1)}, bf16[768,384]{1,0:T(8,128)(2,1)S(1)}, u32[]{:S(2)}, u32[]{:S(2)}) %collective-permute-start.8) | collective-permute-done | bytes 589856 | tf_op jit(solution)/shard_map/ppermute | solution.py:885
  87.3 1.5 collective-permute-start.13
  90.6 12.5 %attention_forward.4 = (bf16[320,768]{1,0:T(8,128)(2,1)}, bf16[320,768]{1,0:T(8,128)(2,1)}, bf16[320,768]{1,0:T(8,128)(2,1)}, bf16[320,768]{1,0:T(8,128)(2,1)}, bf16[12,320,320]{2,1,0:T(8,128)(2,1)}) custom-call(s32[3]{0:T(128)} %pad_add_fusion.1.place.slot_ref, bf16[320,768]{1,0:T(8,128)(2,1)} %get-tuple-element.219.refs_0_.refs_2_, ...), custom_call_target="tpu_custom_call" | custom-call | flops 99999997952 | bytes 1 | tf_op jit(solution)/shard_map/attention_forward/pallas_call | solution.py:218
  106.9 26.4 %feed_forward.2 = (bf16[160,768]{1,0:T(8,128)(2,1)}, bf16[160,768]{1,0:T(8,128)(2,1)}, f32[320,768]{1,0:T(8,128)}, bf16[320,768]{1,0:T(8,128)(2,1)}, f32[4,768]{...) custom-call(s32[3]{0:T(128)} %pad_add_fusion.1.place.slot_ref, ...), custom_call_target="tpu_custom_call" | custom-call | flops 99999997952 | bytes 1 | tf_op jit(solution)/shard_map/feed_forward/pallas_call | solution.py:358
  134.3 1.5 collective-permute-start.24
  136.2 22.2 %attention_backward.5 = (f32[320,768]{1,0:T(8,128)}, bf16[320,768]{1,0:T(8,128)(2,1)}, f32[2,768]{1,0:T(2,128)}, bf16[768,1536]{1,0:T(8,128)(2,1)}, bf16[768,1536]{1,0:T(8,128)(2,1)}) custom-call(s32[3]{0:T(128)} %pad_add_fusion.1.place.slot_ref, bf16[320,768]{1,0:T(8,128)(2,1)} %get-tuple-element.238.refs_0_, f32[320,768]{1,0:T(8,128)} %get-tuple-element.239.refs_1_, ...), custom_call_target="tpu_custom_call" | custom-call | flops 99999997952 | bytes 1 | tf_op jit(solution)/shard_map/attention_backward/pallas_call | solution.py:644
  158.6 1.6 collective-permute-start.18
  160.2 1.8 collective-permute-done.19.u0.d0
  164.4 2.8 collective-permute-done.18
  167.2 1.5 collective-permute-start.23
  168.7 1.5 collective-permute-start.22
  170.2 19.1 %attention_forward.5 = (bf16[576,768]{1,0:T(8,128)(2,1)}, bf16[576,768]{1,0:T(8,128)(2,1)}, bf16[576,768]{1,0:T(8,128)(2,1)}, bf16[576,768]{1,0:T(8,128)(2,1)}, bf16[12,576,576]{2,1,0:T(8,128)(2,1)}) custom-call(s32[3]{0:T(128)} %pad_add_fusion.1.place.slot_ref, bf16[576,768]{1,0:T(8,128)(2,1)} %get-tuple-element.253.refs_0_.refs_2_, ...), custom_call_target="tpu_custom_call" | custom-call | flops 99999997952 | bytes 1 | tf_op jit(solution)/shard_map/attention_forward/pallas_call | solution.py:218
  191.3 4.6 %add_up.13 = (bf16[384,1536]{1,0:T(8,128)(2,1)}, bf16[384,1536]{1,0:T(8,128)(2,1)}, bf16[384,1536]{1,0:T(8,128)(2,1)}) custom-call(bf16[1536,1536]{1,0:T(8,128)(2,1)} %get-tuple-element.265.refs_0_.refs_2_.refs_4_.refs_9_.refs_6_.refs_10_.refs_5_, bf16[1536,1536]{1,0:T(8,128)(2,1)} %copy-done, ...), custom_call_target="tpu_custom_call" | custom-call | flops 1 | bytes 1 | tf_op jit(solution)/shard_map/add_up/pallas_call | solution.py:768
  197.0 1.5 collective-permute-start.34
  199.6 38.1 %feed_forward.3 = (bf16[288,768]{1,0:T(8,128)(2,1)}, bf16[288,768]{1,0:T(8,128)(2,1)}, f32[576,768]{1,0:T(8,128)}, bf16[576,768]{1,0:T(8,128)(2,1)}, f32[4,768]{...) custom-call(s32[3]{0:T(128)} %pad_add_fusion.1.place.slot_ref, ...), custom_call_target="tpu_custom_call" | custom-call | flops 99999997952 | bytes 1 | tf_op jit(solution)/shard_map/feed_forward/pallas_call | solution.py:358
  242.2 3.8 add_up.14
  246.0 1.6 collective-permute-start.38
  247.6 1.5 collective-permute-start.37
  249.1 20.3 %attention_backward.6 = (f32[576,768]{1,0:T(8,128)}, bf16[768,576]{1,0:T(8,128)(2,1)}, bf16[768,576]{1,0:T(8,128)(2,1)}, bf16[384,1536]{1,0:T(8,128)(2,1)}, bf16[384,1536]{1,0:T(8,128)(2,1)}) custom-call(s32[3]{0:T(128)} %pad_add_fusion.1.place.slot_ref, bf16[576,768]{1,0:T(8,128)(2,1)} %get-tuple-element.280.refs_0_, ...), custom_call_target="tpu_custom_call" | custom-call | flops 99999997952 | bytes 1 | tf_op jit(solution)/shard_map/attention_backward/pallas_call | solution.py:644
  269.5 5.8 %collective-permute-done.37.refs_9_.refs_17_.refs_21_.refs_8_.refs_13_.refs_3_.refs_15_ = bf16[384,1536]{1,0:T(8,128)(2,1)S(1)} collective-permute-done((bf16[384,1536]{1,0:T(8,128)(2,1)}, bf16[384,1536]{1,0:T(8,128)(2,1)S(1)}, u32[]{:S(2)}, u32[]{:S(2)}) %collective-permute-start.37) | collective-permute-done | bytes 1179680 | tf_op jit(solution)/shard_map/ppermute | solution.py:885
  276.3 1.5 copy-done.1
  277.8 4.9 %add_up.15 = (bf16[384,1536]{1,0:T(8,128)(2,1)}, bf16[384,1536]{1,0:T(8,128)(2,1)}, bf16[192,1536]{1,0:T(8,128)(2,1)}, bf16[96,1536]{1,0:T(8,128)(2,1)}) custom-call(bf16[1536,1536]{1,0:T(8,128)(2,1)} %get-tuple-element.294.refs_0_.refs_2_.refs_4_.refs_3_.refs_7_.refs_8_.refs_5_.refs_6_, bf16[1536,1536]{1,0:T(8,128)(2,1)} %copy-done.1, ...), custom_call_target="tpu_custom_call" | custom-call | flops 1 | bytes 1 | tf_op jit(solution)/shard_map/add_up/pallas_call | solution.py:768
  282.7 2.6 collective-permute-start.49
  285.4 1.5 collective-permute-start.48
  287.4 1.5 collective-permute-start.43
  288.9 19.4 %attention_backward.7 = (f32[576,768]{1,0:T(8,128)}, bf16[576,768]{1,0:T(8,128)(2,1)}, f32[2,768]{1,0:T(2,128)}, bf16[384,1536]{1,0:T(8,128)(2,1)}, bf16[384,1536]{1,0:T(8,128)(2,1)}) custom-call(s32[3]{0:T(128)} %pad_add_fusion.1.place.slot_ref, bf16[576,768]{1,0:T(8,128)(2,1)} %get-tuple-element.280.refs_0_, f32[576,768]{1,0:T(8,128)} %get-tuple-element.287.refs_1_, ...), custom_call_target="tpu_custom_call" | custom-call | flops 99999997952 | bytes 1 | tf_op jit(solution)/shard_map/attention_backward/pallas_call | solution.py:644
  308.9 3.0 collective-permute-done.48.refs_9_.refs_6_.refs_7_.refs_8_
  314.3 3.8 add_up.16
  319.2 1.5 collective-permute-start.45
  320.7 25.4 %attention_backward.8 = (f32[896,768]{1,0:T(8,128)}, bf16[768,896]{1,0:T(8,128)(2,1)}, bf16[768,896]{1,0:T(8,128)(2,1)}, bf16[384,768]{1,0:T(8,128)(2,1)}, bf16[...) custom-call(s32[3]{0:T(128)} %pad_add_fusion.1.place.slot_ref, ...), custom_call_target="tpu_custom_call" | custom-call | flops 99999997952 | bytes 1 | tf_op jit(solution)/shard_map/attention_backward/pallas_call | solution.py:644
  347.8 3.7 add_up.17
  352.1 1.5 collective-permute-start.54
  353.6 1.5 collective-permute-start.53
  355.1 22.8 %attention_backward.9 = (f32[448,768]{1,0:T(8,128)}, bf16[448,768]{1,0:T(8,128)(2,1)}, bf16[384,768]{1,0:T(8,128)(2,1)}, bf16[384,768]{1,0:T(8,128)(2,1)}, bf16[...) custom-call(s32[3]{0:T(128)} %pad_add_fusion.1.place.slot_ref, bf16[320,768]{1,0:T(8,128)(2,1)} %get-tuple-element.306.refs_0_, ...), custom_call_target="tpu_custom_call" | custom-call | flops 99999997952 | bytes 1 | tf_op jit(solution)/shard_map/attention_backward/pallas_call | solution.py:644
  380.7 2.8 add_up.18
  385.1 2.6 add_up.19
  388.4 1.5 collective-permute-start.58
  390.8 2.2 maximum_select_fusion.2
  393.0 2.6 collective-permute-start.61
  396.3 6.0 %collective-permute-done.60.refs_4_.refs_9_.refs_10_.refs_16_ = bf16[192,1536]{1,0:T(8,128)(2,1)S(1)} collective-permute-done((bf16[192,1536]{1,0:T(8,128)(2,1)}, bf16[192,1536]{1,0:T(8,128)(2,1)S(1)}, u32[]{:S(2)}, u32[]{:S(2)}) %collective-permute-start.60) | collective-permute-done | bytes 589856 | tf_op jit(solution)/shard_map/ppermute | solution.py:885
  403.1 2.2 add_up.22
  407.0 2.4 add_up.20
  413.5 2.7 add_up.24
  418.2 1.5 collective-permute-done.70
  421.4 1.5 collective-permute-start.71
  423.0 2.2 add_up.21
  425.2 1.6 collective-permute-start.68
  427.1 2.5 collective-permute-start.66
  429.6 2.7 add_up.25
  432.3 1.9 pad_maximum_fusion.2
  436.8 5.9 %collective-permute-done.72 = f32[10,768]{1,0:T(8,128)} collective-permute-done((f32[10,768]{1,0:T(8,128)S(1)}, f32[10,768]{1,0:T(8,128)}, u32[]{:S(2)}, u32[]{:S(2)}) %collective-permute-start.72) | collective-permute-done | bytes 30752 | tf_op jit(solution)/shard_map/ppermute | solution.py:888
  445.4 1.9 add_up.23
  (315 shorter events, 63.7 us)
Async XLA Ops:
  4.9 16.6 %collective-permute-start = (bf16[768,384]{1,0:T(8,128)(2,1)}, bf16[768,384]{1,0:T(8,128)(2,1)S(1)}, u32[]{:S(2)}, u32[]{:S(2)}) collective-permute-start(bf16[768,384]{1,0:T(8,128)(2,1)} %get-tuple-element.199), channel_id=1, source_target_pairs={{0,1},{1,0},{2,3},{3,2},{4,5},{5,4},{6,7},{7,6},{8,9},{9,8},{10,11... | collective-permute-start | bytes 1769480 | tf_op jit(solution)/shard_map/ppermute | solution.py:884
  21.5 14.5 %collective-permute-start.3 = (bf16[768,384]{1,0:T(8,128)(2,1)S(1)}, bf16[768,384]{1,0:T(8,128)(2,1)S(1)}, u32[]{:S(2)}, u32[]{:S(2)}) collective-permute-start(bf16[768,384]{1,0:T(8,128)(2,1)S(1)} %collective-permute-done.refs_5_.refs_10_.refs_7_.refs_11_), channel_id=1, source_target_pairs={{0,4},{2,6},{4,0},{6,2},{8,12},{10,14},{12,8},{14,10},{16,20},{18,... | collective-permute-start | bytes 1769480 | tf_op jit(solution)/shard_map/ppermute | solution.py:885
  24.3 16.1 %collective-permute-start.1 = (bf16[448,768]{1,0:T(8,128)(2,1)S(1)}, bf16[448,768]{1,0:T(8,128)(2,1)S(1)}, u32[]{:S(2)}, u32[]{:S(2)}) collective-permute-start(bf16[448,768]{1,0:T(8,128)(2,1)S(1)} %copy-done.54), channel_id=1, source_target_pairs={{0,1},{1,0},{2,3},{3,2},{4,5},{5,4},{6,7},{7,6},{8,9},{9,8},{10,11... | collective-permute-start | bytes 2064392 | tf_op jit(solution)/shard_map/ppermute | solution.py:884
  26.7 15.8 %collective-permute-start.4 = (bf16[768,384]{1,0:T(8,128)(2,1)S(1)}, bf16[768,384]{1,0:T(8,128)(2,1)S(1)}, u32[]{:S(2)}, u32[]{:S(2)}) collective-permute-start(bf16[768,384]{1,0:T(8,128)(2,1)S(1)} %collective-permute-done.refs_5_.refs_10_.refs_7_.refs_11_), channel_id=1, source_target_pairs={{0,2},{2,0},{4,6},{6,4},{8,10},{10,8},{12,14},{14,12},{16,18},{18,... | collective-permute-start | bytes 1769480 | tf_op jit(solution)/shard_map/ppermute | solution.py:885
  36.0 6.5 %collective-permute-start.5 = (bf16[768,384]{1,0:T(8,128)(2,1)S(1)}, bf16[768,384]{1,0:T(8,128)(2,1)S(1)}, u32[]{:S(2)}, u32[]{:S(2)}) collective-permute-start(bf16[768,384]{1,0:T(8,128)(2,1)S(1)} %collective-permute-done.3.refs_6_.refs_11_.refs_8_.refs_12_), channel_id=1, source_target_pairs={{0,2},{2,0},{4,6},{6,4},{8,10},{10,8},{12,14},{14,12},{16,18},{18,... | collective-permute-start | bytes 1769480 | tf_op jit(solution)/shard_map/ppermute | solution.py:885
  40.4 35.2 %collective-permute-start.2 = (bf16[768,384]{1,0:T(8,128)(2,1)S(1)}, bf16[768,384]{1,0:T(8,128)(2,1)S(1)}, u32[]{:S(2)}, u32[]{:S(2)}) collective-permute-start(bf16[768,384]{1,0:T(8,128)(2,1)S(1)} %copy-done.65), channel_id=1, source_target_pairs={{0,1},{1,0},{2,3},{3,2},{4,5},{5,4},{6,7},{7,6},{8,9},{9,8},{10,11... | collective-permute-start | bytes 1769480 | tf_op jit(solution)/shard_map/ppermute | solution.py:884
  42.0 30.5 %collective-permute-start.7 = (bf16[768,384]{1,0:T(8,128)(2,1)S(1)}, bf16[768,384]{1,0:T(8,128)(2,1)S(1)}, u32[]{:S(2)}, u32[]{:S(2)}) collective-permute-start(bf16[768,384]{1,0:T(8,128)(2,1)S(1)} %copy-done.67), channel_id=1, source_target_pairs={{0,1},{1,0},{2,3},{3,2},{4,5},{5,4},{6,7},{7,6},{8,9},{9,8},{10,11... | collective-permute-start | bytes 1769480 | tf_op jit(solution)/shard_map/ppermute | solution.py:884
  72.5 13.6 %collective-permute-start.8 = (bf16[768,384]{1,0:T(8,128)(2,1)S(1)}, bf16[768,384]{1,0:T(8,128)(2,1)S(1)}, u32[]{:S(2)}, u32[]{:S(2)}) collective-permute-start(bf16[768,384]{1,0:T(8,128)(2,1)S(1)} %collective-permute-done.7.refs_4_.w0.refs_6_.refs_10_), channel_id=1, source_target_pairs={{0,8},{2,10},{4,12},{6,14},{8,0},{10,2},{12,4},{14,6},{16,24},{18,... | collective-permute-start | bytes 1769480 | tf_op jit(solution)/shard_map/ppermute | solution.py:885
  74.1 13.1 %collective-permute-start.10 = (bf16[768,384]{1,0:T(8,128)(2,1)S(1)}, bf16[768,384]{1,0:T(8,128)(2,1)S(1)}, u32[]{:S(2)}, u32[]{:S(2)}) collective-permute-start(bf16[768,384]{1,0:T(8,128)(2,1)S(1)} %copy-done.61), channel_id=1, source_target_pairs={{0,1},{1,0},{2,3},{3,2},{4,5},{5,4},{6,7},{7,6},{8,9},{9,8},{10,11... | collective-permute-start | bytes 1769480 | tf_op jit(solution)/shard_map/ppermute | solution.py:884
  75.7 13.1 %collective-permute-start.6 = (bf16[768,384]{1,0:T(8,128)(2,1)S(1)}, bf16[768,384]{1,0:T(8,128)(2,1)S(1)}, u32[]{:S(2)}, u32[]{:S(2)}) collective-permute-start(bf16[768,384]{1,0:T(8,128)(2,1)S(1)} %collective-permute-done.2.u0), channel_id=1, source_target_pairs={{0,4},{2,6},{4,0},{6,2},{8,12},{10,14},{12,8},{14,10},{16,20},{18,... | collective-permute-start | bytes 1769480 | tf_op jit(solution)/shard_map/ppermute | solution.py:885
  76.2 13.0 %collective-permute-start.11 = (bf16[768,384]{1,0:T(8,128)(2,1)S(1)}, bf16[768,384]{1,0:T(8,128)(2,1)S(1)}, u32[]{:S(2)}, u32[]{:S(2)}) collective-permute-start(bf16[768,384]{1,0:T(8,128)(2,1)S(1)} %collective-permute-done.7.refs_4_.w0.refs_6_.refs_10_), channel_id=1, source_target_pairs={{0,2},{2,0},{4,6},{6,4},{8,10},{10,8},{12,14},{14,12},{16,18},{18,... | collective-permute-start | bytes 1769480 | tf_op jit(solution)/shard_map/ppermute | solution.py:885
  87.3 16.7 %collective-permute-start.13 = (bf16[448,768]{1,0:T(8,128)(2,1)S(1)}, bf16[448,768]{1,0:T(8,128)(2,1)S(1)}, u32[]{:S(2)}, u32[]{:S(2)}) collective-permute-start(bf16[448,768]{1,0:T(8,128)(2,1)S(1)} %copy-done.53), channel_id=1, source_target_pairs={{0,1},{1,0},{2,3},{3,2},{4,5},{5,4},{6,7},{7,6},{8,9},{9,8},{10,11... | collective-permute-start | bytes 2064392 | tf_op jit(solution)/shard_map/ppermute | solution.py:884
  88.8 14.4 %collective-permute-start.15 = (bf16[768,384]{1,0:T(8,128)(2,1)S(1)}, bf16[768,384]{1,0:T(8,128)(2,1)S(1)}, u32[]{:S(2)}, u32[]{:S(2)}) collective-permute-start(bf16[768,384]{1,0:T(8,128)(2,1)S(1)} %collective-permute-done.10.d0), channel_id=1, source_target_pairs={{0,8},{2,10},{4,12},{6,14},{8,0},{10,2},{12,4},{14,6},{16,24},{18,... | collective-permute-start | bytes 1769480 | tf_op jit(solution)/shard_map/ppermute | solution.py:885
  89.2 16.2 %collective-permute-start.14 = (bf16[768,384]{1,0:T(8,128)(2,1)S(1)}, bf16[768,384]{1,0:T(8,128)(2,1)S(1)}, u32[]{:S(2)}, u32[]{:S(2)}) collective-permute-start(bf16[768,384]{1,0:T(8,128)(2,1)S(1)} %collective-permute-done.2.u0), channel_id=1, source_target_pairs={{0,2},{2,0},{4,6},{6,4},{8,10},{10,8},{12,14},{14,12},{16,18},{18,... | collective-permute-start | bytes 1769480 | tf_op jit(solution)/shard_map/ppermute | solution.py:885
  89.3 16.2 %collective-permute-start.9 = (bf16[768,384]{1,0:T(8,128)(2,1)S(1)}, bf16[768,384]{1,0:T(8,128)(2,1)}, u32[]{:S(2)}, u32[]{:S(2)}) collective-permute-start(bf16[768,384]{1,0:T(8,128)(2,1)S(1)} %collective-permute-done.6.u1), channel_id=1, source_target_pairs={{0,2},{2,0},{4,6},{6,4},{8,10},{10,8},{12,14},{14,12},{16,18},{18,... | collective-permute-start | bytes 1769480 | tf_op jit(solution)/shard_map/ppermute | solution.py:885
  104.0 30.3 %collective-permute-start.20 = (bf16[768,384]{1,0:T(8,128)(2,1)S(1)}, bf16[768,384]{1,0:T(8,128)(2,1)}, u32[]{:S(2)}, u32[]{:S(2)}) collective-permute-start(bf16[768,384]{1,0:T(8,128)(2,1)S(1)} %copy-done.59), channel_id=1, source_target_pairs={{0,1},{1,0},{2,3},{3,2},{4,5},{5,4},{6,7},{7,6},{8,9},{9,8},{10,11... | collective-permute-start | bytes 1769480 | tf_op jit(solution)/shard_map/ppermute | solution.py:884
  133.6 28.3 %collective-permute-start.19 = (bf16[1536,384]{1,0:T(8,128)(2,1)S(1)}, bf16[1536,384]{1,0:T(8,128)(2,1)}, u32[]{:S(2)}, u32[]{:S(2)}) collective-permute-start(bf16[1536,384]{1,0:T(8,128)(2,1)S(1)} %copy-done.50), channel_id=1, source_target_pairs={{0,1},{1,0},{2,3},{3,2},{4,5},{5,4},{6,7},{7,6},{8,9},{9,8},{10,11... | collective-permute-start | bytes 3538952 | tf_op jit(solution)/shard_map/ppermute | solution.py:884
  134.3 24.2 %collective-permute-start.24 = (bf16[768,384]{1,0:T(8,128)(2,1)}, bf16[768,384]{1,0:T(8,128)(2,1)}, u32[]{:S(2)}, u32[]{:S(2)}) collective-permute-start(bf16[768,384]{1,0:T(8,128)(2,1)} %collective-permute-done.20.refs_4_.w0.refs_8_), channel_id=1, source_target_pairs={{0,8},{2,10},{4,12},{6,14},{8,0},{10,2},{12,4},{14,6},{16,24},{18,... | collective-permute-start | bytes 1769480 | tf_op jit(solution)/shard_map/ppermute | solution.py:885
  135.7 34.4 %collective-permute-start.27 = (bf16[768,384]{1,0:T(8,128)(2,1)}, bf16[768,384]{1,0:T(8,128)(2,1)}, u32[]{:S(2)}, u32[]{:S(2)}) collective-permute-start(bf16[768,384]{1,0:T(8,128)(2,1)} %collective-permute-done.20.refs_4_.w0.refs_8_), channel_id=1, source_target_pairs={{0,2},{2,0},{4,6},{6,4},{8,10},{10,8},{12,14},{14,12},{16,18},{18,... | collective-permute-start | bytes 1769480 | tf_op jit(solution)/shard_map/ppermute | solution.py:885
  135.7 32.9 %collective-permute-start.26 = (bf16[1536,1536]{1,0:T(8,128)(2,1)}, bf16[1536,1536]{1,0:T(8,128)(2,1)S(1)}, u32[]{:S(2)}, u32[]{:S(2)}) collective-permute-start(bf16[1536,1536]{1,0:T(8,128)(2,1)} %get-tuple-element.251), channel_id=1, source_target_pairs={{0,2},{2,0},{4,6},{6,4},{8,10},{10,8},{12,14},{14,12},{16,18},{18,... | collective-permute-start | bytes 14155784 | tf_op jit(solution)/shard_map/ppermute | solution.py:885
  158.5 11.7 %collective-permute-start.28 = (bf16[768,384]{1,0:T(8,128)(2,1)}, bf16[768,384]{1,0:T(8,128)(2,1)}, u32[]{:S(2)}, u32[]{:S(2)}) collective-permute-start(bf16[768,384]{1,0:T(8,128)(2,1)} %collective-permute-done.24.refs_5_.w1.refs_9_), channel_id=1, source_target_pairs={{0,2},{2,0},{4,6},{6,4},{8,10},{10,8},{12,14},{14,12},{16,18},{18,... | collective-permute-start | bytes 1769480 | tf_op jit(solution)/shard_map/ppermute | solution.py:885
  158.6 8.6 %collective-permute-start.18 = (bf16[160,768]{1,0:T(8,128)(2,1)}, bf16[160,768]{1,0:T(8,128)(2,1)S(1)}, u32[]{:S(2)}, u32[]{:S(2)}) collective-permute-start(bf16[160,768]{1,0:T(8,128)(2,1)} %get-tuple-element.233), channel_id=1, source_target_pairs={{0,1},{1,0},{2,3},{3,2},{4,5},{5,4},{6,7},{7,6},{8,9},{9,8},{10,11... | collective-permute-start | bytes 737288 | tf_op jit(solution)/shard_map/ppermute | solution.py:884
  163.9 26.0 %collective-permute-start.33 = (bf16[768,1536]{1,0:T(8,128)(2,1)}, bf16[768,1536]{1,0:T(8,128)(2,1)S(1)}, u32[]{:S(2)}, u32[]{:S(2)}) collective-permute-start(bf16[768,1536]{1,0:T(8,128)(2,1)} %get-tuple-element.267), channel_id=1, source_target_pairs={{0,2},{2,0},{4,6},{6,4},{8,10},{10,8},{12,14},{14,12},{16,18},{18,... | collective-permute-start | bytes 7077896 | tf_op jit(solution)/shard_map/ppermute | solution.py:885
  167.2 22.1 %collective-permute-start.23 = (bf16[768,384]{1,0:T(8,128)(2,1)S(1)}, bf16[768,384]{1,0:T(8,128)(2,1)}, u32[]{:S(2)}, u32[]{:S(2)}) collective-permute-start(bf16[768,384]{1,0:T(8,128)(2,1)S(1)} %get-tuple-element.247), channel_id=1, source_target_pairs={{0,8},{2,10},{4,12},{6,14},{8,0},{10,2},{12,4},{14,6},{16,24},{18,... | collective-permute-start | bytes 1769480 | tf_op jit(solution)/shard_map/ppermute | solution.py:885
  168.7 21.1 %collective-permute-start.22 = (bf16[768,384]{1,0:T(8,128)(2,1)S(1)}, bf16[768,384]{1,0:T(8,128)(2,1)}, u32[]{:S(2)}, u32[]{:S(2)}) collective-permute-start(bf16[768,384]{1,0:T(8,128)(2,1)S(1)} %get-tuple-element.246), channel_id=1, source_target_pairs={{0,4},{2,6},{4,0},{6,2},{8,12},{10,14},{12,8},{14,10},{16,20},{18,... | collective-permute-start | bytes 1769480 | tf_op jit(solution)/shard_map/ppermute | solution.py:885
  170.2 26.9 %collective-permute-start.29 = (bf16[1536,384]{1,0:T(8,128)(2,1)}, bf16[1536,384]{1,0:T(8,128)(2,1)}, u32[]{:S(2)}, u32[]{:S(2)}) collective-permute-start(bf16[1536,384]{1,0:T(8,128)(2,1)} %collective-permute-done.19.u0.d0), channel_id=1, source_target_pairs={{0,2},{2,0},{4,6},{6,4},{8,10},{10,8},{12,14},{14,12},{16,18},{18,... | collective-permute-start | bytes 3538952 | tf_op jit(solution)/shard_map/ppermute | solution.py:885
  189.2 9.3 %collective-permute-start.31 = (bf16[768,384]{1,0:T(8,128)(2,1)}, bf16[768,384]{1,0:T(8,128)(2,1)S(1)}, u32[]{:S(2)}, u32[]{:S(2)}) collective-permute-start(bf16[768,384]{1,0:T(8,128)(2,1)} %collective-permute-done.23.d1), channel_id=1, source_target_pairs={{0,2},{2,0},{4,6},{6,4},{8,10},{10,8},{12,14},{14,12},{16,18},{18,... | collective-permute-start | bytes 1769480 | tf_op jit(solution)/shard_map/ppermute | solution.py:885
  189.8 8.8 %collective-permute-start.30 = (bf16[768,384]{1,0:T(8,128)(2,1)}, bf16[768,384]{1,0:T(8,128)(2,1)S(1)}, u32[]{:S(2)}, u32[]{:S(2)}) collective-permute-start(bf16[768,384]{1,0:T(8,128)(2,1)} %collective-permute-done.22.u1), channel_id=1, source_target_pairs={{0,2},{2,0},{4,6},{6,4},{8,10},{10,8},{12,14},{14,12},{16,18},{18,... | collective-permute-start | bytes 1769480 | tf_op jit(solution)/shard_map/ppermute | solution.py:885
  195.9 43.8 %collective-permute-start.36 = (bf16[384,1536]{1,0:T(8,128)(2,1)}, bf16[384,1536]{1,0:T(8,128)(2,1)S(1)}, u32[]{:S(2)}, u32[]{:S(2)}) collective-permute-start(bf16[384,1536]{1,0:T(8,128)(2,1)} %get-tuple-element.273), channel_id=1, source_target_pairs={{0,4},{2,6},{4,0},{6,2},{8,12},{10,14},{12,8},{14,10},{16,20},{18,... | collective-permute-start | bytes 3538952 | tf_op jit(solution)/shard_map/ppermute | solution.py:885
  196.5 43.2 %collective-permute-start.35 = (bf16[384,1536]{1,0:T(8,128)(2,1)}, bf16[384,1536]{1,0:T(8,128)(2,1)S(1)}, u32[]{:S(2)}, u32[]{:S(2)}) collective-permute-start(bf16[384,1536]{1,0:T(8,128)(2,1)} %get-tuple-element.271), channel_id=1, source_target_pairs={{0,8},{2,10},{4,12},{6,14},{8,0},{10,2},{12,4},{14,6},{16,24},{18,... | collective-permute-start | bytes 3538952 | tf_op jit(solution)/shard_map/ppermute | solution.py:885
  197.0 42.7 %collective-permute-start.34 = (bf16[384,1536]{1,0:T(8,128)(2,1)}, bf16[384,1536]{1,0:T(8,128)(2,1)S(1)}, u32[]{:S(2)}, u32[]{:S(2)}) collective-permute-start(bf16[384,1536]{1,0:T(8,128)(2,1)} %get-tuple-element.269), channel_id=1, source_target_pairs={{0,1},{1,0},{2,3},{3,2},{4,5},{5,4},{6,7},{7,6},{8,9},{9,8},{10,11... | collective-permute-start | bytes 3538952 | tf_op jit(solution)/shard_map/ppermute | solution.py:884
  237.8 37.5 %collective-permute-start.39 = (bf16[1536,1536]{1,0:T(8,128)(2,1)}, bf16[1536,1536]{1,0:T(8,128)(2,1)S(1)}, u32[]{:S(2)}, u32[]{:S(2)}) collective-permute-start(bf16[1536,1536]{1,0:T(8,128)(2,1)} %get-tuple-element.278), channel_id=1, source_target_pairs={{0,2},{2,0},{4,6},{6,4},{8,10},{10,8},{12,14},{14,12},{16,18},{18,... | collective-permute-start | bytes 14155784 | tf_op jit(solution)/shard_map/ppermute | solution.py:885
  239.2 30.3 %collective-permute-start.32 = (bf16[288,768]{1,0:T(8,128)(2,1)}, bf16[288,768]{1,0:T(8,128)(2,1)}, u32[]{:S(2)}, u32[]{:S(2)}) collective-permute-start(bf16[288,768]{1,0:T(8,128)(2,1)} %get-tuple-element.264), channel_id=1, source_target_pairs={{0,1},{1,0},{2,3},{3,2},{4,5},{5,4},{6,7},{7,6},{8,9},{9,8},{10,11... | collective-permute-start | bytes 1327112 | tf_op jit(solution)/shard_map/ppermute | solution.py:884
  246.0 23.5 %collective-permute-start.38 = (bf16[192,1536]{1,0:T(8,128)(2,1)}, bf16[192,1536]{1,0:T(8,128)(2,1)S(1)}, u32[]{:S(2)}, u32[]{:S(2)}) collective-permute-start(bf16[192,1536]{1,0:T(8,128)(2,1)} %get-tuple-element.277), channel_id=1, source_target_pairs={{0,1},{1,0},{2,3},{3,2},{4,5},{5,4},{6,7},{7,6},{8,9},{9,8},{10,11... | collective-permute-start | bytes 1769480 | tf_op jit(solution)/shard_map/ppermute | solution.py:884
  247.6 27.7 %collective-permute-start.37 = (bf16[384,1536]{1,0:T(8,128)(2,1)}, bf16[384,1536]{1,0:T(8,128)(2,1)S(1)}, u32[]{:S(2)}, u32[]{:S(2)}) collective-permute-start(bf16[384,1536]{1,0:T(8,128)(2,1)} %get-tuple-element.275), channel_id=1, source_target_pairs={{0,4},{2,6},{4,0},{6,2},{8,12},{10,14},{12,8},{14,10},{16,20},{18,... | collective-permute-start | bytes 3538952 | tf_op jit(solution)/shard_map/ppermute | solution.py:885
  269.4 43.9 %collective-permute-start.42 = (bf16[384,1536]{1,0:T(8,128)(2,1)}, bf16[384,1536]{1,0:T(8,128)(2,1)}, u32[]{:S(2)}, u32[]{:S(2)}) collective-permute-start(bf16[384,1536]{1,0:T(8,128)(2,1)} %get-tuple-element.293), channel_id=1, source_target_pairs={{0,2},{2,0},{4,6},{6,4},{8,10},{10,8},{12,14},{14,12},{16,18},{18,... | collective-permute-start | bytes 3538952 | tf_op jit(solution)/shard_map/ppermute | solution.py:885
  282.7 25.6 %collective-permute-start.49 = (bf16[96,1536]{1,0:T(8,128)(2,1)}, bf16[96,1536]{1,0:T(8,128)(2,1)S(1)}, u32[]{:S(2)}, u32[]{:S(2)}) collective-permute-start(bf16[96,1536]{1,0:T(8,128)(2,1)} %get-tuple-element.311), channel_id=1, source_target_pairs={{0,16},{2,18},{4,20},{6,22},{8,24},{10,26},{12,28},{14,30},{16,0},... | collective-permute-start | bytes 884744 | tf_op jit(solution)/shard_map/ppermute | solution.py:885
  285.4 26.5 %collective-permute-start.48 = (bf16[384,1536]{1,0:T(8,128)(2,1)}, bf16[384,1536]{1,0:T(8,128)(2,1)S(1)}, u32[]{:S(2)}, u32[]{:S(2)}) collective-permute-start(bf16[384,1536]{1,0:T(8,128)(2,1)} %get-tuple-element.309), channel_id=1, source_target_pairs={{0,4},{2,6},{4,0},{6,2},{8,12},{10,14},{12,8},{14,10},{16,20},{18,... | collective-permute-start | bytes 3538952 | tf_op jit(solution)/shard_map/ppermute | solution.py:885
  286.9 21.5 %collective-permute-start.44 = (bf16[192,1536]{1,0:T(8,128)(2,1)}, bf16[192,1536]{1,0:T(8,128)(2,1)S(1)}, u32[]{:S(2)}, u32[]{:S(2)}) collective-permute-start(bf16[192,1536]{1,0:T(8,128)(2,1)} %get-tuple-element.298), channel_id=1, source_target_pairs={{0,8},{2,10},{4,12},{6,14},{8,0},{10,2},{12,4},{14,6},{16,24},{18,... | collective-permute-start | bytes 1769480 | tf_op jit(solution)/shard_map/ppermute | solution.py:885
  287.4 25.9 %collective-permute-start.43 = (bf16[384,1536]{1,0:T(8,128)(2,1)}, bf16[384,1536]{1,0:T(8,128)(2,1)S(1)}, u32[]{:S(2)}, u32[]{:S(2)}) collective-permute-start(bf16[384,1536]{1,0:T(8,128)(2,1)} %get-tuple-element.296), channel_id=1, source_target_pairs={{0,1},{1,0},{2,3},{3,2},{4,5},{5,4},{6,7},{7,6},{8,9},{9,8},{10,11... | collective-permute-start | bytes 3538952 | tf_op jit(solution)/shard_map/ppermute | solution.py:884
  308.3 37.7 %collective-permute-start.41 = (f32[2,768]{1,0:T(2,128)}, f32[2,768]{1,0:T(2,128)S(1)}, u32[]{:S(2)}, u32[]{:S(2)}) collective-permute-start(f32[2,768]{1,0:T(2,128)} %get-tuple-element.291), channel_id=1, source_target_pairs={{0,2},{2,0},{4,6},{6,4},{8,10},{10,8},{12,14},{14,12},{16,18},{18,... | collective-permute-start | bytes 18440 | tf_op jit(solution)/shard_map/ppermute | solution.py:885
  308.4 37.7 %collective-permute-start.52 = (bf16[384,1536]{1,0:T(8,128)(2,1)}, bf16[384,1536]{1,0:T(8,128)(2,1)S(1)}, u32[]{:S(2)}, u32[]{:S(2)}) collective-permute-start(bf16[384,1536]{1,0:T(8,128)(2,1)} %get-tuple-element.331), channel_id=1, source_target_pairs={{0,2},{2,0},{4,6},{6,4},{8,10},{10,8},{12,14},{14,12},{16,18},{18,... | collective-permute-start | bytes 3538952 | tf_op jit(solution)/shard_map/ppermute | solution.py:885
  318.2 27.9 %collective-permute-start.47 = (bf16[96,1536]{1,0:T(8,128)(2,1)}, bf16[96,1536]{1,0:T(8,128)(2,1)S(1)}, u32[]{:S(2)}, u32[]{:S(2)}) collective-permute-start(bf16[96,1536]{1,0:T(8,128)(2,1)} %get-tuple-element.304), channel_id=1, source_target_pairs={{0,16},{2,18},{4,20},{6,22},{8,24},{10,26},{12,28},{14,30},{16,0},... | collective-permute-start | bytes 884744 | tf_op jit(solution)/shard_map/ppermute | solution.py:885
  318.6 27.5 %collective-permute-start.46 = (bf16[192,1536]{1,0:T(8,128)(2,1)}, bf16[192,1536]{1,0:T(8,128)(2,1)S(1)}, u32[]{:S(2)}, u32[]{:S(2)}) collective-permute-start(bf16[192,1536]{1,0:T(8,128)(2,1)} %get-tuple-element.302), channel_id=1, source_target_pairs={{0,4},{2,6},{4,0},{6,2},{8,12},{10,14},{12,8},{14,10},{16,20},{18,... | collective-permute-start | bytes 1769480 | tf_op jit(solution)/shard_map/ppermute | solution.py:885
  319.2 26.9 %collective-permute-start.45 = (bf16[384,1536]{1,0:T(8,128)(2,1)}, bf16[384,1536]{1,0:T(8,128)(2,1)S(1)}, u32[]{:S(2)}, u32[]{:S(2)}) collective-permute-start(bf16[384,1536]{1,0:T(8,128)(2,1)} %get-tuple-element.300), channel_id=1, source_target_pairs={{0,1},{1,0},{2,3},{3,2},{4,5},{5,4},{6,7},{7,6},{8,9},{9,8},{10,11... | collective-permute-start | bytes 3538952 | tf_op jit(solution)/shard_map/ppermute | solution.py:884
  351.5 27.0 %collective-permute-start.55 = (bf16[96,1536]{1,0:T(8,128)(2,1)}, bf16[96,1536]{1,0:T(8,128)(2,1)S(1)}, u32[]{:S(2)}, u32[]{:S(2)}) collective-permute-start(bf16[96,1536]{1,0:T(8,128)(2,1)} %get-tuple-element.337), channel_id=1, source_target_pairs={{0,8},{2,10},{4,12},{6,14},{8,0},{10,2},{12,4},{14,6},{16,24},{18,... | collective-permute-start | bytes 884744 | tf_op jit(solution)/shard_map/ppermute | solution.py:885
  352.1 27.7 %collective-permute-start.54 = (bf16[240,1536]{1,0:T(8,128)(2,1)}, bf16[240,1536]{1,0:T(8,128)(2,1)S(1)}, u32[]{:S(2)}, u32[]{:S(2)}) collective-permute-start(bf16[240,1536]{1,0:T(8,128)(2,1)} %get-tuple-element.335), channel_id=1, source_target_pairs={{0,1},{1,0},{2,3},{3,2},{4,5},{5,4},{6,7},{7,6},{8,9},{9,8},{10,11... | collective-permute-start | bytes 2211848 | tf_op jit(solution)/shard_map/ppermute | solution.py:884
  353.6 25.0 %collective-permute-start.53 = (bf16[192,1536]{1,0:T(8,128)(2,1)}, bf16[192,1536]{1,0:T(8,128)(2,1)S(1)}, u32[]{:S(2)}, u32[]{:S(2)}) collective-permute-start(bf16[192,1536]{1,0:T(8,128)(2,1)} %get-tuple-element.333), channel_id=1, source_target_pairs={{0,4},{2,6},{4,0},{6,2},{8,12},{10,14},{12,8},{14,10},{16,20},{18,... | collective-permute-start | bytes 1769480 | tf_op jit(solution)/shard_map/ppermute | solution.py:885
  378.6 9.1 %collective-permute-start.57 = (bf16[384,768]{1,0:T(8,128)(2,1)}, bf16[384,768]{1,0:T(8,128)(2,1)S(1)}, u32[]{:S(2)}, u32[]{:S(2)}) collective-permute-start(bf16[384,768]{1,0:T(8,128)(2,1)} %get-tuple-element.344), channel_id=1, source_target_pairs={{0,2},{2,0},{4,6},{6,4},{8,10},{10,8},{12,14},{14,12},{16,18},{18,... | collective-permute-start | bytes 1769480 | tf_op jit(solution)/shard_map/ppermute | solution.py:885
  383.5 18.8 %collective-permute-start.60 = (bf16[192,1536]{1,0:T(8,128)(2,1)}, bf16[192,1536]{1,0:T(8,128)(2,1)S(1)}, u32[]{:S(2)}, u32[]{:S(2)}) collective-permute-start(bf16[192,1536]{1,0:T(8,128)(2,1)} %get-tuple-element.348), channel_id=1, source_target_pairs={{0,8},{2,10},{4,12},{6,14},{8,0},{10,2},{12,4},{14,6},{16,24},{18,... | collective-permute-start | bytes 1769480 | tf_op jit(solution)/shard_map/ppermute | solution.py:885
  387.8 17.6 %collective-permute-start.59 = (bf16[384,768]{1,0:T(8,128)(2,1)}, bf16[384,768]{1,0:T(8,128)(2,1)S(1)}, u32[]{:S(2)}, u32[]{:S(2)}) collective-permute-start(bf16[384,768]{1,0:T(8,128)(2,1)} %get-tuple-element.347), channel_id=1, source_target_pairs={{0,4},{2,6},{4,0},{6,2},{8,12},{10,14},{12,8},{14,10},{16,20},{18,... | collective-permute-start | bytes 1769480 | tf_op jit(solution)/shard_map/ppermute | solution.py:885
  388.4 17.6 %collective-permute-start.58 = (bf16[384,768]{1,0:T(8,128)(2,1)}, bf16[384,768]{1,0:T(8,128)(2,1)S(1)}, u32[]{:S(2)}, u32[]{:S(2)}) collective-permute-start(bf16[384,768]{1,0:T(8,128)(2,1)} %get-tuple-element.345), channel_id=1, source_target_pairs={{0,1},{1,0},{2,3},{3,2},{4,5},{5,4},{6,7},{7,6},{8,9},{9,8},{10,11... | collective-permute-start | bytes 1769480 | tf_op jit(solution)/shard_map/ppermute | solution.py:884
  393.0 12.3 %collective-permute-start.61 = (bf16[48,1536]{1,0:T(8,128)(2,1)S(1)}, bf16[48,1536]{1,0:T(8,128)(2,1)S(1)}, u32[]{:S(2)}, u32[]{:S(2)}) collective-permute-start(bf16[48,1536]{1,0:T(8,128)(2,1)S(1)} %copy-done.76), channel_id=1, source_target_pairs={{0,16},{2,18},{4,20},{6,22},{8,24},{10,26},{12,28},{14,30},{16,0},... | collective-permute-start | bytes 442376 | tf_op jit(solution)/shard_map/ppermute | solution.py:885
  395.8 16.2 %collective-permute-start.69 = (f32[10,768]{1,0:T(8,128)S(1)}, f32[10,768]{1,0:T(8,128)S(1)}, u32[]{:S(2)}, u32[]{:S(2)}) collective-permute-start(f32[10,768]{1,0:T(8,128)S(1)} %concatenate.39), channel_id=1, source_target_pairs={{0,1},{1,0},{2,3},{3,2},{4,5},{5,4},{6,7},{7,6},{8,9},{9,8},{10,11... | collective-permute-start | bytes 92168 | tf_op jit(solution)/shard_map/ppermute | solution.py:884
  406.0 15.4 %collective-permute-start.65 = (bf16[96,1536]{1,0:T(8,128)(2,1)}, bf16[96,1536]{1,0:T(8,128)(2,1)S(1)}, u32[]{:S(2)}, u32[]{:S(2)}) collective-permute-start(bf16[96,1536]{1,0:T(8,128)(2,1)} %add_up.22), channel_id=1, source_target_pairs={{0,16},{2,18},{4,20},{6,22},{8,24},{10,26},{12,28},{14,30},{16,0},... | collective-permute-start | bytes 884744 | tf_op jit(solution)/shard_map/ppermute | solution.py:885
  409.5 12.0 %collective-permute-start.64 = (bf16[192,768]{1,0:T(8,128)(2,1)}, bf16[192,768]{1,0:T(8,128)(2,1)S(1)}, u32[]{:S(2)}, u32[]{:S(2)}) collective-permute-start(bf16[192,768]{1,0:T(8,128)(2,1)} %get-tuple-element.356), channel_id=1, source_target_pairs={{0,1},{1,0},{2,3},{3,2},{4,5},{5,4},{6,7},{7,6},{8,9},{9,8},{10,11... | collective-permute-start | bytes 884744 | tf_op jit(solution)/shard_map/ppermute | solution.py:884
  410.8 10.6 %collective-permute-start.63 = (bf16[192,768]{1,0:T(8,128)(2,1)}, bf16[192,768]{1,0:T(8,128)(2,1)S(1)}, u32[]{:S(2)}, u32[]{:S(2)}) collective-permute-start(bf16[192,768]{1,0:T(8,128)(2,1)} %get-tuple-element.354), channel_id=1, source_target_pairs={{0,4},{2,6},{4,0},{6,2},{8,12},{10,14},{12,8},{14,10},{16,20},{18,... | collective-permute-start | bytes 884744 | tf_op jit(solution)/shard_map/ppermute | solution.py:885
  412.6 7.0 %collective-permute-start.70 = (f32[10,768]{1,0:T(8,128)}, f32[10,768]{1,0:T(8,128)}, u32[]{:S(2)}, u32[]{:S(2)}) collective-permute-start(f32[10,768]{1,0:T(8,128)} %add.147), channel_id=1, source_target_pairs={{0,4},{2,6},{4,0},{6,2},{8,12},{10,14},{12,8},{14,10},{16,20},{18,... | collective-permute-start | bytes 92168 | tf_op jit(solution)/shard_map/ppermute | solution.py:885
  417.4 32.8 %collective-permute-start.62 = (bf16[448,768]{1,0:T(8,128)(2,1)}, bf16[448,768]{1,0:T(8,128)(2,1)S(1)}, u32[]{:S(2)}, u32[]{:S(2)}) collective-permute-start(bf16[448,768]{1,0:T(8,128)(2,1)} %get-tuple-element.350), channel_id=1, source_target_pairs={{0,1},{1,0},{2,3},{3,2},{4,5},{5,4},{6,7},{7,6},{8,9},{9,8},{10,11... | collective-permute-start | bytes 2064392 | tf_op jit(solution)/shard_map/ppermute | solution.py:884
  421.4 12.8 %collective-permute-start.71 = (f32[10,768]{1,0:T(8,128)S(1)}, f32[10,768]{1,0:T(8,128)S(1)}, u32[]{:S(2)}, u32[]{:S(2)}) collective-permute-start(f32[10,768]{1,0:T(8,128)S(1)} %add.148), channel_id=1, source_target_pairs={{0,8},{2,10},{4,12},{6,14},{8,0},{10,2},{12,4},{14,6},{16,24},{18,... | collective-permute-start | bytes 92168 | tf_op jit(solution)/shard_map/ppermute | solution.py:885
  425.2 18.9 %collective-permute-start.68 = (bf16[96,768]{1,0:T(8,128)(2,1)}, bf16[96,768]{1,0:T(8,128)(2,1)S(1)}, u32[]{:S(2)}, u32[]{:S(2)}) collective-permute-start(bf16[96,768]{1,0:T(8,128)(2,1)} %get-tuple-element.363), channel_id=1, source_target_pairs={{0,24},{2,26},{4,28},{6,30},{8,16},{10,18},{12,20},{14,22},{16,8},... | collective-permute-start | bytes 442376 | tf_op jit(solution)/shard_map/ppermute | solution.py:888
  426.8 17.3 %collective-permute-start.67 = (bf16[96,768]{1,0:T(8,128)(2,1)}, bf16[96,768]{1,0:T(8,128)(2,1)S(1)}, u32[]{:S(2)}, u32[]{:S(2)}) collective-permute-start(bf16[96,768]{1,0:T(8,128)(2,1)} %get-tuple-element.361), channel_id=1, source_target_pairs={{0,8},{2,10},{4,12},{6,14},{8,0},{10,2},{12,4},{14,6},{16,24},{18,... | collective-permute-start | bytes 442376 | tf_op jit(solution)/shard_map/ppermute | solution.py:888
  427.1 17.0 %collective-permute-start.66 = (bf16[96,768]{1,0:T(8,128)(2,1)}, bf16[96,768]{1,0:T(8,128)(2,1)S(1)}, u32[]{:S(2)}, u32[]{:S(2)}) collective-permute-start(bf16[96,768]{1,0:T(8,128)(2,1)} %get-tuple-element.359), channel_id=1, source_target_pairs={{0,16},{2,18},{4,20},{6,22},{8,24},{10,26},{12,28},{14,30},{16,0},... | collective-permute-start | bytes 442376 | tf_op jit(solution)/shard_map/ppermute | solution.py:888
  434.2 8.4 %collective-permute-start.72 = (f32[10,768]{1,0:T(8,128)S(1)}, f32[10,768]{1,0:T(8,128)}, u32[]{:S(2)}, u32[]{:S(2)}) collective-permute-start(f32[10,768]{1,0:T(8,128)S(1)} %add.149), channel_id=1, source_target_pairs={{0,16},{2,18},{4,20},{6,22},{8,24},{10,26},{12,28},{14,30},{16,0},... | collective-permute-start | bytes 92168 | tf_op jit(solution)/shard_map/ppermute | solution.py:888
  (86 other events, 549.2 us)

commit v6 on v5

--- a/solution.py
+++ b/solution.py
@@ -1025,7 +1025,7 @@
     tok = ffn_v[4]
     near_fv = exchange(ffn_v[4], C)
     core_fv = exchange(ffn_v[5], C)
-    got5 = send_all([ful, fdl, sl], exchange, tok)
+    got5 = send_all([ful, fdl], exchange, tok)
     out_v_recv = exchange(after(ffn_v[1], tok), Y)
     bva = self_back(1, (ffn_v[3], ffn_v[2], norms[1][2]), self_v, self_v_pack, after(slot, near_fv, *got4), 1)
 
@@ -1035,14 +1035,14 @@
         Sum(part((ffn_v[6], core_fv), i), part((ffn_v[6], core_fv), 2 + i), rows, way, hid)
         for i, way in enumerate((y_first, x_first))
     ]
-    got6 = send_all([fuv, fdv, ful, fdl, sl], exchange, tok)
+    got6 = send_all([fuv, fdv, ful, fdl], exchange, tok)
     bvb = self_back(1, (ffn_v[3], bva[0], bva[1], bva[2]), self_v, self_v_pack, after(slot, out_v_recv, *got5, core_fv), 0)
 
     tok = bvb[2]
     near_bv = exchange(bvb[2], C)
     core_svo = exchange(bvb[3], C)
     sv = Sum(part((bvb[4], core_svo), 0), part((bva[4], core_svr), 0), rows, y_first, hid)
-    got7 = send_all([sv, fuv, ful, fdl], exchange, tok)
+    got7 = send_all([sv, fuv, ful, fdl, sl], exchange, tok)
     xa = attention_backward(
         (back_l[1], bvb[1], back_l[0], bvb[0], x_own, x_recv), perm, in_proj, cross_pack, 0, SX, out_proj, cross,
         None, after(slot, *got6), cross_dirs, 1, spans,

time: 461 us -> 458 us (level)
    ppermute x50, waiting for transfers between devices: 37.9 us -> 32.9 us  [exchange(): return lax.ppermute(x, 'dp', [(i, i ^ 1 << stage) for i in range(n_dp)])]
    ppermute x19 -> x20, waiting for transfers between devices: 15.7 us -> 18.6 us  [exchange(): return lax.ppermute(x, 'tensor', SWAP)]
    unnamed x160 -> x170, local copies, waits for them, and re-layouts: 19.1 us -> 16.9 us
    ppermute x19 -> x20, starting transfers between devices: 25.6 us -> 25.8 us  [exchange(): return lax.ppermute(x, 'tensor', SWAP)]
  transfers between devices with their start and end apart: 73 -> 74, of which waited for: 17 -> 18; matrix products, arithmetic and copies ran while one was open for 5% -> 4% of each run, Pallas kernels for 61% -> 62%
where the time goes in v6:
time: 458 us; the launch traced here: 450 us
  Pallas kernels  285 us (62%)
  starting transfers between devices  66.6 us (15%)
  waiting for transfers between devices  57.8 us (13%)
  local copies, waits for them, and re-layouts  20.7 us (5%)
  other arithmetic  18.5 us (4%)
    pallas_call x5, Pallas kernels, attention_backward(): pl.pallas_call(functools.partial(bwd_kernel, dirs, each, which, spans, ha...  110 us
    pallas_call x2, Pallas kernels, feed_forward(): pl.pallas_call(functools.partial(ffn_kernel, blocks, which, stream, spans...  64.5 us
    pallas_call x3, Pallas kernels, attention_forward(): pl.pallas_call(functools.partial(fwd_kernel, dirs, each, which, spans), g...  59.9 us
    pallas_call x13, Pallas kernels, add_up(): pl.pallas_call(functools.partial(add_kernel, plan, len(arrays)), grid=(AD...  40.5 us
    ppermute x50, starting transfers between devices, exchange(): return lax.ppermute(x, 'dp', [(i, i ^ 1 << stage) for i in range(n_dp)])  33.9 us
    ppermute x50, waiting for transfers between devices, exchange(): return lax.ppermute(x, 'dp', [(i, i ^ 1 << stage) for i in range(n_dp)])  32.9 us
    ppermute x20, starting transfers between devices, exchange(): return lax.ppermute(x, 'tensor', SWAP)  25.8 us
    ppermute x20, waiting for transfers between devices, exchange(): return lax.ppermute(x, 'tensor', SWAP)  18.6 us
  transfers between devices with their start and end apart: 74, of which 18 were waited for; matrix products, arithmetic and copies ran while one was open for 4% of the time, Pallas kernels for 62%

profile of v6, /device:TPU:0, one launch (start us, length us, event | category | flops | bytes accessed | tf_op | source)
XLA Modules:
  0.0 450.2 jit_solution(5423853033320439705)
XLA Ops:
  1.2 3.6 cut.2
  4.9 3.0 collective-permute-start
  7.9 5.7 %cut.3 = (bf16[768,384]{1,0:T(8,128)(2,1)}, bf16[768,384]{1,0:T(8,128)(2,1)}, bf16[768,384]{1,0:T(8,128)(2,1)}, bf16[768,384]{1,0:T(8,128)(2,1)}, bf16[1536,384]...) custom-call(s32[3]{0:T(128)} %pad_add_fusion.1.place.slot_ref, bf16[3,3,768,384]{3,2,1,0:T(8,128)(2,1)} %refs_5_.5, ...), custom_call_target="tpu_custom_call" | custom-call | flops 1 | bytes 1 | tf_op jit(solution)/shard_map/cut/pallas_call | solution.py:723
  14.9 6.6 %collective-permute-done.refs_5_.refs_10_.refs_7_.refs_11_ = bf16[768,384]{1,0:T(8,128)(2,1)S(1)} collective-permute-done((bf16[768,384]{1,0:T(8,128)(2,1)}, bf16[768,384]{1,0:T(8,128)(2,1)S(1)}, u32[]{:S(2)}, u32[]{:S(2)}) %collective-permute-start) | collective-permute-done | bytes 589856 | tf_op jit(solution)/shard_map/ppermute | solution.py:884
  21.4 1.7 collective-permute-start.3
  24.3 1.6 collective-permute-start.1
  26.7 9.3 %collective-permute-done.3.refs_6_.refs_11_.refs_8_.refs_12_ = bf16[768,384]{1,0:T(8,128)(2,1)S(1)} collective-permute-done((bf16[768,384]{1,0:T(8,128)(2,1)S(1)}, bf16[768,384]{1,0:T(8,128)(2,1)S(1)}, u32[]{:S(2)}, u32[]{:S(2)}) %collective-permute-start.3) | collective-permute-done | bytes 589856 | tf_op jit(solution)/shard_map/ppermute | solution.py:885
  38.6 1.8 collective-permute-done.1.refs_1_.refs_5_
  40.4 1.5 collective-permute-start.2
  44.1 28.4 %attention_forward.3 = (bf16[896,768]{1,0:T(8,128)(2,1)}, bf16[896,768]{1,0:T(8,128)(2,1)}, bf16[896,768]{1,0:T(8,128)(2,1)}, bf16[896,768]{1,0:T(8,128)(2,1)}, ...) custom-call(s32[3]{0:T(128)} %pad_add_fusion.1.place.slot_ref, ...), custom_call_target="tpu_custom_call" | custom-call | flops 99999997952 | bytes 1 | tf_op jit(solution)/shard_map/attention_forward/pallas_call | solution.py:218
  72.5 1.6 collective-permute-start.8
  74.1 1.5 collective-permute-start.10
  76.2 9.8 %collective-permute-done.8.refs_5_.w1.refs_7_.refs_11_ = bf16[768,384]{1,0:T(8,128)(2,1)S(1)} collective-permute-done((bf16[768,384]{1,0:T(8,128)(2,1)S(1)}, bf16[768,384]{1,0:T(8,128)(2,1)S(1)}, u32[]{:S(2)}, u32[]{:S(2)}) %collective-permute-start.8) | collective-permute-done | bytes 589856 | tf_op jit(solution)/shard_map/ppermute | solution.py:885
  87.3 1.5 collective-permute-start.13
  90.6 12.5 %attention_forward.4 = (bf16[320,768]{1,0:T(8,128)(2,1)}, bf16[320,768]{1,0:T(8,128)(2,1)}, bf16[320,768]{1,0:T(8,128)(2,1)}, bf16[320,768]{1,0:T(8,128)(2,1)}, bf16[12,320,320]{2,1,0:T(8,128)(2,1)}) custom-call(s32[3]{0:T(128)} %pad_add_fusion.1.place.slot_ref, bf16[320,768]{1,0:T(8,128)(2,1)} %get-tuple-element.221.refs_0_.refs_2_, ...), custom_call_target="tpu_custom_call" | custom-call | flops 99999997952 | bytes 1 | tf_op jit(solution)/shard_map/attention_forward/pallas_call | solution.py:218
  104.0 1.4 collective-permute-start.20
  106.8 26.4 %feed_forward.2 = (bf16[160,768]{1,0:T(8,128)(2,1)}, bf16[160,768]{1,0:T(8,128)(2,1)}, f32[320,768]{1,0:T(8,128)}, bf16[320,768]{1,0:T(8,128)(2,1)}, f32[4,768]{...) custom-call(s32[3]{0:T(128)} %pad_add_fusion.1.place.slot_ref, ...), custom_call_target="tpu_custom_call" | custom-call | flops 99999997952 | bytes 1 | tf_op jit(solution)/shard_map/feed_forward/pallas_call | solution.py:358
  134.1 1.5 collective-permute-start.24
  136.1 22.2 %attention_backward.5 = (f32[320,768]{1,0:T(8,128)}, bf16[320,768]{1,0:T(8,128)(2,1)}, f32[2,768]{1,0:T(2,128)}, bf16[768,1536]{1,0:T(8,128)(2,1)}, bf16[768,1536]{1,0:T(8,128)(2,1)}) custom-call(s32[3]{0:T(128)} %pad_add_fusion.1.place.slot_ref, bf16[320,768]{1,0:T(8,128)(2,1)} %get-tuple-element.240.refs_0_, f32[320,768]{1,0:T(8,128)} %get-tuple-element.241.refs_1_, ...), custom_call_target="tpu_custom_call" | custom-call | flops 99999997952 | bytes 1 | tf_op jit(solution)/shard_map/attention_backward/pallas_call | solution.py:644
  158.4 1.6 collective-permute-start.18
  160.0 1.7 collective-permute-done.19.u0.d0
  163.3 3.7 collective-permute-done.18
  167.0 1.5 collective-permute-start.23
  168.6 1.5 collective-permute-start.22
  170.2 19.1 %attention_forward.5 = (bf16[576,768]{1,0:T(8,128)(2,1)}, bf16[576,768]{1,0:T(8,128)(2,1)}, bf16[576,768]{1,0:T(8,128)(2,1)}, bf16[576,768]{1,0:T(8,128)(2,1)}, bf16[12,576,576]{2,1,0:T(8,128)(2,1)}) custom-call(s32[3]{0:T(128)} %pad_add_fusion.1.place.slot_ref, bf16[576,768]{1,0:T(8,128)(2,1)} %get-tuple-element.255.refs_0_.refs_2_, ...), custom_call_target="tpu_custom_call" | custom-call | flops 99999997952 | bytes 1 | tf_op jit(solution)/shard_map/attention_forward/pallas_call | solution.py:218
  191.2 4.7 %add_up.13 = (bf16[384,1536]{1,0:T(8,128)(2,1)}, bf16[384,1536]{1,0:T(8,128)(2,1)}, bf16[384,1536]{1,0:T(8,128)(2,1)}) custom-call(bf16[1536,1536]{1,0:T(8,128)(2,1)} %get-tuple-element.267.refs_0_.refs_2_.refs_4_.refs_3_.refs_6_.refs_10_.refs_11_.refs_16_, bf16[1536,1536]{1,0:T(8,128)(2,1)} %copy-done, ...), custom_call_target="tpu_custom_call" | custom-call | flops 1 | bytes 1 | tf_op jit(solution)/shard_map/add_up/pallas_call | solution.py:768
  197.0 1.5 collective-permute-start.34
  199.5 38.2 %feed_forward.3 = (bf16[288,768]{1,0:T(8,128)(2,1)}, bf16[288,768]{1,0:T(8,128)(2,1)}, f32[576,768]{1,0:T(8,128)}, bf16[576,768]{1,0:T(8,128)(2,1)}, f32[4,768]{...) custom-call(s32[3]{0:T(128)} %pad_add_fusion.1.place.slot_ref, ...), custom_call_target="tpu_custom_call" | custom-call | flops 99999997952 | bytes 1 | tf_op jit(solution)/shard_map/feed_forward/pallas_call | solution.py:358
  241.9 3.0 add_up.14
  244.9 1.5 collective-permute-start.37
  246.4 1.5 collective-permute-start.36
  247.9 20.3 %attention_backward.6 = (f32[576,768]{1,0:T(8,128)}, bf16[768,576]{1,0:T(8,128)(2,1)}, bf16[768,576]{1,0:T(8,128)(2,1)}, bf16[384,1536]{1,0:T(8,128)(2,1)}, bf16[384,1536]{1,0:T(8,128)(2,1)}) custom-call(s32[3]{0:T(128)} %pad_add_fusion.1.place.slot_ref, bf16[576,768]{1,0:T(8,128)(2,1)} %get-tuple-element.280.refs_0_, ...), custom_call_target="tpu_custom_call" | custom-call | flops 99999997952 | bytes 1 | tf_op jit(solution)/shard_map/attention_backward/pallas_call | solution.py:644
  269.4 1.4 copy-done.1
  270.8 4.5 add_up.15
  276.5 1.4 collective-permute-start.43
  277.9 19.4 %attention_backward.7 = (f32[576,768]{1,0:T(8,128)}, bf16[576,768]{1,0:T(8,128)(2,1)}, f32[2,768]{1,0:T(2,128)}, bf16[384,1536]{1,0:T(8,128)(2,1)}, bf16[384,1536]{1,0:T(8,128)(2,1)}) custom-call(s32[3]{0:T(128)} %pad_add_fusion.1.place.slot_ref, bf16[576,768]{1,0:T(8,128)(2,1)} %get-tuple-element.280.refs_0_, f32[576,768]{1,0:T(8,128)} %get-tuple-element.289.refs_1_, ...), custom_call_target="tpu_custom_call" | custom-call | flops 99999997952 | bytes 1 | tf_op jit(solution)/shard_map/attention_backward/pallas_call | solution.py:644
  297.9 6.0 %collective-permute-done.48.refs_9_.refs_6_.refs_7_.refs_8_ = bf16[384,1536]{1,0:T(8,128)(2,1)S(1)} collective-permute-done((bf16[384,1536]{1,0:T(8,128)(2,1)}, bf16[384,1536]{1,0:T(8,128)(2,1)S(1)}, u32[]{:S(2)}, u32[]{:S(2)}) %collective-permute-start.48) | collective-permute-done | bytes 1179680 | tf_op jit(solution)/shard_map/ppermute | solution.py:885
  305.6 4.6 %add_up.16 = (bf16[384,1536]{1,0:T(8,128)(2,1)}, bf16[384,1536]{1,0:T(8,128)(2,1)}, bf16[96,1536]{1,0:T(8,128)(2,1)}) custom-call(bf16[384,1536]{1,0:T(8,128)(2,1)} %get-tuple-element.294.refs_0_, bf16[384,1536]{1,0:T(8,128)(2,1)} %collective-permute-done.42.refs_1_, ...), custom_call_target="tpu_custom_call" | custom-call | flops 1 | bytes 1 | tf_op jit(solution)/shard_map/add_up/pallas_call | solution.py:768
  310.2 2.7 collective-permute-start.47
  312.8 1.5 collective-permute-start.46
  314.3 1.4 collective-permute-start.45
  315.7 25.5 %attention_backward.8 = (f32[896,768]{1,0:T(8,128)}, bf16[768,896]{1,0:T(8,128)(2,1)}, bf16[768,896]{1,0:T(8,128)(2,1)}, bf16[384,768]{1,0:T(8,128)(2,1)}, bf16[...) custom-call(s32[3]{0:T(128)} %pad_add_fusion.1.place.slot_ref, ...), custom_call_target="tpu_custom_call" | custom-call | flops 99999997952 | bytes 1 | tf_op jit(solution)/shard_map/attention_backward/pallas_call | solution.py:644
  343.2 3.9 add_up.17
  350.1 22.9 %attention_backward.9 = (f32[448,768]{1,0:T(8,128)}, bf16[448,768]{1,0:T(8,128)(2,1)}, bf16[384,768]{1,0:T(8,128)(2,1)}, bf16[384,768]{1,0:T(8,128)(2,1)}, bf16[...) custom-call(s32[3]{0:T(128)} %pad_add_fusion.1.place.slot_ref, bf16[320,768]{1,0:T(8,128)(2,1)} %get-tuple-element.308.refs_0_, ...), custom_call_target="tpu_custom_call" | custom-call | flops 99999997952 | bytes 1 | tf_op jit(solution)/shard_map/attention_backward/pallas_call | solution.py:644
  376.4 3.1 add_up.18
  381.4 2.6 add_up.19
  384.0 1.4 collective-permute-start.59
  385.4 1.4 collective-permute-start.58
  387.7 2.2 maximum_select_fusion.2
  390.7 2.6 collective-permute-start.61
  393.4 4.9 %collective-permute-done.60.refs_4_.refs_9_.refs_10_.refs_16_ = bf16[192,1536]{1,0:T(8,128)(2,1)S(1)} collective-permute-done((bf16[192,1536]{1,0:T(8,128)(2,1)}, bf16[192,1536]{1,0:T(8,128)(2,1)S(1)}, u32[]{:S(2)}, u32[]{:S(2)}) %collective-permute-start.60) | collective-permute-done | bytes 589856 | tf_op jit(solution)/shard_map/ppermute | solution.py:885
  399.1 2.2 add_up.22
  401.3 2.8 collective-permute-done.62.refs_17_
  404.1 2.7 collective-permute-start.66
  406.8 2.4 add_up.20
  411.3 1.5 collective-permute-start.71
  412.9 2.7 add_up.24
  419.5 2.2 add_up.21
  421.8 3.5 collective-permute-start.69
  426.2 2.6 add_up.25
  428.9 1.9 pad_maximum_fusion.2
  430.8 2.4 collective-permute-start.73
  434.3 6.2 %collective-permute-done.73 = f32[10,768]{1,0:T(8,128)S(1)} collective-permute-done((f32[10,768]{1,0:T(8,128)S(1)}, f32[10,768]{1,0:T(8,128)S(1)}, u32[]{:S(2)}, u32[]{:S(2)}) %collective-permute-start.73) | collective-permute-done | bytes 30752 | tf_op jit(solution)/shard_map/ppermute | solution.py:888
  442.6 1.9 add_up.23
  (327 shorter events, 58.3 us)
Async XLA Ops:
  4.9 16.6 %collective-permute-start = (bf16[768,384]{1,0:T(8,128)(2,1)}, bf16[768,384]{1,0:T(8,128)(2,1)S(1)}, u32[]{:S(2)}, u32[]{:S(2)}) collective-permute-start(bf16[768,384]{1,0:T(8,128)(2,1)} %get-tuple-element.201), channel_id=1, source_target_pairs={{0,1},{1,0},{2,3},{3,2},{4,5},{5,4},{6,7},{7,6},{8,9},{9,8},{10,11... | collective-permute-start | bytes 1769480 | tf_op jit(solution)/shard_map/ppermute | solution.py:884
  21.4 14.5 %collective-permute-start.3 = (bf16[768,384]{1,0:T(8,128)(2,1)S(1)}, bf16[768,384]{1,0:T(8,128)(2,1)S(1)}, u32[]{:S(2)}, u32[]{:S(2)}) collective-permute-start(bf16[768,384]{1,0:T(8,128)(2,1)S(1)} %collective-permute-done.refs_5_.refs_10_.refs_7_.refs_11_), channel_id=1, source_target_pairs={{0,4},{2,6},{4,0},{6,2},{8,12},{10,14},{12,8},{14,10},{16,20},{18,... | collective-permute-start | bytes 1769480 | tf_op jit(solution)/shard_map/ppermute | solution.py:885
  24.3 16.1 %collective-permute-start.1 = (bf16[448,768]{1,0:T(8,128)(2,1)S(1)}, bf16[448,768]{1,0:T(8,128)(2,1)S(1)}, u32[]{:S(2)}, u32[]{:S(2)}) collective-permute-start(bf16[448,768]{1,0:T(8,128)(2,1)S(1)} %copy-done.57), channel_id=1, source_target_pairs={{0,1},{1,0},{2,3},{3,2},{4,5},{5,4},{6,7},{7,6},{8,9},{9,8},{10,11... | collective-permute-start | bytes 2064392 | tf_op jit(solution)/shard_map/ppermute | solution.py:884
  26.7 15.7 %collective-permute-start.4 = (bf16[768,384]{1,0:T(8,128)(2,1)S(1)}, bf16[768,384]{1,0:T(8,128)(2,1)S(1)}, u32[]{:S(2)}, u32[]{:S(2)}) collective-permute-start(bf16[768,384]{1,0:T(8,128)(2,1)S(1)} %collective-permute-done.refs_5_.refs_10_.refs_7_.refs_11_), channel_id=1, source_target_pairs={{0,2},{2,0},{4,6},{6,4},{8,10},{10,8},{12,14},{14,12},{16,18},{18,... | collective-permute-start | bytes 1769480 | tf_op jit(solution)/shard_map/ppermute | solution.py:885
  40.4 35.3 %collective-permute-start.2 = (bf16[768,384]{1,0:T(8,128)(2,1)S(1)}, bf16[768,384]{1,0:T(8,128)(2,1)S(1)}, u32[]{:S(2)}, u32[]{:S(2)}) collective-permute-start(bf16[768,384]{1,0:T(8,128)(2,1)S(1)} %copy-done.68), channel_id=1, source_target_pairs={{0,1},{1,0},{2,3},{3,2},{4,5},{5,4},{6,7},{7,6},{8,9},{9,8},{10,11... | collective-permute-start | bytes 1769480 | tf_op jit(solution)/shard_map/ppermute | solution.py:884
  41.9 30.6 %collective-permute-start.7 = (bf16[768,384]{1,0:T(8,128)(2,1)S(1)}, bf16[768,384]{1,0:T(8,128)(2,1)S(1)}, u32[]{:S(2)}, u32[]{:S(2)}) collective-permute-start(bf16[768,384]{1,0:T(8,128)(2,1)S(1)} %copy-done.70), channel_id=1, source_target_pairs={{0,1},{1,0},{2,3},{3,2},{4,5},{5,4},{6,7},{7,6},{8,9},{9,8},{10,11... | collective-permute-start | bytes 1769480 | tf_op jit(solution)/shard_map/ppermute | solution.py:884
  72.5 13.5 %collective-permute-start.8 = (bf16[768,384]{1,0:T(8,128)(2,1)S(1)}, bf16[768,384]{1,0:T(8,128)(2,1)S(1)}, u32[]{:S(2)}, u32[]{:S(2)}) collective-permute-start(bf16[768,384]{1,0:T(8,128)(2,1)S(1)} %collective-permute-done.7.refs_4_.w0.refs_6_.refs_10_), channel_id=1, source_target_pairs={{0,8},{2,10},{4,12},{6,14},{8,0},{10,2},{12,4},{14,6},{16,24},{18,... | collective-permute-start | bytes 1769480 | tf_op jit(solution)/shard_map/ppermute | solution.py:885
  74.1 13.1 %collective-permute-start.10 = (bf16[768,384]{1,0:T(8,128)(2,1)S(1)}, bf16[768,384]{1,0:T(8,128)(2,1)S(1)}, u32[]{:S(2)}, u32[]{:S(2)}) collective-permute-start(bf16[768,384]{1,0:T(8,128)(2,1)S(1)} %copy-done.64), channel_id=1, source_target_pairs={{0,1},{1,0},{2,3},{3,2},{4,5},{5,4},{6,7},{7,6},{8,9},{9,8},{10,11... | collective-permute-start | bytes 1769480 | tf_op jit(solution)/shard_map/ppermute | solution.py:884
  75.7 13.1 %collective-permute-start.6 = (bf16[768,384]{1,0:T(8,128)(2,1)S(1)}, bf16[768,384]{1,0:T(8,128)(2,1)S(1)}, u32[]{:S(2)}, u32[]{:S(2)}) collective-permute-start(bf16[768,384]{1,0:T(8,128)(2,1)S(1)} %collective-permute-done.2.u0), channel_id=1, source_target_pairs={{0,4},{2,6},{4,0},{6,2},{8,12},{10,14},{12,8},{14,10},{16,20},{18,... | collective-permute-start | bytes 1769480 | tf_op jit(solution)/shard_map/ppermute | solution.py:885
  76.2 13.0 %collective-permute-start.11 = (bf16[768,384]{1,0:T(8,128)(2,1)S(1)}, bf16[768,384]{1,0:T(8,128)(2,1)S(1)}, u32[]{:S(2)}, u32[]{:S(2)}) collective-permute-start(bf16[768,384]{1,0:T(8,128)(2,1)S(1)} %collective-permute-done.7.refs_4_.w0.refs_6_.refs_10_), channel_id=1, source_target_pairs={{0,2},{2,0},{4,6},{6,4},{8,10},{10,8},{12,14},{14,12},{16,18},{18,... | collective-permute-start | bytes 1769480 | tf_op jit(solution)/shard_map/ppermute | solution.py:885
  87.3 16.7 %collective-permute-start.13 = (bf16[448,768]{1,0:T(8,128)(2,1)S(1)}, bf16[448,768]{1,0:T(8,128)(2,1)S(1)}, u32[]{:S(2)}, u32[]{:S(2)}) collective-permute-start(bf16[448,768]{1,0:T(8,128)(2,1)S(1)} %copy-done.56), channel_id=1, source_target_pairs={{0,1},{1,0},{2,3},{3,2},{4,5},{5,4},{6,7},{7,6},{8,9},{9,8},{10,11... | collective-permute-start | bytes 2064392 | tf_op jit(solution)/shard_map/ppermute | solution.py:884
  88.8 14.3 %collective-permute-start.15 = (bf16[768,384]{1,0:T(8,128)(2,1)S(1)}, bf16[768,384]{1,0:T(8,128)(2,1)S(1)}, u32[]{:S(2)}, u32[]{:S(2)}) collective-permute-start(bf16[768,384]{1,0:T(8,128)(2,1)S(1)} %collective-permute-done.10.d0), channel_id=1, source_target_pairs={{0,8},{2,10},{4,12},{6,14},{8,0},{10,2},{12,4},{14,6},{16,24},{18,... | collective-permute-start | bytes 1769480 | tf_op jit(solution)/shard_map/ppermute | solution.py:885
  89.2 16.2 %collective-permute-start.14 = (bf16[768,384]{1,0:T(8,128)(2,1)S(1)}, bf16[768,384]{1,0:T(8,128)(2,1)S(1)}, u32[]{:S(2)}, u32[]{:S(2)}) collective-permute-start(bf16[768,384]{1,0:T(8,128)(2,1)S(1)} %collective-permute-done.2.u0), channel_id=1, source_target_pairs={{0,2},{2,0},{4,6},{6,4},{8,10},{10,8},{12,14},{14,12},{16,18},{18,... | collective-permute-start | bytes 1769480 | tf_op jit(solution)/shard_map/ppermute | solution.py:885
  89.2 16.2 %collective-permute-start.9 = (bf16[768,384]{1,0:T(8,128)(2,1)S(1)}, bf16[768,384]{1,0:T(8,128)(2,1)S(1)}, u32[]{:S(2)}, u32[]{:S(2)}) collective-permute-start(bf16[768,384]{1,0:T(8,128)(2,1)S(1)} %collective-permute-done.6.u1), channel_id=1, source_target_pairs={{0,2},{2,0},{4,6},{6,4},{8,10},{10,8},{12,14},{14,12},{16,18},{18,... | collective-permute-start | bytes 1769480 | tf_op jit(solution)/shard_map/ppermute | solution.py:885
  104.0 30.2 %collective-permute-start.20 = (bf16[768,384]{1,0:T(8,128)(2,1)S(1)}, bf16[768,384]{1,0:T(8,128)(2,1)}, u32[]{:S(2)}, u32[]{:S(2)}) collective-permute-start(bf16[768,384]{1,0:T(8,128)(2,1)S(1)} %copy-done.62), channel_id=1, source_target_pairs={{0,1},{1,0},{2,3},{3,2},{4,5},{5,4},{6,7},{7,6},{8,9},{9,8},{10,11... | collective-permute-start | bytes 1769480 | tf_op jit(solution)/shard_map/ppermute | solution.py:884
  133.5 28.2 %collective-permute-start.19 = (bf16[1536,384]{1,0:T(8,128)(2,1)S(1)}, bf16[1536,384]{1,0:T(8,128)(2,1)S(1)}, u32[]{:S(2)}, u32[]{:S(2)}) collective-permute-start(bf16[1536,384]{1,0:T(8,128)(2,1)S(1)} %copy-done.53), channel_id=1, source_target_pairs={{0,1},{1,0},{2,3},{3,2},{4,5},{5,4},{6,7},{7,6},{8,9},{9,8},{10,11... | collective-permute-start | bytes 3538952 | tf_op jit(solution)/shard_map/ppermute | solution.py:884
  134.1 24.2 %collective-permute-start.24 = (bf16[768,384]{1,0:T(8,128)(2,1)}, bf16[768,384]{1,0:T(8,128)(2,1)}, u32[]{:S(2)}, u32[]{:S(2)}) collective-permute-start(bf16[768,384]{1,0:T(8,128)(2,1)} %collective-permute-done.20.refs_4_.w0.refs_8_), channel_id=1, source_target_pairs={{0,8},{2,10},{4,12},{6,14},{8,0},{10,2},{12,4},{14,6},{16,24},{18,... | collective-permute-start | bytes 1769480 | tf_op jit(solution)/shard_map/ppermute | solution.py:885
  135.6 34.4 %collective-permute-start.27 = (bf16[768,384]{1,0:T(8,128)(2,1)}, bf16[768,384]{1,0:T(8,128)(2,1)}, u32[]{:S(2)}, u32[]{:S(2)}) collective-permute-start(bf16[768,384]{1,0:T(8,128)(2,1)} %collective-permute-done.20.refs_4_.w0.refs_8_), channel_id=1, source_target_pairs={{0,2},{2,0},{4,6},{6,4},{8,10},{10,8},{12,14},{14,12},{16,18},{18,... | collective-permute-start | bytes 1769480 | tf_op jit(solution)/shard_map/ppermute | solution.py:885
  135.6 32.9 %collective-permute-start.26 = (bf16[1536,1536]{1,0:T(8,128)(2,1)}, bf16[1536,1536]{1,0:T(8,128)(2,1)S(1)}, u32[]{:S(2)}, u32[]{:S(2)}) collective-permute-start(bf16[1536,1536]{1,0:T(8,128)(2,1)} %get-tuple-element.253), channel_id=1, source_target_pairs={{0,2},{2,0},{4,6},{6,4},{8,10},{10,8},{12,14},{14,12},{16,18},{18,... | collective-permute-start | bytes 14155784 | tf_op jit(solution)/shard_map/ppermute | solution.py:885
  158.4 11.8 %collective-permute-start.28 = (bf16[768,384]{1,0:T(8,128)(2,1)}, bf16[768,384]{1,0:T(8,128)(2,1)}, u32[]{:S(2)}, u32[]{:S(2)}) collective-permute-start(bf16[768,384]{1,0:T(8,128)(2,1)} %collective-permute-done.24.refs_5_.w1.refs_9_), channel_id=1, source_target_pairs={{0,2},{2,0},{4,6},{6,4},{8,10},{10,8},{12,14},{14,12},{16,18},{18,... | collective-permute-start | bytes 1769480 | tf_op jit(solution)/shard_map/ppermute | solution.py:885
  158.4 8.6 %collective-permute-start.18 = (bf16[160,768]{1,0:T(8,128)(2,1)}, bf16[160,768]{1,0:T(8,128)(2,1)S(1)}, u32[]{:S(2)}, u32[]{:S(2)}) collective-permute-start(bf16[160,768]{1,0:T(8,128)(2,1)} %get-tuple-element.235), channel_id=1, source_target_pairs={{0,1},{1,0},{2,3},{3,2},{4,5},{5,4},{6,7},{7,6},{8,9},{9,8},{10,11... | collective-permute-start | bytes 737288 | tf_op jit(solution)/shard_map/ppermute | solution.py:884
  163.1 26.8 %collective-permute-start.33 = (bf16[768,1536]{1,0:T(8,128)(2,1)}, bf16[768,1536]{1,0:T(8,128)(2,1)S(1)}, u32[]{:S(2)}, u32[]{:S(2)}) collective-permute-start(bf16[768,1536]{1,0:T(8,128)(2,1)} %get-tuple-element.269), channel_id=1, source_target_pairs={{0,2},{2,0},{4,6},{6,4},{8,10},{10,8},{12,14},{14,12},{16,18},{18,... | collective-permute-start | bytes 7077896 | tf_op jit(solution)/shard_map/ppermute | solution.py:885
  167.0 22.2 %collective-permute-start.23 = (bf16[768,384]{1,0:T(8,128)(2,1)}, bf16[768,384]{1,0:T(8,128)(2,1)}, u32[]{:S(2)}, u32[]{:S(2)}) collective-permute-start(bf16[768,384]{1,0:T(8,128)(2,1)} %get-tuple-element.249), channel_id=1, source_target_pairs={{0,8},{2,10},{4,12},{6,14},{8,0},{10,2},{12,4},{14,6},{16,24},{18,... | collective-permute-start | bytes 1769480 | tf_op jit(solution)/shard_map/ppermute | solution.py:885
  168.6 21.2 %collective-permute-start.22 = (bf16[768,384]{1,0:T(8,128)(2,1)}, bf16[768,384]{1,0:T(8,128)(2,1)}, u32[]{:S(2)}, u32[]{:S(2)}) collective-permute-start(bf16[768,384]{1,0:T(8,128)(2,1)} %get-tuple-element.248), channel_id=1, source_target_pairs={{0,4},{2,6},{4,0},{6,2},{8,12},{10,14},{12,8},{14,10},{16,20},{18,... | collective-permute-start | bytes 1769480 | tf_op jit(solution)/shard_map/ppermute | solution.py:885
  170.1 26.9 %collective-permute-start.29 = (bf16[1536,384]{1,0:T(8,128)(2,1)S(1)}, bf16[1536,384]{1,0:T(8,128)(2,1)}, u32[]{:S(2)}, u32[]{:S(2)}) collective-permute-start(bf16[1536,384]{1,0:T(8,128)(2,1)S(1)} %collective-permute-done.19.u0.d0), channel_id=1, source_target_pairs={{0,2},{2,0},{4,6},{6,4},{8,10},{10,8},{12,14},{14,12},{16,18},{18,... | collective-permute-start | bytes 3538952 | tf_op jit(solution)/shard_map/ppermute | solution.py:885
  189.2 9.3 %collective-permute-start.31 = (bf16[768,384]{1,0:T(8,128)(2,1)}, bf16[768,384]{1,0:T(8,128)(2,1)S(1)}, u32[]{:S(2)}, u32[]{:S(2)}) collective-permute-start(bf16[768,384]{1,0:T(8,128)(2,1)} %collective-permute-done.23.d1), channel_id=1, source_target_pairs={{0,2},{2,0},{4,6},{6,4},{8,10},{10,8},{12,14},{14,12},{16,18},{18,... | collective-permute-start | bytes 1769480 | tf_op jit(solution)/shard_map/ppermute | solution.py:885
  189.8 8.7 %collective-permute-start.30 = (bf16[768,384]{1,0:T(8,128)(2,1)}, bf16[768,384]{1,0:T(8,128)(2,1)S(1)}, u32[]{:S(2)}, u32[]{:S(2)}) collective-permute-start(bf16[768,384]{1,0:T(8,128)(2,1)} %collective-permute-done.22.u1), channel_id=1, source_target_pairs={{0,2},{2,0},{4,6},{6,4},{8,10},{10,8},{12,14},{14,12},{16,18},{18,... | collective-permute-start | bytes 1769480 | tf_op jit(solution)/shard_map/ppermute | solution.py:885
  195.9 43.7 %collective-permute-start.40 = (bf16[384,1536]{1,0:T(8,128)(2,1)}, bf16[384,1536]{1,0:T(8,128)(2,1)S(1)}, u32[]{:S(2)}, u32[]{:S(2)}) collective-permute-start(bf16[384,1536]{1,0:T(8,128)(2,1)} %get-tuple-element.282), channel_id=1, source_target_pairs={{0,8},{2,10},{4,12},{6,14},{8,0},{10,2},{12,4},{14,6},{16,24},{18,... | collective-permute-start | bytes 3538952 | tf_op jit(solution)/shard_map/ppermute | solution.py:885
  196.4 43.2 %collective-permute-start.35 = (bf16[384,1536]{1,0:T(8,128)(2,1)}, bf16[384,1536]{1,0:T(8,128)(2,1)S(1)}, u32[]{:S(2)}, u32[]{:S(2)}) collective-permute-start(bf16[384,1536]{1,0:T(8,128)(2,1)} %get-tuple-element.273), channel_id=1, source_target_pairs={{0,4},{2,6},{4,0},{6,2},{8,12},{10,14},{12,8},{14,10},{16,20},{18,... | collective-permute-start | bytes 3538952 | tf_op jit(solution)/shard_map/ppermute | solution.py:885
  197.0 42.8 %collective-permute-start.34 = (bf16[384,1536]{1,0:T(8,128)(2,1)}, bf16[384,1536]{1,0:T(8,128)(2,1)S(1)}, u32[]{:S(2)}, u32[]{:S(2)}) collective-permute-start(bf16[384,1536]{1,0:T(8,128)(2,1)} %get-tuple-element.271), channel_id=1, source_target_pairs={{0,1},{1,0},{2,3},{3,2},{4,5},{5,4},{6,7},{7,6},{8,9},{9,8},{10,11... | collective-permute-start | bytes 3538952 | tf_op jit(solution)/shard_map/ppermute | solution.py:884
  237.7 30.6 %collective-permute-start.38 = (bf16[1536,1536]{1,0:T(8,128)(2,1)}, bf16[1536,1536]{1,0:T(8,128)(2,1)S(1)}, u32[]{:S(2)}, u32[]{:S(2)}) collective-permute-start(bf16[1536,1536]{1,0:T(8,128)(2,1)} %get-tuple-element.278), channel_id=1, source_target_pairs={{0,2},{2,0},{4,6},{6,4},{8,10},{10,8},{12,14},{14,12},{16,18},{18,... | collective-permute-start | bytes 14155784 | tf_op jit(solution)/shard_map/ppermute | solution.py:885
  239.1 29.2 %collective-permute-start.32 = (bf16[288,768]{1,0:T(8,128)(2,1)}, bf16[288,768]{1,0:T(8,128)(2,1)}, u32[]{:S(2)}, u32[]{:S(2)}) collective-permute-start(bf16[288,768]{1,0:T(8,128)(2,1)} %get-tuple-element.266), channel_id=1, source_target_pairs={{0,1},{1,0},{2,3},{3,2},{4,5},{5,4},{6,7},{7,6},{8,9},{9,8},{10,11... | collective-permute-start | bytes 1327112 | tf_op jit(solution)/shard_map/ppermute | solution.py:884
  244.9 23.4 %collective-permute-start.37 = (bf16[192,1536]{1,0:T(8,128)(2,1)}, bf16[192,1536]{1,0:T(8,128)(2,1)S(1)}, u32[]{:S(2)}, u32[]{:S(2)}) collective-permute-start(bf16[192,1536]{1,0:T(8,128)(2,1)} %get-tuple-element.277), channel_id=1, source_target_pairs={{0,1},{1,0},{2,3},{3,2},{4,5},{5,4},{6,7},{7,6},{8,9},{9,8},{10,11... | collective-permute-start | bytes 1769480 | tf_op jit(solution)/shard_map/ppermute | solution.py:884
  246.4 22.0 %collective-permute-start.36 = (bf16[192,1536]{1,0:T(8,128)(2,1)}, bf16[192,1536]{1,0:T(8,128)(2,1)S(1)}, u32[]{:S(2)}, u32[]{:S(2)}) collective-permute-start(bf16[192,1536]{1,0:T(8,128)(2,1)} %get-tuple-element.275), channel_id=1, source_target_pairs={{0,4},{2,6},{4,0},{6,2},{8,12},{10,14},{12,8},{14,10},{16,20},{18,... | collective-permute-start | bytes 1769480 | tf_op jit(solution)/shard_map/ppermute | solution.py:885
  268.2 36.3 %collective-permute-start.42 = (bf16[384,1536]{1,0:T(8,128)(2,1)}, bf16[384,1536]{1,0:T(8,128)(2,1)}, u32[]{:S(2)}, u32[]{:S(2)}) collective-permute-start(bf16[384,1536]{1,0:T(8,128)(2,1)} %get-tuple-element.295), channel_id=1, source_target_pairs={{0,2},{2,0},{4,6},{6,4},{8,10},{10,8},{12,14},{14,12},{16,18},{18,... | collective-permute-start | bytes 3538952 | tf_op jit(solution)/shard_map/ppermute | solution.py:885
  275.3 28.6 %collective-permute-start.48 = (bf16[384,1536]{1,0:T(8,128)(2,1)}, bf16[384,1536]{1,0:T(8,128)(2,1)S(1)}, u32[]{:S(2)}, u32[]{:S(2)}) collective-permute-start(bf16[384,1536]{1,0:T(8,128)(2,1)} %get-tuple-element.311), channel_id=1, source_target_pairs={{0,4},{2,6},{4,0},{6,2},{8,12},{10,14},{12,8},{14,10},{16,20},{18,... | collective-permute-start | bytes 3538952 | tf_op jit(solution)/shard_map/ppermute | solution.py:885
  275.9 21.6 %collective-permute-start.44 = (bf16[192,1536]{1,0:T(8,128)(2,1)}, bf16[192,1536]{1,0:T(8,128)(2,1)S(1)}, u32[]{:S(2)}, u32[]{:S(2)}) collective-permute-start(bf16[192,1536]{1,0:T(8,128)(2,1)} %get-tuple-element.300), channel_id=1, source_target_pairs={{0,8},{2,10},{4,12},{6,14},{8,0},{10,2},{12,4},{14,6},{16,24},{18,... | collective-permute-start | bytes 1769480 | tf_op jit(solution)/shard_map/ppermute | solution.py:885
  276.5 28.0 %collective-permute-start.43 = (bf16[384,1536]{1,0:T(8,128)(2,1)}, bf16[384,1536]{1,0:T(8,128)(2,1)S(1)}, u32[]{:S(2)}, u32[]{:S(2)}) collective-permute-start(bf16[384,1536]{1,0:T(8,128)(2,1)} %get-tuple-element.298), channel_id=1, source_target_pairs={{0,1},{1,0},{2,3},{3,2},{4,5},{5,4},{6,7},{7,6},{8,9},{9,8},{10,11... | collective-permute-start | bytes 3538952 | tf_op jit(solution)/shard_map/ppermute | solution.py:884
  297.4 43.9 %collective-permute-start.41 = (f32[2,768]{1,0:T(2,128)}, f32[2,768]{1,0:T(2,128)S(1)}, u32[]{:S(2)}, u32[]{:S(2)}) collective-permute-start(f32[2,768]{1,0:T(2,128)} %get-tuple-element.293), channel_id=1, source_target_pairs={{0,2},{2,0},{4,6},{6,4},{8,10},{10,8},{12,14},{14,12},{16,18},{18,... | collective-permute-start | bytes 18440 | tf_op jit(solution)/shard_map/ppermute | solution.py:885
  297.5 43.9 %collective-permute-start.51 = (bf16[384,1536]{1,0:T(8,128)(2,1)}, bf16[384,1536]{1,0:T(8,128)(2,1)S(1)}, u32[]{:S(2)}, u32[]{:S(2)}) collective-permute-start(bf16[384,1536]{1,0:T(8,128)(2,1)} %get-tuple-element.331), channel_id=1, source_target_pairs={{0,2},{2,0},{4,6},{6,4},{8,10},{10,8},{12,14},{14,12},{16,18},{18,... | collective-permute-start | bytes 3538952 | tf_op jit(solution)/shard_map/ppermute | solution.py:885
  310.2 31.1 %collective-permute-start.47 = (bf16[96,1536]{1,0:T(8,128)(2,1)}, bf16[96,1536]{1,0:T(8,128)(2,1)S(1)}, u32[]{:S(2)}, u32[]{:S(2)}) collective-permute-start(bf16[96,1536]{1,0:T(8,128)(2,1)} %get-tuple-element.306), channel_id=1, source_target_pairs={{0,16},{2,18},{4,20},{6,22},{8,24},{10,26},{12,28},{14,30},{16,0},... | collective-permute-start | bytes 884744 | tf_op jit(solution)/shard_map/ppermute | solution.py:885
  312.8 28.4 %collective-permute-start.46 = (bf16[384,1536]{1,0:T(8,128)(2,1)}, bf16[384,1536]{1,0:T(8,128)(2,1)S(1)}, u32[]{:S(2)}, u32[]{:S(2)}) collective-permute-start(bf16[384,1536]{1,0:T(8,128)(2,1)} %get-tuple-element.304), channel_id=1, source_target_pairs={{0,4},{2,6},{4,0},{6,2},{8,12},{10,14},{12,8},{14,10},{16,20},{18,... | collective-permute-start | bytes 3538952 | tf_op jit(solution)/shard_map/ppermute | solution.py:885
  314.3 27.0 %collective-permute-start.45 = (bf16[384,1536]{1,0:T(8,128)(2,1)}, bf16[384,1536]{1,0:T(8,128)(2,1)S(1)}, u32[]{:S(2)}, u32[]{:S(2)}) collective-permute-start(bf16[384,1536]{1,0:T(8,128)(2,1)} %get-tuple-element.302), channel_id=1, source_target_pairs={{0,1},{1,0},{2,3},{3,2},{4,5},{5,4},{6,7},{7,6},{8,9},{9,8},{10,11... | collective-permute-start | bytes 3538952 | tf_op jit(solution)/shard_map/ppermute | solution.py:884
  347.1 25.9 %collective-permute-start.55 = (bf16[96,1536]{1,0:T(8,128)(2,1)}, bf16[96,1536]{1,0:T(8,128)(2,1)S(1)}, u32[]{:S(2)}, u32[]{:S(2)}) collective-permute-start(bf16[96,1536]{1,0:T(8,128)(2,1)} %get-tuple-element.339), channel_id=1, source_target_pairs={{0,16},{2,18},{4,20},{6,22},{8,24},{10,26},{12,28},{14,30},{16,0},... | collective-permute-start | bytes 884744 | tf_op jit(solution)/shard_map/ppermute | solution.py:885
  347.5 26.0 %collective-permute-start.54 = (bf16[96,1536]{1,0:T(8,128)(2,1)}, bf16[96,1536]{1,0:T(8,128)(2,1)S(1)}, u32[]{:S(2)}, u32[]{:S(2)}) collective-permute-start(bf16[96,1536]{1,0:T(8,128)(2,1)} %get-tuple-element.337), channel_id=1, source_target_pairs={{0,8},{2,10},{4,12},{6,14},{8,0},{10,2},{12,4},{14,6},{16,24},{18,... | collective-permute-start | bytes 884744 | tf_op jit(solution)/shard_map/ppermute | solution.py:885
  348.2 25.5 %collective-permute-start.53 = (bf16[192,1536]{1,0:T(8,128)(2,1)}, bf16[192,1536]{1,0:T(8,128)(2,1)S(1)}, u32[]{:S(2)}, u32[]{:S(2)}) collective-permute-start(bf16[192,1536]{1,0:T(8,128)(2,1)} %get-tuple-element.335), channel_id=1, source_target_pairs={{0,1},{1,0},{2,3},{3,2},{4,5},{5,4},{6,7},{7,6},{8,9},{9,8},{10,11... | collective-permute-start | bytes 1769480 | tf_op jit(solution)/shard_map/ppermute | solution.py:884
  349.5 26.0 %collective-permute-start.52 = (bf16[192,1536]{1,0:T(8,128)(2,1)}, bf16[192,1536]{1,0:T(8,128)(2,1)S(1)}, u32[]{:S(2)}, u32[]{:S(2)}) collective-permute-start(bf16[192,1536]{1,0:T(8,128)(2,1)} %get-tuple-element.333), channel_id=1, source_target_pairs={{0,4},{2,6},{4,0},{6,2},{8,12},{10,14},{12,8},{14,10},{16,20},{18,... | collective-permute-start | bytes 1769480 | tf_op jit(solution)/shard_map/ppermute | solution.py:885
  373.0 7.4 %collective-permute-start.50 = (bf16[384,768]{1,0:T(8,128)(2,1)}, bf16[384,768]{1,0:T(8,128)(2,1)S(1)}, u32[]{:S(2)}, u32[]{:S(2)}) collective-permute-start(bf16[384,768]{1,0:T(8,128)(2,1)} %get-tuple-element.329), channel_id=1, source_target_pairs={{0,2},{2,0},{4,6},{6,4},{8,10},{10,8},{12,14},{14,12},{16,18},{18,... | collective-permute-start | bytes 1769480 | tf_op jit(solution)/shard_map/ppermute | solution.py:885
  373.6 10.3 %collective-permute-start.57 = (bf16[384,768]{1,0:T(8,128)(2,1)}, bf16[384,768]{1,0:T(8,128)(2,1)S(1)}, u32[]{:S(2)}, u32[]{:S(2)}) collective-permute-start(bf16[384,768]{1,0:T(8,128)(2,1)} %get-tuple-element.347), channel_id=1, source_target_pairs={{0,2},{2,0},{4,6},{6,4},{8,10},{10,8},{12,14},{14,12},{16,18},{18,... | collective-permute-start | bytes 1769480 | tf_op jit(solution)/shard_map/ppermute | solution.py:885
  379.5 18.8 %collective-permute-start.60 = (bf16[192,1536]{1,0:T(8,128)(2,1)}, bf16[192,1536]{1,0:T(8,128)(2,1)S(1)}, u32[]{:S(2)}, u32[]{:S(2)}) collective-permute-start(bf16[192,1536]{1,0:T(8,128)(2,1)} %get-tuple-element.351), channel_id=1, source_target_pairs={{0,8},{2,10},{4,12},{6,14},{8,0},{10,2},{12,4},{14,6},{16,24},{18,... | collective-permute-start | bytes 1769480 | tf_op jit(solution)/shard_map/ppermute | solution.py:885
  384.0 20.1 %collective-permute-start.59 = (bf16[384,768]{1,0:T(8,128)(2,1)}, bf16[384,768]{1,0:T(8,128)(2,1)S(1)}, u32[]{:S(2)}, u32[]{:S(2)}) collective-permute-start(bf16[384,768]{1,0:T(8,128)(2,1)} %get-tuple-element.350), channel_id=1, source_target_pairs={{0,4},{2,6},{4,0},{6,2},{8,12},{10,14},{12,8},{14,10},{16,20},{18,... | collective-permute-start | bytes 1769480 | tf_op jit(solution)/shard_map/ppermute | solution.py:885
  385.4 18.7 %collective-permute-start.58 = (bf16[384,768]{1,0:T(8,128)(2,1)}, bf16[384,768]{1,0:T(8,128)(2,1)S(1)}, u32[]{:S(2)}, u32[]{:S(2)}) collective-permute-start(bf16[384,768]{1,0:T(8,128)(2,1)} %get-tuple-element.348), channel_id=1, source_target_pairs={{0,1},{1,0},{2,3},{3,2},{4,5},{5,4},{6,7},{7,6},{8,9},{9,8},{10,11... | collective-permute-start | bytes 1769480 | tf_op jit(solution)/shard_map/ppermute | solution.py:884
  390.0 14.1 %collective-permute-start.62 = (bf16[48,1536]{1,0:T(8,128)(2,1)S(1)}, bf16[48,1536]{1,0:T(8,128)(2,1)S(1)}, u32[]{:S(2)}, u32[]{:S(2)}) collective-permute-start(bf16[48,1536]{1,0:T(8,128)(2,1)S(1)} %copy-done.81), channel_id=1, source_target_pairs={{0,1},{1,0},{2,3},{3,2},{4,5},{5,4},{6,7},{7,6},{8,9},{9,8},{10,11... | collective-permute-start | bytes 442376 | tf_op jit(solution)/shard_map/ppermute | solution.py:884
  390.7 13.4 %collective-permute-start.61 = (bf16[48,1536]{1,0:T(8,128)(2,1)S(1)}, bf16[48,1536]{1,0:T(8,128)(2,1)S(1)}, u32[]{:S(2)}, u32[]{:S(2)}) collective-permute-start(bf16[48,1536]{1,0:T(8,128)(2,1)S(1)} %copy-done.80), channel_id=1, source_target_pairs={{0,16},{2,18},{4,20},{6,22},{8,24},{10,26},{12,28},{14,30},{16,0},... | collective-permute-start | bytes 442376 | tf_op jit(solution)/shard_map/ppermute | solution.py:885
  398.3 13.0 %collective-permute-start.70 = (f32[10,768]{1,0:T(8,128)S(1)}, f32[10,768]{1,0:T(8,128)S(1)}, u32[]{:S(2)}, u32[]{:S(2)}) collective-permute-start(f32[10,768]{1,0:T(8,128)S(1)} %concatenate.39), channel_id=1, source_target_pairs={{0,1},{1,0},{2,3},{3,2},{4,5},{5,4},{6,7},{7,6},{8,9},{9,8},{10,11... | collective-permute-start | bytes 92168 | tf_op jit(solution)/shard_map/ppermute | solution.py:884
  404.1 14.5 %collective-permute-start.66 = (bf16[96,1536]{1,0:T(8,128)(2,1)}, bf16[96,1536]{1,0:T(8,128)(2,1)S(1)}, u32[]{:S(2)}, u32[]{:S(2)}) collective-permute-start(bf16[96,1536]{1,0:T(8,128)(2,1)} %add_up.22), channel_id=1, source_target_pairs={{0,16},{2,18},{4,20},{6,22},{8,24},{10,26},{12,28},{14,30},{16,0},... | collective-permute-start | bytes 884744 | tf_op jit(solution)/shard_map/ppermute | solution.py:885
  409.2 9.5 %collective-permute-start.65 = (bf16[192,768]{1,0:T(8,128)(2,1)}, bf16[192,768]{1,0:T(8,128)(2,1)S(1)}, u32[]{:S(2)}, u32[]{:S(2)}) collective-permute-start(bf16[192,768]{1,0:T(8,128)(2,1)} %get-tuple-element.360), channel_id=1, source_target_pairs={{0,1},{1,0},{2,3},{3,2},{4,5},{5,4},{6,7},{7,6},{8,9},{9,8},{10,11... | collective-permute-start | bytes 884744 | tf_op jit(solution)/shard_map/ppermute | solution.py:884
  410.6 8.1 %collective-permute-start.64 = (bf16[192,768]{1,0:T(8,128)(2,1)}, bf16[192,768]{1,0:T(8,128)(2,1)S(1)}, u32[]{:S(2)}, u32[]{:S(2)}) collective-permute-start(bf16[192,768]{1,0:T(8,128)(2,1)} %get-tuple-element.358), channel_id=1, source_target_pairs={{0,4},{2,6},{4,0},{6,2},{8,12},{10,14},{12,8},{14,10},{16,20},{18,... | collective-permute-start | bytes 884744 | tf_op jit(solution)/shard_map/ppermute | solution.py:885
  416.7 30.6 %collective-permute-start.63 = (bf16[448,768]{1,0:T(8,128)(2,1)}, bf16[448,768]{1,0:T(8,128)(2,1)S(1)}, u32[]{:S(2)}, u32[]{:S(2)}) collective-permute-start(bf16[448,768]{1,0:T(8,128)(2,1)} %get-tuple-element.354), channel_id=1, source_target_pairs={{0,1},{1,0},{2,3},{3,2},{4,5},{5,4},{6,7},{7,6},{8,9},{9,8},{10,11... | collective-permute-start | bytes 2064392 | tf_op jit(solution)/shard_map/ppermute | solution.py:884
  418.7 12.1 %collective-permute-start.72 = (f32[10,768]{1,0:T(8,128)S(1)}, f32[10,768]{1,0:T(8,128)S(1)}, u32[]{:S(2)}, u32[]{:S(2)}) collective-permute-start(f32[10,768]{1,0:T(8,128)S(1)} %add.148), channel_id=1, source_target_pairs={{0,8},{2,10},{4,12},{6,14},{8,0},{10,2},{12,4},{14,6},{16,24},{18,... | collective-permute-start | bytes 92168 | tf_op jit(solution)/shard_map/ppermute | solution.py:885
  421.8 19.4 %collective-permute-start.69 = (bf16[96,768]{1,0:T(8,128)(2,1)}, bf16[96,768]{1,0:T(8,128)(2,1)S(1)}, u32[]{:S(2)}, u32[]{:S(2)}) collective-permute-start(bf16[96,768]{1,0:T(8,128)(2,1)} %get-tuple-element.367), channel_id=1, source_target_pairs={{0,24},{2,26},{4,28},{6,30},{8,16},{10,18},{12,20},{14,22},{16,8},... | collective-permute-start | bytes 442376 | tf_op jit(solution)/shard_map/ppermute | solution.py:888
  425.2 16.0 %collective-permute-start.68 = (bf16[96,768]{1,0:T(8,128)(2,1)}, bf16[96,768]{1,0:T(8,128)(2,1)S(1)}, u32[]{:S(2)}, u32[]{:S(2)}) collective-permute-start(bf16[96,768]{1,0:T(8,128)(2,1)} %get-tuple-element.365), channel_id=1, source_target_pairs={{0,8},{2,10},{4,12},{6,14},{8,0},{10,2},{12,4},{14,6},{16,24},{18,... | collective-permute-start | bytes 442376 | tf_op jit(solution)/shard_map/ppermute | solution.py:888
  425.6 15.6 %collective-permute-start.67 = (bf16[96,768]{1,0:T(8,128)(2,1)}, bf16[96,768]{1,0:T(8,128)(2,1)S(1)}, u32[]{:S(2)}, u32[]{:S(2)}) collective-permute-start(bf16[96,768]{1,0:T(8,128)(2,1)} %get-tuple-element.363), channel_id=1, source_target_pairs={{0,16},{2,18},{4,20},{6,22},{8,24},{10,26},{12,28},{14,30},{16,0},... | collective-permute-start | bytes 442376 | tf_op jit(solution)/shard_map/ppermute | solution.py:888
  430.8 9.7 %collective-permute-start.73 = (f32[10,768]{1,0:T(8,128)S(1)}, f32[10,768]{1,0:T(8,128)S(1)}, u32[]{:S(2)}, u32[]{:S(2)}) collective-permute-start(f32[10,768]{1,0:T(8,128)S(1)} %add.149), channel_id=1, source_target_pairs={{0,16},{2,18},{4,20},{6,22},{8,24},{10,26},{12,28},{14,30},{16,0},... | collective-permute-start | bytes 92168 | tf_op jit(solution)/shard_map/ppermute | solution.py:888
  (92 other events, 578.5 us)

commit v7 on v6

--- a/solution.py
+++ b/solution.py
@@ -17,8 +17,8 @@
 PAIR = 2
 FAR = 2.0**30
 MIB = 1024 * 1024
-ATTENTION_VMEM = 56 * MIB
-FFN_VMEM = (56 * MIB, 56 * MIB)
+ATTENTION_VMEM = 61 * MIB
+FFN_VMEM = (61 * MIB, 61 * MIB)
 
 
 def dot(a, b):

time: 458 us -> 456 us (level)
    unnamed x170 -> x124, local copies, waits for them, and re-layouts: 16.9 us -> 13.5 us
  transfers between devices with their start and end apart: 74 -> 74, of which waited for: 18 -> 16; matrix products, arithmetic and copies ran while one was open for 4% -> 5% of each run, Pallas kernels for 62% -> 62%
where the time goes in v7:
time: 456 us; the launch traced here: 448 us
  Pallas kernels  285 us (62%)
  starting transfers between devices  64 us (14%)
  waiting for transfers between devices  55.3 us (12%)
  other arithmetic  22.4 us (5%)
  local copies, waits for them, and re-layouts  19.3 us (4%)
    pallas_call x5, Pallas kernels, attention_backward(): pl.pallas_call(functools.partial(bwd_kernel, dirs, each, which, spans, ha...  110 us
    pallas_call x2, Pallas kernels, feed_forward(): pl.pallas_call(functools.partial(ffn_kernel, blocks, which, stream, spans...  64.5 us
    pallas_call x3, Pallas kernels, attention_forward(): pl.pallas_call(functools.partial(fwd_kernel, dirs, each, which, spans), g...  60 us
    pallas_call x13, Pallas kernels, add_up(): pl.pallas_call(functools.partial(add_kernel, plan, len(arrays)), grid=(AD...  40.5 us
    ppermute x50, starting transfers between devices, exchange(): return lax.ppermute(x, 'dp', [(i, i ^ 1 << stage) for i in range(n_dp)])  34.6 us
    ppermute x50, waiting for transfers between devices, exchange(): return lax.ppermute(x, 'dp', [(i, i ^ 1 << stage) for i in range(n_dp)])  30.2 us
    ppermute x20, starting transfers between devices, exchange(): return lax.ppermute(x, 'tensor', SWAP)  24.8 us
    ppermute x20, waiting for transfers between devices, exchange(): return lax.ppermute(x, 'tensor', SWAP)  18.9 us
  transfers between devices with their start and end apart: 74, of which 16 were waited for; matrix products, arithmetic and copies ran while one was open for 5% of the time, Pallas kernels for 62%

profile of v7, /device:TPU:0, one launch (start us, length us, event | category | flops | bytes accessed | tf_op | source)
XLA Modules:
  0.0 447.6 jit_solution(17212485747906301806)
XLA Ops:
  1.3 3.6 cut.2
  4.9 3.0 collective-permute-start
  8.0 5.7 %cut.3 = (bf16[768,384]{1,0:T(8,128)(2,1)}, bf16[768,384]{1,0:T(8,128)(2,1)}, bf16[768,384]{1,0:T(8,128)(2,1)}, bf16[768,384]{1,0:T(8,128)(2,1)}, bf16[1536,384]...) custom-call(s32[3]{0:T(128)} %pad_add_fusion.1.place.slot_ref, bf16[3,3,768,384]{3,2,1,0:T(8,128)(2,1)} %refs_5_.5, ...), custom_call_target="tpu_custom_call" | custom-call | flops 1 | bytes 1 | tf_op jit(solution)/shard_map/cut/pallas_call | solution.py:723
  14.9 6.6 %collective-permute-done.refs_5_.refs_10_.refs_7_.refs_11_ = bf16[768,384]{1,0:T(8,128)(2,1)S(1)} collective-permute-done((bf16[768,384]{1,0:T(8,128)(2,1)}, bf16[768,384]{1,0:T(8,128)(2,1)S(1)}, u32[]{:S(2)}, u32[]{:S(2)}) %collective-permute-start) | collective-permute-done | bytes 589856 | tf_op jit(solution)/shard_map/ppermute | solution.py:884
  21.5 1.7 collective-permute-start.3
  24.3 1.5 collective-permute-start.1
  26.7 9.3 %collective-permute-done.3.refs_6_.refs_11_.refs_8_.refs_12_ = bf16[768,384]{1,0:T(8,128)(2,1)S(1)} collective-permute-done((bf16[768,384]{1,0:T(8,128)(2,1)S(1)}, bf16[768,384]{1,0:T(8,128)(2,1)S(1)}, u32[]{:S(2)}, u32[]{:S(2)}) %collective-permute-start.3) | collective-permute-done | bytes 589856 | tf_op jit(solution)/shard_map/ppermute | solution.py:885
  38.6 1.8 collective-permute-done.1.refs_1_.refs_5_
  40.4 1.5 collective-permute-start.2
  43.2 28.4 %attention_forward.3 = (bf16[896,768]{1,0:T(8,128)(2,1)}, bf16[896,768]{1,0:T(8,128)(2,1)}, bf16[896,768]{1,0:T(8,128)(2,1)}, bf16[896,768]{1,0:T(8,128)(2,1)}, ...) custom-call(s32[3]{0:T(128)} %pad_add_fusion.1.place.slot_ref, ...), custom_call_target="tpu_custom_call" | custom-call | flops 99999997952 | bytes 1 | tf_op jit(solution)/shard_map/attention_forward/pallas_call | solution.py:218
  71.7 1.6 collective-permute-start.8
  73.3 1.5 collective-permute-start.10
  75.4 10.0 %collective-permute-done.8.refs_5_.w1.refs_7_.refs_11_ = bf16[768,384]{1,0:T(8,128)(2,1)S(1)} collective-permute-done((bf16[768,384]{1,0:T(8,128)(2,1)}, bf16[768,384]{1,0:T(8,128)(2,1)S(1)}, u32[]{:S(2)}, u32[]{:S(2)}) %collective-permute-start.8) | collective-permute-done | bytes 589856 | tf_op jit(solution)/shard_map/ppermute | solution.py:885
  86.7 1.5 collective-permute-start.13
  90.3 12.5 %attention_forward.4 = (bf16[320,768]{1,0:T(8,128)(2,1)}, bf16[320,768]{1,0:T(8,128)(2,1)}, bf16[320,768]{1,0:T(8,128)(2,1)}, bf16[320,768]{1,0:T(8,128)(2,1)}, bf16[12,320,320]{2,1,0:T(8,128)(2,1)}) custom-call(s32[3]{0:T(128)} %pad_add_fusion.1.place.slot_ref, bf16[320,768]{1,0:T(8,128)(2,1)} %get-tuple-element.221.refs_0_.refs_2_, ...), custom_call_target="tpu_custom_call" | custom-call | flops 99999997952 | bytes 1 | tf_op jit(solution)/shard_map/attention_forward/pallas_call | solution.py:218
  106.9 26.4 %feed_forward.2 = (bf16[160,768]{1,0:T(8,128)(2,1)}, bf16[160,768]{1,0:T(8,128)(2,1)}, f32[320,768]{1,0:T(8,128)}, bf16[320,768]{1,0:T(8,128)(2,1)}, f32[4,768]{...) custom-call(s32[3]{0:T(128)} %pad_add_fusion.1.place.slot_ref, ...), custom_call_target="tpu_custom_call" | custom-call | flops 99999997952 | bytes 1 | tf_op jit(solution)/shard_map/feed_forward/pallas_call | solution.py:358
  134.4 1.5 collective-permute-start.24
  136.3 22.2 %attention_backward.5 = (f32[320,768]{1,0:T(8,128)}, bf16[320,768]{1,0:T(8,128)(2,1)}, f32[2,768]{1,0:T(2,128)}, bf16[768,1536]{1,0:T(8,128)(2,1)}, bf16[768,1536]{1,0:T(8,128)(2,1)}) custom-call(s32[3]{0:T(128)} %pad_add_fusion.1.place.slot_ref, bf16[320,768]{1,0:T(8,128)(2,1)} %get-tuple-element.240.refs_0_, f32[320,768]{1,0:T(8,128)} %get-tuple-element.241.refs_1_, ...), custom_call_target="tpu_custom_call" | custom-call | flops 99999997952 | bytes 1 | tf_op jit(solution)/shard_map/attention_backward/pallas_call | solution.py:644
  158.7 1.6 collective-permute-start.18
  160.3 1.5 collective-permute-done.19.u0.d0
  163.9 3.3 collective-permute-done.18
  168.6 1.5 collective-permute-start.22
  170.1 19.1 %attention_forward.5 = (bf16[576,768]{1,0:T(8,128)(2,1)}, bf16[576,768]{1,0:T(8,128)(2,1)}, bf16[576,768]{1,0:T(8,128)(2,1)}, bf16[576,768]{1,0:T(8,128)(2,1)}, bf16[12,576,576]{2,1,0:T(8,128)(2,1)}) custom-call(s32[3]{0:T(128)} %pad_add_fusion.1.place.slot_ref, bf16[576,768]{1,0:T(8,128)(2,1)} %get-tuple-element.255.refs_0_.refs_2_, ...), custom_call_target="tpu_custom_call" | custom-call | flops 99999997952 | bytes 1 | tf_op jit(solution)/shard_map/attention_forward/pallas_call | solution.py:218
  189.9 1.4 copy-done
  191.2 4.7 %add_up.13 = (bf16[384,1536]{1,0:T(8,128)(2,1)}, bf16[384,1536]{1,0:T(8,128)(2,1)}, bf16[384,1536]{1,0:T(8,128)(2,1)}) custom-call(bf16[1536,1536]{1,0:T(8,128)(2,1)} %get-tuple-element.267.refs_0_.refs_2_.refs_4_.refs_3_.refs_6_.refs_10_.refs_11_.refs_16_, ...), custom_call_target="tpu_custom_call" | custom-call | flops 1 | bytes 1 | tf_op jit(solution)/shard_map/add_up/pallas_call | solution.py:768
  197.1 1.5 collective-permute-start.34
  198.7 38.1 %feed_forward.3 = (bf16[288,768]{1,0:T(8,128)(2,1)}, bf16[288,768]{1,0:T(8,128)(2,1)}, f32[576,768]{1,0:T(8,128)}, bf16[576,768]{1,0:T(8,128)(2,1)}, f32[4,768]{...) custom-call(s32[3]{0:T(128)} %pad_add_fusion.1.place.slot_ref, ...), custom_call_target="tpu_custom_call" | custom-call | flops 99999997952 | bytes 1 | tf_op jit(solution)/shard_map/feed_forward/pallas_call | solution.py:358
  240.0 3.0 add_up.14
  243.0 1.4 collective-permute-start.37
  244.5 1.5 collective-permute-start.36
  246.0 20.3 %attention_backward.6 = (f32[576,768]{1,0:T(8,128)}, bf16[768,576]{1,0:T(8,128)(2,1)}, bf16[768,576]{1,0:T(8,128)(2,1)}, bf16[384,1536]{1,0:T(8,128)(2,1)}, bf16[384,1536]{1,0:T(8,128)(2,1)}) custom-call(s32[3]{0:T(128)} %pad_add_fusion.1.place.slot_ref, bf16[576,768]{1,0:T(8,128)(2,1)} %get-tuple-element.280.refs_0_, ...), custom_call_target="tpu_custom_call" | custom-call | flops 99999997952 | bytes 1 | tf_op jit(solution)/shard_map/attention_backward/pallas_call | solution.py:644
  267.4 4.5 %add_up.15 = (bf16[384,1536]{1,0:T(8,128)(2,1)}, bf16[384,1536]{1,0:T(8,128)(2,1)}, bf16[192,1536]{1,0:T(8,128)(2,1)}) custom-call(bf16[1536,1536]{1,0:T(8,128)(2,1)} %get-tuple-element.296.refs_0_.refs_2_.refs_4_.refs_3_.refs_7_.refs_8_.refs_5_.refs_6_, ...), custom_call_target="tpu_custom_call" | custom-call | flops 1 | bytes 1 | tf_op jit(solution)/shard_map/add_up/pallas_call | solution.py:768
  273.0 1.4 collective-permute-start.43
  274.4 19.4 %attention_backward.7 = (f32[576,768]{1,0:T(8,128)}, bf16[576,768]{1,0:T(8,128)(2,1)}, f32[2,768]{1,0:T(2,128)}, bf16[384,1536]{1,0:T(8,128)(2,1)}, bf16[384,1536]{1,0:T(8,128)(2,1)}) custom-call(s32[3]{0:T(128)} %pad_add_fusion.1.place.slot_ref, bf16[576,768]{1,0:T(8,128)(2,1)} %get-tuple-element.280.refs_0_, f32[576,768]{1,0:T(8,128)} %get-tuple-element.289.refs_1_, ...), custom_call_target="tpu_custom_call" | custom-call | flops 99999997952 | bytes 1 | tf_op jit(solution)/shard_map/attention_backward/pallas_call | solution.py:644
  294.4 6.2 %collective-permute-done.48.refs_9_.refs_6_.refs_7_.refs_8_ = bf16[384,1536]{1,0:T(8,128)(2,1)S(1)} collective-permute-done((bf16[384,1536]{1,0:T(8,128)(2,1)}, bf16[384,1536]{1,0:T(8,128)(2,1)S(1)}, u32[]{:S(2)}, u32[]{:S(2)}) %collective-permute-start.48) | collective-permute-done | bytes 1179680 | tf_op jit(solution)/shard_map/ppermute | solution.py:885
  302.1 4.6 %add_up.16 = (bf16[384,1536]{1,0:T(8,128)(2,1)}, bf16[384,1536]{1,0:T(8,128)(2,1)}, bf16[96,1536]{1,0:T(8,128)(2,1)}) custom-call(bf16[384,1536]{1,0:T(8,128)(2,1)} %get-tuple-element.294.refs_0_, bf16[384,1536]{1,0:T(8,128)(2,1)} %collective-permute-done.42.refs_1_, ...), custom_call_target="tpu_custom_call" | custom-call | flops 1 | bytes 1 | tf_op jit(solution)/shard_map/add_up/pallas_call | solution.py:768
  306.7 2.6 collective-permute-start.47
  309.4 1.5 collective-permute-start.46
  310.8 1.4 collective-permute-start.45
  312.3 25.6 %attention_backward.8 = (f32[896,768]{1,0:T(8,128)}, bf16[768,896]{1,0:T(8,128)(2,1)}, bf16[768,896]{1,0:T(8,128)(2,1)}, bf16[384,768]{1,0:T(8,128)(2,1)}, bf16[...) custom-call(s32[3]{0:T(128)} %pad_add_fusion.1.place.slot_ref, ...), custom_call_target="tpu_custom_call" | custom-call | flops 99999997952 | bytes 1 | tf_op jit(solution)/shard_map/attention_backward/pallas_call | solution.py:644
  339.4 4.0 add_up.17
  346.5 22.9 %attention_backward.9 = (f32[448,768]{1,0:T(8,128)}, bf16[448,768]{1,0:T(8,128)(2,1)}, bf16[384,768]{1,0:T(8,128)(2,1)}, bf16[384,768]{1,0:T(8,128)(2,1)}, bf16[...) custom-call(s32[3]{0:T(128)} %pad_add_fusion.1.place.slot_ref, bf16[320,768]{1,0:T(8,128)(2,1)} %get-tuple-element.308.refs_0_, ...), custom_call_target="tpu_custom_call" | custom-call | flops 99999997952 | bytes 1 | tf_op jit(solution)/shard_map/attention_backward/pallas_call | solution.py:644
  372.1 3.1 add_up.18
  376.6 2.6 add_up.19
  379.2 1.5 collective-permute-start.59
  380.7 1.4 collective-permute-start.58
  382.1 1.9 maximum_select_fusion.3
  384.8 2.3 maximum_select_fusion.2
  387.8 2.6 collective-permute-start.61
  390.4 2.0 collective-permute-done.60.refs_4_.refs_9_.refs_10_.refs_16_
  393.2 2.2 add_up.22
  395.4 4.0 collective-permute-done.62.refs_17_
  399.5 2.6 collective-permute-start.66
  402.1 2.3 add_up.20
  404.5 1.4 collective-permute-start.65
  407.6 1.6 collective-permute-start.71
  410.3 2.7 add_up.24
  415.7 1.6 collective-permute-start.72
  417.3 2.2 add_up.21
  421.1 2.9 collective-permute-start.67
  424.0 2.7 add_up.25
  426.7 1.9 pad_maximum_fusion.2
  429.9 6.1 %collective-permute-done.73 = f32[10,768]{1,0:T(8,128)S(1)} collective-permute-done((f32[10,768]{1,0:T(8,128)S(1)}, f32[10,768]{1,0:T(8,128)S(1)}, u32[]{:S(2)}, u32[]{:S(2)}) %collective-permute-start.73) | collective-permute-done | bytes 30752 | tf_op jit(solution)/shard_map/ppermute | solution.py:888
  438.0 1.9 add_up.23
  (281 shorter events, 58.6 us)
Async XLA Ops:
  4.9 16.6 %collective-permute-start = (bf16[768,384]{1,0:T(8,128)(2,1)}, bf16[768,384]{1,0:T(8,128)(2,1)S(1)}, u32[]{:S(2)}, u32[]{:S(2)}) collective-permute-start(bf16[768,384]{1,0:T(8,128)(2,1)} %get-tuple-element.201), channel_id=1, source_target_pairs={{0,1},{1,0},{2,3},{3,2},{4,5},{5,4},{6,7},{7,6},{8,9},{9,8},{10,11... | collective-permute-start | bytes 1769480 | tf_op jit(solution)/shard_map/ppermute | solution.py:884
  21.5 14.5 %collective-permute-start.3 = (bf16[768,384]{1,0:T(8,128)(2,1)S(1)}, bf16[768,384]{1,0:T(8,128)(2,1)S(1)}, u32[]{:S(2)}, u32[]{:S(2)}) collective-permute-start(bf16[768,384]{1,0:T(8,128)(2,1)S(1)} %collective-permute-done.refs_5_.refs_10_.refs_7_.refs_11_), channel_id=1, source_target_pairs={{0,4},{2,6},{4,0},{6,2},{8,12},{10,14},{12,8},{14,10},{16,20},{18,... | collective-permute-start | bytes 1769480 | tf_op jit(solution)/shard_map/ppermute | solution.py:885
  24.3 16.0 %collective-permute-start.1 = (bf16[448,768]{1,0:T(8,128)(2,1)S(1)}, bf16[448,768]{1,0:T(8,128)(2,1)S(1)}, u32[]{:S(2)}, u32[]{:S(2)}) collective-permute-start(bf16[448,768]{1,0:T(8,128)(2,1)S(1)} %copy-done.49), channel_id=1, source_target_pairs={{0,1},{1,0},{2,3},{3,2},{4,5},{5,4},{6,7},{7,6},{8,9},{9,8},{10,11... | collective-permute-start | bytes 2064392 | tf_op jit(solution)/shard_map/ppermute | solution.py:884
  26.6 15.7 %collective-permute-start.4 = (bf16[768,384]{1,0:T(8,128)(2,1)S(1)}, bf16[768,384]{1,0:T(8,128)(2,1)S(1)}, u32[]{:S(2)}, u32[]{:S(2)}) collective-permute-start(bf16[768,384]{1,0:T(8,128)(2,1)S(1)} %collective-permute-done.refs_5_.refs_10_.refs_7_.refs_11_), channel_id=1, source_target_pairs={{0,2},{2,0},{4,6},{6,4},{8,10},{10,8},{12,14},{14,12},{16,18},{18,... | collective-permute-start | bytes 1769480 | tf_op jit(solution)/shard_map/ppermute | solution.py:885
  36.0 7.2 %collective-permute-start.5 = (bf16[768,384]{1,0:T(8,128)(2,1)S(1)}, bf16[768,384]{1,0:T(8,128)(2,1)}, u32[]{:S(2)}, u32[]{:S(2)}) collective-permute-start(bf16[768,384]{1,0:T(8,128)(2,1)S(1)} %collective-permute-done.3.refs_6_.refs_11_.refs_8_.refs_12_), channel_id=1, source_target_pairs={{0,2},{2,0},{4,6},{6,4},{8,10},{10,8},{12,14},{14,12},{16,18},{18,... | collective-permute-start | bytes 1769480 | tf_op jit(solution)/shard_map/ppermute | solution.py:885
  40.4 34.5 %collective-permute-start.2 = (bf16[768,384]{1,0:T(8,128)(2,1)}, bf16[768,384]{1,0:T(8,128)(2,1)}, u32[]{:S(2)}, u32[]{:S(2)}) collective-permute-start(bf16[768,384]{1,0:T(8,128)(2,1)} %get-tuple-element.204), channel_id=1, source_target_pairs={{0,1},{1,0},{2,3},{3,2},{4,5},{5,4},{6,7},{7,6},{8,9},{9,8},{10,11... | collective-permute-start | bytes 1769480 | tf_op jit(solution)/shard_map/ppermute | solution.py:884
  41.9 29.8 %collective-permute-start.7 = (bf16[768,384]{1,0:T(8,128)(2,1)}, bf16[768,384]{1,0:T(8,128)(2,1)}, u32[]{:S(2)}, u32[]{:S(2)}) collective-permute-start(bf16[768,384]{1,0:T(8,128)(2,1)} %get-tuple-element.213), channel_id=1, source_target_pairs={{0,1},{1,0},{2,3},{3,2},{4,5},{5,4},{6,7},{7,6},{8,9},{9,8},{10,11... | collective-permute-start | bytes 1769480 | tf_op jit(solution)/shard_map/ppermute | solution.py:884
  71.7 13.7 %collective-permute-start.8 = (bf16[768,384]{1,0:T(8,128)(2,1)}, bf16[768,384]{1,0:T(8,128)(2,1)S(1)}, u32[]{:S(2)}, u32[]{:S(2)}) collective-permute-start(bf16[768,384]{1,0:T(8,128)(2,1)} %collective-permute-done.7.refs_4_.w0.refs_6_.refs_10_), channel_id=1, source_target_pairs={{0,8},{2,10},{4,12},{6,14},{8,0},{10,2},{12,4},{14,6},{16,24},{18,... | collective-permute-start | bytes 1769480 | tf_op jit(solution)/shard_map/ppermute | solution.py:885
  73.3 13.4 %collective-permute-start.10 = (bf16[768,384]{1,0:T(8,128)(2,1)}, bf16[768,384]{1,0:T(8,128)(2,1)}, u32[]{:S(2)}, u32[]{:S(2)}) collective-permute-start(bf16[768,384]{1,0:T(8,128)(2,1)} %get-tuple-element.219), channel_id=1, source_target_pairs={{0,1},{1,0},{2,3},{3,2},{4,5},{5,4},{6,7},{7,6},{8,9},{9,8},{10,11... | collective-permute-start | bytes 1769480 | tf_op jit(solution)/shard_map/ppermute | solution.py:884
  74.8 13.4 %collective-permute-start.6 = (bf16[768,384]{1,0:T(8,128)(2,1)}, bf16[768,384]{1,0:T(8,128)(2,1)}, u32[]{:S(2)}, u32[]{:S(2)}) collective-permute-start(bf16[768,384]{1,0:T(8,128)(2,1)} %collective-permute-done.2.u0), channel_id=1, source_target_pairs={{0,4},{2,6},{4,0},{6,2},{8,12},{10,14},{12,8},{14,10},{16,20},{18,... | collective-permute-start | bytes 1769480 | tf_op jit(solution)/shard_map/ppermute | solution.py:885
  75.4 13.3 %collective-permute-start.11 = (bf16[768,384]{1,0:T(8,128)(2,1)}, bf16[768,384]{1,0:T(8,128)(2,1)S(1)}, u32[]{:S(2)}, u32[]{:S(2)}) collective-permute-start(bf16[768,384]{1,0:T(8,128)(2,1)} %collective-permute-done.7.refs_4_.w0.refs_6_.refs_10_), channel_id=1, source_target_pairs={{0,2},{2,0},{4,6},{6,4},{8,10},{10,8},{12,14},{14,12},{16,18},{18,... | collective-permute-start | bytes 1769480 | tf_op jit(solution)/shard_map/ppermute | solution.py:885
  86.7 16.8 %collective-permute-start.13 = (bf16[448,768]{1,0:T(8,128)(2,1)S(1)}, bf16[448,768]{1,0:T(8,128)(2,1)S(1)}, u32[]{:S(2)}, u32[]{:S(2)}) collective-permute-start(bf16[448,768]{1,0:T(8,128)(2,1)S(1)} %copy-done.48), channel_id=1, source_target_pairs={{0,1},{1,0},{2,3},{3,2},{4,5},{5,4},{6,7},{7,6},{8,9},{9,8},{10,11... | collective-permute-start | bytes 2064392 | tf_op jit(solution)/shard_map/ppermute | solution.py:884
  88.2 14.7 %collective-permute-start.15 = (bf16[768,384]{1,0:T(8,128)(2,1)}, bf16[768,384]{1,0:T(8,128)(2,1)}, u32[]{:S(2)}, u32[]{:S(2)}) collective-permute-start(bf16[768,384]{1,0:T(8,128)(2,1)} %collective-permute-done.10.d0), channel_id=1, source_target_pairs={{0,8},{2,10},{4,12},{6,14},{8,0},{10,2},{12,4},{14,6},{16,24},{18,... | collective-permute-start | bytes 1769480 | tf_op jit(solution)/shard_map/ppermute | solution.py:885
  88.7 16.0 %collective-permute-start.14 = (bf16[768,384]{1,0:T(8,128)(2,1)}, bf16[768,384]{1,0:T(8,128)(2,1)}, u32[]{:S(2)}, u32[]{:S(2)}) collective-permute-start(bf16[768,384]{1,0:T(8,128)(2,1)} %collective-permute-done.2.u0), channel_id=1, source_target_pairs={{0,2},{2,0},{4,6},{6,4},{8,10},{10,8},{12,14},{14,12},{16,18},{18,... | collective-permute-start | bytes 1769480 | tf_op jit(solution)/shard_map/ppermute | solution.py:885
  88.7 16.0 %collective-permute-start.9 = (bf16[768,384]{1,0:T(8,128)(2,1)}, bf16[768,384]{1,0:T(8,128)(2,1)}, u32[]{:S(2)}, u32[]{:S(2)}) collective-permute-start(bf16[768,384]{1,0:T(8,128)(2,1)} %collective-permute-done.6.u1), channel_id=1, source_target_pairs={{0,2},{2,0},{4,6},{6,4},{8,10},{10,8},{12,14},{14,12},{16,18},{18,... | collective-permute-start | bytes 1769480 | tf_op jit(solution)/shard_map/ppermute | solution.py:885
  103.5 30.9 %collective-permute-start.20 = (bf16[768,384]{1,0:T(8,128)(2,1)S(1)}, bf16[768,384]{1,0:T(8,128)(2,1)}, u32[]{:S(2)}, u32[]{:S(2)}) collective-permute-start(bf16[768,384]{1,0:T(8,128)(2,1)S(1)} %copy-done.53), channel_id=1, source_target_pairs={{0,1},{1,0},{2,3},{3,2},{4,5},{5,4},{6,7},{7,6},{8,9},{9,8},{10,11... | collective-permute-start | bytes 1769480 | tf_op jit(solution)/shard_map/ppermute | solution.py:884
  133.8 28.0 %collective-permute-start.19 = (bf16[1536,384]{1,0:T(8,128)(2,1)S(1)}, bf16[1536,384]{1,0:T(8,128)(2,1)S(1)}, u32[]{:S(2)}, u32[]{:S(2)}) collective-permute-start(bf16[1536,384]{1,0:T(8,128)(2,1)S(1)} %copy-done.45), channel_id=1, source_target_pairs={{0,1},{1,0},{2,3},{3,2},{4,5},{5,4},{6,7},{7,6},{8,9},{9,8},{10,11... | collective-permute-start | bytes 3538952 | tf_op jit(solution)/shard_map/ppermute | solution.py:884
  134.4 24.2 %collective-permute-start.24 = (bf16[768,384]{1,0:T(8,128)(2,1)}, bf16[768,384]{1,0:T(8,128)(2,1)}, u32[]{:S(2)}, u32[]{:S(2)}) collective-permute-start(bf16[768,384]{1,0:T(8,128)(2,1)} %collective-permute-done.20.refs_4_.w0.refs_8_), channel_id=1, source_target_pairs={{0,8},{2,10},{4,12},{6,14},{8,0},{10,2},{12,4},{14,6},{16,24},{18,... | collective-permute-start | bytes 1769480 | tf_op jit(solution)/shard_map/ppermute | solution.py:885
  135.8 34.3 %collective-permute-start.27 = (bf16[768,384]{1,0:T(8,128)(2,1)}, bf16[768,384]{1,0:T(8,128)(2,1)}, u32[]{:S(2)}, u32[]{:S(2)}) collective-permute-start(bf16[768,384]{1,0:T(8,128)(2,1)} %collective-permute-done.20.refs_4_.w0.refs_8_), channel_id=1, source_target_pairs={{0,2},{2,0},{4,6},{6,4},{8,10},{10,8},{12,14},{14,12},{16,18},{18,... | collective-permute-start | bytes 1769480 | tf_op jit(solution)/shard_map/ppermute | solution.py:885
  135.8 32.8 %collective-permute-start.26 = (bf16[1536,1536]{1,0:T(8,128)(2,1)}, bf16[1536,1536]{1,0:T(8,128)(2,1)}, u32[]{:S(2)}, u32[]{:S(2)}) collective-permute-start(bf16[1536,1536]{1,0:T(8,128)(2,1)} %get-tuple-element.253), channel_id=1, source_target_pairs={{0,2},{2,0},{4,6},{6,4},{8,10},{10,8},{12,14},{14,12},{16,18},{18,... | collective-permute-start | bytes 14155784 | tf_op jit(solution)/shard_map/ppermute | solution.py:885
  158.6 11.6 %collective-permute-start.28 = (bf16[768,384]{1,0:T(8,128)(2,1)}, bf16[768,384]{1,0:T(8,128)(2,1)}, u32[]{:S(2)}, u32[]{:S(2)}) collective-permute-start(bf16[768,384]{1,0:T(8,128)(2,1)} %collective-permute-done.24.refs_5_.w1.refs_9_), channel_id=1, source_target_pairs={{0,2},{2,0},{4,6},{6,4},{8,10},{10,8},{12,14},{14,12},{16,18},{18,... | collective-permute-start | bytes 1769480 | tf_op jit(solution)/shard_map/ppermute | solution.py:885
  158.7 8.6 %collective-permute-start.18 = (bf16[160,768]{1,0:T(8,128)(2,1)}, bf16[160,768]{1,0:T(8,128)(2,1)S(1)}, u32[]{:S(2)}, u32[]{:S(2)}) collective-permute-start(bf16[160,768]{1,0:T(8,128)(2,1)} %get-tuple-element.235), channel_id=1, source_target_pairs={{0,1},{1,0},{2,3},{3,2},{4,5},{5,4},{6,7},{7,6},{8,9},{9,8},{10,11... | collective-permute-start | bytes 737288 | tf_op jit(solution)/shard_map/ppermute | solution.py:884
  163.8 26.1 %collective-permute-start.33 = (bf16[768,1536]{1,0:T(8,128)(2,1)}, bf16[768,1536]{1,0:T(8,128)(2,1)S(1)}, u32[]{:S(2)}, u32[]{:S(2)}) collective-permute-start(bf16[768,1536]{1,0:T(8,128)(2,1)} %get-tuple-element.269), channel_id=1, source_target_pairs={{0,2},{2,0},{4,6},{6,4},{8,10},{10,8},{12,14},{14,12},{16,18},{18,... | collective-permute-start | bytes 7077896 | tf_op jit(solution)/shard_map/ppermute | solution.py:885
  167.2 22.0 %collective-permute-start.23 = (bf16[768,384]{1,0:T(8,128)(2,1)}, bf16[768,384]{1,0:T(8,128)(2,1)}, u32[]{:S(2)}, u32[]{:S(2)}) collective-permute-start(bf16[768,384]{1,0:T(8,128)(2,1)} %get-tuple-element.249), channel_id=1, source_target_pairs={{0,8},{2,10},{4,12},{6,14},{8,0},{10,2},{12,4},{14,6},{16,24},{18,... | collective-permute-start | bytes 1769480 | tf_op jit(solution)/shard_map/ppermute | solution.py:885
  168.6 21.1 %collective-permute-start.22 = (bf16[768,384]{1,0:T(8,128)(2,1)S(1)}, bf16[768,384]{1,0:T(8,128)(2,1)}, u32[]{:S(2)}, u32[]{:S(2)}) collective-permute-start(bf16[768,384]{1,0:T(8,128)(2,1)S(1)} %get-tuple-element.248), channel_id=1, source_target_pairs={{0,4},{2,6},{4,0},{6,2},{8,12},{10,14},{12,8},{14,10},{16,20},{18,... | collective-permute-start | bytes 1769480 | tf_op jit(solution)/shard_map/ppermute | solution.py:885
  170.1 27.0 %collective-permute-start.29 = (bf16[1536,384]{1,0:T(8,128)(2,1)}, bf16[1536,384]{1,0:T(8,128)(2,1)}, u32[]{:S(2)}, u32[]{:S(2)}) collective-permute-start(bf16[1536,384]{1,0:T(8,128)(2,1)} %copy-done.19), channel_id=1, source_target_pairs={{0,2},{2,0},{4,6},{6,4},{8,10},{10,8},{12,14},{14,12},{16,18},{18,... | collective-permute-start | bytes 3538952 | tf_op jit(solution)/shard_map/ppermute | solution.py:885
  189.2 9.5 %collective-permute-start.31 = (bf16[768,384]{1,0:T(8,128)(2,1)}, bf16[768,384]{1,0:T(8,128)(2,1)}, u32[]{:S(2)}, u32[]{:S(2)}) collective-permute-start(bf16[768,384]{1,0:T(8,128)(2,1)} %collective-permute-done.23.d1), channel_id=1, source_target_pairs={{0,2},{2,0},{4,6},{6,4},{8,10},{10,8},{12,14},{14,12},{16,18},{18,... | collective-permute-start | bytes 1769480 | tf_op jit(solution)/shard_map/ppermute | solution.py:885
  189.8 8.9 %collective-permute-start.30 = (bf16[768,384]{1,0:T(8,128)(2,1)}, bf16[768,384]{1,0:T(8,128)(2,1)}, u32[]{:S(2)}, u32[]{:S(2)}) collective-permute-start(bf16[768,384]{1,0:T(8,128)(2,1)} %collective-permute-done.22.u1), channel_id=1, source_target_pairs={{0,2},{2,0},{4,6},{6,4},{8,10},{10,8},{12,14},{14,12},{16,18},{18,... | collective-permute-start | bytes 1769480 | tf_op jit(solution)/shard_map/ppermute | solution.py:885
  195.9 42.9 %collective-permute-start.40 = (bf16[384,1536]{1,0:T(8,128)(2,1)}, bf16[384,1536]{1,0:T(8,128)(2,1)S(1)}, u32[]{:S(2)}, u32[]{:S(2)}) collective-permute-start(bf16[384,1536]{1,0:T(8,128)(2,1)} %get-tuple-element.282), channel_id=1, source_target_pairs={{0,8},{2,10},{4,12},{6,14},{8,0},{10,2},{12,4},{14,6},{16,24},{18,... | collective-permute-start | bytes 3538952 | tf_op jit(solution)/shard_map/ppermute | solution.py:885
  196.6 42.2 %collective-permute-start.35 = (bf16[384,1536]{1,0:T(8,128)(2,1)}, bf16[384,1536]{1,0:T(8,128)(2,1)S(1)}, u32[]{:S(2)}, u32[]{:S(2)}) collective-permute-start(bf16[384,1536]{1,0:T(8,128)(2,1)} %get-tuple-element.273), channel_id=1, source_target_pairs={{0,4},{2,6},{4,0},{6,2},{8,12},{10,14},{12,8},{14,10},{16,20},{18,... | collective-permute-start | bytes 3538952 | tf_op jit(solution)/shard_map/ppermute | solution.py:885
  197.1 41.7 %collective-permute-start.34 = (bf16[384,1536]{1,0:T(8,128)(2,1)}, bf16[384,1536]{1,0:T(8,128)(2,1)}, u32[]{:S(2)}, u32[]{:S(2)}) collective-permute-start(bf16[384,1536]{1,0:T(8,128)(2,1)} %get-tuple-element.271), channel_id=1, source_target_pairs={{0,1},{1,0},{2,3},{3,2},{4,5},{5,4},{6,7},{7,6},{8,9},{9,8},{10,11... | collective-permute-start | bytes 3538952 | tf_op jit(solution)/shard_map/ppermute | solution.py:884
  236.9 29.5 %collective-permute-start.38 = (bf16[1536,1536]{1,0:T(8,128)(2,1)}, bf16[1536,1536]{1,0:T(8,128)(2,1)}, u32[]{:S(2)}, u32[]{:S(2)}) collective-permute-start(bf16[1536,1536]{1,0:T(8,128)(2,1)} %get-tuple-element.278), channel_id=1, source_target_pairs={{0,2},{2,0},{4,6},{6,4},{8,10},{10,8},{12,14},{14,12},{16,18},{18,... | collective-permute-start | bytes 14155784 | tf_op jit(solution)/shard_map/ppermute | solution.py:885
  238.3 28.1 %collective-permute-start.32 = (bf16[288,768]{1,0:T(8,128)(2,1)}, bf16[288,768]{1,0:T(8,128)(2,1)S(1)}, u32[]{:S(2)}, u32[]{:S(2)}) collective-permute-start(bf16[288,768]{1,0:T(8,128)(2,1)} %get-tuple-element.266), channel_id=1, source_target_pairs={{0,1},{1,0},{2,3},{3,2},{4,5},{5,4},{6,7},{7,6},{8,9},{9,8},{10,11... | collective-permute-start | bytes 1327112 | tf_op jit(solution)/shard_map/ppermute | solution.py:884
  243.0 23.3 %collective-permute-start.37 = (bf16[192,1536]{1,0:T(8,128)(2,1)}, bf16[192,1536]{1,0:T(8,128)(2,1)S(1)}, u32[]{:S(2)}, u32[]{:S(2)}) collective-permute-start(bf16[192,1536]{1,0:T(8,128)(2,1)} %get-tuple-element.277), channel_id=1, source_target_pairs={{0,1},{1,0},{2,3},{3,2},{4,5},{5,4},{6,7},{7,6},{8,9},{9,8},{10,11... | collective-permute-start | bytes 1769480 | tf_op jit(solution)/shard_map/ppermute | solution.py:884
  244.5 21.9 %collective-permute-start.36 = (bf16[192,1536]{1,0:T(8,128)(2,1)}, bf16[192,1536]{1,0:T(8,128)(2,1)S(1)}, u32[]{:S(2)}, u32[]{:S(2)}) collective-permute-start(bf16[192,1536]{1,0:T(8,128)(2,1)} %get-tuple-element.275), channel_id=1, source_target_pairs={{0,4},{2,6},{4,0},{6,2},{8,12},{10,14},{12,8},{14,10},{16,20},{18,... | collective-permute-start | bytes 1769480 | tf_op jit(solution)/shard_map/ppermute | solution.py:885
  266.2 34.8 %collective-permute-start.42 = (bf16[384,1536]{1,0:T(8,128)(2,1)}, bf16[384,1536]{1,0:T(8,128)(2,1)}, u32[]{:S(2)}, u32[]{:S(2)}) collective-permute-start(bf16[384,1536]{1,0:T(8,128)(2,1)} %get-tuple-element.295), channel_id=1, source_target_pairs={{0,2},{2,0},{4,6},{6,4},{8,10},{10,8},{12,14},{14,12},{16,18},{18,... | collective-permute-start | bytes 3538952 | tf_op jit(solution)/shard_map/ppermute | solution.py:885
  272.0 28.6 %collective-permute-start.48 = (bf16[384,1536]{1,0:T(8,128)(2,1)}, bf16[384,1536]{1,0:T(8,128)(2,1)S(1)}, u32[]{:S(2)}, u32[]{:S(2)}) collective-permute-start(bf16[384,1536]{1,0:T(8,128)(2,1)} %get-tuple-element.311), channel_id=1, source_target_pairs={{0,4},{2,6},{4,0},{6,2},{8,12},{10,14},{12,8},{14,10},{16,20},{18,... | collective-permute-start | bytes 3538952 | tf_op jit(solution)/shard_map/ppermute | solution.py:885
  272.6 21.3 %collective-permute-start.44 = (bf16[192,1536]{1,0:T(8,128)(2,1)}, bf16[192,1536]{1,0:T(8,128)(2,1)S(1)}, u32[]{:S(2)}, u32[]{:S(2)}) collective-permute-start(bf16[192,1536]{1,0:T(8,128)(2,1)} %get-tuple-element.300), channel_id=1, source_target_pairs={{0,8},{2,10},{4,12},{6,14},{8,0},{10,2},{12,4},{14,6},{16,24},{18,... | collective-permute-start | bytes 1769480 | tf_op jit(solution)/shard_map/ppermute | solution.py:885
  273.0 28.0 %collective-permute-start.43 = (bf16[384,1536]{1,0:T(8,128)(2,1)}, bf16[384,1536]{1,0:T(8,128)(2,1)S(1)}, u32[]{:S(2)}, u32[]{:S(2)}) collective-permute-start(bf16[384,1536]{1,0:T(8,128)(2,1)} %get-tuple-element.298), channel_id=1, source_target_pairs={{0,1},{1,0},{2,3},{3,2},{4,5},{5,4},{6,7},{7,6},{8,9},{9,8},{10,11... | collective-permute-start | bytes 3538952 | tf_op jit(solution)/shard_map/ppermute | solution.py:884
  293.8 44.1 %collective-permute-start.41 = (f32[2,768]{1,0:T(2,128)}, f32[2,768]{1,0:T(2,128)S(1)}, u32[]{:S(2)}, u32[]{:S(2)}) collective-permute-start(f32[2,768]{1,0:T(2,128)} %get-tuple-element.293), channel_id=1, source_target_pairs={{0,2},{2,0},{4,6},{6,4},{8,10},{10,8},{12,14},{14,12},{16,18},{18,... | collective-permute-start | bytes 18440 | tf_op jit(solution)/shard_map/ppermute | solution.py:885
  293.9 44.0 %collective-permute-start.51 = (bf16[384,1536]{1,0:T(8,128)(2,1)}, bf16[384,1536]{1,0:T(8,128)(2,1)}, u32[]{:S(2)}, u32[]{:S(2)}) collective-permute-start(bf16[384,1536]{1,0:T(8,128)(2,1)} %get-tuple-element.331), channel_id=1, source_target_pairs={{0,2},{2,0},{4,6},{6,4},{8,10},{10,8},{12,14},{14,12},{16,18},{18,... | collective-permute-start | bytes 3538952 | tf_op jit(solution)/shard_map/ppermute | solution.py:885
  306.7 31.2 %collective-permute-start.47 = (bf16[96,1536]{1,0:T(8,128)(2,1)}, bf16[96,1536]{1,0:T(8,128)(2,1)S(1)}, u32[]{:S(2)}, u32[]{:S(2)}) collective-permute-start(bf16[96,1536]{1,0:T(8,128)(2,1)} %get-tuple-element.306), channel_id=1, source_target_pairs={{0,16},{2,18},{4,20},{6,22},{8,24},{10,26},{12,28},{14,30},{16,0},... | collective-permute-start | bytes 884744 | tf_op jit(solution)/shard_map/ppermute | solution.py:885
  309.4 28.6 %collective-permute-start.46 = (bf16[384,1536]{1,0:T(8,128)(2,1)}, bf16[384,1536]{1,0:T(8,128)(2,1)S(1)}, u32[]{:S(2)}, u32[]{:S(2)}) collective-permute-start(bf16[384,1536]{1,0:T(8,128)(2,1)} %get-tuple-element.304), channel_id=1, source_target_pairs={{0,4},{2,6},{4,0},{6,2},{8,12},{10,14},{12,8},{14,10},{16,20},{18,... | collective-permute-start | bytes 3538952 | tf_op jit(solution)/shard_map/ppermute | solution.py:885
  310.8 27.1 %collective-permute-start.45 = (bf16[384,1536]{1,0:T(8,128)(2,1)}, bf16[384,1536]{1,0:T(8,128)(2,1)S(1)}, u32[]{:S(2)}, u32[]{:S(2)}) collective-permute-start(bf16[384,1536]{1,0:T(8,128)(2,1)} %get-tuple-element.302), channel_id=1, source_target_pairs={{0,1},{1,0},{2,3},{3,2},{4,5},{5,4},{6,7},{7,6},{8,9},{9,8},{10,11... | collective-permute-start | bytes 3538952 | tf_op jit(solution)/shard_map/ppermute | solution.py:884
  343.3 26.1 %collective-permute-start.55 = (bf16[96,1536]{1,0:T(8,128)(2,1)}, bf16[96,1536]{1,0:T(8,128)(2,1)S(1)}, u32[]{:S(2)}, u32[]{:S(2)}) collective-permute-start(bf16[96,1536]{1,0:T(8,128)(2,1)} %get-tuple-element.339), channel_id=1, source_target_pairs={{0,16},{2,18},{4,20},{6,22},{8,24},{10,26},{12,28},{14,30},{16,0},... | collective-permute-start | bytes 884744 | tf_op jit(solution)/shard_map/ppermute | solution.py:885
  343.7 26.2 %collective-permute-start.54 = (bf16[96,1536]{1,0:T(8,128)(2,1)}, bf16[96,1536]{1,0:T(8,128)(2,1)S(1)}, u32[]{:S(2)}, u32[]{:S(2)}) collective-permute-start(bf16[96,1536]{1,0:T(8,128)(2,1)} %get-tuple-element.337), channel_id=1, source_target_pairs={{0,8},{2,10},{4,12},{6,14},{8,0},{10,2},{12,4},{14,6},{16,24},{18,... | collective-permute-start | bytes 884744 | tf_op jit(solution)/shard_map/ppermute | solution.py:885
  344.6 25.4 %collective-permute-start.53 = (bf16[192,1536]{1,0:T(8,128)(2,1)}, bf16[192,1536]{1,0:T(8,128)(2,1)S(1)}, u32[]{:S(2)}, u32[]{:S(2)}) collective-permute-start(bf16[192,1536]{1,0:T(8,128)(2,1)} %get-tuple-element.335), channel_id=1, source_target_pairs={{0,1},{1,0},{2,3},{3,2},{4,5},{5,4},{6,7},{7,6},{8,9},{9,8},{10,11... | collective-permute-start | bytes 1769480 | tf_op jit(solution)/shard_map/ppermute | solution.py:884
  345.9 25.3 %collective-permute-start.52 = (bf16[192,1536]{1,0:T(8,128)(2,1)}, bf16[192,1536]{1,0:T(8,128)(2,1)S(1)}, u32[]{:S(2)}, u32[]{:S(2)}) collective-permute-start(bf16[192,1536]{1,0:T(8,128)(2,1)} %get-tuple-element.333), channel_id=1, source_target_pairs={{0,4},{2,6},{4,0},{6,2},{8,12},{10,14},{12,8},{14,10},{16,20},{18,... | collective-permute-start | bytes 1769480 | tf_op jit(solution)/shard_map/ppermute | solution.py:885
  370.0 9.1 %collective-permute-start.57 = (bf16[384,768]{1,0:T(8,128)(2,1)}, bf16[384,768]{1,0:T(8,128)(2,1)S(1)}, u32[]{:S(2)}, u32[]{:S(2)}) collective-permute-start(bf16[384,768]{1,0:T(8,128)(2,1)} %get-tuple-element.347), channel_id=1, source_target_pairs={{0,2},{2,0},{4,6},{6,4},{8,10},{10,8},{12,14},{14,12},{16,18},{18,... | collective-permute-start | bytes 1769480 | tf_op jit(solution)/shard_map/ppermute | solution.py:885
  375.2 17.2 %collective-permute-start.60 = (bf16[192,1536]{1,0:T(8,128)(2,1)}, bf16[192,1536]{1,0:T(8,128)(2,1)S(1)}, u32[]{:S(2)}, u32[]{:S(2)}) collective-permute-start(bf16[192,1536]{1,0:T(8,128)(2,1)} %get-tuple-element.351), channel_id=1, source_target_pairs={{0,8},{2,10},{4,12},{6,14},{8,0},{10,2},{12,4},{14,6},{16,24},{18,... | collective-permute-start | bytes 1769480 | tf_op jit(solution)/shard_map/ppermute | solution.py:885
  379.2 20.3 %collective-permute-start.59 = (bf16[384,768]{1,0:T(8,128)(2,1)}, bf16[384,768]{1,0:T(8,128)(2,1)S(1)}, u32[]{:S(2)}, u32[]{:S(2)}) collective-permute-start(bf16[384,768]{1,0:T(8,128)(2,1)} %get-tuple-element.350), channel_id=1, source_target_pairs={{0,4},{2,6},{4,0},{6,2},{8,12},{10,14},{12,8},{14,10},{16,20},{18,... | collective-permute-start | bytes 1769480 | tf_op jit(solution)/shard_map/ppermute | solution.py:885
  380.7 18.7 %collective-permute-start.58 = (bf16[384,768]{1,0:T(8,128)(2,1)}, bf16[384,768]{1,0:T(8,128)(2,1)S(1)}, u32[]{:S(2)}, u32[]{:S(2)}) collective-permute-start(bf16[384,768]{1,0:T(8,128)(2,1)} %get-tuple-element.348), channel_id=1, source_target_pairs={{0,1},{1,0},{2,3},{3,2},{4,5},{5,4},{6,7},{7,6},{8,9},{9,8},{10,11... | collective-permute-start | bytes 1769480 | tf_op jit(solution)/shard_map/ppermute | solution.py:884
  387.1 12.3 %collective-permute-start.62 = (bf16[48,1536]{1,0:T(8,128)(2,1)}, bf16[48,1536]{1,0:T(8,128)(2,1)S(1)}, u32[]{:S(2)}, u32[]{:S(2)}) collective-permute-start(bf16[48,1536]{1,0:T(8,128)(2,1)} %get-tuple-element.353), channel_id=1, source_target_pairs={{0,1},{1,0},{2,3},{3,2},{4,5},{5,4},{6,7},{7,6},{8,9},{9,8},{10,11... | collective-permute-start | bytes 442376 | tf_op jit(solution)/shard_map/ppermute | solution.py:884
  387.8 11.6 %collective-permute-start.61 = (bf16[48,1536]{1,0:T(8,128)(2,1)}, bf16[48,1536]{1,0:T(8,128)(2,1)S(1)}, u32[]{:S(2)}, u32[]{:S(2)}) collective-permute-start(bf16[48,1536]{1,0:T(8,128)(2,1)} %get-tuple-element.352), channel_id=1, source_target_pairs={{0,16},{2,18},{4,20},{6,22},{8,24},{10,26},{12,28},{14,30},{16,0},... | collective-permute-start | bytes 442376 | tf_op jit(solution)/shard_map/ppermute | solution.py:885
  392.4 15.2 %collective-permute-start.70 = (f32[10,768]{1,0:T(8,128)S(1)}, f32[10,768]{1,0:T(8,128)S(1)}, u32[]{:S(2)}, u32[]{:S(2)}) collective-permute-start(f32[10,768]{1,0:T(8,128)S(1)} %concatenate.39), channel_id=1, source_target_pairs={{0,1},{1,0},{2,3},{3,2},{4,5},{5,4},{6,7},{7,6},{8,9},{9,8},{10,11... | collective-permute-start | bytes 92168 | tf_op jit(solution)/shard_map/ppermute | solution.py:884
  399.5 16.2 %collective-permute-start.66 = (bf16[96,1536]{1,0:T(8,128)(2,1)}, bf16[96,1536]{1,0:T(8,128)(2,1)S(1)}, u32[]{:S(2)}, u32[]{:S(2)}) collective-permute-start(bf16[96,1536]{1,0:T(8,128)(2,1)} %add_up.22), channel_id=1, source_target_pairs={{0,16},{2,18},{4,20},{6,22},{8,24},{10,26},{12,28},{14,30},{16,0},... | collective-permute-start | bytes 884744 | tf_op jit(solution)/shard_map/ppermute | solution.py:885
  404.5 11.2 %collective-permute-start.65 = (bf16[192,768]{1,0:T(8,128)(2,1)}, bf16[192,768]{1,0:T(8,128)(2,1)S(1)}, u32[]{:S(2)}, u32[]{:S(2)}) collective-permute-start(bf16[192,768]{1,0:T(8,128)(2,1)} %get-tuple-element.360), channel_id=1, source_target_pairs={{0,1},{1,0},{2,3},{3,2},{4,5},{5,4},{6,7},{7,6},{8,9},{9,8},{10,11... | collective-permute-start | bytes 884744 | tf_op jit(solution)/shard_map/ppermute | solution.py:884
  405.8 9.8 %collective-permute-start.64 = (bf16[192,768]{1,0:T(8,128)(2,1)}, bf16[192,768]{1,0:T(8,128)(2,1)S(1)}, u32[]{:S(2)}, u32[]{:S(2)}) collective-permute-start(bf16[192,768]{1,0:T(8,128)(2,1)} %get-tuple-element.358), channel_id=1, source_target_pairs={{0,4},{2,6},{4,0},{6,2},{8,12},{10,14},{12,8},{14,10},{16,20},{18,... | collective-permute-start | bytes 884744 | tf_op jit(solution)/shard_map/ppermute | solution.py:885
  414.1 28.7 %collective-permute-start.63 = (bf16[448,768]{1,0:T(8,128)(2,1)}, bf16[448,768]{1,0:T(8,128)(2,1)}, u32[]{:S(2)}, u32[]{:S(2)}) collective-permute-start(bf16[448,768]{1,0:T(8,128)(2,1)} %get-tuple-element.354), channel_id=1, source_target_pairs={{0,1},{1,0},{2,3},{3,2},{4,5},{5,4},{6,7},{7,6},{8,9},{9,8},{10,11... | collective-permute-start | bytes 2064392 | tf_op jit(solution)/shard_map/ppermute | solution.py:884
  415.7 12.9 %collective-permute-start.72 = (f32[10,768]{1,0:T(8,128)S(1)}, f32[10,768]{1,0:T(8,128)S(1)}, u32[]{:S(2)}, u32[]{:S(2)}) collective-permute-start(f32[10,768]{1,0:T(8,128)S(1)} %add.148), channel_id=1, source_target_pairs={{0,8},{2,10},{4,12},{6,14},{8,0},{10,2},{12,4},{14,6},{16,24},{18,... | collective-permute-start | bytes 92168 | tf_op jit(solution)/shard_map/ppermute | solution.py:885
  419.6 17.1 %collective-permute-start.69 = (bf16[96,768]{1,0:T(8,128)(2,1)}, bf16[96,768]{1,0:T(8,128)(2,1)S(1)}, u32[]{:S(2)}, u32[]{:S(2)}) collective-permute-start(bf16[96,768]{1,0:T(8,128)(2,1)} %get-tuple-element.367), channel_id=1, source_target_pairs={{0,24},{2,26},{4,28},{6,30},{8,16},{10,18},{12,20},{14,22},{16,8},... | collective-permute-start | bytes 442376 | tf_op jit(solution)/shard_map/ppermute | solution.py:888
  420.8 15.9 %collective-permute-start.68 = (bf16[96,768]{1,0:T(8,128)(2,1)}, bf16[96,768]{1,0:T(8,128)(2,1)S(1)}, u32[]{:S(2)}, u32[]{:S(2)}) collective-permute-start(bf16[96,768]{1,0:T(8,128)(2,1)} %get-tuple-element.365), channel_id=1, source_target_pairs={{0,8},{2,10},{4,12},{6,14},{8,0},{10,2},{12,4},{14,6},{16,24},{18,... | collective-permute-start | bytes 442376 | tf_op jit(solution)/shard_map/ppermute | solution.py:888
  421.1 15.5 %collective-permute-start.67 = (bf16[96,768]{1,0:T(8,128)(2,1)}, bf16[96,768]{1,0:T(8,128)(2,1)S(1)}, u32[]{:S(2)}, u32[]{:S(2)}) collective-permute-start(bf16[96,768]{1,0:T(8,128)(2,1)} %get-tuple-element.363), channel_id=1, source_target_pairs={{0,16},{2,18},{4,20},{6,22},{8,24},{10,26},{12,28},{14,30},{16,0},... | collective-permute-start | bytes 442376 | tf_op jit(solution)/shard_map/ppermute | solution.py:888
  428.6 7.3 %collective-permute-start.73 = (f32[10,768]{1,0:T(8,128)S(1)}, f32[10,768]{1,0:T(8,128)S(1)}, u32[]{:S(2)}, u32[]{:S(2)}) collective-permute-start(f32[10,768]{1,0:T(8,128)S(1)} %add.149), channel_id=1, source_target_pairs={{0,16},{2,18},{4,20},{6,22},{8,24},{10,26},{12,28},{14,30},{16,0},... | collective-permute-start | bytes 92168 | tf_op jit(solution)/shard_map/ppermute | solution.py:888
  (69 other events, 393.3 us)

commit v8 on v7

--- a/solution.py
+++ b/solution.py
@@ -693,14 +693,13 @@
     return pairs
 
 
-def first_cut_kernel(place, in_proj, out_proj, lang, visn, pack, own, other, sem):
-    copies(
-        attention_cuts(in_proj, out_proj, 0, place[0], pack) + row_cuts((lang, visn), place[2], own, other), sem
-    )
+def first_cut_kernel(place, in_proj, out_proj, pack, sem):
+    copies(attention_cuts(in_proj, out_proj, 0, place[0], pack), sem)
 
 
 def second_cut_kernel(
-    place, in_proj, out_proj, up, down, lang, visn, self_l, self_v, up_l, down_l, ffn_v, own, other, sem
+    place, in_proj, out_proj, up, down, lang, visn, lang_cot, visn_cot, self_l, self_v, up_l, down_l, ffn_v, x_own, x_other,
+    own, other, sem
 ):
     px, pz = place[0], place[1]
     pairs = attention_cuts(in_proj, out_proj, 1, pz, self_l) + attention_cuts(in_proj, out_proj, 2, pz, self_v)
@@ -715,7 +714,8 @@
                     d.at[pl.ds(c * cols, cols), :],
                 )
             )
-    copies(pairs + row_cuts((lang, visn), place[2], own, other), sem)
+    pairs += row_cuts((lang, visn), place[2], x_own, x_other)
+    copies(pairs + row_cuts((lang_cot, visn_cot), place[2], own, other), sem)
 
 
 def cut_call(kernel, n_copies, shapes, place, *arrays):
@@ -905,13 +905,11 @@
     slot = jnp.stack([piece_of(X), piece_of(Z), t]).astype(jnp.int32)
     attn_pack = (width, half)
     rows_shape = (sum(spans), width)
-    cross_piece, x_own, x_other = cut_call(
-        first_cut_kernel, 9, [attn_pack, rows_shape, rows_shape], slot, in_proj, out_proj, lang_input, visn_input
-    )
+    (cross_piece,) = cut_call(first_cut_kernel, 5, [attn_pack], slot, in_proj, out_proj)
     cross_y = exchange(cross_piece, Y)
-    self_l_piece, self_v_piece, up_l_piece, down_l_piece, ffn_v_piece, cot_own, cot_other = cut_call(
-        second_cut_kernel, 20, [attn_pack] * 4 + [(2 * width, half)] + [rows_shape] * 2, after(slot, x_own),
-        in_proj, out_proj, up_proj, down_proj, lang_cotan, visn_cotan,
+    self_l_piece, self_v_piece, up_l_piece, down_l_piece, ffn_v_piece, x_own, x_other, cot_own, cot_other = cut_call(
+        second_cut_kernel, 24, [attn_pack] * 4 + [(2 * width, half)] + [rows_shape] * 4, after(slot, cross_piece),
+        in_proj, out_proj, up_proj, down_proj, lang_input, visn_input, lang_cotan, visn_cotan,
     )
     lane = jnp.arange(LANES)[None, :]
 
@@ -1084,9 +1082,9 @@
             grad_recv = exchange(after(xb[1], *tied), Y)
         tied = got + beside
     got = send_last(cxs, across, bits, *tied)
-    stats = stats + exchange(after(stats, *tied), bits - 2 if bits > 3 else Y)
     far = after(stats, *tied)
-    stats = stats + across(far, 1 << (bits - 1))
+    last_bits = [1 << (bits - 1), 1 << (bits - 2), 3 << (bits - 2)]
+    stats = stats + sum(across(far, value) for value in last_bits)
     while any(s.order for s in others):
         send_all([s for s in others if s.order], exchange, *tied)
     sums = finish({"ful": ful, "fdl": fdl, "sl": sl}, xb[0])

time: 456 us -> 457 us (level)
    ppermute x50 -> x49, starting transfers between devices: 34.6 us -> 33.1 us  [exchange(): return lax.ppermute(x, 'dp', [(i, i ^ 1 << stage) for i in range(n_dp)])]
    unnamed x124 -> x134, local copies, waits for them, and re-layouts: 13.5 us -> 14.4 us
    ppermute x50 -> x49, waiting for transfers between devices: 30.2 us -> 29.7 us  [exchange(): return lax.ppermute(x, 'dp', [(i, i ^ 1 << stage) for i in range(n_dp)])]
  transfers between devices with their start and end apart: 74 -> 75, of which waited for: 16 -> 17; matrix products, arithmetic and copies ran while one was open for 5% -> 5% of each run, Pallas kernels for 62% -> 62%
where the time goes in v8:
time: 457 us; the launch traced here: 449 us
  Pallas kernels  284 us (62%)
  starting transfers between devices  67.1 us (15%)
  waiting for transfers between devices  54.3 us (12%)
  other arithmetic  21.5 us (5%)
  local copies, waits for them, and re-layouts  20.2 us (4%)
    pallas_call x5, Pallas kernels, attention_backward(): pl.pallas_call(functools.partial(bwd_kernel, dirs, each, which, spans, ha...  110 us
    pallas_call x2, Pallas kernels, feed_forward(): pl.pallas_call(functools.partial(ffn_kernel, blocks, which, stream, spans...  64.5 us
    pallas_call x3, Pallas kernels, attention_forward(): pl.pallas_call(functools.partial(fwd_kernel, dirs, each, which, spans), g...  60.1 us
    pallas_call x13, Pallas kernels, add_up(): pl.pallas_call(functools.partial(add_kernel, plan, len(arrays)), grid=(AD...  40.3 us
    ppermute x49, starting transfers between devices, exchange(): return lax.ppermute(x, 'dp', [(i, i ^ 1 << stage) for i in range(n_dp)])  33.1 us
    ppermute x49, waiting for transfers between devices, exchange(): return lax.ppermute(x, 'dp', [(i, i ^ 1 << stage) for i in range(n_dp)])  29.7 us
    ppermute x20, starting transfers between devices, exchange(): return lax.ppermute(x, 'tensor', SWAP)  25 us
    ppermute x20, waiting for transfers between devices, exchange(): return lax.ppermute(x, 'tensor', SWAP)  18.2 us
  transfers between devices with their start and end apart: 75, of which 17 were waited for; matrix products, arithmetic and copies ran while one was open for 5% of the time, Pallas kernels for 62%

profile of v8, /device:TPU:0, one launch (start us, length us, event | category | flops | bytes accessed | tf_op | source)
XLA Modules:
  0.0 449.3 jit_solution(6487195398275049690)
XLA Ops:
  1.3 2.7 cut.2
  3.9 3.0 collective-permute-start
  7.0 6.6 %cut.3 = (bf16[768,384]{1,0:T(8,128)(2,1)}, bf16[768,384]{1,0:T(8,128)(2,1)}, bf16[768,384]{1,0:T(8,128)(2,1)}, bf16[768,384]{1,0:T(8,128)(2,1)}, bf16[1536,384]...) custom-call(s32[3]{0:T(128)} %pad_add_fusion.1.place.slot_ref, ...), custom_call_target="tpu_custom_call" | custom-call | flops 1 | bytes 1 | tf_op jit(solution)/shard_map/cut/pallas_call | solution.py:723
  14.8 5.7 %collective-permute-done.refs_5_.refs_10_.refs_7_.refs_11_ = bf16[768,384]{1,0:T(8,128)(2,1)S(1)} collective-permute-done((bf16[768,384]{1,0:T(8,128)(2,1)}, bf16[768,384]{1,0:T(8,128)(2,1)S(1)}, u32[]{:S(2)}, u32[]{:S(2)}) %collective-permute-start) | collective-permute-done | bytes 589856 | tf_op jit(solution)/shard_map/ppermute | solution.py:884
  20.5 1.7 collective-permute-start.3
  23.4 1.5 collective-permute-start.1
  25.7 9.3 %collective-permute-done.3.refs_6_.refs_11_.refs_8_.refs_12_ = bf16[768,384]{1,0:T(8,128)(2,1)S(1)} collective-permute-done((bf16[768,384]{1,0:T(8,128)(2,1)S(1)}, bf16[768,384]{1,0:T(8,128)(2,1)S(1)}, u32[]{:S(2)}, u32[]{:S(2)}) %collective-permute-start.3) | collective-permute-done | bytes 589856 | tf_op jit(solution)/shard_map/ppermute | solution.py:885
  37.6 2.0 collective-permute-done.1.refs_1_.refs_5_
  39.6 1.5 collective-permute-start.2
  43.3 28.6 %attention_forward.3 = (bf16[896,768]{1,0:T(8,128)(2,1)}, bf16[896,768]{1,0:T(8,128)(2,1)}, bf16[896,768]{1,0:T(8,128)(2,1)}, bf16[896,768]{1,0:T(8,128)(2,1)}, ...) custom-call(s32[3]{0:T(128)} %pad_add_fusion.1.place.slot_ref, ...), custom_call_target="tpu_custom_call" | custom-call | flops 99999997952 | bytes 1 | tf_op jit(solution)/shard_map/attention_forward/pallas_call | solution.py:218
  71.9 1.6 collective-permute-start.8
  73.5 1.5 collective-permute-start.10
  75.6 9.8 %collective-permute-done.8.refs_5_.w1.refs_7_.refs_11_ = bf16[768,384]{1,0:T(8,128)(2,1)S(1)} collective-permute-done((bf16[768,384]{1,0:T(8,128)(2,1)}, bf16[768,384]{1,0:T(8,128)(2,1)S(1)}, u32[]{:S(2)}, u32[]{:S(2)}) %collective-permute-start.8) | collective-permute-done | bytes 589856 | tf_op jit(solution)/shard_map/ppermute | solution.py:885
  86.5 1.5 collective-permute-start.13
  90.1 12.5 %attention_forward.4 = (bf16[320,768]{1,0:T(8,128)(2,1)}, bf16[320,768]{1,0:T(8,128)(2,1)}, bf16[320,768]{1,0:T(8,128)(2,1)}, bf16[320,768]{1,0:T(8,128)(2,1)}, bf16[12,320,320]{2,1,0:T(8,128)(2,1)}) custom-call(s32[3]{0:T(128)} %pad_add_fusion.1.place.slot_ref, bf16[320,768]{1,0:T(8,128)(2,1)} %get-tuple-element.218.refs_0_.refs_2_, ...), custom_call_target="tpu_custom_call" | custom-call | flops 99999997952 | bytes 1 | tf_op jit(solution)/shard_map/attention_forward/pallas_call | solution.py:218
  106.7 26.4 %feed_forward.2 = (bf16[160,768]{1,0:T(8,128)(2,1)}, bf16[160,768]{1,0:T(8,128)(2,1)}, f32[320,768]{1,0:T(8,128)}, bf16[320,768]{1,0:T(8,128)(2,1)}, f32[4,768]{...) custom-call(s32[3]{0:T(128)} %pad_add_fusion.1.place.slot_ref, ...), custom_call_target="tpu_custom_call" | custom-call | flops 99999997952 | bytes 1 | tf_op jit(solution)/shard_map/feed_forward/pallas_call | solution.py:358
  134.2 1.5 collective-permute-start.24
  136.1 22.2 %attention_backward.5 = (f32[320,768]{1,0:T(8,128)}, bf16[320,768]{1,0:T(8,128)(2,1)}, f32[2,768]{1,0:T(2,128)}, bf16[768,1536]{1,0:T(8,128)(2,1)}, bf16[768,1536]{1,0:T(8,128)(2,1)}) custom-call(s32[3]{0:T(128)} %pad_add_fusion.1.place.slot_ref, bf16[320,768]{1,0:T(8,128)(2,1)} %get-tuple-element.237.refs_0_, f32[320,768]{1,0:T(8,128)} %get-tuple-element.238.refs_1_, ...), custom_call_target="tpu_custom_call" | custom-call | flops 99999997952 | bytes 1 | tf_op jit(solution)/shard_map/attention_backward/pallas_call | solution.py:644
  158.5 1.6 collective-permute-start.18
  160.1 1.5 collective-permute-done.19.u0.d0
  163.7 3.3 collective-permute-done.18
  168.4 1.5 collective-permute-start.22
  169.9 19.0 %attention_forward.5 = (bf16[576,768]{1,0:T(8,128)(2,1)}, bf16[576,768]{1,0:T(8,128)(2,1)}, bf16[576,768]{1,0:T(8,128)(2,1)}, bf16[576,768]{1,0:T(8,128)(2,1)}, bf16[12,576,576]{2,1,0:T(8,128)(2,1)}) custom-call(s32[3]{0:T(128)} %pad_add_fusion.1.place.slot_ref, bf16[576,768]{1,0:T(8,128)(2,1)} %get-tuple-element.252.refs_0_.refs_2_, ...), custom_call_target="tpu_custom_call" | custom-call | flops 99999997952 | bytes 1 | tf_op jit(solution)/shard_map/attention_forward/pallas_call | solution.py:218
  189.6 1.4 copy-done
  191.0 4.7 %add_up.13 = (bf16[384,1536]{1,0:T(8,128)(2,1)}, bf16[384,1536]{1,0:T(8,128)(2,1)}, bf16[384,1536]{1,0:T(8,128)(2,1)}) custom-call(bf16[1536,1536]{1,0:T(8,128)(2,1)} %get-tuple-element.264.refs_0_.refs_2_.refs_4_.refs_3_.refs_6_.refs_10_.refs_11_.refs_16_, ...), custom_call_target="tpu_custom_call" | custom-call | flops 1 | bytes 1 | tf_op jit(solution)/shard_map/add_up/pallas_call | solution.py:768
  196.9 1.5 collective-permute-start.34
  199.3 38.1 %feed_forward.3 = (bf16[288,768]{1,0:T(8,128)(2,1)}, bf16[288,768]{1,0:T(8,128)(2,1)}, f32[576,768]{1,0:T(8,128)}, bf16[576,768]{1,0:T(8,128)(2,1)}, f32[4,768]{...) custom-call(s32[3]{0:T(128)} %pad_add_fusion.1.place.slot_ref, ...), custom_call_target="tpu_custom_call" | custom-call | flops 99999997952 | bytes 1 | tf_op jit(solution)/shard_map/feed_forward/pallas_call | solution.py:358
  240.6 2.9 add_up.14
  243.5 1.4 collective-permute-start.37
  245.0 1.5 collective-permute-start.36
  246.5 20.2 %attention_backward.6 = (f32[576,768]{1,0:T(8,128)}, bf16[768,576]{1,0:T(8,128)(2,1)}, bf16[768,576]{1,0:T(8,128)(2,1)}, bf16[384,1536]{1,0:T(8,128)(2,1)}, bf16[384,1536]{1,0:T(8,128)(2,1)}) custom-call(s32[3]{0:T(128)} %pad_add_fusion.1.place.slot_ref, bf16[576,768]{1,0:T(8,128)(2,1)} %get-tuple-element.277.refs_0_, ...), custom_call_target="tpu_custom_call" | custom-call | flops 99999997952 | bytes 1 | tf_op jit(solution)/shard_map/attention_backward/pallas_call | solution.py:644
  267.9 4.5 add_up.15
  273.5 1.4 collective-permute-start.43
  274.9 19.4 %attention_backward.7 = (f32[576,768]{1,0:T(8,128)}, bf16[576,768]{1,0:T(8,128)(2,1)}, f32[2,768]{1,0:T(2,128)}, bf16[384,1536]{1,0:T(8,128)(2,1)}, bf16[384,1536]{1,0:T(8,128)(2,1)}) custom-call(s32[3]{0:T(128)} %pad_add_fusion.1.place.slot_ref, bf16[576,768]{1,0:T(8,128)(2,1)} %get-tuple-element.277.refs_0_, f32[576,768]{1,0:T(8,128)} %get-tuple-element.286.refs_1_, ...), custom_call_target="tpu_custom_call" | custom-call | flops 99999997952 | bytes 1 | tf_op jit(solution)/shard_map/attention_backward/pallas_call | solution.py:644
  294.9 6.1 %collective-permute-done.48.refs_9_.refs_6_.refs_7_.refs_8_ = bf16[384,1536]{1,0:T(8,128)(2,1)S(1)} collective-permute-done((bf16[384,1536]{1,0:T(8,128)(2,1)}, bf16[384,1536]{1,0:T(8,128)(2,1)S(1)}, u32[]{:S(2)}, u32[]{:S(2)}) %collective-permute-start.48) | collective-permute-done | bytes 1179680 | tf_op jit(solution)/shard_map/ppermute | solution.py:885
  302.5 4.6 %add_up.16 = (bf16[384,1536]{1,0:T(8,128)(2,1)}, bf16[384,1536]{1,0:T(8,128)(2,1)}, bf16[96,1536]{1,0:T(8,128)(2,1)}) custom-call(bf16[384,1536]{1,0:T(8,128)(2,1)} %get-tuple-element.291.refs_0_, bf16[384,1536]{1,0:T(8,128)(2,1)} %collective-permute-done.42.refs_1_, ...), custom_call_target="tpu_custom_call" | custom-call | flops 1 | bytes 1 | tf_op jit(solution)/shard_map/add_up/pallas_call | solution.py:768
  307.1 2.6 collective-permute-start.47
  309.7 1.5 collective-permute-start.46
  311.2 1.4 collective-permute-start.45
  312.6 25.4 %attention_backward.8 = (f32[896,768]{1,0:T(8,128)}, bf16[768,896]{1,0:T(8,128)(2,1)}, bf16[768,896]{1,0:T(8,128)(2,1)}, bf16[384,768]{1,0:T(8,128)(2,1)}, bf16[...) custom-call(s32[3]{0:T(128)} %pad_add_fusion.1.place.slot_ref, ...), custom_call_target="tpu_custom_call" | custom-call | flops 99999997952 | bytes 1 | tf_op jit(solution)/shard_map/attention_backward/pallas_call | solution.py:644
  339.6 3.9 add_up.17
  346.6 22.8 %attention_backward.9 = (f32[448,768]{1,0:T(8,128)}, bf16[448,768]{1,0:T(8,128)(2,1)}, bf16[384,768]{1,0:T(8,128)(2,1)}, bf16[384,768]{1,0:T(8,128)(2,1)}, bf16[...) custom-call(s32[3]{0:T(128)} %pad_add_fusion.1.place.slot_ref, bf16[320,768]{1,0:T(8,128)(2,1)} %get-tuple-element.305.refs_0_, ...), custom_call_target="tpu_custom_call" | custom-call | flops 99999997952 | bytes 1 | tf_op jit(solution)/shard_map/attention_backward/pallas_call | solution.py:644
  372.1 3.1 add_up.18
  376.8 2.6 add_up.19
  379.4 1.4 collective-permute-start.59
  382.2 1.9 maximum_select_fusion.3
  384.9 2.2 maximum_select_fusion.2
  387.9 2.6 collective-permute-start.61
  390.5 2.0 collective-permute-done.60.refs_4_.refs_9_.refs_10_.refs_16_
  393.3 2.2 add_up.22
  395.5 4.1 collective-permute-done.62.refs_17_
  399.6 2.7 collective-permute-start.66
  402.3 2.3 add_up.20
  407.7 1.6 collective-permute-start.71
  410.4 2.7 add_up.24
  416.1 2.2 collective-permute-start.73
  419.5 2.2 add_up.21
  421.7 2.7 collective-permute-start.69
  424.4 2.7 add_up.25
  427.1 1.9 pad_maximum_fusion.2
  430.2 1.8 collective-permute-start.67
  432.7 4.0 collective-permute-done.68.refs_5_.refs_12_
  436.7 2.4 collective-permute-done.67.refs_4_.refs_11_
  439.7 1.9 add_up.23
  (292 shorter events, 62.1 us)
Async XLA Ops:
  3.9 16.6 %collective-permute-start = (bf16[768,384]{1,0:T(8,128)(2,1)}, bf16[768,384]{1,0:T(8,128)(2,1)S(1)}, u32[]{:S(2)}, u32[]{:S(2)}) collective-permute-start(bf16[768,384]{1,0:T(8,128)(2,1)} %cut.2), channel_id=1, source_target_pairs={{0,1},{1,0},{2,3},{3,2},{4,5},{5,4},{6,7},{7,6},{8,9},{9,8},{10,11... | collective-permute-start | bytes 1769480 | tf_op jit(solution)/shard_map/ppermute | solution.py:884
  20.5 14.5 %collective-permute-start.3 = (bf16[768,384]{1,0:T(8,128)(2,1)S(1)}, bf16[768,384]{1,0:T(8,128)(2,1)S(1)}, u32[]{:S(2)}, u32[]{:S(2)}) collective-permute-start(bf16[768,384]{1,0:T(8,128)(2,1)S(1)} %collective-permute-done.refs_5_.refs_10_.refs_7_.refs_11_), channel_id=1, source_target_pairs={{0,4},{2,6},{4,0},{6,2},{8,12},{10,14},{12,8},{14,10},{16,20},{18,... | collective-permute-start | bytes 1769480 | tf_op jit(solution)/shard_map/ppermute | solution.py:885
  23.4 16.2 %collective-permute-start.1 = (bf16[448,768]{1,0:T(8,128)(2,1)}, bf16[448,768]{1,0:T(8,128)(2,1)S(1)}, u32[]{:S(2)}, u32[]{:S(2)}) collective-permute-start(bf16[448,768]{1,0:T(8,128)(2,1)} %get-tuple-element.199), channel_id=1, source_target_pairs={{0,1},{1,0},{2,3},{3,2},{4,5},{5,4},{6,7},{7,6},{8,9},{9,8},{10,11... | collective-permute-start | bytes 2064392 | tf_op jit(solution)/shard_map/ppermute | solution.py:884
  25.7 16.0 %collective-permute-start.4 = (bf16[768,384]{1,0:T(8,128)(2,1)S(1)}, bf16[768,384]{1,0:T(8,128)(2,1)S(1)}, u32[]{:S(2)}, u32[]{:S(2)}) collective-permute-start(bf16[768,384]{1,0:T(8,128)(2,1)S(1)} %collective-permute-done.refs_5_.refs_10_.refs_7_.refs_11_), channel_id=1, source_target_pairs={{0,2},{2,0},{4,6},{6,4},{8,10},{10,8},{12,14},{14,12},{16,18},{18,... | collective-permute-start | bytes 1769480 | tf_op jit(solution)/shard_map/ppermute | solution.py:885
  39.6 35.4 %collective-permute-start.2 = (bf16[768,384]{1,0:T(8,128)(2,1)}, bf16[768,384]{1,0:T(8,128)(2,1)}, u32[]{:S(2)}, u32[]{:S(2)}) collective-permute-start(bf16[768,384]{1,0:T(8,128)(2,1)} %get-tuple-element.200), channel_id=1, source_target_pairs={{0,1},{1,0},{2,3},{3,2},{4,5},{5,4},{6,7},{7,6},{8,9},{9,8},{10,11... | collective-permute-start | bytes 1769480 | tf_op jit(solution)/shard_map/ppermute | solution.py:884
  41.1 30.7 %collective-permute-start.7 = (bf16[768,384]{1,0:T(8,128)(2,1)}, bf16[768,384]{1,0:T(8,128)(2,1)}, u32[]{:S(2)}, u32[]{:S(2)}) collective-permute-start(bf16[768,384]{1,0:T(8,128)(2,1)} %get-tuple-element.210), channel_id=1, source_target_pairs={{0,1},{1,0},{2,3},{3,2},{4,5},{5,4},{6,7},{7,6},{8,9},{9,8},{10,11... | collective-permute-start | bytes 1769480 | tf_op jit(solution)/shard_map/ppermute | solution.py:884
  71.9 13.5 %collective-permute-start.8 = (bf16[768,384]{1,0:T(8,128)(2,1)}, bf16[768,384]{1,0:T(8,128)(2,1)S(1)}, u32[]{:S(2)}, u32[]{:S(2)}) collective-permute-start(bf16[768,384]{1,0:T(8,128)(2,1)} %collective-permute-done.7.refs_4_.w0.refs_6_.refs_10_), channel_id=1, source_target_pairs={{0,8},{2,10},{4,12},{6,14},{8,0},{10,2},{12,4},{14,6},{16,24},{18,... | collective-permute-start | bytes 1769480 | tf_op jit(solution)/shard_map/ppermute | solution.py:885
  73.5 12.9 %collective-permute-start.10 = (bf16[768,384]{1,0:T(8,128)(2,1)S(1)}, bf16[768,384]{1,0:T(8,128)(2,1)}, u32[]{:S(2)}, u32[]{:S(2)}) collective-permute-start(bf16[768,384]{1,0:T(8,128)(2,1)S(1)} %copy-done.54), channel_id=1, source_target_pairs={{0,1},{1,0},{2,3},{3,2},{4,5},{5,4},{6,7},{7,6},{8,9},{9,8},{10,11... | collective-permute-start | bytes 1769480 | tf_op jit(solution)/shard_map/ppermute | solution.py:884
  75.1 12.9 %collective-permute-start.6 = (bf16[768,384]{1,0:T(8,128)(2,1)}, bf16[768,384]{1,0:T(8,128)(2,1)}, u32[]{:S(2)}, u32[]{:S(2)}) collective-permute-start(bf16[768,384]{1,0:T(8,128)(2,1)} %collective-permute-done.2.u0), channel_id=1, source_target_pairs={{0,4},{2,6},{4,0},{6,2},{8,12},{10,14},{12,8},{14,10},{16,20},{18,... | collective-permute-start | bytes 1769480 | tf_op jit(solution)/shard_map/ppermute | solution.py:885
  75.6 12.9 %collective-permute-start.11 = (bf16[768,384]{1,0:T(8,128)(2,1)}, bf16[768,384]{1,0:T(8,128)(2,1)S(1)}, u32[]{:S(2)}, u32[]{:S(2)}) collective-permute-start(bf16[768,384]{1,0:T(8,128)(2,1)} %collective-permute-done.7.refs_4_.w0.refs_6_.refs_10_), channel_id=1, source_target_pairs={{0,2},{2,0},{4,6},{6,4},{8,10},{10,8},{12,14},{14,12},{16,18},{18,... | collective-permute-start | bytes 1769480 | tf_op jit(solution)/shard_map/ppermute | solution.py:885
  86.5 16.8 %collective-permute-start.13 = (bf16[448,768]{1,0:T(8,128)(2,1)S(1)}, bf16[448,768]{1,0:T(8,128)(2,1)S(1)}, u32[]{:S(2)}, u32[]{:S(2)}) collective-permute-start(bf16[448,768]{1,0:T(8,128)(2,1)S(1)} %copy-done.48), channel_id=1, source_target_pairs={{0,1},{1,0},{2,3},{3,2},{4,5},{5,4},{6,7},{7,6},{8,9},{9,8},{10,11... | collective-permute-start | bytes 2064392 | tf_op jit(solution)/shard_map/ppermute | solution.py:884
  88.0 14.6 %collective-permute-start.15 = (bf16[768,384]{1,0:T(8,128)(2,1)}, bf16[768,384]{1,0:T(8,128)(2,1)S(1)}, u32[]{:S(2)}, u32[]{:S(2)}) collective-permute-start(bf16[768,384]{1,0:T(8,128)(2,1)} %collective-permute-done.10.d0), channel_id=1, source_target_pairs={{0,8},{2,10},{4,12},{6,14},{8,0},{10,2},{12,4},{14,6},{16,24},{18,... | collective-permute-start | bytes 1769480 | tf_op jit(solution)/shard_map/ppermute | solution.py:885
  88.5 16.2 %collective-permute-start.14 = (bf16[768,384]{1,0:T(8,128)(2,1)}, bf16[768,384]{1,0:T(8,128)(2,1)}, u32[]{:S(2)}, u32[]{:S(2)}) collective-permute-start(bf16[768,384]{1,0:T(8,128)(2,1)} %collective-permute-done.2.u0), channel_id=1, source_target_pairs={{0,2},{2,0},{4,6},{6,4},{8,10},{10,8},{12,14},{14,12},{16,18},{18,... | collective-permute-start | bytes 1769480 | tf_op jit(solution)/shard_map/ppermute | solution.py:885
  88.5 16.2 %collective-permute-start.9 = (bf16[768,384]{1,0:T(8,128)(2,1)}, bf16[768,384]{1,0:T(8,128)(2,1)}, u32[]{:S(2)}, u32[]{:S(2)}) collective-permute-start(bf16[768,384]{1,0:T(8,128)(2,1)} %collective-permute-done.6.u1), channel_id=1, source_target_pairs={{0,2},{2,0},{4,6},{6,4},{8,10},{10,8},{12,14},{14,12},{16,18},{18,... | collective-permute-start | bytes 1769480 | tf_op jit(solution)/shard_map/ppermute | solution.py:885
  103.3 30.9 %collective-permute-start.20 = (bf16[768,384]{1,0:T(8,128)(2,1)S(1)}, bf16[768,384]{1,0:T(8,128)(2,1)}, u32[]{:S(2)}, u32[]{:S(2)}) collective-permute-start(bf16[768,384]{1,0:T(8,128)(2,1)S(1)} %copy-done.53), channel_id=1, source_target_pairs={{0,1},{1,0},{2,3},{3,2},{4,5},{5,4},{6,7},{7,6},{8,9},{9,8},{10,11... | collective-permute-start | bytes 1769480 | tf_op jit(solution)/shard_map/ppermute | solution.py:884
  133.6 28.0 %collective-permute-start.19 = (bf16[1536,384]{1,0:T(8,128)(2,1)S(1)}, bf16[1536,384]{1,0:T(8,128)(2,1)S(1)}, u32[]{:S(2)}, u32[]{:S(2)}) collective-permute-start(bf16[1536,384]{1,0:T(8,128)(2,1)S(1)} %copy-done.45), channel_id=1, source_target_pairs={{0,1},{1,0},{2,3},{3,2},{4,5},{5,4},{6,7},{7,6},{8,9},{9,8},{10,11... | collective-permute-start | bytes 3538952 | tf_op jit(solution)/shard_map/ppermute | solution.py:884
  134.2 24.2 %collective-permute-start.24 = (bf16[768,384]{1,0:T(8,128)(2,1)}, bf16[768,384]{1,0:T(8,128)(2,1)}, u32[]{:S(2)}, u32[]{:S(2)}) collective-permute-start(bf16[768,384]{1,0:T(8,128)(2,1)} %collective-permute-done.20.refs_4_.w0.refs_8_), channel_id=1, source_target_pairs={{0,8},{2,10},{4,12},{6,14},{8,0},{10,2},{12,4},{14,6},{16,24},{18,... | collective-permute-start | bytes 1769480 | tf_op jit(solution)/shard_map/ppermute | solution.py:885
  135.6 34.3 %collective-permute-start.27 = (bf16[768,384]{1,0:T(8,128)(2,1)}, bf16[768,384]{1,0:T(8,128)(2,1)}, u32[]{:S(2)}, u32[]{:S(2)}) collective-permute-start(bf16[768,384]{1,0:T(8,128)(2,1)} %collective-permute-done.20.refs_4_.w0.refs_8_), channel_id=1, source_target_pairs={{0,2},{2,0},{4,6},{6,4},{8,10},{10,8},{12,14},{14,12},{16,18},{18,... | collective-permute-start | bytes 1769480 | tf_op jit(solution)/shard_map/ppermute | solution.py:885
  135.6 32.8 %collective-permute-start.26 = (bf16[1536,1536]{1,0:T(8,128)(2,1)}, bf16[1536,1536]{1,0:T(8,128)(2,1)}, u32[]{:S(2)}, u32[]{:S(2)}) collective-permute-start(bf16[1536,1536]{1,0:T(8,128)(2,1)} %get-tuple-element.250), channel_id=1, source_target_pairs={{0,2},{2,0},{4,6},{6,4},{8,10},{10,8},{12,14},{14,12},{16,18},{18,... | collective-permute-start | bytes 14155784 | tf_op jit(solution)/shard_map/ppermute | solution.py:885
  158.4 11.6 %collective-permute-start.28 = (bf16[768,384]{1,0:T(8,128)(2,1)}, bf16[768,384]{1,0:T(8,128)(2,1)}, u32[]{:S(2)}, u32[]{:S(2)}) collective-permute-start(bf16[768,384]{1,0:T(8,128)(2,1)} %collective-permute-done.24.refs_5_.w1.refs_9_), channel_id=1, source_target_pairs={{0,2},{2,0},{4,6},{6,4},{8,10},{10,8},{12,14},{14,12},{16,18},{18,... | collective-permute-start | bytes 1769480 | tf_op jit(solution)/shard_map/ppermute | solution.py:885
  158.5 8.6 %collective-permute-start.18 = (bf16[160,768]{1,0:T(8,128)(2,1)}, bf16[160,768]{1,0:T(8,128)(2,1)S(1)}, u32[]{:S(2)}, u32[]{:S(2)}) collective-permute-start(bf16[160,768]{1,0:T(8,128)(2,1)} %get-tuple-element.232), channel_id=1, source_target_pairs={{0,1},{1,0},{2,3},{3,2},{4,5},{5,4},{6,7},{7,6},{8,9},{9,8},{10,11... | collective-permute-start | bytes 737288 | tf_op jit(solution)/shard_map/ppermute | solution.py:884
  163.6 26.1 %collective-permute-start.33 = (bf16[768,1536]{1,0:T(8,128)(2,1)}, bf16[768,1536]{1,0:T(8,128)(2,1)S(1)}, u32[]{:S(2)}, u32[]{:S(2)}) collective-permute-start(bf16[768,1536]{1,0:T(8,128)(2,1)} %get-tuple-element.266), channel_id=1, source_target_pairs={{0,2},{2,0},{4,6},{6,4},{8,10},{10,8},{12,14},{14,12},{16,18},{18,... | collective-permute-start | bytes 7077896 | tf_op jit(solution)/shard_map/ppermute | solution.py:885
  167.0 21.9 %collective-permute-start.23 = (bf16[768,384]{1,0:T(8,128)(2,1)}, bf16[768,384]{1,0:T(8,128)(2,1)}, u32[]{:S(2)}, u32[]{:S(2)}) collective-permute-start(bf16[768,384]{1,0:T(8,128)(2,1)} %get-tuple-element.246), channel_id=1, source_target_pairs={{0,8},{2,10},{4,12},{6,14},{8,0},{10,2},{12,4},{14,6},{16,24},{18,... | collective-permute-start | bytes 1769480 | tf_op jit(solution)/shard_map/ppermute | solution.py:885
  168.4 21.1 %collective-permute-start.22 = (bf16[768,384]{1,0:T(8,128)(2,1)S(1)}, bf16[768,384]{1,0:T(8,128)(2,1)}, u32[]{:S(2)}, u32[]{:S(2)}) collective-permute-start(bf16[768,384]{1,0:T(8,128)(2,1)S(1)} %get-tuple-element.245), channel_id=1, source_target_pairs={{0,4},{2,6},{4,0},{6,2},{8,12},{10,14},{12,8},{14,10},{16,20},{18,... | collective-permute-start | bytes 1769480 | tf_op jit(solution)/shard_map/ppermute | solution.py:885
  169.9 27.0 %collective-permute-start.29 = (bf16[1536,384]{1,0:T(8,128)(2,1)}, bf16[1536,384]{1,0:T(8,128)(2,1)}, u32[]{:S(2)}, u32[]{:S(2)}) collective-permute-start(bf16[1536,384]{1,0:T(8,128)(2,1)} %copy-done.19), channel_id=1, source_target_pairs={{0,2},{2,0},{4,6},{6,4},{8,10},{10,8},{12,14},{14,12},{16,18},{18,... | collective-permute-start | bytes 3538952 | tf_op jit(solution)/shard_map/ppermute | solution.py:885
  189.0 9.5 %collective-permute-start.31 = (bf16[768,384]{1,0:T(8,128)(2,1)}, bf16[768,384]{1,0:T(8,128)(2,1)}, u32[]{:S(2)}, u32[]{:S(2)}) collective-permute-start(bf16[768,384]{1,0:T(8,128)(2,1)} %collective-permute-done.23.d1), channel_id=1, source_target_pairs={{0,2},{2,0},{4,6},{6,4},{8,10},{10,8},{12,14},{14,12},{16,18},{18,... | collective-permute-start | bytes 1769480 | tf_op jit(solution)/shard_map/ppermute | solution.py:885
  189.5 8.9 %collective-permute-start.30 = (bf16[768,384]{1,0:T(8,128)(2,1)}, bf16[768,384]{1,0:T(8,128)(2,1)S(1)}, u32[]{:S(2)}, u32[]{:S(2)}) collective-permute-start(bf16[768,384]{1,0:T(8,128)(2,1)} %collective-permute-done.22.u1), channel_id=1, source_target_pairs={{0,2},{2,0},{4,6},{6,4},{8,10},{10,8},{12,14},{14,12},{16,18},{18,... | collective-permute-start | bytes 1769480 | tf_op jit(solution)/shard_map/ppermute | solution.py:885
  195.7 43.7 %collective-permute-start.40 = (bf16[384,1536]{1,0:T(8,128)(2,1)}, bf16[384,1536]{1,0:T(8,128)(2,1)S(1)}, u32[]{:S(2)}, u32[]{:S(2)}) collective-permute-start(bf16[384,1536]{1,0:T(8,128)(2,1)} %get-tuple-element.279), channel_id=1, source_target_pairs={{0,8},{2,10},{4,12},{6,14},{8,0},{10,2},{12,4},{14,6},{16,24},{18,... | collective-permute-start | bytes 3538952 | tf_op jit(solution)/shard_map/ppermute | solution.py:885
  196.4 43.0 %collective-permute-start.35 = (bf16[384,1536]{1,0:T(8,128)(2,1)}, bf16[384,1536]{1,0:T(8,128)(2,1)S(1)}, u32[]{:S(2)}, u32[]{:S(2)}) collective-permute-start(bf16[384,1536]{1,0:T(8,128)(2,1)} %get-tuple-element.270), channel_id=1, source_target_pairs={{0,4},{2,6},{4,0},{6,2},{8,12},{10,14},{12,8},{14,10},{16,20},{18,... | collective-permute-start | bytes 3538952 | tf_op jit(solution)/shard_map/ppermute | solution.py:885
  196.9 42.5 %collective-permute-start.34 = (bf16[384,1536]{1,0:T(8,128)(2,1)}, bf16[384,1536]{1,0:T(8,128)(2,1)}, u32[]{:S(2)}, u32[]{:S(2)}) collective-permute-start(bf16[384,1536]{1,0:T(8,128)(2,1)} %get-tuple-element.268), channel_id=1, source_target_pairs={{0,1},{1,0},{2,3},{3,2},{4,5},{5,4},{6,7},{7,6},{8,9},{9,8},{10,11... | collective-permute-start | bytes 3538952 | tf_op jit(solution)/shard_map/ppermute | solution.py:884
  237.5 29.3 %collective-permute-start.38 = (bf16[1536,1536]{1,0:T(8,128)(2,1)}, bf16[1536,1536]{1,0:T(8,128)(2,1)}, u32[]{:S(2)}, u32[]{:S(2)}) collective-permute-start(bf16[1536,1536]{1,0:T(8,128)(2,1)} %get-tuple-element.275), channel_id=1, source_target_pairs={{0,2},{2,0},{4,6},{6,4},{8,10},{10,8},{12,14},{14,12},{16,18},{18,... | collective-permute-start | bytes 14155784 | tf_op jit(solution)/shard_map/ppermute | solution.py:885
  238.9 27.9 %collective-permute-start.32 = (bf16[288,768]{1,0:T(8,128)(2,1)}, bf16[288,768]{1,0:T(8,128)(2,1)S(1)}, u32[]{:S(2)}, u32[]{:S(2)}) collective-permute-start(bf16[288,768]{1,0:T(8,128)(2,1)} %get-tuple-element.263), channel_id=1, source_target_pairs={{0,1},{1,0},{2,3},{3,2},{4,5},{5,4},{6,7},{7,6},{8,9},{9,8},{10,11... | collective-permute-start | bytes 1327112 | tf_op jit(solution)/shard_map/ppermute | solution.py:884
  243.5 23.3 %collective-permute-start.37 = (bf16[192,1536]{1,0:T(8,128)(2,1)}, bf16[192,1536]{1,0:T(8,128)(2,1)S(1)}, u32[]{:S(2)}, u32[]{:S(2)}) collective-permute-start(bf16[192,1536]{1,0:T(8,128)(2,1)} %get-tuple-element.274), channel_id=1, source_target_pairs={{0,1},{1,0},{2,3},{3,2},{4,5},{5,4},{6,7},{7,6},{8,9},{9,8},{10,11... | collective-permute-start | bytes 1769480 | tf_op jit(solution)/shard_map/ppermute | solution.py:884
  245.0 21.8 %collective-permute-start.36 = (bf16[192,1536]{1,0:T(8,128)(2,1)}, bf16[192,1536]{1,0:T(8,128)(2,1)S(1)}, u32[]{:S(2)}, u32[]{:S(2)}) collective-permute-start(bf16[192,1536]{1,0:T(8,128)(2,1)} %get-tuple-element.272), channel_id=1, source_target_pairs={{0,4},{2,6},{4,0},{6,2},{8,12},{10,14},{12,8},{14,10},{16,20},{18,... | collective-permute-start | bytes 1769480 | tf_op jit(solution)/shard_map/ppermute | solution.py:885
  266.7 34.8 %collective-permute-start.42 = (bf16[384,1536]{1,0:T(8,128)(2,1)}, bf16[384,1536]{1,0:T(8,128)(2,1)}, u32[]{:S(2)}, u32[]{:S(2)}) collective-permute-start(bf16[384,1536]{1,0:T(8,128)(2,1)} %get-tuple-element.292), channel_id=1, source_target_pairs={{0,2},{2,0},{4,6},{6,4},{8,10},{10,8},{12,14},{14,12},{16,18},{18,... | collective-permute-start | bytes 3538952 | tf_op jit(solution)/shard_map/ppermute | solution.py:885
  272.4 28.6 %collective-permute-start.48 = (bf16[384,1536]{1,0:T(8,128)(2,1)}, bf16[384,1536]{1,0:T(8,128)(2,1)S(1)}, u32[]{:S(2)}, u32[]{:S(2)}) collective-permute-start(bf16[384,1536]{1,0:T(8,128)(2,1)} %get-tuple-element.308), channel_id=1, source_target_pairs={{0,4},{2,6},{4,0},{6,2},{8,12},{10,14},{12,8},{14,10},{16,20},{18,... | collective-permute-start | bytes 3538952 | tf_op jit(solution)/shard_map/ppermute | solution.py:885
  273.0 21.4 %collective-permute-start.44 = (bf16[192,1536]{1,0:T(8,128)(2,1)}, bf16[192,1536]{1,0:T(8,128)(2,1)S(1)}, u32[]{:S(2)}, u32[]{:S(2)}) collective-permute-start(bf16[192,1536]{1,0:T(8,128)(2,1)} %get-tuple-element.297), channel_id=1, source_target_pairs={{0,8},{2,10},{4,12},{6,14},{8,0},{10,2},{12,4},{14,6},{16,24},{18,... | collective-permute-start | bytes 1769480 | tf_op jit(solution)/shard_map/ppermute | solution.py:885
  273.5 28.0 %collective-permute-start.43 = (bf16[384,1536]{1,0:T(8,128)(2,1)}, bf16[384,1536]{1,0:T(8,128)(2,1)S(1)}, u32[]{:S(2)}, u32[]{:S(2)}) collective-permute-start(bf16[384,1536]{1,0:T(8,128)(2,1)} %get-tuple-element.295), channel_id=1, source_target_pairs={{0,1},{1,0},{2,3},{3,2},{4,5},{5,4},{6,7},{7,6},{8,9},{9,8},{10,11... | collective-permute-start | bytes 3538952 | tf_op jit(solution)/shard_map/ppermute | solution.py:884
  294.3 43.8 %collective-permute-start.41 = (f32[2,768]{1,0:T(2,128)}, f32[2,768]{1,0:T(2,128)S(1)}, u32[]{:S(2)}, u32[]{:S(2)}) collective-permute-start(f32[2,768]{1,0:T(2,128)} %get-tuple-element.290), channel_id=1, source_target_pairs={{0,2},{2,0},{4,6},{6,4},{8,10},{10,8},{12,14},{14,12},{16,18},{18,... | collective-permute-start | bytes 18440 | tf_op jit(solution)/shard_map/ppermute | solution.py:885
  294.4 43.8 %collective-permute-start.51 = (bf16[384,1536]{1,0:T(8,128)(2,1)}, bf16[384,1536]{1,0:T(8,128)(2,1)}, u32[]{:S(2)}, u32[]{:S(2)}) collective-permute-start(bf16[384,1536]{1,0:T(8,128)(2,1)} %get-tuple-element.328), channel_id=1, source_target_pairs={{0,2},{2,0},{4,6},{6,4},{8,10},{10,8},{12,14},{14,12},{16,18},{18,... | collective-permute-start | bytes 3538952 | tf_op jit(solution)/shard_map/ppermute | solution.py:885
  307.1 31.0 %collective-permute-start.47 = (bf16[96,1536]{1,0:T(8,128)(2,1)}, bf16[96,1536]{1,0:T(8,128)(2,1)S(1)}, u32[]{:S(2)}, u32[]{:S(2)}) collective-permute-start(bf16[96,1536]{1,0:T(8,128)(2,1)} %get-tuple-element.303), channel_id=1, source_target_pairs={{0,16},{2,18},{4,20},{6,22},{8,24},{10,26},{12,28},{14,30},{16,0},... | collective-permute-start | bytes 884744 | tf_op jit(solution)/shard_map/ppermute | solution.py:885
  309.7 28.4 %collective-permute-start.46 = (bf16[384,1536]{1,0:T(8,128)(2,1)}, bf16[384,1536]{1,0:T(8,128)(2,1)S(1)}, u32[]{:S(2)}, u32[]{:S(2)}) collective-permute-start(bf16[384,1536]{1,0:T(8,128)(2,1)} %get-tuple-element.301), channel_id=1, source_target_pairs={{0,4},{2,6},{4,0},{6,2},{8,12},{10,14},{12,8},{14,10},{16,20},{18,... | collective-permute-start | bytes 3538952 | tf_op jit(solution)/shard_map/ppermute | solution.py:885
  311.2 26.9 %collective-permute-start.45 = (bf16[384,1536]{1,0:T(8,128)(2,1)}, bf16[384,1536]{1,0:T(8,128)(2,1)S(1)}, u32[]{:S(2)}, u32[]{:S(2)}) collective-permute-start(bf16[384,1536]{1,0:T(8,128)(2,1)} %get-tuple-element.299), channel_id=1, source_target_pairs={{0,1},{1,0},{2,3},{3,2},{4,5},{5,4},{6,7},{7,6},{8,9},{9,8},{10,11... | collective-permute-start | bytes 3538952 | tf_op jit(solution)/shard_map/ppermute | solution.py:884
  343.5 26.0 %collective-permute-start.55 = (bf16[96,1536]{1,0:T(8,128)(2,1)}, bf16[96,1536]{1,0:T(8,128)(2,1)S(1)}, u32[]{:S(2)}, u32[]{:S(2)}) collective-permute-start(bf16[96,1536]{1,0:T(8,128)(2,1)} %get-tuple-element.336), channel_id=1, source_target_pairs={{0,16},{2,18},{4,20},{6,22},{8,24},{10,26},{12,28},{14,30},{16,0},... | collective-permute-start | bytes 884744 | tf_op jit(solution)/shard_map/ppermute | solution.py:885
  343.9 26.1 %collective-permute-start.54 = (bf16[96,1536]{1,0:T(8,128)(2,1)}, bf16[96,1536]{1,0:T(8,128)(2,1)S(1)}, u32[]{:S(2)}, u32[]{:S(2)}) collective-permute-start(bf16[96,1536]{1,0:T(8,128)(2,1)} %get-tuple-element.334), channel_id=1, source_target_pairs={{0,8},{2,10},{4,12},{6,14},{8,0},{10,2},{12,4},{14,6},{16,24},{18,... | collective-permute-start | bytes 884744 | tf_op jit(solution)/shard_map/ppermute | solution.py:885
  344.7 25.4 %collective-permute-start.53 = (bf16[192,1536]{1,0:T(8,128)(2,1)}, bf16[192,1536]{1,0:T(8,128)(2,1)S(1)}, u32[]{:S(2)}, u32[]{:S(2)}) collective-permute-start(bf16[192,1536]{1,0:T(8,128)(2,1)} %get-tuple-element.332), channel_id=1, source_target_pairs={{0,1},{1,0},{2,3},{3,2},{4,5},{5,4},{6,7},{7,6},{8,9},{9,8},{10,11... | collective-permute-start | bytes 1769480 | tf_op jit(solution)/shard_map/ppermute | solution.py:884
  346.1 25.2 %collective-permute-start.52 = (bf16[192,1536]{1,0:T(8,128)(2,1)}, bf16[192,1536]{1,0:T(8,128)(2,1)S(1)}, u32[]{:S(2)}, u32[]{:S(2)}) collective-permute-start(bf16[192,1536]{1,0:T(8,128)(2,1)} %get-tuple-element.330), channel_id=1, source_target_pairs={{0,4},{2,6},{4,0},{6,2},{8,12},{10,14},{12,8},{14,10},{16,20},{18,... | collective-permute-start | bytes 1769480 | tf_op jit(solution)/shard_map/ppermute | solution.py:885
  370.1 9.3 %collective-permute-start.57 = (bf16[384,768]{1,0:T(8,128)(2,1)}, bf16[384,768]{1,0:T(8,128)(2,1)S(1)}, u32[]{:S(2)}, u32[]{:S(2)}) collective-permute-start(bf16[384,768]{1,0:T(8,128)(2,1)} %get-tuple-element.344), channel_id=1, source_target_pairs={{0,2},{2,0},{4,6},{6,4},{8,10},{10,8},{12,14},{14,12},{16,18},{18,... | collective-permute-start | bytes 1769480 | tf_op jit(solution)/shard_map/ppermute | solution.py:885
  375.3 17.2 %collective-permute-start.60 = (bf16[192,1536]{1,0:T(8,128)(2,1)}, bf16[192,1536]{1,0:T(8,128)(2,1)S(1)}, u32[]{:S(2)}, u32[]{:S(2)}) collective-permute-start(bf16[192,1536]{1,0:T(8,128)(2,1)} %get-tuple-element.348), channel_id=1, source_target_pairs={{0,8},{2,10},{4,12},{6,14},{8,0},{10,2},{12,4},{14,6},{16,24},{18,... | collective-permute-start | bytes 1769480 | tf_op jit(solution)/shard_map/ppermute | solution.py:885
  379.4 20.1 %collective-permute-start.59 = (bf16[384,768]{1,0:T(8,128)(2,1)}, bf16[384,768]{1,0:T(8,128)(2,1)S(1)}, u32[]{:S(2)}, u32[]{:S(2)}) collective-permute-start(bf16[384,768]{1,0:T(8,128)(2,1)} %get-tuple-element.347), channel_id=1, source_target_pairs={{0,4},{2,6},{4,0},{6,2},{8,12},{10,14},{12,8},{14,10},{16,20},{18,... | collective-permute-start | bytes 1769480 | tf_op jit(solution)/shard_map/ppermute | solution.py:885
  380.9 18.7 %collective-permute-start.58 = (bf16[384,768]{1,0:T(8,128)(2,1)}, bf16[384,768]{1,0:T(8,128)(2,1)S(1)}, u32[]{:S(2)}, u32[]{:S(2)}) collective-permute-start(bf16[384,768]{1,0:T(8,128)(2,1)} %get-tuple-element.345), channel_id=1, source_target_pairs={{0,1},{1,0},{2,3},{3,2},{4,5},{5,4},{6,7},{7,6},{8,9},{9,8},{10,11... | collective-permute-start | bytes 1769480 | tf_op jit(solution)/shard_map/ppermute | solution.py:884
  387.1 12.4 %collective-permute-start.62 = (bf16[48,1536]{1,0:T(8,128)(2,1)}, bf16[48,1536]{1,0:T(8,128)(2,1)S(1)}, u32[]{:S(2)}, u32[]{:S(2)}) collective-permute-start(bf16[48,1536]{1,0:T(8,128)(2,1)} %get-tuple-element.350), channel_id=1, source_target_pairs={{0,1},{1,0},{2,3},{3,2},{4,5},{5,4},{6,7},{7,6},{8,9},{9,8},{10,11... | collective-permute-start | bytes 442376 | tf_op jit(solution)/shard_map/ppermute | solution.py:884
  387.9 11.7 %collective-permute-start.61 = (bf16[48,1536]{1,0:T(8,128)(2,1)}, bf16[48,1536]{1,0:T(8,128)(2,1)S(1)}, u32[]{:S(2)}, u32[]{:S(2)}) collective-permute-start(bf16[48,1536]{1,0:T(8,128)(2,1)} %get-tuple-element.349), channel_id=1, source_target_pairs={{0,16},{2,18},{4,20},{6,22},{8,24},{10,26},{12,28},{14,30},{16,0},... | collective-permute-start | bytes 442376 | tf_op jit(solution)/shard_map/ppermute | solution.py:885
  392.5 15.2 %collective-permute-start.70 = (f32[10,768]{1,0:T(8,128)S(1)}, f32[10,768]{1,0:T(8,128)S(1)}, u32[]{:S(2)}, u32[]{:S(2)}) collective-permute-start(f32[10,768]{1,0:T(8,128)S(1)} %concatenate.39), channel_id=1, source_target_pairs={{0,1},{1,0},{2,3},{3,2},{4,5},{5,4},{6,7},{7,6},{8,9},{9,8},{10,11... | collective-permute-start | bytes 92168 | tf_op jit(solution)/shard_map/ppermute | solution.py:884
  399.6 15.4 %collective-permute-start.66 = (bf16[96,1536]{1,0:T(8,128)(2,1)}, bf16[96,1536]{1,0:T(8,128)(2,1)S(1)}, u32[]{:S(2)}, u32[]{:S(2)}) collective-permute-start(bf16[96,1536]{1,0:T(8,128)(2,1)} %add_up.22), channel_id=1, source_target_pairs={{0,16},{2,18},{4,20},{6,22},{8,24},{10,26},{12,28},{14,30},{16,0},... | collective-permute-start | bytes 884744 | tf_op jit(solution)/shard_map/ppermute | solution.py:885
  404.6 10.4 %collective-permute-start.65 = (bf16[192,768]{1,0:T(8,128)(2,1)}, bf16[192,768]{1,0:T(8,128)(2,1)S(1)}, u32[]{:S(2)}, u32[]{:S(2)}) collective-permute-start(bf16[192,768]{1,0:T(8,128)(2,1)} %get-tuple-element.357), channel_id=1, source_target_pairs={{0,1},{1,0},{2,3},{3,2},{4,5},{5,4},{6,7},{7,6},{8,9},{9,8},{10,11... | collective-permute-start | bytes 884744 | tf_op jit(solution)/shard_map/ppermute | solution.py:884
  405.9 9.1 %collective-permute-start.64 = (bf16[192,768]{1,0:T(8,128)(2,1)}, bf16[192,768]{1,0:T(8,128)(2,1)S(1)}, u32[]{:S(2)}, u32[]{:S(2)}) collective-permute-start(bf16[192,768]{1,0:T(8,128)(2,1)} %get-tuple-element.355), channel_id=1, source_target_pairs={{0,4},{2,6},{4,0},{6,2},{8,12},{10,14},{12,8},{14,10},{16,20},{18,... | collective-permute-start | bytes 884744 | tf_op jit(solution)/shard_map/ppermute | solution.py:885
  407.7 7.3 %collective-permute-start.71 = (f32[10,768]{1,0:T(8,128)S(1)}, f32[10,768]{1,0:T(8,128)S(1)}, u32[]{:S(2)}, u32[]{:S(2)}) collective-permute-start(f32[10,768]{1,0:T(8,128)S(1)} %add.150), channel_id=1, source_target_pairs={{0,4},{2,6},{4,0},{6,2},{8,12},{10,14},{12,8},{14,10},{16,20},{18,... | collective-permute-start | bytes 92168 | tf_op jit(solution)/shard_map/ppermute | solution.py:885
  414.3 30.2 %collective-permute-start.63 = (bf16[448,768]{1,0:T(8,128)(2,1)}, bf16[448,768]{1,0:T(8,128)(2,1)}, u32[]{:S(2)}, u32[]{:S(2)}) collective-permute-start(bf16[448,768]{1,0:T(8,128)(2,1)} %get-tuple-element.351), channel_id=1, source_target_pairs={{0,1},{1,0},{2,3},{3,2},{4,5},{5,4},{6,7},{7,6},{8,9},{9,8},{10,11... | collective-permute-start | bytes 2064392 | tf_op jit(solution)/shard_map/ppermute | solution.py:884
  415.1 15.0 %collective-permute-start.72 = (f32[10,768]{1,0:T(8,128)S(1)}, f32[10,768]{1,0:T(8,128)S(1)}, u32[]{:S(2)}, u32[]{:S(2)}) collective-permute-start(f32[10,768]{1,0:T(8,128)S(1)} %add.151), channel_id=1, source_target_pairs={{0,16},{2,18},{4,20},{6,22},{8,24},{10,26},{12,28},{14,30},{16,0},... | collective-permute-start | bytes 92168 | tf_op jit(solution)/shard_map/ppermute | solution.py:888
  416.1 14.1 %collective-permute-start.73 = (f32[10,768]{1,0:T(8,128)S(1)}, f32[10,768]{1,0:T(8,128)S(1)}, u32[]{:S(2)}, u32[]{:S(2)}) collective-permute-start(f32[10,768]{1,0:T(8,128)S(1)} %add.151), channel_id=1, source_target_pairs={{0,8},{2,10},{4,12},{6,14},{8,0},{10,2},{12,4},{14,6},{16,24},{18,... | collective-permute-start | bytes 92168 | tf_op jit(solution)/shard_map/ppermute | solution.py:888
  418.3 13.7 %collective-permute-start.74 = (f32[10,768]{1,0:T(8,128)S(1)}, f32[10,768]{1,0:T(8,128)S(1)}, u32[]{:S(2)}, u32[]{:S(2)}) collective-permute-start(f32[10,768]{1,0:T(8,128)S(1)} %add.151), channel_id=1, source_target_pairs={{0,24},{2,26},{4,28},{6,30},{8,16},{10,18},{12,20},{14,22},{16,8},... | collective-permute-start | bytes 92168 | tf_op jit(solution)/shard_map/ppermute | solution.py:888
  421.7 10.9 %collective-permute-start.69 = (bf16[96,768]{1,0:T(8,128)(2,1)}, bf16[96,768]{1,0:T(8,128)(2,1)S(1)}, u32[]{:S(2)}, u32[]{:S(2)}) collective-permute-start(bf16[96,768]{1,0:T(8,128)(2,1)} %get-tuple-element.364), channel_id=1, source_target_pairs={{0,24},{2,26},{4,28},{6,30},{8,16},{10,18},{12,20},{14,22},{16,8},... | collective-permute-start | bytes 442376 | tf_op jit(solution)/shard_map/ppermute | solution.py:888
  430.2 8.8 %collective-permute-start.67 = (bf16[96,768]{1,0:T(8,128)(2,1)S(1)}, bf16[96,768]{1,0:T(8,128)(2,1)S(1)}, u32[]{:S(2)}, u32[]{:S(2)}) collective-permute-start(bf16[96,768]{1,0:T(8,128)(2,1)S(1)} %copy-done.62), channel_id=1, source_target_pairs={{0,16},{2,18},{4,20},{6,22},{8,24},{10,26},{12,28},{14,30},{16,0},... | collective-permute-start | bytes 442376 | tf_op jit(solution)/shard_map/ppermute | solution.py:888
  (75 other events, 435.5 us)
